TPU v7x, 32 devices: a whole 2x2x4 slice. The times are simulated.
32 devices in a mesh: seq: 8 (over z, x), expert: 4 (over y, core).
Axes of the slice: x: 2, y: 2, z: 4, core: 2. Of those that a mesh axis runs over, the one named last changes fastest.
Arguments:
- byte_states: bfloat16 [8192, 512], P(('seq', 'expert')), may hold values from -6 to 6
- patch_start: int32 [8192], P(('seq', 'expert')), may hold values from 0 to 1, as said below
- expert_ids: int32 [1280, 2], P(('seq', 'expert')), may hold values from 0 to 3, all different within a row; in each aligned block of 40 rows (0 to 39, 40 to 79, ...) at most 24 rows name the same one
- enc_gain: float32 [512], replicated, may hold values from 0.1 to 1.9
- w_qkv: bfloat16 [512, 1536], replicated, may hold values from -0.25 to 0.25
- w_out: bfloat16 [512, 512], replicated, may hold values from -0.25 to 0.25
- w_xq: bfloat16 [512, 512], replicated, may hold values from -0.25 to 0.25
- w_xkv: bfloat16 [512, 1024], replicated, may hold values from -0.25 to 0.25
- w_up: bfloat16 [512, 2048], replicated, may hold values from -0.25 to 0.25
- moe_gain: float32 [2048], replicated, may hold values from 0.1 to 1.9
- w_router: float32 [2048, 4], replicated, may hold values from -0.03125 to 0.03125
- w_in: bfloat16 [4, 2048, 2, 6144], P('expert', None, None, 'seq'), may hold values from -0.125 to 0.125
- w_down: bfloat16 [4, 6144, 2048], P('expert', 'seq'), may hold values from -0.15625 to 0.15625
- dec_gain: float32 [512], replicated, may hold values from 0.1 to 1.9
- w_dq: bfloat16 [512, 512], replicated, may hold values from -0.25 to 0.25
- w_dkv: bfloat16 [2048, 1024], replicated, may hold values from -0.125 to 0.125
- w_do: bfloat16 [512, 512], replicated, may hold values from -0.25 to 0.25
Outputs:
- bytes_out: bfloat16 [8192, 512], P(('seq', 'expert'))
- patch_out: bfloat16 [1280, 2048], P(('seq', 'expert'))
Inputs may be any that keep to these rules, and one draw needn't show every extreme that they name: `patch_start`: the first byte of every block of 256 bytes has a 1; every block has between 20 and 40 ones, and some block has exactly 40. `expert_ids`: the two experts of a slot differ. Among the 80 entries of one block's slots no expert appears more than 24 times, and some expert appears exactly 24 times in some block.
All inputs are finite; a program needn't handle non-finite values.
Results may differ from a plain program's by a relative error of at most 0.025.
Values may be sent and summed in bfloat16 or wider, within the bound.
No kernel may reach another device: no remote copies, remote signals or barrier semaphores. Data moves between devices by JAX's collectives and lax.ppermute only.
A program may use at most 128 MiB of HBM per device.

v0:
```python
import math

import jax
import jax.numpy as jnp
from jax import lax
from jax.sharding import PartitionSpec as P

HEADS_L = 8
HEAD = 64
WINDOW = 512


epsilon = 1e-06
very_negative = -1e30


def passed_along(x, axis, by):
    length = lax.axis_size(axis)
    pairs = [(i, i + by) for i in range(length) if 0 <= i + by < length]
    return lax.ppermute(x, axis, pairs)


def rms_scale(inputs, gain_vector):
    widened = inputs.astype(jnp.float32)
    return (
        widened
        * lax.rsqrt(jnp.mean(widened * widened, axis=-1, keepdims=True) + epsilon)
        * gain_vector
    )


def softmax_rows(scores):
    highest = jnp.max(scores, axis=-1, keepdims=True)
    raised = jnp.exp(scores - highest)
    return raised / jnp.sum(raised, axis=-1, keepdims=True)


def heads_split(inputs):
    return inputs.reshape(inputs.shape[0], HEADS_L, HEAD).transpose(1, 0, 2)


def heads_merge(inputs):
    return inputs.transpose(1, 0, 2).reshape(inputs.shape[1], HEADS_L * HEAD)


def attend(queries, keys, values, allowed):
    scores = jnp.einsum(
        "hqd,hkd->hqk", queries, keys, preferred_element_type=jnp.float32
    ) / math.sqrt(HEAD)
    scores = jnp.where(allowed[None], scores, very_negative)
    weights = softmax_rows(scores).astype(jnp.bfloat16)
    mixed = jnp.einsum("hqk,hkd->hqd", weights, values, preferred_element_type=jnp.float32)
    return heads_merge(mixed)


def window_mask(query_place, key_place):
    later = key_place[None, :]
    return (later >= 0) & (later <= query_place[:, None]) & (later > query_place[:, None] - WINDOW)


def patch_block(encoded, flags, w_xq, w_xkv, w_up):
    patch_cap = encoded.shape[0] * 5 // 32
    patch_index = jnp.cumsum(flags) - 1
    patch_count = jnp.sum(flags)
    slot_list = jnp.arange(patch_cap, dtype=jnp.int32)
    member = patch_index[None, :] == slot_list[:, None]
    live = slot_list < patch_count
    pooled = jnp.max(
        jnp.where(member[:, :, None], encoded[None], jnp.asarray(very_negative, encoded.dtype)),
        axis=1,
    )
    pooled = jnp.where(live[:, None], pooled, jnp.zeros_like(pooled))
    queries = jnp.dot(pooled, w_xq, preferred_element_type=jnp.float32).astype(jnp.bfloat16)
    pairs = jnp.dot(encoded, w_xkv, preferred_element_type=jnp.float32).astype(jnp.bfloat16)
    width_local = pairs.shape[1] // 2
    mixed = attend(
        heads_split(queries),
        heads_split(pairs[:, :width_local]),
        heads_split(pairs[:, width_local:]),
        member,
    )
    patch_input = (pooled.astype(jnp.float32) + mixed).astype(jnp.bfloat16)
    state = jnp.dot(patch_input, w_up, preferred_element_type=jnp.float32)
    return jnp.where(live[:, None], state, jnp.zeros_like(state)).astype(jnp.bfloat16)


def decode_block(encoded, flags, states, dec_gain, w_dq, w_dkv, w_do):
    patch_index = jnp.cumsum(flags) - 1
    slot_list = jnp.arange(states.shape[0], dtype=jnp.int32)
    normed = rms_scale(encoded, dec_gain).astype(jnp.bfloat16)
    queries = jnp.dot(normed, w_dq, preferred_element_type=jnp.float32).astype(jnp.bfloat16)
    pairs = jnp.dot(states, w_dkv, preferred_element_type=jnp.float32).astype(jnp.bfloat16)
    width_local = pairs.shape[1] // 2
    allowed = slot_list[None, :] <= patch_index[:, None]
    mixed = attend(
        heads_split(queries),
        heads_split(pairs[:, :width_local]),
        heads_split(pairs[:, width_local:]),
        allowed,
    ).astype(jnp.bfloat16)
    return (
        encoded.astype(jnp.float32) + jnp.dot(mixed, w_do, preferred_element_type=jnp.float32)
    ).astype(jnp.bfloat16)


def route_slots(expert_ids, experts):
    flat = expert_ids.reshape(-1)
    onehot = (flat[:, None] == jnp.arange(experts, dtype=jnp.int32)[None, :]).astype(jnp.int32)
    ranked = jnp.cumsum(onehot, axis=0) - 1
    return jnp.sum(ranked * onehot, axis=1).reshape(expert_ids.shape)


def mixture(patch_state, expert_ids, moe_gain, w_router, w_in, w_down):
    patch_cap = patch_state.shape[0]
    global_width = patch_state.shape[1]
    experts = w_router.shape[1]
    local_experts = w_in.shape[0]
    expert_devices = experts // local_experts
    capacity = 12 * patch_cap // (5 * experts)
    hidden_share = w_in.shape[3]
    normed = rms_scale(patch_state, moe_gain).astype(jnp.bfloat16)
    logits = jnp.dot(normed.astype(jnp.float32), w_router, precision=lax.Precision.HIGHEST)
    gates = softmax_rows(jnp.take_along_axis(logits, expert_ids, axis=1))
    slot_number = route_slots(expert_ids, experts)
    target = (
        expert_ids // local_experts * capacity + slot_number
    ) * local_experts + expert_ids % local_experts
    places = jnp.arange(experts * capacity, dtype=jnp.int32)
    dispatch = jnp.sum((target[None, :, :] == places[:, None, None]).astype(jnp.bfloat16), axis=2)
    routed = jnp.dot(dispatch, normed, preferred_element_type=jnp.float32).astype(jnp.bfloat16)
    arrived = lax.all_to_all(
        routed.reshape(expert_devices, capacity * local_experts, global_width),
        "expert",
        split_axis=0,
        concat_axis=0,
        tiled=True,
    )
    rows = arrived.reshape(expert_devices * capacity, local_experts, global_width)
    paired = w_in.reshape(local_experts, global_width, 2 * hidden_share)
    both = jnp.einsum(
        "red,edk->rek",
        lax.all_gather(rows, "seq", axis=0, tiled=True),
        paired,
        preferred_element_type=jnp.float32,
    )
    hidden = (jax.nn.silu(both[..., :hidden_share]) * both[..., hidden_share:]).astype(jnp.bfloat16)
    term = jnp.einsum("ref,efd->red", hidden, w_down, preferred_element_type=jnp.float32).astype(
        jnp.bfloat16
    )
    term = lax.optimization_barrier(term)
    summed = lax.psum_scatter(
        term.astype(jnp.float32).astype(jnp.bfloat16), "seq", scatter_dimension=0, tiled=True
    )
    results = summed.reshape(expert_devices, capacity * local_experts, global_width)
    returned = lax.all_to_all(results, "expert", split_axis=0, concat_axis=0, tiled=True)
    chosen = returned.reshape(experts * capacity, global_width)[target]
    combined = jnp.sum(gates[..., None] * chosen.astype(jnp.float32), axis=1)
    return (patch_state.astype(jnp.float32) + combined).astype(jnp.bfloat16)


def per_device(
    byte_states,
    patch_start,
    expert_ids,
    enc_gain,
    w_qkv,
    w_out,
    w_xq,
    w_xkv,
    w_up,
    moe_gain,
    w_router,
    w_in,
    w_down,
    dec_gain,
    w_dq,
    w_dkv,
    w_do,
):
    byte_dev = byte_states.shape[0]
    model_width = byte_states.shape[1]
    normed = rms_scale(byte_states, enc_gain).astype(jnp.bfloat16)
    projected = jnp.dot(normed, w_qkv, preferred_element_type=jnp.float32).astype(jnp.bfloat16)
    queries = projected[:, :model_width]
    own_pairs = projected[:, model_width:]
    reach = -(-WINDOW // byte_dev)
    earlier = []
    for distance in range(reach, 0, -1):
        moved = passed_along(normed, ("seq", "expert"), distance)
        earlier.append(
            jnp.dot(moved, w_qkv[:, model_width:], preferred_element_type=jnp.float32).astype(
                jnp.bfloat16
            )
        )
    pairs = jnp.concatenate(earlier + [own_pairs], axis=0)
    offset = lax.axis_index(("seq", "expert")) * byte_dev
    query_place = offset + jnp.arange(byte_dev, dtype=jnp.int32)
    key_place = offset - reach * byte_dev + jnp.arange((reach + 1) * byte_dev, dtype=jnp.int32)
    mixed = attend(
        heads_split(queries),
        heads_split(pairs[:, :model_width]),
        heads_split(pairs[:, model_width:]),
        window_mask(query_place, key_place),
    ).astype(jnp.bfloat16)
    encoded = (
        byte_states.astype(jnp.float32) + jnp.dot(mixed, w_out, preferred_element_type=jnp.float32)
    ).astype(jnp.bfloat16)
    patch_state = patch_block(encoded, patch_start, w_xq, w_xkv, w_up)
    patch_out = mixture(patch_state, expert_ids, moe_gain, w_router, w_in, w_down)
    bytes_out = decode_block(encoded, patch_start, patch_out, dec_gain, w_dq, w_dkv, w_do)
    return (bytes_out, patch_out)


def solution(mesh):
    in_specs = (
        P(("seq", "expert"), None),
        P(("seq", "expert")),
        P(("seq", "expert"), None),
        P(),
        P(),
        P(),
        P(),
        P(),
        P(),
        P(),
        P(),
        P("expert", None, None, "seq"),
        P("expert", "seq", None),
        P(),
        P(),
        P(),
        P(),
    )
    out_specs = (P(("seq", "expert"), None), P(("seq", "expert"), None))
    return jax.shard_map(
        per_device, mesh=mesh, in_specs=in_specs, out_specs=out_specs, check_vma=False
    )
```

profile of v0, /device:TPU:0, one launch (start us, length us, event | category | flops | bytes accessed | tf_op | source)
XLA Modules:
  0.0 259.5 jit_solution(14362653059563799152)
XLA Ops:
  7.2 1.2 fusion.31
  8.5 1.1 fusion.33
  9.6 3.1 %collective-permute-start.1 = (bf16[256,512]{1,0:T(8,128)(2,1)S(1)}, bf16[256,512]{1,0:T(8,128)(2,1)}, u32[]{:S(2)}, u32[]{:S(2)}) collective-permute-start(bf16[256,512]{1,0:T(8,128)(2,1)S(1)} %fusion.33), channel_id=1, source_target_pairs={{0,1},{1,2},{2,3},{3,4},{4,5},{5,6},{6,7},{7,8},{8,9},{9,10},{10,1... | collective-permute-start | bytes 786440 | tf_op jit(solution)/shard_map/ppermute | solution.py:20
  12.7 4.5 %collective-permute-start = (bf16[256,512]{1,0:T(8,128)(2,1)S(1)}, bf16[256,512]{1,0:T(8,128)(2,1)}, u32[]{:S(2)}, u32[]{:S(2)}) collective-permute-start(bf16[256,512]{1,0:T(8,128)(2,1)S(1)} %fusion.33), channel_id=1, source_target_pairs={{0,2},{1,3},{2,4},{3,5},{4,6},{5,7},{6,8},{7,9},{8,10},{9,11},{10,... | collective-permute-start | bytes 786440 | tf_op jit(solution)/shard_map/ppermute | solution.py:20
  17.1 2.9 %convolution_convert_fusion.1 = bf16[256,1536]{1,0:T(8,128)(2,1)} fusion(bf16[256,512]{1,0:T(8,128)(2,1)S(1)} %fusion.33, bf16[512,1536]{1,0:T(8,128)(2,1)} %param.21), kind=kOutput, calls=%fused_computation.19 | convolution fusion | flops 403046400 | bytes 2621440 | tf_op jit(solution)/shard_map/dot_general | solution.py:183
  20.0 0.6 reduce_sum.105
  20.6 0.3 reduce-window.9
  21.7 0.2 select_reduce_fusion.1
  22.2 0.7 iota_compare_fusion.4
  22.8 1.7 slice.58
  24.5 1.8 copy.79
  26.3 1.0 compare_and_fusion
  27.2 1.8 convolution_convert_fusion.4
  29.0 1.8 convolution_convert_fusion.5
  30.9 1.3 fusion.62
  32.2 2.3 copy.80
  34.5 2.3 copy.81
  36.8 6.2 %fusion.65 = (f32[8,256]{1,0:T(8,128)S(1)}, f32[8,256,768]{2,1,0:T(8,128)}) fusion(pred[256,768]{1,0:T(8,128)(4,1)} %compare_and_fusion, bf16[8,256,64]{1,2,0:T(8,128)(2,1)S(1)} %bitcast.113, bf16[8,768,64]{1,2,0:T(8,128)(2,1)} %bitcast.109), kind=kOutput, calls=%fused_computation.120 | convolution fusion | flops 207618816 | bytes 7544832 | tf_op jit(solution)/shard_map/sub | solution.py:34
  43.0 4.2 %fusion.20 = bf16[8,256,64]{1,2,0:T(8,128)(2,1)S(1)} fusion(bf16[8,768,64]{1,2,0:T(8,128)(2,1)} %bitcast.110, f32[8,256,768]{2,1,0:T(8,128)} %get-tuple-element.13, f32[8,256]{1,0:T(8,128)S(1)} %get-tuple-element.12), kind=kOutput, calls=%fused_computation.38 | convolution fusion | flops 204603392 | bytes 7348224 | tf_op jit(solution)/shard_map/hqk,hkd->hqd/dot_general | solution.py:52
  47.2 1.0 fusion.34
  48.2 1.8 select_reduce_fusion
  50.0 0.2 convolution_convert_fusion.9
  50.3 0.8 reshape.325
  51.0 1.7 convolution_convert_fusion.3
  52.7 0.8 fusion.63
  53.5 1.8 copy.84
  55.3 1.2 fusion.22
  56.5 0.7 copy-done.4
  57.2 0.2 fusion.66
  57.4 1.8 copy.85
  59.2 2.4 convolution_bitcast_fusion.1
  61.6 1.6 copy.86
  63.2 1.6 reshape.328
  64.9 2.3 multiply_reduce_fusion.1
  67.2 0.3 convolution_convert_fusion.2
  67.5 10.5 %all_to_all.10 = bf16[4,24,2048]{2,1,0:T(8,128)(2,1)} all-to-all(bf16[4,24,2048]{2,1,0:T(8,128)(2,1)S(1)} %bitcast.106), channel_id=1, replica_groups=mesh['seq'=8,'expert'=4] {'expert'}, dimensions={0} | all-to-all | bytes 786432 | tf_op jit(solution)/shard_map/all_to_all | solution.py:131
  78.0 0.2 reduce-scatter.2.cloned.1.call-start
  78.3 6.8 %copy.95 = bf16[256,8,2,768]{3,1,2,0:T(8,128)(2,1)} copy(bf16[256,8,2,768]{3,2,1,0:T(2,128)(2,1)} %bitcast.103) | data formatting | bytes 12582912
  85.1 53.2 %all-gather.2.cloned.1.call-done = bf16[768,1,2048]{2,0,1:T(8,128)(2,1)} async-done(((bf16[96,1,2048]{2,0,1:T(8,128)(2,1)}), bf16[768,1,2048]{2,0,1:T(8,128)(2,1)}) %all-gather.2.cloned.1.call-update) | async-done | bytes 3145744 | tf_op jit(solution)/shard_map/all_gather | solution.py:142
  138.3 8.1 %convolution_bitcast_fusion = f32[768,1,1536]{2,0,1:T(8,128)S(1)} fusion(bf16[2048,1536]{1,0:T(8,128)(2,1)} %bitcast.104, bf16[768,1,2048]{2,0,1:T(8,128)(2,1)} %all-gather.2.cloned.1.call-done), kind=kOutput, calls=%fused_computation.10 | convolution fusion | flops 4831838208 | bytes 14155776 | tf_op jit(solution)/shard_map/red,edk->rek/dot_general | solution.py:140
  146.4 4.1 %fusion.10 = bf16[768,1,2048]{2,0,1:T(8,128)(2,1)} fusion(bf16[1,768,2048]{2,1,0:T(8,128)(2,1)S(1)} %copy-done, f32[768,1,1536]{2,0,1:T(8,128)S(1)} %convolution_bitcast_fusion), kind=kOutput, calls=%fused_computation.18 | convolution fusion | flops 2421030912 | bytes 11010048 | tf_op jit(solution)/shard_map/ref,efd->red/dot_general | solution.py:147
  150.9 0.2 copy-done.15
  151.2 1.0 fusion.60
  152.2 2.1 gather_fusion.1
  154.5 0.5 fusion.53
  155.0 68.4 %reduce-scatter.2.cloned.1.call-done = bf16[96,1,2048]{2,0,1:T(8,128)(2,1)} async-done(((bf16[768,1,2048]{2,0,1:T(8,128)(2,1)}), bf16[96,1,2048]{2,0,1:T(8,128)(2,1)}) %reduce-scatter.2.cloned.1.call-update) | async-done | bytes 393232 | tf_op jit(solution)/shard_map/reduce_scatter | solution.py:151
  223.4 3.5 %all-to-all-start.1 = ((bf16[4,24,2048]{2,1,0:T(8,128)(2,1)}), bf16[4,24,2048]{2,1,0:T(8,128)(2,1)S(1)}, u32[]{:S(2)}, u32[]{:S(2)}) async-start(bf16[4,24,2048]{2,1,0:T(8,128)(2,1)} %bitcast.111), calls=%async_computation.2 | async-start | bytes 786432 | tf_op jit(solution)/shard_map/all_to_all | solution.py:155
  226.9 1.3 add_rsqrt_fusion
  228.2 1.3 copy.89
  229.5 2.2 convolution_convert_fusion.7
  231.6 1.8 copy.82
  233.4 0.9 all-to-all-done.1
  234.3 1.5 gather_fusion
  235.8 2.2 reshape.357
  238.1 2.0 multiply_reduce_fusion
  240.1 1.0 add_convert_fusion
  241.1 0.7 copy-done.6
  241.8 3.1 %convolution_convert_fusion.8 = bf16[40,1024]{1,0:T(8,128)(2,1)S(1)} fusion(bf16[40,2048]{1,0:T(8,128)(2,1)S(1)} %add_convert_fusion, bf16[2048,1024]{1,0:T(8,128)(2,1)} %param.32), kind=kOutput, calls=%fused_computation.47 | convolution fusion | flops 167813120 | bytes 4440064 | tf_op jit(solution)/shard_map/dot_general | solution.py:92
  244.9 0.6 fusion.64
  245.5 0.9 reshape.339
  246.4 1.1 fusion.21
  247.5 0.7 copy-done.8
  248.4 2.0 convolution_convert_fusion.6
  250.5 2.1 fusion.19
  (73 shorter events, 2.2 us)
Async XLA Ops:
  7.2 139.2 %copy-start = (bf16[1,768,2048]{2,1,0:T(8,128)(2,1)S(1)}, bf16[1,768,2048]{2,1,0:T(8,128)(2,1)}, u32[]{:S(2)}) copy-start(bf16[1,768,2048]{2,1,0:T(8,128)(2,1)} %param.29) | copy-start | bytes 9437188
  7.2 12.8 %copy-start.16 = (s32[256]{0:T(256)S(1)}, s32[256]{0:T(256)}, u32[]{:S(2)}) copy-start(s32[256]{0:T(256)} %param.18) | copy-start | bytes 3076
  7.2 14.1 %copy-start.12 = (s32[40,2]{0,1:T(2,128)S(1)}, s32[40,2]{0,1:T(2,128)}, u32[]{:S(2)}) copy-start(s32[40,2]{0,1:T(2,128)} %param.19) | copy-start | bytes 964
  7.2 131.1 %all-gather.2.cloned.1.call-start = ((), (), s32[]{:S(2)}) async-start(), calls=%async_computation.3 | async-start | bytes 3538944 | tf_op jit(solution)/shard_map/all_gather | solution.py:142
  9.6 17.7 %collective-permute-start.1 = (bf16[256,512]{1,0:T(8,128)(2,1)S(1)}, bf16[256,512]{1,0:T(8,128)(2,1)}, u32[]{:S(2)}, u32[]{:S(2)}) collective-permute-start(bf16[256,512]{1,0:T(8,128)(2,1)S(1)} %fusion.33), channel_id=1, source_target_pairs={{0,1},{1,2},{2,3},{3,4},{4,5},{5,6},{6,7},{7,8},{8,9},{9,10},{10,1... | collective-permute-start | bytes 786440 | tf_op jit(solution)/shard_map/ppermute | solution.py:20
  12.7 16.3 %collective-permute-start = (bf16[256,512]{1,0:T(8,128)(2,1)S(1)}, bf16[256,512]{1,0:T(8,128)(2,1)}, u32[]{:S(2)}, u32[]{:S(2)}) collective-permute-start(bf16[256,512]{1,0:T(8,128)(2,1)S(1)} %fusion.33), channel_id=1, source_target_pairs={{0,2},{1,3},{2,4},{3,5},{4,6},{5,7},{6,8},{7,9},{8,10},{9,11},{10,... | collective-permute-start | bytes 786440 | tf_op jit(solution)/shard_map/ppermute | solution.py:20
  21.2 9.5 %copy-start.14 = (s32[256]{0:T(256)}, s32[256]{0:T(256)S(1)}, u32[]{:S(2)}) copy-start(s32[256]{0:T(256)S(1)} %add_bitcast_fusion) | copy-start | bytes 3076
  22.8 27.2 %copy-start.17 = (pred[40]{0:T(512)(128)(4,1)}, pred[40]{0:T(512)(128)(4,1)S(1)}, u32[]{:S(2)}) copy-start(pred[40]{0:T(512)(128)(4,1)S(1)} %iota_compare_fusion.4) | copy-start | bytes 124
  26.3 4.5 %slice-start = ((bf16[256,1536]{1,0:T(8,128)(2,1)}), bf16[256,1024]{1,0:T(8,128)(2,1)S(1)}, s32[]{:S(2)}) async-start(bf16[256,1536]{1,0:T(8,128)(2,1)} %convolution_convert_fusion.1), calls=%async_computation.5 | async-start | bytes 1048576 | tf_op jit(solution)/shard_map/slice | solution.py:185
  30.9 5.9 %copy-start.9 = (bf16[256,512]{0,1:T(8,128)(2,1)S(1)}, bf16[256,512]{0,1:T(8,128)(2,1)}, u32[]{:S(2)}) copy-start(bf16[256,512]{0,1:T(8,128)(2,1)} %copy.79) | copy-start | bytes 786436
  43.0 4.2 %copy-start.5 = (bf16[256,512]{1,0:T(8,128)(2,1)S(1)}, bf16[256,512]{1,0:T(8,128)(2,1)}, u32[]{:S(2)}) copy-start(bf16[256,512]{1,0:T(8,128)(2,1)} %param.17) | copy-start | bytes 786436
  43.0 4.2 %copy-start.18 = (bf16[512,512]{1,0:T(8,128)(2,1)S(1)}, bf16[512,512]{1,0:T(8,128)(2,1)}, u32[]{:S(2)}) copy-start(bf16[512,512]{1,0:T(8,128)(2,1)} %param.22) | copy-start | bytes 1572868
  43.0 7.1 %copy-start.7 = (bf16[512,512]{1,0:T(8,128)(2,1)S(1)}, bf16[512,512]{1,0:T(8,128)(2,1)}, u32[]{:S(2)}) copy-start(bf16[512,512]{1,0:T(8,128)(2,1)} %param.23) | copy-start | bytes 1572868
  48.2 13.5 %copy-start.2 = (bf16[256,512]{1,0:T(8,128)(2,1)}, bf16[256,512]{1,0:T(8,128)(2,1)S(1)}, u32[]{:S(2)}) copy-start(bf16[256,512]{1,0:T(8,128)(2,1)S(1)} %get-tuple-element.15) | copy-start | bytes 786436
  55.3 11.9 %copy-start.10 = (f32[2048]{0:T(1024)S(1)}, f32[2048]{0:T(1024)}, u32[]{:S(2)}) copy-start(f32[2048]{0:T(1024)} %param.26) | copy-start | bytes 24580
  56.5 0.7 copy-start.4
  67.2 84.0 %copy-start.1 = (f32[40,2048]{1,0:T(8,128)}, f32[40,2048]{1,0:T(8,128)S(1)}, u32[]{:S(2)}) copy-start(f32[40,2048]{1,0:T(8,128)S(1)} %get-tuple-element.17) | copy-start | bytes 983044
  78.0 145.4 %reduce-scatter.2.cloned.1.call-start = ((), (), s32[]{:S(2)}) async-start(), calls=%async_computation.4 | async-start | bytes 3538944 | tf_op jit(solution)/shard_map/reduce_scatter | solution.py:151
  150.4 0.7 copy-start.15
  150.4 0.7 copy-start.11
  152.2 2.3 copy-start.13
  223.4 10.9 %all-to-all-start.1 = ((bf16[4,24,2048]{2,1,0:T(8,128)(2,1)}), bf16[4,24,2048]{2,1,0:T(8,128)(2,1)S(1)}, u32[]{:S(2)}, u32[]{:S(2)}) async-start(bf16[4,24,2048]{2,1,0:T(8,128)(2,1)} %bitcast.111), calls=%async_computation.2 | async-start | bytes 786432 | tf_op jit(solution)/shard_map/all_to_all | solution.py:155
  241.1 0.7 copy-start.6
  241.8 8.7 %copy-start.3 = (bf16[256,512]{1,0:T(8,128)(2,1)S(1)}, bf16[256,512]{1,0:T(8,128)(2,1)}, u32[]{:S(2)}) copy-start(bf16[256,512]{1,0:T(8,128)(2,1)} %copy-done.2) | copy-start | bytes 786436
  247.5 0.7 copy-start.8
Sparse Core Ops, SparseCore 0:
  78.2 60.0 all-gather.1
  150.6 72.8 reduce-scatter.1
where the time goes:
time: 261 us; the launch traced here: 259 us
  waiting for transfers between devices  123 us (47%)
  matrix products  49.6 us (19%)
  local copies, waits for them, and re-layouts  38.5 us (15%)
  between operations  14.4 us (6%)
  other arithmetic  12.6 us (5%)
  starting transfers between devices  11.2 us (4%)
  blocking collectives  10.5 us (4%)
    reduce_scatter x1, waiting for transfers between devices, mixture(): lax.psum_scatter(term.astype(jnp.float32).astype(jnp.bfloat16), 'seq', sc...  68.4 us
    all_gather x1, waiting for transfers between devices, mixture(): lax.all_gather(rows, 'seq', axis=0, tiled=True)  53.2 us
    all_to_all x1, blocking collectives, mixture(): lax.all_to_all(routed.reshape(expert_devices, capacity * local_experts, g...  10.5 us
    unnamed x40, local copies, waits for them, and re-layouts  9.24 us
    dot_general x3, matrix products, attend(): jnp.einsum('hqk,hkd->hqd', weights, values, preferred_element_type=jnp.fl...  8.68 us
    dot_general x1, matrix products, mixture(): jnp.einsum('red,edk->rek', lax.all_gather(rows, 'seq', axis=0, tiled=True...  8.08 us
    ppermute x2, starting transfers between devices, passed_along(): return lax.ppermute(x, axis, pairs)  7.53 us
    sub x1, matrix products, softmax_rows(): raised = jnp.exp(scores - highest)  6.15 us
  transfers between devices with their start and end apart: 5, of which 3 were waited for; matrix products, arithmetic and copies ran while one was open for 11% of the time, Pallas kernels for 0%

commit v1 on v0

--- a/solution.py
+++ b/solution.py
@@ -58,7 +58,7 @@
     return (later >= 0) & (later <= query_place[:, None]) & (later > query_place[:, None] - WINDOW)
 
 
-def patch_block(encoded, flags, w_xq, w_xkv, w_up):
+def patch_block(encoded, flags, w_xq, w_xkv):
     patch_cap = encoded.shape[0] * 5 // 32
     patch_index = jnp.cumsum(flags) - 1
     patch_count = jnp.sum(flags)
@@ -79,9 +79,8 @@
         heads_split(pairs[:, width_local:]),
         member,
     )
-    patch_input = (pooled.astype(jnp.float32) + mixed).astype(jnp.bfloat16)
-    state = jnp.dot(patch_input, w_up, preferred_element_type=jnp.float32)
-    return jnp.where(live[:, None], state, jnp.zeros_like(state)).astype(jnp.bfloat16)
+    patch_input = jnp.where(live[:, None], pooled.astype(jnp.float32) + mixed, 0.0)
+    return patch_input.astype(jnp.bfloat16)
 
 
 def decode_block(encoded, flags, states, dec_gain, w_dq, w_dkv, w_do):
@@ -110,52 +109,105 @@
     return jnp.sum(ranked * onehot, axis=1).reshape(expert_ids.shape)
 
 
-def mixture(patch_state, expert_ids, moe_gain, w_router, w_in, w_down):
-    patch_cap = patch_state.shape[0]
-    global_width = patch_state.shape[1]
+def digits():
+    seq, expert = lax.axis_size("seq"), lax.axis_size("expert")
+    inner = 2 if seq % 2 == 0 else 1
+    core = 2 if expert % 2 == 0 else 1
+    return {
+        "z": ("seq", inner, seq // inner),
+        "x": ("seq", 1, inner),
+        "y": ("expert", core, expert // core),
+        "c": ("expert", 1, core),
+    }
+
+
+def shift(x, digit, by):
+    axis, stride, radix = digit
+    pairs = []
+    for i in range(lax.axis_size(axis)):
+        g = i // stride % radix
+        pairs.append((i, i + ((g + by) % radix - g) * stride))
+    return lax.ppermute(x, axis, pairs)
+
+
+def gathered(x, digit, place=0):
+    return jnp.stack([x] + [shift(x, digit, d) for d in range(1, digit[2])], axis=place)
+
+
+def gather_all(x):
+    d = digits()
+    half = x.shape[1] // 2
+    x = gathered(x, d["z"])
+    left = gathered(gathered(x[..., :half], d["x"]), d["y"])
+    right = gathered(gathered(x[..., half:], d["y"]), d["x"], 1)
+    return gathered(jnp.concatenate([left, right], axis=-1), d["c"])
+
+
+def summed(parts):
+    total = parts[0].astype(jnp.float32)
+    for part in parts[1:]:
+        total = total + part.astype(jnp.float32)
+    return total
+
+
+def reduced(x, digit, place=0):
+    parts = [lax.index_in_dim(x, d, place, keepdims=False) for d in range(digit[2])]
+    return summed([parts[0]] + [shift(parts[d], digit, -d) for d in range(1, digit[2])])
+
+
+def scatter_all(x):
+    d = digits()
+    half = x.shape[-1] // 2
+
+    def narrow(v):
+        return v.astype(jnp.bfloat16)
+
+    left = narrow(reduced(x[..., :half], d["c"]))
+    right = narrow(reduced(x[..., half:], d["c"]))
+    left = narrow(reduced(narrow(reduced(left, d["x"], 1)), d["y"]))
+    right = narrow(reduced(narrow(reduced(right, d["y"])), d["x"]))
+    return reduced(jnp.concatenate([left, right], axis=-1), d["z"])
+
+
+def mixture(patch_input, expert_ids, w_up, moe_gain, w_router, w_in, w_down):
+    patch_cap, local_width = patch_input.shape
     experts = w_router.shape[1]
-    local_experts = w_in.shape[0]
-    expert_devices = experts // local_experts
+    hidden_share = w_in.shape[3]
     capacity = 12 * patch_cap // (5 * experts)
-    hidden_share = w_in.shape[3]
-    normed = rms_scale(patch_state, moe_gain).astype(jnp.bfloat16)
+    target = expert_ids * capacity + route_slots(expert_ids, experts)
+    table = jnp.pad(target.T.astype(jnp.bfloat16), ((0, 6), (0, local_width - patch_cap)))
+    gathered_rows = gather_all(jnp.concatenate([patch_input, table], axis=0))
+    lead = gathered_rows.shape[:4]
+    everything = gathered_rows.reshape((-1,) + gathered_rows.shape[4:])
+    sources = everything.shape[0]
+    rows = everything[:, :patch_cap]
+    targets = everything[:, patch_cap : patch_cap + 2, :patch_cap].astype(jnp.int32)
+    me = lax.axis_index("expert")
+    places = me * capacity + jnp.arange(capacity, dtype=jnp.int32)
+    hit = targets[:, :, None, :] == places[None, None, :, None]
+    dispatch = jnp.any(hit, axis=1)
+    other = jnp.sum(jnp.where(hit, targets[:, ::-1, None, :] // capacity, 0), axis=(1, 3))
+    one_hot = dispatch.astype(jnp.bfloat16)
+    routed = jnp.einsum("scp,spd->scd", one_hot, rows, preferred_element_type=jnp.float32)
+    routed = routed.astype(jnp.bfloat16).reshape(sources * capacity, local_width)
+    state = jnp.dot(routed, w_up, preferred_element_type=jnp.float32).astype(jnp.bfloat16)
+    normed = rms_scale(state, moe_gain).astype(jnp.bfloat16)
     logits = jnp.dot(normed.astype(jnp.float32), w_router, precision=lax.Precision.HIGHEST)
-    gates = softmax_rows(jnp.take_along_axis(logits, expert_ids, axis=1))
-    slot_number = route_slots(expert_ids, experts)
-    target = (
-        expert_ids // local_experts * capacity + slot_number
-    ) * local_experts + expert_ids % local_experts
-    places = jnp.arange(experts * capacity, dtype=jnp.int32)
-    dispatch = jnp.sum((target[None, :, :] == places[:, None, None]).astype(jnp.bfloat16), axis=2)
-    routed = jnp.dot(dispatch, normed, preferred_element_type=jnp.float32).astype(jnp.bfloat16)
-    arrived = lax.all_to_all(
-        routed.reshape(expert_devices, capacity * local_experts, global_width),
-        "expert",
-        split_axis=0,
-        concat_axis=0,
-        tiled=True,
-    )
-    rows = arrived.reshape(expert_devices * capacity, local_experts, global_width)
-    paired = w_in.reshape(local_experts, global_width, 2 * hidden_share)
-    both = jnp.einsum(
-        "red,edk->rek",
-        lax.all_gather(rows, "seq", axis=0, tiled=True),
-        paired,
-        preferred_element_type=jnp.float32,
-    )
-    hidden = (jax.nn.silu(both[..., :hidden_share]) * both[..., hidden_share:]).astype(jnp.bfloat16)
-    term = jnp.einsum("ref,efd->red", hidden, w_down, preferred_element_type=jnp.float32).astype(
-        jnp.bfloat16
-    )
-    term = lax.optimization_barrier(term)
-    summed = lax.psum_scatter(
-        term.astype(jnp.float32).astype(jnp.bfloat16), "seq", scatter_dimension=0, tiled=True
-    )
-    results = summed.reshape(expert_devices, capacity * local_experts, global_width)
-    returned = lax.all_to_all(results, "expert", split_axis=0, concat_axis=0, tiled=True)
-    chosen = returned.reshape(experts * capacity, global_width)[target]
-    combined = jnp.sum(gates[..., None] * chosen.astype(jnp.float32), axis=1)
-    return (patch_state.astype(jnp.float32) + combined).astype(jnp.bfloat16)
+    own_logit = jnp.sum(jnp.where(jnp.arange(experts)[None] == me, logits, 0.0), axis=1)
+    other_logit = jnp.sum(
+        jnp.where(jnp.arange(experts)[None] == other.reshape(-1, 1), logits, 0.0), axis=1
+    )
+    gates = softmax_rows(jnp.stack([own_logit, other_logit], axis=1))[:, :1]
+    paired = w_in.reshape(w_in.shape[1], 2 * hidden_share)
+    both = jnp.dot(normed, paired, preferred_element_type=jnp.float32)
+    hidden = (jax.nn.silu(both[:, :hidden_share]) * both[:, hidden_share:]).astype(jnp.bfloat16)
+    term = jnp.dot(hidden, w_down[0], preferred_element_type=jnp.float32)
+    term = (term * gates).astype(jnp.bfloat16).reshape(sources, capacity, -1)
+    spread = jnp.einsum("scp,scd->spd", one_hot, term, preferred_element_type=jnp.float32)
+    spread = spread.astype(jnp.bfloat16)
+    combined = scatter_all(spread.reshape(lead + spread.shape[1:]))
+    own_state = jnp.dot(patch_input, w_up, preferred_element_type=jnp.float32).astype(jnp.bfloat16)
+    return (own_state.astype(jnp.float32) + combined).astype(jnp.bfloat16)
 
 
 def per_device(
@@ -205,8 +257,8 @@
     encoded = (
         byte_states.astype(jnp.float32) + jnp.dot(mixed, w_out, preferred_element_type=jnp.float32)
     ).astype(jnp.bfloat16)
-    patch_state = patch_block(encoded, patch_start, w_xq, w_xkv, w_up)
-    patch_out = mixture(patch_state, expert_ids, moe_gain, w_router, w_in, w_down)
+    patch_input = patch_block(encoded, patch_start, w_xq, w_xkv)
+    patch_out = mixture(patch_input, expert_ids, w_up, moe_gain, w_router, w_in, w_down)
     bytes_out = decode_block(encoded, patch_start, patch_out, dec_gain, w_dq, w_dkv, w_do)
     return (bytes_out, patch_out)
 

time: 261 us -> 180 us (0.69)
  waiting for transfers between devices: 123 us -> 47 us
  starting transfers between devices: 11.2 us -> 25.2 us
  between operations: 14.4 us -> 1.31 us
  blocking collectives: 10.5 us -> 0 us
  matrix products: 49.6 us -> 55.1 us
  local copies, waits for them, and re-layouts: 38.5 us -> 33.8 us
  other arithmetic: 12.6 us -> 16.9 us
    reduce_scatter x1 -> x0, waiting for transfers between devices: 68.4 us -> none  [mixture(): lax.psum_scatter(term.astype(jnp.float32).astype(jnp.bfloat16), 'seq', sc...]
    all_gather x1 -> x0, waiting for transfers between devices: 53.2 us -> none  [mixture(): lax.all_gather(rows, 'seq', axis=0, tiled=True)]
    ppermute x0 -> x17, waiting for transfers between devices: none -> 47 us  [shift(): return lax.ppermute(x, axis, pairs)]
    ppermute x0 -> x17, starting transfers between devices: none -> 17.7 us  [shift(): return lax.ppermute(x, axis, pairs)]
    all_to_all x1 -> x0, blocking collectives: 10.5 us -> none  [mixture(): lax.all_to_all(routed.reshape(expert_devices, capacity * local_experts, g...]
    dot_general x4 -> x6, matrix products: 14.7 us -> 19.4 us  [the longest x1 7.52 us: mixture(): both = jnp.dot(normed, paired, preferred_element_type=jnp.float32)]
    gather x6 -> x0, local copies, waits for them, and re-layouts: 3.95 us -> none  [the longest x5 2.44 us: mixture(): gates = softmax_rows(jnp.take_along_axis(logits, expert_ids, axis=1))]
    dot_general x1, matrix products: 1.03 us -> 4.7 us  [mixture(): jnp.dot(normed.astype(jnp.float32), w_router, precision=lax.Precision.HIG...]
  transfers between devices with their start and end apart: 5 -> 19, of which waited for: 3 -> 13; matrix products, arithmetic and copies ran while one was open for 11% -> 14% of each run, Pallas kernels for 0% -> 0%
where the time goes in v1:
time: 180 us; the launch traced here: 179 us
  matrix products  55.1 us (31%)
  waiting for transfers between devices  47 us (26%)
  local copies, waits for them, and re-layouts  33.8 us (19%)
  starting transfers between devices  25.2 us (14%)
  other arithmetic  16.9 us (9%)
    ppermute x17, waiting for transfers between devices, shift(): return lax.ppermute(x, axis, pairs)  47 us
    ppermute x17, starting transfers between devices, shift(): return lax.ppermute(x, axis, pairs)  17.7 us
    unnamed x60, local copies, waits for them, and re-layouts  9.79 us
    dot_general x3, matrix products, attend(): jnp.einsum('hqk,hkd->hqd', weights, values, preferred_element_type=jnp.fl...  8.68 us
    ppermute x2, starting transfers between devices, passed_along(): return lax.ppermute(x, axis, pairs)  7.53 us
    dot_general x1, matrix products, mixture(): both = jnp.dot(normed, paired, preferred_element_type=jnp.float32)  7.52 us
    sub x1, matrix products, softmax_rows(): raised = jnp.exp(scores - highest)  6.15 us
    dot_general x1, matrix products, mixture(): jnp.dot(routed, w_up, preferred_element_type=jnp.float32)  5.13 us
  transfers between devices with their start and end apart: 19, of which 13 were waited for; matrix products, arithmetic and copies ran while one was open for 14% of the time, Pallas kernels for 0%

profile of v1, /device:TPU:0, one launch (start us, length us, event | category | flops | bytes accessed | tf_op | source)
XLA Modules:
  0.0 179.3 jit_solution(1467744744586074268)
XLA Ops:
  0.7 1.2 fusion.41
  1.9 1.1 fusion.43
  3.0 3.1 %collective-permute-start.1 = (bf16[256,512]{1,0:T(8,128)(2,1)S(1)}, bf16[256,512]{1,0:T(8,128)(2,1)}, u32[]{:S(2)}, u32[]{:S(2)}) collective-permute-start(bf16[256,512]{1,0:T(8,128)(2,1)S(1)} %fusion.43), channel_id=1, source_target_pairs={{0,1},{1,2},{2,3},{3,4},{4,5},{5,6},{6,7},{7,8},{8,9},{9,10},{10,1... | collective-permute-start | bytes 786440 | tf_op jit(solution)/shard_map/ppermute | solution.py:20
  6.1 4.5 %collective-permute-start = (bf16[256,512]{1,0:T(8,128)(2,1)S(1)}, bf16[256,512]{1,0:T(8,128)(2,1)}, u32[]{:S(2)}, u32[]{:S(2)}) collective-permute-start(bf16[256,512]{1,0:T(8,128)(2,1)S(1)} %fusion.43), channel_id=1, source_target_pairs={{0,2},{1,3},{2,4},{3,5},{4,6},{5,7},{6,8},{7,9},{8,10},{9,11},{10,... | collective-permute-start | bytes 786440 | tf_op jit(solution)/shard_map/ppermute | solution.py:20
  10.5 2.9 %convolution_convert_fusion.2 = bf16[256,1536]{1,0:T(8,128)(2,1)} fusion(bf16[256,512]{1,0:T(8,128)(2,1)S(1)} %fusion.43, bf16[512,1536]{1,0:T(8,128)(2,1)} %param.21), kind=kOutput, calls=%fused_computation.25 | convolution fusion | flops 403046400 | bytes 2621440 | tf_op jit(solution)/shard_map/dot_general | solution.py:235
  16.1 1.7 slice.144
  17.8 1.8 copy.49
  19.6 1.0 compare_and_fusion
  20.6 1.8 convolution_convert_fusion.6
  22.3 1.8 convolution_convert_fusion.7
  24.3 1.3 fusion.86
  25.5 2.3 %copy.50 = bf16[768,512]{0,1:T(8,128)(2,1)} copy(bf16[768,512]{1,0:T(8,128)(2,1)} %get-tuple-element.10) | data formatting | bytes 1572864 | tf_op jit(solution)/shard_map/slice | solution.py:253
  27.8 2.3 %copy.51 = bf16[768,512]{0,1:T(8,128)(2,1)} copy(bf16[768,512]{1,0:T(8,128)(2,1)} %get-tuple-element.11) | data formatting | bytes 1572864 | tf_op jit(solution)/shard_map/slice | solution.py:254
  30.1 6.1 %fusion.89 = (f32[8,256]{1,0:T(8,128)S(1)}, f32[8,256,768]{2,1,0:T(8,128)}) fusion(pred[256,768]{1,0:T(8,128)(4,1)} %compare_and_fusion, bf16[8,256,64]{1,2,0:T(8,128)(2,1)S(1)} %bitcast.175, bf16[8,768,64]{1,2,0:T(8,128)(2,1)} %bitcast.171), kind=kOutput, calls=%fused_computation.178 | convolution fusion | flops 207618816 | bytes 7544832 | tf_op jit(solution)/shard_map/sub | solution.py:34
  36.3 4.2 %fusion.23 = bf16[8,256,64]{1,2,0:T(8,128)(2,1)S(1)} fusion(bf16[8,768,64]{1,2,0:T(8,128)(2,1)} %bitcast.172, f32[8,256,768]{2,1,0:T(8,128)} %get-tuple-element.32, f32[8,256]{1,0:T(8,128)S(1)} %get-tuple-element.31), kind=kOutput, calls=%fused_computation.53 | convolution fusion | flops 204603392 | bytes 7348224 | tf_op jit(solution)/shard_map/hqk,hkd->hqd/dot_general | solution.py:52
  40.5 1.0 fusion.44
  41.5 1.8 %select_reduce_fusion = bf16[40,512]{1,0:T(8,128)(2,1)S(1)} fusion(pred[40,256]{1,0:T(8,128)(4,1)S(1)} %iota_compare_fusion.2, bf16[256,512]{1,0:T(8,128)(2,1)S(1)} %get-tuple-element.34), kind=kLoop, calls=%fused_computation.3 | loop fusion | flops 10465280 | bytes 313344 | tf_op jit(solution)/shard_map/reduce_max | solution.py:68
  44.2 0.9 reshape.326
  45.1 1.7 convolution_convert_fusion.5
  47.6 1.8 copy.54
  49.4 1.1 fusion.25
  51.4 1.8 copy.55
  53.2 2.4 %convolution_bitcast_fusion = f32[40,8,64]{2,0,1:T(8,128)} fusion(bf16[8,256,64]{1,2,0:T(8,128)(2,1)} %bitcast.176, f32[8,40]{1,0:T(8,128)S(1)} %fusion.90, f32[8,40,256]{2,1,0:T(8,128)} %copy-done.7), kind=kOutput, calls=%fused_computation.61 | convolution fusion | flops 10732095 | bytes 673024 | tf_op jit(solution)/shard_map/hqk,hkd->hqd/dot_general | solution.py:52
  55.7 1.6 copy.56
  57.3 1.0 reshape.329
  58.4 0.9 collective-permute-start.2
  59.4 2.6 %collective-permute-start.3 = (bf16[48,512]{1,0:T(8,128)(2,1)S(1)}, bf16[48,512]{1,0:T(8,128)(2,1)S(1)}, u32[]{:S(2)}, u32[]{:S(2)}) collective-permute-start(bf16[48,512]{1,0:T(8,128)(2,1)S(1)} %get-tuple-element.30), channel_id=1, source_target_pairs={{0,16},{4,20},{8,24},{12,28},{16,0},{20,4},{24,8},{28,12},{1,17},{... | collective-permute-start | bytes 147464 | tf_op jit(solution)/shard_map/ppermute | solution.py:130
  61.9 1.3 collective-permute-start.4
  63.3 1.4 collective-permute-done.2
  64.7 2.4 %collective-permute-done.3 = bf16[48,512]{1,0:T(8,128)(2,1)S(1)} collective-permute-done((bf16[48,512]{1,0:T(8,128)(2,1)S(1)}, bf16[48,512]{1,0:T(8,128)(2,1)S(1)}, u32[]{:S(2)}, u32[]{:S(2)}) %collective-permute-start.3) | collective-permute-done | bytes 49184 | tf_op jit(solution)/shard_map/ppermute | solution.py:130
  68.0 1.4 collective-permute-start.7
  69.4 2.6 %collective-permute-done.5 = bf16[4,48,256]{2,1,0:T(8,128)(2,1)S(1)} collective-permute-done((bf16[4,48,256]{2,1,0:T(8,128)(2,1)S(1)}, bf16[4,48,256]{2,1,0:T(8,128)(2,1)S(1)}, u32[]{:S(2)}, u32[]{:S(2)}) %collective-permute-start.5) | collective-permute-done | bytes 98336 | tf_op jit(solution)/shard_map/ppermute | solution.py:130
  72.0 1.0 collective-permute-start.6
  73.0 1.4 collective-permute-start.8
  74.4 3.3 %collective-permute-done.6 = bf16[2,4,48,256]{3,2,1,0:T(8,128)(2,1)S(1)} collective-permute-done((bf16[2,4,48,256]{3,2,1,0:T(8,128)(2,1)S(1)}, bf16[2,4,48,256]{3,2,1,0:T(8,128)(2,1)S(1)}, u32[]{:S(2)}, u32[]{:S(2)}) %collective-permute-start.6) | collective-permute-done | bytes 196640 | tf_op jit(solution)/shard_map/ppermute | solution.py:130
  77.8 1.0 collective-permute-done.8
  78.8 1.3 fusion.83
  80.1 6.9 %copy.65 = bf16[256,8,2,768]{3,1,2,0:T(8,128)(2,1)} copy(bf16[256,8,2,768]{3,2,1,0:T(2,128)(2,1)} %bitcast.164) | data formatting | bytes 12582912
  87.6 1.3 pad_maximum_fusion.1
  89.0 1.1 copy-done.1
  91.0 1.7 convolution_convert_fusion.4
  92.8 5.1 %fusion.3 = (f32[768]{0:T(1024)S(1)}, bf16[768,2048]{1,0:T(8,128)(2,1)}) fusion(bf16[768,512]{1,0:T(8,128)(2,1)S(1)} %bitcast.173, bf16[512,2048]{1,0:T(8,128)(2,1)} %param.25), kind=kOutput, calls=%fused_computation.6 | convolution fusion | flops 1616903424 | bytes 6032384 | tf_op jit(solution)/shard_map/dot_general | solution.py:193
  99.4 4.7 %select_reduce_fusion.3 = (f32[768]{0:T(1024)S(1)}, f32[768]{0:T(1024)S(1)}) fusion(pred[4]{0:T(512)(128)(4,1)} %iota_compare_fusion.5, s32[768]{0:T(1024)S(1)} %eq.88, f32[2048,4]{0,1:T(4,128)} %param.27, bf16[768,2048]{1,0:T(8,128)(2,1)} %get-tuple-element.36, f32[2048]{0:T(1024)} %param.26, f32[768]{0:T(1024)} %add_rsqrt_fusion), kind=kOutput, calls=%fused_computation.144 | convolution fusion | flops 81802752 | bytes 3198980 | tf_op jit(solution)/shard_map/dot_general | solution.py:195
  104.2 7.5 %fusion.34 = f32[768,1536]{1,0:T(8,128)S(1)} fusion(bf16[2048,1536]{1,0:T(8,128)(2,1)} %bitcast.165, bf16[768,2048]{1,0:T(8,128)(2,1)S(1)} %copy-done.28, f32[2048]{0:T(1024)S(1)} %copy-done.26, f32[768]{0:T(1024)S(1)} %copy-done.18), kind=kOutput, calls=%fused_computation.69 | convolution fusion | flops 4838129664 | bytes 14167040 | tf_op jit(solution)/shard_map/dot_general | solution.py:202
  111.8 3.0 %multiply_convert_fusion = bf16[768,2048]{1,0:T(8,128)(2,1)S(1)} fusion(bf16[1,768,2048]{2,1,0:T(8,128)(2,1)S(1)} %copy-done, f32[768]{0:T(1024)S(1)} %divide_reduce_fusion, f32[768,1536]{1,0:T(8,128)S(1)} %fusion.34), kind=kOutput, calls=%fused_computation.9 | convolution fusion | flops 2422603776 | bytes 11013120 | tf_op jit(solution)/shard_map/dot_general | solution.py:204
  114.8 1.6 convolution_convert_fusion
  117.3 2.6 %collective-permute-done.10 = bf16[2,2,4,40,1024]{4,3,2,1,0:T(8,128)(2,1)S(1)} collective-permute-done((bf16[2,2,4,40,1024]{4,3,2,1,0:T(8,128)(2,1)S(1)}, bf16[2,2,4,40,1024]{4,3,2,1,0:T(8,128)(2,1)S(1)}, u32[]{:S(2)}, u32[]{:S(2)}) %collective-permute-start.10) | collective-permute-done | bytes 1310752 | tf_op jit(solution)/shard_map/ppermute | solution.py:130
  119.9 1.9 %collective-permute-done.13 = bf16[2,2,4,40,1024]{4,3,2,1,0:T(8,128)(2,1)S(1)} collective-permute-done((bf16[2,2,4,40,1024]{4,3,2,1,0:T(8,128)(2,1)S(1)}, bf16[2,2,4,40,1024]{4,3,2,1,0:T(8,128)(2,1)S(1)}, u32[]{:S(2)}, u32[]{:S(2)}) %collective-permute-start.13) | collective-permute-done | bytes 1310752 | tf_op jit(solution)/shard_map/ppermute | solution.py:130
  121.8 1.2 fusion.13
  123.1 1.2 collective-permute-start.14
  125.3 14.9 %collective-permute-done.14 = bf16[2,4,40,1024]{3,2,1,0:T(8,128)(2,1)S(1)} collective-permute-done((bf16[2,4,40,1024]{3,2,1,0:T(8,128)(2,1)S(1)}, bf16[2,4,40,1024]{3,2,1,0:T(8,128)(2,1)S(1)}, u32[]{:S(2)}, u32[]{:S(2)}) %collective-permute-start.14) | collective-permute-done | bytes 655392 | tf_op jit(solution)/shard_map/ppermute | solution.py:130
  141.2 1.5 collective-permute-start.15
  144.4 1.1 convolution_convert_fusion.9
  145.4 1.8 copy.52
  147.2 3.5 %collective-permute-done.15 = bf16[4,40,1024]{2,1,0:T(8,128)(2,1)} collective-permute-done((bf16[4,40,1024]{2,1,0:T(8,128)(2,1)}, bf16[4,40,1024]{2,1,0:T(8,128)(2,1)}, u32[]{:S(2)}, u32[]{:S(2)}) %collective-permute-start.15) | collective-permute-done | bytes 327712 | tf_op jit(solution)/shard_map/ppermute | solution.py:130
  150.7 1.2 fusion.37
  151.9 1.2 collective-permute-done.12
  153.1 1.2 fusion.38
  154.4 3.0 %collective-permute-start.16 = (bf16[40,2048]{1,0:T(8,128)(2,1)S(1)}, bf16[40,2048]{1,0:T(8,128)(2,1)S(1)}, u32[]{:S(2)}, u32[]{:S(2)}) collective-permute-start(bf16[40,2048]{1,0:T(8,128)(2,1)S(1)} %get-tuple-element.14), channel_id=1, source_target_pairs={{0,24},{4,28},{8,0},{12,4},{16,8},{20,12},{24,16},{28,20},{1,25},{... | collective-permute-start | bytes 491528 | tf_op jit(solution)/shard_map/ppermute | solution.py:130
  158.4 3.6 %collective-permute-done.16 = bf16[40,2048]{1,0:T(8,128)(2,1)S(1)} collective-permute-done((bf16[40,2048]{1,0:T(8,128)(2,1)S(1)}, bf16[40,2048]{1,0:T(8,128)(2,1)S(1)}, u32[]{:S(2)}, u32[]{:S(2)}) %collective-permute-start.16) | collective-permute-done | bytes 163872 | tf_op jit(solution)/shard_map/ppermute | solution.py:130
  162.0 8.6 %collective-permute-done.17 = bf16[40,2048]{1,0:T(8,128)(2,1)S(1)} collective-permute-done((bf16[40,2048]{1,0:T(8,128)(2,1)S(1)}, bf16[40,2048]{1,0:T(8,128)(2,1)S(1)}, u32[]{:S(2)}, u32[]{:S(2)}) %collective-permute-start.17) | collective-permute-done | bytes 163872 | tf_op jit(solution)/shard_map/ppermute | solution.py:130
  173.1 1.1 fusion.24
  175.1 2.0 %convolution_convert_fusion.8 = bf16[8,256,64]{1,2,0:T(8,128)(2,1)} fusion(f32[8,256]{1,0:T(8,128)S(1)} %fusion.91, bf16[40,8,64]{2,1,0:T(8,128)(2,1)S(1)} %reshape.337, f32[8,256,40]{1,2,0:T(8,128)} %copy-done.13), kind=kOutput, calls=%fused_computation.51 | convolution fusion | flops 10864679 | bytes 638976 | tf_op jit(solution)/shard_map/hqk,hkd->hqd/dot_general | solution.py:52
  177.2 2.1 %fusion.22 = bf16[256,512]{1,0:T(8,128)(2,1)} fusion(bf16[256,512]{0,1:T(8,128)(2,1)} %bitcast.174, bf16[512,512]{1,0:T(8,128)(2,1)} %param.33, bf16[256,512]{1,0:T(8,128)(2,1)S(1)} %get-tuple-element.34), kind=kOutput, calls=%fused_computation.50 | convolution fusion | flops 134610944 | bytes 1310720 | tf_op jit(solution)/shard_map/dot_general | solution.py:101
  (136 shorter events, 18.8 us)
Async XLA Ops:
  0.6 111.2 %copy-start = (bf16[1,768,2048]{2,1,0:T(8,128)(2,1)S(1)}, bf16[1,768,2048]{2,1,0:T(8,128)(2,1)}, u32[]{:S(2)}) copy-start(bf16[1,768,2048]{2,1,0:T(8,128)(2,1)} %param.29) | copy-start | bytes 9437188
  0.6 12.8 %copy-start.19 = (s32[256]{0:T(256)S(1)}, s32[256]{0:T(256)}, u32[]{:S(2)}) copy-start(s32[256]{0:T(256)} %param.18) | copy-start | bytes 3076
  0.7 14.0 %copy-start.20 = (s32[40,2]{0,1:T(2,128)S(1)}, s32[40,2]{0,1:T(2,128)}, u32[]{:S(2)}) copy-start(s32[40,2]{0,1:T(2,128)} %param.19) | copy-start | bytes 964
  3.0 17.6 %collective-permute-start.1 = (bf16[256,512]{1,0:T(8,128)(2,1)S(1)}, bf16[256,512]{1,0:T(8,128)(2,1)}, u32[]{:S(2)}, u32[]{:S(2)}) collective-permute-start(bf16[256,512]{1,0:T(8,128)(2,1)S(1)} %fusion.43), channel_id=1, source_target_pairs={{0,1},{1,2},{2,3},{3,4},{4,5},{5,6},{6,7},{7,8},{8,9},{9,10},{10,1... | collective-permute-start | bytes 786440 | tf_op jit(solution)/shard_map/ppermute | solution.py:20
  6.1 16.2 %collective-permute-start = (bf16[256,512]{1,0:T(8,128)(2,1)S(1)}, bf16[256,512]{1,0:T(8,128)(2,1)}, u32[]{:S(2)}, u32[]{:S(2)}) collective-permute-start(bf16[256,512]{1,0:T(8,128)(2,1)S(1)} %fusion.43), channel_id=1, source_target_pairs={{0,2},{1,3},{2,4},{3,5},{4,6},{5,7},{6,8},{7,9},{8,10},{9,11},{10,... | collective-permute-start | bytes 786440 | tf_op jit(solution)/shard_map/ppermute | solution.py:20
  14.7 9.4 %copy-start.16 = (s32[256]{0:T(256)}, s32[256]{0:T(256)S(1)}, u32[]{:S(2)}) copy-start(s32[256]{0:T(256)S(1)} %add_bitcast_fusion) | copy-start | bytes 3076
  19.6 4.5 %slice-start = ((bf16[256,1536]{1,0:T(8,128)(2,1)}), bf16[256,1024]{1,0:T(8,128)(2,1)S(1)}, s32[]{:S(2)}) async-start(bf16[256,1536]{1,0:T(8,128)(2,1)} %convolution_convert_fusion.2), calls=%async_computation | async-start | bytes 1048576 | tf_op jit(solution)/shard_map/slice | solution.py:237
  24.2 5.9 %copy-start.14 = (bf16[256,512]{0,1:T(8,128)(2,1)S(1)}, bf16[256,512]{0,1:T(8,128)(2,1)}, u32[]{:S(2)}) copy-start(bf16[256,512]{0,1:T(8,128)(2,1)} %copy.49) | copy-start | bytes 786436
  36.3 4.2 %copy-start.8 = (bf16[256,512]{1,0:T(8,128)(2,1)S(1)}, bf16[256,512]{1,0:T(8,128)(2,1)}, u32[]{:S(2)}) copy-start(bf16[256,512]{1,0:T(8,128)(2,1)} %param.17) | copy-start | bytes 786436
  36.3 4.2 %copy-start.24 = (bf16[512,512]{1,0:T(8,128)(2,1)S(1)}, bf16[512,512]{1,0:T(8,128)(2,1)}, u32[]{:S(2)}) copy-start(bf16[512,512]{1,0:T(8,128)(2,1)} %param.22) | copy-start | bytes 1572868
  36.3 7.1 %copy-start.10 = (bf16[512,512]{1,0:T(8,128)(2,1)S(1)}, bf16[512,512]{1,0:T(8,128)(2,1)}, u32[]{:S(2)}) copy-start(bf16[512,512]{1,0:T(8,128)(2,1)} %param.23) | copy-start | bytes 1572868
  50.5 0.7 copy-start.7
  58.4 8.9 %copy-start.11 = (bf16[40,512]{1,0:T(8,128)(2,1)}, bf16[40,512]{1,0:T(8,128)(2,1)S(1)}, u32[]{:S(2)}) copy-start(bf16[40,512]{1,0:T(8,128)(2,1)S(1)} %select_convert_fusion) | copy-start | bytes 122884
  58.4 6.3 %collective-permute-start.2 = (bf16[48,512]{1,0:T(8,128)(2,1)S(1)}, bf16[48,512]{1,0:T(8,128)(2,1)S(1)}, u32[]{:S(2)}, u32[]{:S(2)}) collective-permute-start(bf16[48,512]{1,0:T(8,128)(2,1)S(1)} %get-tuple-element.30), channel_id=1, source_target_pairs={{0,8},{4,12},{8,16},{12,20},{16,24},{20,28},{24,0},{28,4},{1,9},{5... | collective-permute-start | bytes 147464 | tf_op jit(solution)/shard_map/ppermute | solution.py:130
  59.4 7.7 %collective-permute-start.3 = (bf16[48,512]{1,0:T(8,128)(2,1)S(1)}, bf16[48,512]{1,0:T(8,128)(2,1)S(1)}, u32[]{:S(2)}, u32[]{:S(2)}) collective-permute-start(bf16[48,512]{1,0:T(8,128)(2,1)S(1)} %get-tuple-element.30), channel_id=1, source_target_pairs={{0,16},{4,20},{8,24},{12,28},{16,0},{20,4},{24,8},{28,12},{1,17},{... | collective-permute-start | bytes 147464 | tf_op jit(solution)/shard_map/ppermute | solution.py:130
  61.9 5.3 %collective-permute-start.4 = (bf16[48,512]{1,0:T(8,128)(2,1)S(1)}, bf16[48,512]{1,0:T(8,128)(2,1)S(1)}, u32[]{:S(2)}, u32[]{:S(2)}) collective-permute-start(bf16[48,512]{1,0:T(8,128)(2,1)S(1)} %get-tuple-element.30), channel_id=1, source_target_pairs={{0,24},{4,28},{8,0},{12,4},{16,8},{20,12},{24,16},{28,20},{1,25},{... | collective-permute-start | bytes 147464 | tf_op jit(solution)/shard_map/ppermute | solution.py:130
  67.3 4.7 %collective-permute-start.5 = (bf16[4,48,256]{2,1,0:T(8,128)(2,1)S(1)}, bf16[4,48,256]{2,1,0:T(8,128)(2,1)S(1)}, u32[]{:S(2)}, u32[]{:S(2)}) collective-permute-start(bf16[4,48,256]{2,1,0:T(8,128)(2,1)S(1)} %get-tuple-element.24), channel_id=1, source_target_pairs={{0,4},{4,0},{8,12},{12,8},{16,20},{20,16},{24,28},{28,24},{1,5},{5... | collective-permute-start | bytes 294920 | tf_op jit(solution)/shard_map/ppermute | solution.py:130
  68.0 5.0 %collective-permute-start.7 = (bf16[4,48,256]{2,1,0:T(8,128)(2,1)S(1)}, bf16[4,48,256]{2,1,0:T(8,128)(2,1)S(1)}, u32[]{:S(2)}, u32[]{:S(2)}) collective-permute-start(bf16[4,48,256]{2,1,0:T(8,128)(2,1)S(1)} %get-tuple-element.23), channel_id=1, source_target_pairs={{0,2},{1,3},{2,0},{3,1},{4,6},{5,7},{6,4},{7,5},{8,10},{9,11},{10,... | collective-permute-start | bytes 294920 | tf_op jit(solution)/shard_map/ppermute | solution.py:130
  72.0 5.7 %collective-permute-start.6 = (bf16[2,4,48,256]{3,2,1,0:T(8,128)(2,1)S(1)}, bf16[2,4,48,256]{3,2,1,0:T(8,128)(2,1)S(1)}, u32[]{:S(2)}, u32[]{:S(2)}) collective-permute-start(bf16[2,4,48,256]{3,2,1,0:T(8,128)(2,1)S(1)} %get-tuple-element.20), channel_id=1, source_target_pairs={{0,2},{1,3},{2,0},{3,1},{4,6},{5,7},{6,4},{7,5},{8,10},{9,11},{10,... | collective-permute-start | bytes 589832 | tf_op jit(solution)/shard_map/ppermute | solution.py:130
  73.0 5.7 %collective-permute-start.8 = (bf16[2,4,48,256]{3,2,1,0:T(8,128)(2,1)S(1)}, bf16[2,4,48,256]{3,2,1,0:T(8,128)(2,1)S(1)}, u32[]{:S(2)}, u32[]{:S(2)}) collective-permute-start(bf16[2,4,48,256]{3,2,1,0:T(8,128)(2,1)S(1)} %get-tuple-element.26), channel_id=1, source_target_pairs={{0,4},{4,0},{8,12},{12,8},{16,20},{20,16},{24,28},{28,24},{1,5},{5... | collective-permute-start | bytes 589832 | tf_op jit(solution)/shard_map/ppermute | solution.py:130
  80.1 7.5 %collective-permute-start.9 = (bf16[2,2,4,48,512]{4,3,2,0,1:T(8,128)(2,1)}, bf16[2,2,4,48,512]{4,3,2,0,1:T(8,128)(2,1)}, u32[]{:S(2)}, u32[]{:S(2)}) collective-permute-start(bf16[2,2,4,48,512]{4,3,2,0,1:T(8,128)(2,1)} %get-tuple-element.13), channel_id=1, source_target_pairs={{0,1},{1,0},{2,3},{3,2},{4,5},{5,4},{6,7},{7,6},{8,9},{9,8},{10,11... | collective-permute-start | bytes 2359304 | tf_op jit(solution)/shard_map/ppermute | solution.py:130
  80.1 7.5 %copy-start.3 = (bf16[1,2,2,4,48,512]{5,4,3,1,2,0:T(8,128)(2,1)S(1)}, bf16[1,2,2,4,48,512]{5,4,3,1,2,0:T(8,128)(2,1)}, u32[]{:S(2)}) copy-start(bf16[1,2,2,4,48,512]{5,4,3,1,2,0:T(8,128)(2,1)} %get-tuple-element.12) | copy-start | bytes 2359300
  87.5 3.3 %copy-start.21 = (s32[24]{0:T(128)}, s32[24]{0:T(128)S(1)}, u32[]{:S(2)}) copy-start(s32[24]{0:T(128)S(1)} %iota_add_fusion.2) | copy-start | bytes 292
  89.0 1.1 copy-start.1
  92.8 5.8 %copy-start.15 = (s32[32,2,40]{2,1,0:T(2,128)S(1)}, s32[32,2,40]{2,1,0:T(2,128)}, u32[]{:S(2)}) copy-start(s32[32,2,40]{2,1,0:T(2,128)} %rev.3) | copy-start | bytes 30724
  92.8 5.8 %copy-start.22 = (s32[24]{0:T(128)S(1)}, s32[24]{0:T(128)}, u32[]{:S(2)}) copy-start(s32[24]{0:T(128)} %copy-done.21) | copy-start | bytes 292
  99.4 4.8 %copy-start.18 = (f32[768]{0:T(1024)S(1)}, f32[768]{0:T(1024)}, u32[]{:S(2)}) copy-start(f32[768]{0:T(1024)} %add_rsqrt_fusion) | copy-start | bytes 9220
  99.4 4.8 %copy-start.26 = (f32[2048]{0:T(1024)S(1)}, f32[2048]{0:T(1024)}, u32[]{:S(2)}) copy-start(f32[2048]{0:T(1024)} %param.26) | copy-start | bytes 24580
  99.4 4.8 %copy-start.28 = (bf16[768,2048]{1,0:T(8,128)(2,1)S(1)}, bf16[768,2048]{1,0:T(8,128)(2,1)}, u32[]{:S(2)}) copy-start(bf16[768,2048]{1,0:T(8,128)(2,1)} %get-tuple-element.36) | copy-start | bytes 9437188
  116.7 3.2 %collective-permute-start.10 = (bf16[2,2,4,40,1024]{4,3,2,1,0:T(8,128)(2,1)S(1)}, bf16[2,2,4,40,1024]{4,3,2,1,0:T(8,128)(2,1)S(1)}, u32[]{:S(2)}, u32[]{:S(2)}) collective-permute-start(bf16[2,2,4,40,1024]{4,3,2,1,0:T(8,128)(2,1)S(1)} %get-tuple-element.8), channel_id=1, source_target_pairs={{0,1},{1,0},{2,3},{3,2},{4,5},{5,4},{6,7},{7,6},{8,9},{9,8},{10,11... | collective-permute-start | bytes 3932168 | tf_op jit(solution)/shard_map/ppermute | solution.py:130
  117.2 7.1 %copy-start.17 = (s32[256]{0:T(256)S(1)}, s32[256]{0:T(256)}, u32[]{:S(2)}) copy-start(s32[256]{0:T(256)} %copy-done.16) | copy-start | bytes 3076
  117.2 4.5 %collective-permute-start.13 = (bf16[2,2,4,40,1024]{4,3,2,1,0:T(8,128)(2,1)S(1)}, bf16[2,2,4,40,1024]{4,3,2,1,0:T(8,128)(2,1)S(1)}, u32[]{:S(2)}, u32[]{:S(2)}) collective-permute-start(bf16[2,2,4,40,1024]{4,3,2,1,0:T(8,128)(2,1)S(1)} %get-tuple-element.9), channel_id=1, source_target_pairs={{0,1},{1,0},{2,3},{3,2},{4,5},{5,4},{6,7},{7,6},{8,9},{9,8},{10,11... | collective-permute-start | bytes 3932168 | tf_op jit(solution)/shard_map/ppermute | solution.py:130
  123.0 2.2 %copy-start.23 = (f32[256]{0:T(256)S(1)}, f32[256]{0:T(256)}, u32[]{:S(2)}) copy-start(f32[256]{0:T(256)} %get-tuple-element.33) | copy-start | bytes 3076
  123.1 17.1 %collective-permute-start.14 = (bf16[2,4,40,1024]{3,2,1,0:T(8,128)(2,1)S(1)}, bf16[2,4,40,1024]{3,2,1,0:T(8,128)(2,1)S(1)}, u32[]{:S(2)}, u32[]{:S(2)}) collective-permute-start(bf16[2,4,40,1024]{3,2,1,0:T(8,128)(2,1)S(1)} %slice_bitcast_fusion.4), channel_id=1, source_target_pairs={{0,2},{1,3},{2,0},{3,1},{4,6},{5,7},{6,4},{7,5},{8,10},{9,11},{10,... | collective-permute-start | bytes 1966088 | tf_op jit(solution)/shard_map/ppermute | solution.py:130
  124.4 18.3 %collective-permute-start.11 = (bf16[2,4,40,1024]{3,2,1,0:T(8,128)(2,1)S(1)}, bf16[2,4,40,1024]{3,2,1,0:T(8,128)(2,1)S(1)}, u32[]{:S(2)}, u32[]{:S(2)}) collective-permute-start(bf16[2,4,40,1024]{3,2,1,0:T(8,128)(2,1)S(1)} %slice_bitcast_fusion.6), channel_id=1, source_target_pairs={{0,4},{4,0},{8,12},{12,8},{16,20},{20,16},{24,28},{28,24},{1,5},{5... | collective-permute-start | bytes 1966088 | tf_op jit(solution)/shard_map/ppermute | solution.py:130
  125.3 19.1 %copy-start.25 = (bf16[512,512]{1,0:T(8,128)(2,1)S(1)}, bf16[512,512]{1,0:T(8,128)(2,1)}, u32[]{:S(2)}) copy-start(bf16[512,512]{1,0:T(8,128)(2,1)} %param.31) | copy-start | bytes 1572868
  125.3 19.1 %copy-start.27 = (f32[512]{0:T(512)S(1)}, f32[512]{0:T(512)}, u32[]{:S(2)}) copy-start(f32[512]{0:T(512)} %param.30) | copy-start | bytes 6148
  140.4 2.6 %copy-start.4 = (bf16[2,4,40,1024]{3,2,1,0:T(8,128)(2,1)}, bf16[2,4,40,1024]{3,2,1,0:T(8,128)(2,1)S(1)}, u32[]{:S(2)}) copy-start(bf16[2,4,40,1024]{3,2,1,0:T(8,128)(2,1)S(1)} %fusion.17) | copy-start | bytes 1966084
  141.2 9.5 %collective-permute-start.15 = (bf16[4,40,1024]{2,1,0:T(8,128)(2,1)}, bf16[4,40,1024]{2,1,0:T(8,128)(2,1)}, u32[]{:S(2)}, u32[]{:S(2)}) collective-permute-start(bf16[4,40,1024]{2,1,0:T(8,128)(2,1)} %slice_bitcast_fusion.8), channel_id=1, source_target_pairs={{0,4},{4,0},{8,12},{12,8},{16,20},{20,16},{24,28},{28,24},{1,5},{5... | collective-permute-start | bytes 983048 | tf_op jit(solution)/shard_map/ppermute | solution.py:130
  143.0 0.9 copy-start.5
  143.0 15.0 %copy-start.12 = (bf16[40,512]{1,0:T(8,128)(2,1)S(1)}, bf16[40,512]{1,0:T(8,128)(2,1)}, u32[]{:S(2)}) copy-start(bf16[40,512]{1,0:T(8,128)(2,1)} %copy-done.11) | copy-start | bytes 122884
  143.9 9.2 %collective-permute-start.12 = (bf16[4,40,1024]{2,1,0:T(8,128)(2,1)}, bf16[4,40,1024]{2,1,0:T(8,128)(2,1)}, u32[]{:S(2)}, u32[]{:S(2)}) collective-permute-start(bf16[4,40,1024]{2,1,0:T(8,128)(2,1)} %slice_bitcast_fusion.10), channel_id=1, source_target_pairs={{0,2},{1,3},{2,0},{3,1},{4,6},{5,7},{6,4},{7,5},{8,10},{9,11},{10,... | collective-permute-start | bytes 983048 | tf_op jit(solution)/shard_map/ppermute | solution.py:130
  147.2 10.7 %copy-start.6 = (bf16[512,2048]{1,0:T(8,128)(2,1)S(1)}, bf16[512,2048]{1,0:T(8,128)(2,1)}, u32[]{:S(2)}) copy-start(bf16[512,2048]{1,0:T(8,128)(2,1)} %param.25) | copy-start | bytes 6291460
  154.3 16.4 %copy-start.2 = (bf16[2048,1024]{1,0:T(8,128)(2,1)S(1)}, bf16[2048,1024]{1,0:T(8,128)(2,1)}, u32[]{:S(2)}) copy-start(bf16[2048,1024]{1,0:T(8,128)(2,1)} %param.32) | copy-start | bytes 12582916
  154.4 7.6 %collective-permute-start.16 = (bf16[40,2048]{1,0:T(8,128)(2,1)S(1)}, bf16[40,2048]{1,0:T(8,128)(2,1)S(1)}, u32[]{:S(2)}, u32[]{:S(2)}) collective-permute-start(bf16[40,2048]{1,0:T(8,128)(2,1)S(1)} %get-tuple-element.14), channel_id=1, source_target_pairs={{0,24},{4,28},{8,0},{12,4},{16,8},{20,12},{24,16},{28,20},{1,25},{... | collective-permute-start | bytes 491528 | tf_op jit(solution)/shard_map/ppermute | solution.py:130
  157.3 13.3 %collective-permute-start.17 = (bf16[40,2048]{1,0:T(8,128)(2,1)S(1)}, bf16[40,2048]{1,0:T(8,128)(2,1)S(1)}, u32[]{:S(2)}, u32[]{:S(2)}) collective-permute-start(bf16[40,2048]{1,0:T(8,128)(2,1)S(1)} %get-tuple-element.16), channel_id=1, source_target_pairs={{0,16},{4,20},{8,24},{12,28},{16,0},{20,4},{24,8},{28,12},{1,17},{... | collective-permute-start | bytes 491528 | tf_op jit(solution)/shard_map/ppermute | solution.py:130
  157.5 13.1 %collective-permute-start.18 = (bf16[40,2048]{1,0:T(8,128)(2,1)S(1)}, bf16[40,2048]{1,0:T(8,128)(2,1)S(1)}, u32[]{:S(2)}, u32[]{:S(2)}) collective-permute-start(bf16[40,2048]{1,0:T(8,128)(2,1)S(1)} %get-tuple-element.15), channel_id=1, source_target_pairs={{0,8},{4,12},{8,16},{12,20},{16,24},{20,28},{24,0},{28,4},{1,9},{5... | collective-permute-start | bytes 491528 | tf_op jit(solution)/shard_map/ppermute | solution.py:130
  170.7 0.9 copy-start.9
  174.2 0.7 copy-start.13

commit v2 on v1

v2 whole, which is shorter than its diff:
```python
import functools
import math

import jax
import jax.numpy as jnp
from jax import lax
from jax.experimental import pallas as pl
from jax.experimental.pallas import tpu as pltpu
from jax.sharding import PartitionSpec as P

HEADS_L = 8
HEAD = 64
WINDOW = 512


epsilon = 1e-06
very_negative = -1e30


def passed_along(x, axis, by):
    length = lax.axis_size(axis)
    pairs = [(i, i + by) for i in range(length) if 0 <= i + by < length]
    return lax.ppermute(x, axis, pairs)


def normed_rows(x, gain_row):
    wide = x.astype(jnp.float32)
    scale = lax.rsqrt(jnp.mean(wide * wide, axis=-1, keepdims=True) + epsilon)
    return (wide * scale * gain_row).astype(jnp.bfloat16)


def mm(a, b):
    return jnp.dot(a, b, preferred_element_type=jnp.float32)


def mm_t(a, b):
    return lax.dot_general(a, b, (((1,), (1,)), ((), ())), preferred_element_type=jnp.float32)


def iota(shape, dim):
    return lax.broadcasted_iota(jnp.int32, shape, dim)


def attend_pair(q, k, v, bias):
    first = iota((1, 2 * HEAD), 1) < HEAD
    q = q * jnp.asarray(1.0 / math.sqrt(HEAD), q.dtype)
    outs = []
    for here in (first, jnp.logical_not(first)):
        scores = mm_t(jnp.where(here, q, jnp.zeros_like(q)), k) + bias
        raised = jnp.exp(scores - jnp.max(scores, axis=-1, keepdims=True)).astype(jnp.bfloat16)
        both = mm(raised, jnp.where(here, v, jnp.ones_like(v)))
        outs.append(both / pltpu.roll(both, HEAD, 1))
    return jnp.where(first, outs[0], outs[1])


def encoder_kernel(reach, experts, capacity, *refs):
    place, own, *earlier = refs[: 2 + reach]
    flags, ids, gain, w_qkv, w_out, w_xq, w_xkv = refs[2 + reach : 9 + reach]
    encoded_out, payload_out = refs[9 + reach : 11 + reach]
    bias_ref, pairs_ref, mixed_ref = refs[11 + reach :]
    rows, width = own.shape
    patch_cap = rows * 5 // 32
    gain_row = gain[...]
    normed = normed_rows(own[...], gain_row)
    projected = mm(normed, w_qkv[...]).astype(jnp.bfloat16)
    queries = projected[:, :width]
    pairs_ref[reach * rows :, :] = projected[:, width:]
    for at, block in enumerate(earlier):
        moved = normed_rows(block[...], gain_row)
        pairs_ref[at * rows : (at + 1) * rows, :] = mm(moved, w_qkv[:, width:]).astype(jnp.bfloat16)
    keys = (reach + 1) * rows
    at_query = iota((rows, keys), 0) + reach * rows
    at_key = iota((rows, keys), 1)
    allowed = (at_key <= at_query) & (at_key > at_query - WINDOW)
    allowed = allowed & (at_key >= (reach - place[0]) * rows)
    bias_ref[...] = jnp.where(allowed, 0.0, very_negative)
    lanes = 2 * HEAD
    for at in range(0, width, lanes):
        mixed = attend_pair(
            queries[:, at : at + lanes],
            pairs_ref[:, at : at + lanes],
            pairs_ref[:, width + at : width + at + lanes],
            bias_ref[...],
        )
        mixed_ref[:, at : at + lanes] = mixed.astype(jnp.bfloat16)
    encoded = (own[...].astype(jnp.float32) + mm(mixed_ref[...], w_out[...])).astype(jnp.bfloat16)
    encoded_out[...] = encoded

    flag = flags[...]
    at_row, at_col = iota((rows, rows), 0), iota((rows, rows), 1)
    upto = at_col <= at_row
    opened = jnp.max(jnp.where(upto & (flag == 1), at_col, 0), axis=1, keepdims=True)
    since = iota((rows, 1), 0) - opened
    eight = jnp.broadcast_to(flag, (8, rows)).astype(jnp.float32).astype(jnp.bfloat16)
    before = (at_row <= at_col).astype(jnp.float32).astype(jnp.bfloat16)
    number = mm(eight, before)[:1].astype(jnp.int32) - 1
    slot = iota((patch_cap, rows), 0)
    at_byte = iota((patch_cap, rows), 1)
    member = number == slot
    last = jnp.max(jnp.where(member, at_byte, -1), axis=1, keepdims=True)
    live = last >= 0
    highest = encoded.astype(jnp.float32)
    step = 1
    while step < rows:
        highest = jnp.where(
            since >= step, jnp.maximum(highest, pltpu.roll(highest, step, 0)), highest
        )
        step *= 2
    ends = (member & (at_byte == last)).astype(jnp.float32).astype(jnp.bfloat16)
    pooled = mm(ends, highest.astype(jnp.bfloat16))
    patch_queries = mm(pooled.astype(jnp.bfloat16), w_xq[...]).astype(jnp.bfloat16)
    byte_pairs = mm(encoded, w_xkv[...]).astype(jnp.bfloat16)
    member_bias = jnp.where(member, 0.0, very_negative)
    for at in range(0, width, lanes):
        mixed = attend_pair(
            patch_queries[:, at : at + lanes],
            byte_pairs[:, at : at + lanes],
            byte_pairs[:, width + at : width + at + lanes],
            member_bias,
        )
        total = jnp.where(live, pooled[:, at : at + lanes] + mixed, 0.0)
        payload_out[:patch_cap, at : at + lanes] = total.astype(jnp.bfloat16)

    square = (patch_cap, patch_cap)
    same = iota(square, 0) == iota(square, 1)
    earlier_slot = iota(square, 0) < iota(square, 1)
    id_rows = [ids[k : k + 1, :] for k in range(2)]
    id_cols = [jnp.sum(jnp.where(same, row, 0), axis=1, keepdims=True) for row in id_rows]
    targets = []
    for row in id_rows:
        named = sum((col == row).astype(jnp.int32) for col in id_cols)
        rank = jnp.sum(jnp.where(earlier_slot, named, 0), axis=0, keepdims=True)
        targets.append(row * capacity + rank)
    extra = payload_out.shape[0] - patch_cap
    at_extra = iota((extra, patch_cap), 0)
    table = jnp.where(at_extra == 0, targets[0], jnp.where(at_extra == 1, targets[1], 0))
    payload_out[patch_cap:, :] = jnp.zeros((extra, width), jnp.bfloat16)
    payload_out[patch_cap:, :patch_cap] = table.astype(jnp.float32).astype(jnp.bfloat16)


def encode(byte_states, earlier, patch_start, expert_ids, experts, capacity, place, enc_gain, *ws):
    rows, width = byte_states.shape
    reach = len(earlier)
    patch_cap = rows * 5 // 32
    payload_rows = -(-(patch_cap + 2) // 16) * 16
    vmem = pl.BlockSpec(memory_space=pltpu.VMEM)
    return pl.pallas_call(
        functools.partial(encoder_kernel, reach, experts, capacity),
        out_shape=(
            jax.ShapeDtypeStruct((rows, width), jnp.bfloat16),
            jax.ShapeDtypeStruct((payload_rows, width), jnp.bfloat16),
        ),
        in_specs=[pl.BlockSpec(memory_space=pltpu.SMEM)] + [vmem] * (8 + reach),
        out_specs=(vmem, vmem),
        scratch_shapes=[
            pltpu.VMEM((rows, (reach + 1) * rows), jnp.float32),
            pltpu.VMEM(((reach + 1) * rows, 2 * width), jnp.bfloat16),
            pltpu.VMEM((rows, width), jnp.bfloat16),
        ],
        compiler_params=pltpu.CompilerParams(vmem_limit_bytes=16 * 1024 * 1024),
    )(
        place,
        byte_states,
        *earlier,
        patch_start.reshape(1, rows),
        expert_ids.T,
        enc_gain.reshape(1, width),
        *ws,
    )


def mm_first(a, b):
    return lax.dot_general(a, b, (((0,), (0,)), ((), ())), preferred_element_type=jnp.float32)


def counted_from(values, step, most):
    return sum((values >= step * k).astype(jnp.int32) for k in range(1, most))


def as_bf16(mask):
    return mask.astype(jnp.float32).astype(jnp.bfloat16)


GROUP = 4


def expert_kernel(patch_cap, capacity, experts, *refs):
    me_ref, rows_ref, w_up, gain, router, w_in, w_down = refs[:7]
    outs = refs[7:-4]
    routed_ref, spread_ref, hidden_ref, parts_ref = refs[-4:]
    sources, held, width = rows_ref.shape
    per = GROUP * capacity
    me = me_ref[0]
    slots = iota((per, 1), 0)
    source_of_slot = counted_from(slots, capacity, GROUP)
    place_of_slot = slots - source_of_slot * capacity + me * capacity
    lanes = 128

    def spreader(block):
        at_from, at_to = iota((GROUP * lanes, GROUP * block), 0), iota((GROUP * lanes, GROUP * block), 1)
        source = counted_from(at_from, lanes, GROUP)
        within = at_from - source * lanes
        return as_bf16((at_to == source * block + within) & (within < block))

    spread_held, spread_cap = spreader(held), spreader(patch_cap)

    def matched(table, spread, block):
        targets = mm(table, spread).astype(jnp.int32)
        at = iota((1, GROUP * block), 1)
        source = counted_from(at, block, GROUP)
        first, second = targets[0:1], targets[1:2]
        hit = (first == place_of_slot) | (second == place_of_slot)
        hit = hit & (source == source_of_slot) & (at - source * block < patch_cap)
        named = [counted_from(t, capacity, experts) for t in (first, second)]
        return hit, jnp.where(named[0] == me, named[1], named[0])

    others = []
    for g in range(sources // GROUP):
        tables = []
        for s in range(g * GROUP, (g + 1) * GROUP):
            block = rows_ref[s, held - 16 : held, :lanes].astype(jnp.float32)
            tables.append(block[patch_cap - (held - 16) : patch_cap - (held - 16) + 8])
        table = jnp.concatenate(tables, axis=1).astype(jnp.bfloat16)
        hit, other = matched(table, spread_held, held)
        others.append(jnp.sum(jnp.where(hit, other, 0), axis=1, keepdims=True))
        block = rows_ref[g * GROUP : (g + 1) * GROUP].reshape(GROUP * held, width)
        routed_ref[g * per : (g + 1) * per, :] = mm(as_bf16(hit), block).astype(jnp.bfloat16)
        hit, _ = matched(table, spread_cap, patch_cap)
        spread_ref[g] = as_bf16(hit)
    other = jnp.concatenate(others, axis=0)

    state = mm(routed_ref[...], w_up[...]).astype(jnp.bfloat16)
    normed = normed_rows(state, gain[...])

    parts_ref[...] = jnp.zeros_like(parts_ref)
    left = router[...]
    for part in range(3):
        here = left.astype(jnp.bfloat16).astype(jnp.float32)
        parts_ref[8 * part : 8 * part + experts, :] = here
        left = left - here
    logits = mm_t(normed, parts_ref[...].astype(jnp.bfloat16))
    expert_of_lane = iota((1, parts_ref.shape[0]), 1) & 7
    own = jnp.sum(jnp.where(expert_of_lane == me, logits, 0.0), axis=1, keepdims=True)
    rival = jnp.sum(jnp.where(expert_of_lane == other, logits, 0.0), axis=1, keepdims=True)
    highest = jnp.maximum(own, rival)
    raised = jnp.exp(own - highest)
    gate = raised / (raised + jnp.exp(rival - highest))

    hidden_share = hidden_ref.shape[1]
    chunk = 256 if hidden_share % 256 == 0 else hidden_share
    for at in range(0, hidden_share, chunk):
        opened = mm(normed, w_in[:, at : at + chunk])
        upper = mm(normed, w_in[:, hidden_share + at : hidden_share + at + chunk])
        hidden_ref[:, at : at + chunk] = (opened / (1.0 + jnp.exp(-opened)) * upper).astype(
            jnp.bfloat16
        )
    hidden = hidden_ref[...]
    wide = outs[0].shape[1]
    chunk = min(512, wide)
    for number, out in enumerate(outs):
        for at in range(0, wide, chunk):
            begin = number * wide + at
            term = (mm(hidden, w_down[:, begin : begin + chunk]) * gate).astype(jnp.bfloat16)
            for g in range(sources // GROUP):
                total = mm_first(spread_ref[g], term[g * per : (g + 1) * per])
                out[g * GROUP * patch_cap : (g + 1) * GROUP * patch_cap, at : at + chunk] = (
                    total.astype(jnp.bfloat16)
                )


def expert_share(rows, patch_cap, capacity, me, w_up, gain, router, w_in, w_down, pieces):
    sources, held, width = rows.shape
    wide = w_up.shape[1]
    experts = router.shape[0]
    vmem = pl.BlockSpec(memory_space=pltpu.VMEM)
    slots = sources * capacity
    return pl.pallas_call(
        functools.partial(expert_kernel, patch_cap, capacity, experts),
        out_shape=tuple(
            jax.ShapeDtypeStruct((sources * patch_cap, wide // pieces), jnp.bfloat16)
            for _ in range(pieces)
        ),
        in_specs=[pl.BlockSpec(memory_space=pltpu.SMEM)] + [vmem] * 6,
        out_specs=(vmem,) * pieces,
        scratch_shapes=[
            pltpu.VMEM((slots, width), jnp.bfloat16),
            pltpu.VMEM((sources // GROUP, GROUP * capacity, GROUP * patch_cap), jnp.bfloat16),
            pltpu.VMEM((slots, w_down.shape[0]), jnp.bfloat16),
            pltpu.VMEM((24, wide), jnp.float32),
        ],
        compiler_params=pltpu.CompilerParams(vmem_limit_bytes=28 * 1024 * 1024),
    )(me, rows, w_up, gain, router, w_in, w_down)


def prepare_kernel(encoded, payload, gain, w_dq, w_up, queries, state):
    queries[...] = mm(normed_rows(encoded[...], gain[...]), w_dq[...]).astype(jnp.bfloat16)
    state[...] = mm(payload[: state.shape[0], :], w_up[...]).astype(jnp.bfloat16)


def prepare(encoded, payload, patch_cap, gain, w_dq, w_up):
    vmem = pl.BlockSpec(memory_space=pltpu.VMEM)
    return pl.pallas_call(
        prepare_kernel,
        out_shape=(
            jax.ShapeDtypeStruct(encoded.shape, jnp.bfloat16),
            jax.ShapeDtypeStruct((patch_cap, w_up.shape[1]), jnp.bfloat16),
        ),
        in_specs=[vmem] * 5,
        out_specs=(vmem, vmem),
        compiler_params=pltpu.CompilerParams(vmem_limit_bytes=8 * 1024 * 1024),
    )(encoded, payload, gain.reshape(1, -1), w_dq, w_up)


def decode_kernel(shares, *refs):
    state, *parts = refs[: 1 + shares]
    encoded, queries, flags, w_dkv, w_do, bytes_out, patch_out, mixed_ref = refs[1 + shares :]
    rows, width = encoded.shape
    patch_cap = state.shape[0]
    total = state[...].astype(jnp.float32)
    for part in parts:
        total = total + part[...].astype(jnp.float32)
    states = total.astype(jnp.bfloat16)
    patch_out[...] = states
    pairs = mm(states, w_dkv[...]).astype(jnp.bfloat16)
    flag = flags[...]
    upto = iota((rows, rows), 1) <= iota((rows, rows), 0)
    number = jnp.sum(jnp.where(upto, flag, 0), axis=1, keepdims=True) - 1
    bias = jnp.where(iota((rows, patch_cap), 1) <= number, 0.0, very_negative)
    lanes = 2 * HEAD
    for at in range(0, width, lanes):
        mixed = attend_pair(
            queries[:, at : at + lanes],
            pairs[:, at : at + lanes],
            pairs[:, width + at : width + at + lanes],
            bias,
        )
        mixed_ref[:, at : at + lanes] = mixed.astype(jnp.bfloat16)
    bytes_out[...] = (encoded[...].astype(jnp.float32) + mm(mixed_ref[...], w_do[...])).astype(
        jnp.bfloat16
    )


def decode(state, parts, encoded, queries, patch_start, w_dkv, w_do):
    vmem = pl.BlockSpec(memory_space=pltpu.VMEM)
    return pl.pallas_call(
        functools.partial(decode_kernel, len(parts)),
        out_shape=(
            jax.ShapeDtypeStruct(encoded.shape, jnp.bfloat16),
            jax.ShapeDtypeStruct(state.shape, jnp.bfloat16),
        ),
        in_specs=[vmem] * (6 + len(parts)),
        out_specs=(vmem, vmem),
        scratch_shapes=[pltpu.VMEM(encoded.shape, jnp.bfloat16)],
        compiler_params=pltpu.CompilerParams(vmem_limit_bytes=12 * 1024 * 1024),
    )(state, *parts, encoded, queries, patch_start.reshape(1, -1), w_dkv, w_do)


def digits():
    seq, expert = lax.axis_size("seq"), lax.axis_size("expert")
    inner = 2 if seq % 2 == 0 else 1
    core = 2 if expert % 2 == 0 else 1
    return {
        "z": ("seq", inner, seq // inner),
        "x": ("seq", 1, inner),
        "y": ("expert", core, expert // core),
        "c": ("expert", 1, core),
    }


def shift(x, digit, by):
    axis, stride, radix = digit
    pairs = []
    for i in range(lax.axis_size(axis)):
        g = i // stride % radix
        pairs.append((i, i + ((g + by) % radix - g) * stride))
    return lax.ppermute(x, axis, pairs)


def gathered(x, digit, place=0):
    return jnp.stack([x] + [shift(x, digit, d) for d in range(1, digit[2])], axis=place)


def gather_all(x):
    d = digits()
    half = x.shape[1] // 2
    x = gathered(x, d["z"])
    left = gathered(gathered(x[..., :half], d["x"]), d["y"])
    right = gathered(gathered(x[..., half:], d["y"]), d["x"], 1)
    return gathered(jnp.concatenate([left, right], axis=-1), d["c"])


def summed(parts):
    total = parts[0].astype(jnp.float32)
    for part in parts[1:]:
        total = total + part.astype(jnp.float32)
    return total


def reduced(x, digit, place=0):
    parts = [lax.index_in_dim(x, d, place, keepdims=False) for d in range(digit[2])]
    return summed([parts[0]] + [shift(parts[d], digit, -d) for d in range(1, digit[2])])


def narrow(v):
    return v.astype(jnp.bfloat16)


def mixture(payload, patch_cap, capacity, w_up, moe_gain, w_router, w_in, w_down):
    d = digits()
    wide = w_up.shape[1]
    rows = gather_all(payload)
    lead = rows.shape[:4]
    me = lax.axis_index("expert").astype(jnp.int32).reshape(1)
    paired = w_in.reshape(w_in.shape[1], -1)
    pieces = 2
    per_call = lead[1] if lead[1] * lead[2] * lead[3] <= 32 else 1

    def shares(core):
        got = [
            expert_share(
                rows[core, at : at + per_call].reshape((-1,) + rows.shape[4:]),
                patch_cap,
                capacity,
                me,
                w_up,
                moe_gain.reshape(1, wide),
                w_router.T,
                paired,
                w_down[0],
                pieces,
            )
            for at in range(0, lead[1], per_call)
        ]
        return [
            jnp.concatenate([g[k] for g in got]).reshape(lead[1:] + (patch_cap, wide // pieces))
            for k in range(pieces)
        ]

    sent = [shares(core) for core in range(lead[0] - 1, 0, -1)]
    sent = [shift(v, d["c"], -1) for part in sent for v in part]
    kept = shares(0)
    left, right = [narrow(summed([kept[k]] + sent[k::pieces])) for k in range(pieces)]
    left = narrow(reduced(narrow(reduced(left, d["x"], 1)), d["y"]))
    right = narrow(reduced(narrow(reduced(right, d["y"])), d["x"]))
    both = jnp.concatenate([left, right], axis=-1)
    return [both[0]] + [shift(both[by], d["z"], -by) for by in range(1, lead[3])]


def per_device(
    byte_states,
    patch_start,
    expert_ids,
    enc_gain,
    w_qkv,
    w_out,
    w_xq,
    w_xkv,
    w_up,
    moe_gain,
    w_router,
    w_in,
    w_down,
    dec_gain,
    w_dq,
    w_dkv,
    w_do,
):
    byte_dev = byte_states.shape[0]
    patch_cap = expert_ids.shape[0]
    experts = w_router.shape[1]
    capacity = 12 * patch_cap // (5 * experts)
    both_axes = ("seq", "expert")
    reach = -(-WINDOW // byte_dev)
    earlier = [passed_along(byte_states, both_axes, by) for by in range(reach, 0, -1)]
    place = lax.axis_index(both_axes).astype(jnp.int32).reshape(1)
    encoded, payload = encode(
        byte_states,
        earlier,
        patch_start,
        expert_ids,
        experts,
        capacity,
        place,
        enc_gain,
        w_qkv,
        w_out,
        w_xq,
        w_xkv,
    )
    parts = mixture(payload, patch_cap, capacity, w_up, moe_gain, w_router, w_in, w_down)
    queries, state = prepare(encoded, payload, patch_cap, dec_gain, w_dq, w_up)
    return decode(state, parts, encoded, queries, patch_start, w_dkv, w_do)


def solution(mesh):
    in_specs = (
        P(("seq", "expert"), None),
        P(("seq", "expert")),
        P(("seq", "expert"), None),
        P(),
        P(),
        P(),
        P(),
        P(),
        P(),
        P(),
        P(),
        P("expert", None, None, "seq"),
        P("expert", "seq", None),
        P(),
        P(),
        P(),
        P(),
    )
    out_specs = (P(("seq", "expert"), None), P(("seq", "expert"), None))
    return jax.shard_map(
        per_device, mesh=mesh, in_specs=in_specs, out_specs=out_specs, check_vma=False
    )
```

time: 180 us -> 122 us (0.68)
  matrix products: 55.1 us -> 0 us
  Pallas kernels: 0 us -> 26.9 us
  local copies, waits for them, and re-layouts: 33.8 us -> 13.1 us
  other arithmetic: 16.9 us -> 1.97 us
  starting transfers between devices: 25.2 us -> 28.7 us
  waiting for transfers between devices: 47 us -> 50.4 us
    dot_general x21 -> x0, matrix products: 49 us -> none  [the longest x3 8.68 us: attend(): jnp.einsum('hqk,hkd->hqd', weights, values, preferred_element_type=jnp.fl...]
    pallas_call x0 -> x5, Pallas kernels: none -> 26.9 us  [the longest x2 15.6 us: expert_share(): pl.pallas_call(functools.partial(expert_kernel, patch_cap, capacity, expe...]
    slice x12 -> x0, local copies, waits for them, and re-layouts: 14.4 us -> none  [the longest x2 3.59 us: per_device(): pairs[:, :model_width]]
    sub x1 -> x0, matrix products: 6.15 us -> none  [softmax_rows(): raised = jnp.exp(scores - highest)]
    ppermute x2, waiting for transfers between devices: 0.01 us -> 5.5 us  [passed_along(): return lax.ppermute(x, axis, pairs)]
    ppermute x17, starting transfers between devices: 17.7 us -> 22.3 us  [shift(): return lax.ppermute(x, axis, pairs)]
    reshape x6 -> x1, local copies, waits for them, and re-layouts: 3.1 us -> 0.11 us  [shares(): jnp.concatenate([g[k] for g in got])]
    unnamed x60 -> x35, local copies, waits for them, and re-layouts: 9.79 us -> 12.7 us
  transfers between devices with their start and end apart: 19 -> 19, of which waited for: 13 -> 13; matrix products, arithmetic and copies ran while one was open for 14% -> 5% of each run, Pallas kernels for 0% -> 7%
where the time goes in v2:
time: 122 us
  waiting for transfers between devices  50.4 us (41%)
  starting transfers between devices  28.7 us (24%)
  Pallas kernels  26.9 us (22%)
  local copies, waits for them, and re-layouts  13.1 us (11%)
  other arithmetic  1.97 us (2%)
    ppermute x17, waiting for transfers between devices, shift(): return lax.ppermute(x, axis, pairs)  44.9 us
    ppermute x17, starting transfers between devices, shift(): return lax.ppermute(x, axis, pairs)  22.3 us
    pallas_call x2, Pallas kernels, expert_share(): pl.pallas_call(functools.partial(expert_kernel, patch_cap, capacity, expe...  15.6 us
    unnamed x35, local copies, waits for them, and re-layouts  12.7 us
    pallas_call x1, Pallas kernels, encode(): pl.pallas_call(functools.partial(encoder_kernel, reach, experts, capacity...  7.51 us
    ppermute x2, starting transfers between devices, passed_along(): return lax.ppermute(x, axis, pairs)  6.36 us
    ppermute x2, waiting for transfers between devices, passed_along(): return lax.ppermute(x, axis, pairs)  5.5 us
    pallas_call x1, Pallas kernels, decode(): pl.pallas_call(functools.partial(decode_kernel, len(parts)), out_shape=(j...  3.06 us
  transfers between devices with their start and end apart: 19, of which 13 were waited for; matrix products, arithmetic and copies ran while one was open for 5% of the time, Pallas kernels for 7%

profile of v2, /device:TPU:0, one launch (start us, length us, event | category | flops | bytes accessed | tf_op | source)
XLA Modules:
  0.0 122.0 jit_solution(5622104529134244986)
XLA Ops:
  0.6 4.9 %collective-permute-start = (bf16[256,512]{1,0:T(8,128)(2,1)}, bf16[256,512]{1,0:T(8,128)(2,1)S(1)}, u32[]{:S(2)}, u32[]{:S(2)}) collective-permute-start(bf16[256,512]{1,0:T(8,128)(2,1)} %refs_1_.1), channel_id=1, source_target_pairs={{0,2},{1,3},{2,4},{3,5},{4,6},{5,7},{6,8},{7,9},{8,10},{9,11},{10,... | collective-permute-start | bytes 786440 | tf_op jit(solution)/shard_map/ppermute | solution.py:23
  5.5 1.5 %collective-permute-start.1 = (bf16[256,512]{1,0:T(8,128)(2,1)}, bf16[256,512]{1,0:T(8,128)(2,1)S(1)}, u32[]{:S(2)}, u32[]{:S(2)}) collective-permute-start(bf16[256,512]{1,0:T(8,128)(2,1)} %refs_1_.1), channel_id=1, source_target_pairs={{0,1},{1,2},{2,3},{3,4},{4,5},{5,6},{6,7},{7,8},{8,9},{9,10},{10,1... | collective-permute-start | bytes 786440 | tf_op jit(solution)/shard_map/ppermute | solution.py:23
  7.0 5.5 %collective-permute-done.refs_2_ = bf16[256,512]{1,0:T(8,128)(2,1)S(1)} collective-permute-done((bf16[256,512]{1,0:T(8,128)(2,1)}, bf16[256,512]{1,0:T(8,128)(2,1)S(1)}, u32[]{:S(2)}, u32[]{:S(2)}) %collective-permute-start) | collective-permute-done | bytes 262176 | tf_op jit(solution)/shard_map/ppermute | solution.py:23
  12.5 0.0 collective-permute-done.1.refs_3_
  12.5 1.4 %copy-done.3 = bf16[512,1536]{1,0:T(8,128)(2,1)S(1)} copy-done((bf16[512,1536]{1,0:T(8,128)(2,1)S(1)}, bf16[512,1536]{1,0:T(8,128)(2,1)}, u32[]{:S(2)}) %copy-start.3) | copy-done | bytes 1572888
  13.9 1.2 %copy-done.4 = bf16[512,1024]{1,0:T(8,128)(2,1)S(1)} copy-done((bf16[512,1024]{1,0:T(8,128)(2,1)S(1)}, bf16[512,1024]{1,0:T(8,128)(2,1)}, u32[]{:S(2)}) %copy-start.4) | copy-done | bytes 1048600
  15.2 1.0 copy-done.7
  16.2 1.0 copy-done.8
  17.2 0.9 copy-done.9
  18.2 0.7 copy-done.12
  18.9 0.7 copy-done.14
  19.6 0.7 copy-done.16
  20.2 7.5 %shard_map.176 = (bf16[256,512]{1,0:T(8,128)(2,1)S(1)}, bf16[48,512]{1,0:T(8,128)(2,1)S(1)}) custom-call(s32[1]{0:T(128)} %bitcast.refs_0_, bf16[256,512]{1,0:T(8,128)(2,1)S(1)} %copy-done.9, bf16[256,512]{1,0:T(8,128)(2,1)S(1)} %collective-permute-done.refs_2_, bf16[256,512]{1,0:T(8,128)(2,1)S(1)} %collective-permute-done.1.refs_3_, s32[1,256]{1,0:T(1,128)S(1)} %bitcast.88, ...), custom_call_target="tpu_custom_call" | custom-call | tf_op jit(solution)/shard_map/pallas_call | solution.py:147
  27.7 5.9 %collective-permute-start.2 = (bf16[48,512]{1,0:T(8,128)(2,1)S(1)}, bf16[48,512]{1,0:T(8,128)(2,1)S(1)}, u32[]{:S(2)}, u32[]{:S(2)}) collective-permute-start(bf16[48,512]{1,0:T(8,128)(2,1)S(1)} %get-tuple-element.11.payload), channel_id=1, source_target_pairs={{0,8},{4,12},{8,16},{12,20},{16,24},{20,28},{24,0},{28,4},{1,9},{5... | collective-permute-start | bytes 147464 | tf_op jit(solution)/shard_map/ppermute | solution.py:376
  33.7 2.6 %collective-permute-start.3 = (bf16[48,512]{1,0:T(8,128)(2,1)S(1)}, bf16[48,512]{1,0:T(8,128)(2,1)S(1)}, u32[]{:S(2)}, u32[]{:S(2)}) collective-permute-start(bf16[48,512]{1,0:T(8,128)(2,1)S(1)} %get-tuple-element.11.payload), channel_id=1, source_target_pairs={{0,16},{4,20},{8,24},{12,28},{16,0},{20,4},{24,8},{28,12},{1,17},{... | collective-permute-start | bytes 147464 | tf_op jit(solution)/shard_map/ppermute | solution.py:376
  36.3 1.4 %collective-permute-start.4 = (bf16[48,512]{1,0:T(8,128)(2,1)S(1)}, bf16[48,512]{1,0:T(8,128)(2,1)S(1)}, u32[]{:S(2)}, u32[]{:S(2)}) collective-permute-start(bf16[48,512]{1,0:T(8,128)(2,1)S(1)} %get-tuple-element.11.payload), channel_id=1, source_target_pairs={{0,24},{4,28},{8,0},{12,4},{16,8},{20,12},{24,16},{28,20},{1,25},{... | collective-permute-start | bytes 147464 | tf_op jit(solution)/shard_map/ppermute | solution.py:376
  37.6 0.1 collective-permute-done.2
  37.8 0.9 collective-permute-done.3
  38.7 1.7 %collective-permute-done.4 = bf16[48,512]{1,0:T(8,128)(2,1)S(1)} collective-permute-done((bf16[48,512]{1,0:T(8,128)(2,1)S(1)}, bf16[48,512]{1,0:T(8,128)(2,1)S(1)}, u32[]{:S(2)}, u32[]{:S(2)}) %collective-permute-start.4) | collective-permute-done | bytes 49184 | tf_op jit(solution)/shard_map/ppermute | solution.py:376
  40.4 0.7 collective-permute-start.5
  41.1 0.6 collective-permute-start.7
  41.7 3.8 %collective-permute-done.5 = bf16[4,48,256]{2,1,0:T(8,128)(2,1)S(1)} collective-permute-done((bf16[4,48,256]{2,1,0:T(8,128)(2,1)S(1)}, bf16[4,48,256]{2,1,0:T(8,128)(2,1)S(1)}, u32[]{:S(2)}, u32[]{:S(2)}) %collective-permute-start.5) | collective-permute-done | bytes 98336 | tf_op jit(solution)/shard_map/ppermute | solution.py:376
  45.6 0.1 collective-permute-start.6
  45.7 0.6 collective-permute-done.7
  46.3 1.1 collective-permute-start.8
  47.5 3.9 %collective-permute-done.6 = bf16[2,4,48,256]{3,2,1,0:T(8,128)(2,1)S(1)} collective-permute-done((bf16[2,4,48,256]{3,2,1,0:T(8,128)(2,1)S(1)}, bf16[2,4,48,256]{3,2,1,0:T(8,128)(2,1)S(1)}, u32[]{:S(2)}, u32[]{:S(2)}) %collective-permute-start.6) | collective-permute-done | bytes 196640 | tf_op jit(solution)/shard_map/ppermute | solution.py:376
  51.3 0.8 collective-permute-done.8
  52.1 0.1 maximum_maximum_fusion
  52.2 0.1 collective-permute-start.9
  52.2 0.0 copy-start
  52.3 0.0 copy-start.1
  52.3 4.3 %copy.27 = bf16[256,8,2,768]{3,1,2,0:T(8,128)(2,1)S(1)} copy(bf16[256,8,2,768]{3,2,1,0:T(2,128)(2,1)} %bitcast.94) | data formatting | bytes 12582912
  56.6 0.0 copy-start.10
  56.6 0.0 copy-start.11
  56.6 0.1 copy.24
  56.7 0.6 copy-done.10
  57.3 7.7 %shard_map.179 = (bf16[640,1024]{1,0:T(8,128)(2,1)S(1)}, bf16[640,1024]{1,0:T(8,128)(2,1)S(1)}) custom-call(s32[1]{0:T(128)} %bitcast.5.refs_0_, bf16[16,48,512]{2,1,0:T(8,128)(2,1)S(1)} %bitcast.79, bf16[512,2048]{1,0:T(8,128)(2,1)S(1)} %copy-done, f32[1,2048]{1,0:T(1,128)S(1)} %bitcast.86, f32[4,2048]{1,0:T(4,128)S(1)} %bitcast.84, ...), custom_call_target="tpu_custom_call" | custom-call | tf_op jit(solution)/shard_map/pallas_call | solution.py:277
  65.1 0.1 copy.25
  65.2 0.5 collective-permute-start.10
  65.7 0.1 collective-permute-start.13
  65.8 0.1 copy.23
  65.9 7.9 %shard_map.178 = (bf16[640,1024]{1,0:T(8,128)(2,1)S(1)}, bf16[640,1024]{1,0:T(8,128)(2,1)S(1)}) custom-call(s32[1]{0:T(128)} %bitcast.5.refs_0_, bf16[16,48,512]{2,1,0:T(8,128)(2,1)S(1)} %bitcast.78, bf16[512,2048]{1,0:T(8,128)(2,1)S(1)} %copy-done, f32[1,2048]{1,0:T(1,128)S(1)} %bitcast.87, f32[4,2048]{1,0:T(4,128)S(1)} %bitcast.85, ...), custom_call_target="tpu_custom_call" | custom-call | tf_op jit(solution)/shard_map/pallas_call | solution.py:277
  73.8 0.0 collective-permute-done.10
  73.8 0.6 fusion.1
  74.4 1.1 collective-permute-start.11
  75.5 0.5 fusion
  76.1 1.3 %collective-permute-start.14 = (bf16[2,4,40,1024]{3,2,1,0:T(8,128)(2,1)S(1)}, bf16[2,4,40,1024]{3,2,1,0:T(8,128)(2,1)S(1)}, u32[]{:S(2)}, u32[]{:S(2)}) collective-permute-start(bf16[2,4,40,1024]{3,2,1,0:T(8,128)(2,1)S(1)} %slice_bitcast_fusion), channel_id=1, source_target_pairs={{0,2},{1,3},{2,0},{3,1},{4,6},{5,7},{6,4},{7,5},{8,10},{9,11},{10,... | collective-permute-start | bytes 1966088 | tf_op jit(solution)/shard_map/ppermute | solution.py:376
  77.5 14.1 %collective-permute-done.11 = bf16[2,4,40,1024]{3,2,1,0:T(8,128)(2,1)S(1)} collective-permute-done((bf16[2,4,40,1024]{3,2,1,0:T(8,128)(2,1)S(1)}, bf16[2,4,40,1024]{3,2,1,0:T(8,128)(2,1)S(1)}, u32[]{:S(2)}, u32[]{:S(2)}) %collective-permute-start.11) | collective-permute-done | bytes 655392 | tf_op jit(solution)/shard_map/ppermute | solution.py:376
  91.6 0.2 fusion.3
  91.8 1.4 %collective-permute-start.12 = (bf16[4,40,1024]{2,1,0:T(8,128)(2,1)S(1)}, bf16[4,40,1024]{2,1,0:T(8,128)(2,1)S(1)}, u32[]{:S(2)}, u32[]{:S(2)}) collective-permute-start(bf16[4,40,1024]{2,1,0:T(8,128)(2,1)S(1)} %slice_bitcast_fusion.6), channel_id=1, source_target_pairs={{0,2},{1,3},{2,0},{3,1},{4,6},{5,7},{6,4},{7,5},{8,10},{9,11},{10,... | collective-permute-start | bytes 983048 | tf_op jit(solution)/shard_map/ppermute | solution.py:376
  93.3 0.2 fusion.2
  93.6 1.0 collective-permute-start.15
  94.6 6.6 %collective-permute-done.12 = bf16[4,40,1024]{2,1,0:T(8,128)(2,1)S(1)} collective-permute-done((bf16[4,40,1024]{2,1,0:T(8,128)(2,1)S(1)}, bf16[4,40,1024]{2,1,0:T(8,128)(2,1)S(1)}, u32[]{:S(2)}, u32[]{:S(2)}) %collective-permute-start.12) | collective-permute-done | bytes 327712 | tf_op jit(solution)/shard_map/ppermute | solution.py:376
  101.2 0.1 fusion.5
  101.3 0.0 copy-start.5
  101.3 1.3 %collective-permute-done.15 = bf16[4,40,1024]{2,1,0:T(8,128)(2,1)S(1)} collective-permute-done((bf16[4,40,1024]{2,1,0:T(8,128)(2,1)S(1)}, bf16[4,40,1024]{2,1,0:T(8,128)(2,1)S(1)}, u32[]{:S(2)}, u32[]{:S(2)}) %collective-permute-start.15) | collective-permute-done | bytes 327712 | tf_op jit(solution)/shard_map/ppermute | solution.py:376
  102.6 0.1 fusion.4
  102.7 0.0 copy-start.2
  102.8 3.7 %collective-permute-start.16 = (bf16[40,2048]{1,0:T(8,128)(2,1)S(1)}, bf16[40,2048]{1,0:T(8,128)(2,1)S(1)}, u32[]{:S(2)}, u32[]{:S(2)}) collective-permute-start(bf16[40,2048]{1,0:T(8,128)(2,1)S(1)} %get-tuple-element.20), channel_id=1, source_target_pairs={{0,24},{4,28},{8,0},{12,4},{16,8},{20,12},{24,16},{28,20},{1,25},{... | collective-permute-start | bytes 491528 | tf_op jit(solution)/shard_map/ppermute | solution.py:376
  106.5 0.6 collective-permute-start.18
  107.2 0.7 shard_map.177
  107.8 3.3 %collective-permute-done.16.refs_2_ = bf16[40,2048]{1,0:T(8,128)(2,1)S(1)} collective-permute-done((bf16[40,2048]{1,0:T(8,128)(2,1)S(1)}, bf16[40,2048]{1,0:T(8,128)(2,1)S(1)}, u32[]{:S(2)}, u32[]{:S(2)}) %collective-permute-start.16) | collective-permute-done | bytes 163872 | tf_op jit(solution)/shard_map/ppermute | solution.py:376
  111.2 7.7 %collective-permute-done.17.refs_3_ = bf16[40,2048]{1,0:T(8,128)(2,1)S(1)} collective-permute-done((bf16[40,2048]{1,0:T(8,128)(2,1)S(1)}, bf16[40,2048]{1,0:T(8,128)(2,1)S(1)}, u32[]{:S(2)}, u32[]{:S(2)}) %collective-permute-start.17) | collective-permute-done | bytes 163872 | tf_op jit(solution)/shard_map/ppermute | solution.py:376
  118.9 3.1 %shard_map.180 = (bf16[256,512]{1,0:T(8,128)(2,1)}, bf16[40,2048]{1,0:T(8,128)(2,1)}) custom-call(bf16[40,2048]{1,0:T(8,128)(2,1)S(1)} %get-tuple-element.12.refs_0_, bf16[40,2048]{1,0:T(8,128)(2,1)S(1)} %get-tuple-element.19.refs_1_, bf16[40,2048]{1,0:T(8,128)(2,1)S(1)} %collective-permute-done.16.refs_2_, ...), custom_call_target="tpu_custom_call" | custom-call | tf_op jit(solution)/shard_map/pallas_call | solution.py:345
  (33 shorter events, 0.3 us)
Async XLA Ops:
  0.6 11.9 %collective-permute-start = (bf16[256,512]{1,0:T(8,128)(2,1)}, bf16[256,512]{1,0:T(8,128)(2,1)S(1)}, u32[]{:S(2)}, u32[]{:S(2)}) collective-permute-start(bf16[256,512]{1,0:T(8,128)(2,1)} %refs_1_.1), channel_id=1, source_target_pairs={{0,2},{1,3},{2,4},{3,5},{4,6},{5,7},{6,8},{7,9},{8,10},{9,11},{10,... | collective-permute-start | bytes 786440 | tf_op jit(solution)/shard_map/ppermute | solution.py:23
  5.5 7.0 %collective-permute-start.1 = (bf16[256,512]{1,0:T(8,128)(2,1)}, bf16[256,512]{1,0:T(8,128)(2,1)S(1)}, u32[]{:S(2)}, u32[]{:S(2)}) collective-permute-start(bf16[256,512]{1,0:T(8,128)(2,1)} %refs_1_.1), channel_id=1, source_target_pairs={{0,1},{1,2},{2,3},{3,4},{4,5},{5,6},{6,7},{7,8},{8,9},{9,10},{10,1... | collective-permute-start | bytes 786440 | tf_op jit(solution)/shard_map/ppermute | solution.py:23
  12.5 1.4 %copy-start.3 = (bf16[512,1536]{1,0:T(8,128)(2,1)S(1)}, bf16[512,1536]{1,0:T(8,128)(2,1)}, u32[]{:S(2)}) copy-start(bf16[512,1536]{1,0:T(8,128)(2,1)} %refs_7_.1) | copy-start | bytes 4718596
  13.9 1.2 %copy-start.4 = (bf16[512,1024]{1,0:T(8,128)(2,1)S(1)}, bf16[512,1024]{1,0:T(8,128)(2,1)}, u32[]{:S(2)}) copy-start(bf16[512,1024]{1,0:T(8,128)(2,1)} %refs_10_.1) | copy-start | bytes 3145732
  15.2 1.0 copy-start.7
  16.2 1.0 copy-start.8
  17.2 0.9 copy-start.9
  18.2 0.7 copy-start.12
  18.9 0.7 copy-start.14
  19.6 0.7 copy-start.16
  27.7 10.0 %collective-permute-start.2 = (bf16[48,512]{1,0:T(8,128)(2,1)S(1)}, bf16[48,512]{1,0:T(8,128)(2,1)S(1)}, u32[]{:S(2)}, u32[]{:S(2)}) collective-permute-start(bf16[48,512]{1,0:T(8,128)(2,1)S(1)} %get-tuple-element.11.payload), channel_id=1, source_target_pairs={{0,8},{4,12},{8,16},{12,20},{16,24},{20,28},{24,0},{28,4},{1,9},{5... | collective-permute-start | bytes 147464 | tf_op jit(solution)/shard_map/ppermute | solution.py:376
  33.7 5.0 %collective-permute-start.3 = (bf16[48,512]{1,0:T(8,128)(2,1)S(1)}, bf16[48,512]{1,0:T(8,128)(2,1)S(1)}, u32[]{:S(2)}, u32[]{:S(2)}) collective-permute-start(bf16[48,512]{1,0:T(8,128)(2,1)S(1)} %get-tuple-element.11.payload), channel_id=1, source_target_pairs={{0,16},{4,20},{8,24},{12,28},{16,0},{20,4},{24,8},{28,12},{1,17},{... | collective-permute-start | bytes 147464 | tf_op jit(solution)/shard_map/ppermute | solution.py:376
  36.3 4.1 %collective-permute-start.4 = (bf16[48,512]{1,0:T(8,128)(2,1)S(1)}, bf16[48,512]{1,0:T(8,128)(2,1)S(1)}, u32[]{:S(2)}, u32[]{:S(2)}) collective-permute-start(bf16[48,512]{1,0:T(8,128)(2,1)S(1)} %get-tuple-element.11.payload), channel_id=1, source_target_pairs={{0,24},{4,28},{8,0},{12,4},{16,8},{20,12},{24,16},{28,20},{1,25},{... | collective-permute-start | bytes 147464 | tf_op jit(solution)/shard_map/ppermute | solution.py:376
  40.4 5.1 %collective-permute-start.5 = (bf16[4,48,256]{2,1,0:T(8,128)(2,1)S(1)}, bf16[4,48,256]{2,1,0:T(8,128)(2,1)S(1)}, u32[]{:S(2)}, u32[]{:S(2)}) collective-permute-start(bf16[4,48,256]{2,1,0:T(8,128)(2,1)S(1)} %get-tuple-element.27), channel_id=1, source_target_pairs={{0,4},{4,0},{8,12},{12,8},{16,20},{20,16},{24,28},{28,24},{1,5},{5... | collective-permute-start | bytes 294920 | tf_op jit(solution)/shard_map/ppermute | solution.py:376
  41.1 5.2 %collective-permute-start.7 = (bf16[4,48,256]{2,1,0:T(8,128)(2,1)S(1)}, bf16[4,48,256]{2,1,0:T(8,128)(2,1)S(1)}, u32[]{:S(2)}, u32[]{:S(2)}) collective-permute-start(bf16[4,48,256]{2,1,0:T(8,128)(2,1)S(1)} %get-tuple-element.26), channel_id=1, source_target_pairs={{0,2},{1,3},{2,0},{3,1},{4,6},{5,7},{6,4},{7,5},{8,10},{9,11},{10,... | collective-permute-start | bytes 294920 | tf_op jit(solution)/shard_map/ppermute | solution.py:376
  45.6 5.7 %collective-permute-start.6 = (bf16[2,4,48,256]{3,2,1,0:T(8,128)(2,1)S(1)}, bf16[2,4,48,256]{3,2,1,0:T(8,128)(2,1)S(1)}, u32[]{:S(2)}, u32[]{:S(2)}) collective-permute-start(bf16[2,4,48,256]{3,2,1,0:T(8,128)(2,1)S(1)} %get-tuple-element.23), channel_id=1, source_target_pairs={{0,2},{1,3},{2,0},{3,1},{4,6},{5,7},{6,4},{7,5},{8,10},{9,11},{10,... | collective-permute-start | bytes 589832 | tf_op jit(solution)/shard_map/ppermute | solution.py:376
  46.3 5.7 %collective-permute-start.8 = (bf16[2,4,48,256]{3,2,1,0:T(8,128)(2,1)S(1)}, bf16[2,4,48,256]{3,2,1,0:T(8,128)(2,1)S(1)}, u32[]{:S(2)}, u32[]{:S(2)}) collective-permute-start(bf16[2,4,48,256]{3,2,1,0:T(8,128)(2,1)S(1)} %get-tuple-element.29), channel_id=1, source_target_pairs={{0,4},{4,0},{8,12},{12,8},{16,20},{20,16},{24,28},{28,24},{1,5},{5... | collective-permute-start | bytes 589832 | tf_op jit(solution)/shard_map/ppermute | solution.py:376
  52.2 4.4 %collective-permute-start.9 = (bf16[2,2,4,48,512]{4,3,2,0,1:T(8,128)(2,1)S(1)}, bf16[2,2,4,48,512]{4,3,2,0,1:T(8,128)(2,1)S(1)}, u32[]{:S(2)}, u32[]{:S(2)}) collective-permute-start(bf16[2,2,4,48,512]{4,3,2,0,1:T(8,128)(2,1)S(1)} %maximum_maximum_fusion), channel_id=1, source_target_pairs={{0,1},{1,0},{2,3},{3,2},{4,5},{5,4},{6,7},{7,6},{8,9},{9,8},{10,11... | collective-permute-start | bytes 2359304 | tf_op jit(solution)/shard_map/ppermute | solution.py:376
  52.2 4.4 %copy-start = (bf16[512,2048]{1,0:T(8,128)(2,1)S(1)}, bf16[512,2048]{1,0:T(8,128)(2,1)}, u32[]{:S(2)}) copy-start(bf16[512,2048]{1,0:T(8,128)(2,1)} %refs_2_.3) | copy-start | bytes 6291460
  52.3 4.4 %copy-start.1 = (bf16[1,768,2048]{2,1,0:T(8,128)(2,1)S(1)}, bf16[1,768,2048]{2,1,0:T(8,128)(2,1)}, u32[]{:S(2)}) copy-start(bf16[1,768,2048]{2,1,0:T(8,128)(2,1)} %param.29) | copy-start | bytes 9437188
  56.6 0.8 copy-start.10
  56.6 0.8 copy-start.11
  65.2 8.6 %collective-permute-start.10 = (bf16[2,2,4,40,1024]{4,3,2,0,1:T(8,128)(2,1)S(1)}, bf16[2,2,4,40,1024]{4,3,2,0,1:T(8,128)(2,1)S(1)}, u32[]{:S(2)}, u32[]{:S(2)}) collective-permute-start(bf16[2,2,4,40,1024]{4,3,2,0,1:T(8,128)(2,1)S(1)} %copy.25), channel_id=1, source_target_pairs={{0,1},{1,0},{2,3},{3,2},{4,5},{5,4},{6,7},{7,6},{8,9},{9,8},{10,11... | collective-permute-start | bytes 3932168 | tf_op jit(solution)/shard_map/ppermute | solution.py:376
  65.7 9.8 %collective-permute-start.13 = (bf16[2,2,4,40,1024]{4,3,2,1,0:T(8,128)(2,1)S(1)}, bf16[2,2,4,40,1024]{4,3,2,1,0:T(8,128)(2,1)S(1)}, u32[]{:S(2)}, u32[]{:S(2)}) collective-permute-start(bf16[2,2,4,40,1024]{4,3,2,1,0:T(8,128)(2,1)S(1)} %bitcast.93), channel_id=1, source_target_pairs={{0,1},{1,0},{2,3},{3,2},{4,5},{5,4},{6,7},{7,6},{8,9},{9,8},{10,11... | collective-permute-start | bytes 3932168 | tf_op jit(solution)/shard_map/ppermute | solution.py:376
  74.4 17.2 %collective-permute-start.11 = (bf16[2,4,40,1024]{3,2,1,0:T(8,128)(2,1)S(1)}, bf16[2,4,40,1024]{3,2,1,0:T(8,128)(2,1)S(1)}, u32[]{:S(2)}, u32[]{:S(2)}) collective-permute-start(bf16[2,4,40,1024]{3,2,1,0:T(8,128)(2,1)S(1)} %slice_bitcast_fusion.2), channel_id=1, source_target_pairs={{0,4},{4,0},{8,12},{12,8},{16,20},{20,16},{24,28},{28,24},{1,5},{5... | collective-permute-start | bytes 1966088 | tf_op jit(solution)/shard_map/ppermute | solution.py:376
  76.1 17.1 %collective-permute-start.14 = (bf16[2,4,40,1024]{3,2,1,0:T(8,128)(2,1)S(1)}, bf16[2,4,40,1024]{3,2,1,0:T(8,128)(2,1)S(1)}, u32[]{:S(2)}, u32[]{:S(2)}) collective-permute-start(bf16[2,4,40,1024]{3,2,1,0:T(8,128)(2,1)S(1)} %slice_bitcast_fusion), channel_id=1, source_target_pairs={{0,2},{1,3},{2,0},{3,1},{4,6},{5,7},{6,4},{7,5},{8,10},{9,11},{10,... | collective-permute-start | bytes 1966088 | tf_op jit(solution)/shard_map/ppermute | solution.py:376
  91.8 9.3 %collective-permute-start.12 = (bf16[4,40,1024]{2,1,0:T(8,128)(2,1)S(1)}, bf16[4,40,1024]{2,1,0:T(8,128)(2,1)S(1)}, u32[]{:S(2)}, u32[]{:S(2)}) collective-permute-start(bf16[4,40,1024]{2,1,0:T(8,128)(2,1)S(1)} %slice_bitcast_fusion.6), channel_id=1, source_target_pairs={{0,2},{1,3},{2,0},{3,1},{4,6},{5,7},{6,4},{7,5},{8,10},{9,11},{10,... | collective-permute-start | bytes 983048 | tf_op jit(solution)/shard_map/ppermute | solution.py:376
  93.6 9.1 %collective-permute-start.15 = (bf16[4,40,1024]{2,1,0:T(8,128)(2,1)S(1)}, bf16[4,40,1024]{2,1,0:T(8,128)(2,1)S(1)}, u32[]{:S(2)}, u32[]{:S(2)}) collective-permute-start(bf16[4,40,1024]{2,1,0:T(8,128)(2,1)S(1)} %slice_bitcast_fusion.4), channel_id=1, source_target_pairs={{0,4},{4,0},{8,12},{12,8},{16,20},{20,16},{24,28},{28,24},{1,5},{5... | collective-permute-start | bytes 983048 | tf_op jit(solution)/shard_map/ppermute | solution.py:376
  101.2 6.0 %copy-start.15 = (f32[512]{0:T(512)S(1)}, f32[512]{0:T(512)}, u32[]{:S(2)}) copy-start(f32[512]{0:T(512)} %param.30) | copy-start | bytes 6148
  101.3 5.9 %copy-start.5 = (bf16[512,512]{1,0:T(8,128)(2,1)S(1)}, bf16[512,512]{1,0:T(8,128)(2,1)}, u32[]{:S(2)}) copy-start(bf16[512,512]{1,0:T(8,128)(2,1)} %w_dq.1) | copy-start | bytes 1572868
  102.6 16.3 %copy-start.6 = (bf16[512,512]{1,0:T(8,128)(2,1)S(1)}, bf16[512,512]{1,0:T(8,128)(2,1)}, u32[]{:S(2)}) copy-start(bf16[512,512]{1,0:T(8,128)(2,1)} %refs_9_.3) | copy-start | bytes 1572868
  102.7 16.2 %copy-start.2 = (bf16[2048,1024]{1,0:T(8,128)(2,1)S(1)}, bf16[2048,1024]{1,0:T(8,128)(2,1)}, u32[]{:S(2)}) copy-start(bf16[2048,1024]{1,0:T(8,128)(2,1)} %refs_8_.3) | copy-start | bytes 12582916
  102.8 8.4 %collective-permute-start.16 = (bf16[40,2048]{1,0:T(8,128)(2,1)S(1)}, bf16[40,2048]{1,0:T(8,128)(2,1)S(1)}, u32[]{:S(2)}, u32[]{:S(2)}) collective-permute-start(bf16[40,2048]{1,0:T(8,128)(2,1)S(1)} %get-tuple-element.20), channel_id=1, source_target_pairs={{0,24},{4,28},{8,0},{12,4},{16,8},{20,12},{24,16},{28,20},{1,25},{... | collective-permute-start | bytes 491528 | tf_op jit(solution)/shard_map/ppermute | solution.py:376
  106.5 12.4 %collective-permute-start.17 = (bf16[40,2048]{1,0:T(8,128)(2,1)S(1)}, bf16[40,2048]{1,0:T(8,128)(2,1)S(1)}, u32[]{:S(2)}, u32[]{:S(2)}) collective-permute-start(bf16[40,2048]{1,0:T(8,128)(2,1)S(1)} %get-tuple-element.21), channel_id=1, source_target_pairs={{0,16},{4,20},{8,24},{12,28},{16,0},{20,4},{24,8},{28,12},{1,17},{... | collective-permute-start | bytes 491528 | tf_op jit(solution)/shard_map/ppermute | solution.py:376
  106.5 12.4 %collective-permute-start.18 = (bf16[40,2048]{1,0:T(8,128)(2,1)S(1)}, bf16[40,2048]{1,0:T(8,128)(2,1)S(1)}, u32[]{:S(2)}, u32[]{:S(2)}) collective-permute-start(bf16[40,2048]{1,0:T(8,128)(2,1)S(1)} %get-tuple-element.18), channel_id=1, source_target_pairs={{0,8},{4,12},{8,16},{12,20},{16,24},{20,28},{24,0},{28,4},{1,9},{5... | collective-permute-start | bytes 491528 | tf_op jit(solution)/shard_map/ppermute | solution.py:376
  107.2 11.7 %copy-start.13 = (s32[256]{0:T(256)S(1)}, s32[256]{0:T(256)}, u32[]{:S(2)}) copy-start(s32[256]{0:T(256)} %param.18) | copy-start | bytes 3076

commit v3 on v2

v3 whole, which is shorter than its diff:
```python
import functools
import math

import jax
import jax.numpy as jnp
from jax import lax
from jax.experimental import pallas as pl
from jax.experimental.pallas import tpu as pltpu
from jax.sharding import PartitionSpec as P

HEADS_L = 8
HEAD = 64
WINDOW = 512


epsilon = 1e-06
very_negative = -1e30


def passed_along(x, axis, by):
    length = lax.axis_size(axis)
    pairs = [(i, i + by) for i in range(length) if 0 <= i + by < length]
    return lax.ppermute(x, axis, pairs)


def normed_rows(x, gain_row):
    wide = x.astype(jnp.float32)
    scale = lax.rsqrt(jnp.mean(wide * wide, axis=-1, keepdims=True) + epsilon)
    return (wide * scale * gain_row).astype(jnp.bfloat16)


def cost(flops):
    return pl.CostEstimate(flops=int(flops), transcendentals=0, bytes_accessed=0)


def mm(a, b):
    return jnp.dot(a, b, preferred_element_type=jnp.float32)


def mm_t(a, b):
    return lax.dot_general(a, b, (((1,), (1,)), ((), ())), preferred_element_type=jnp.float32)


def as_bf16(mask):
    return mask.astype(jnp.float32).astype(jnp.bfloat16)


def iota(shape, dim):
    return lax.broadcasted_iota(jnp.int32, shape, dim)


def attend_pair(q, k, v, bias):
    first = iota((1, 2 * HEAD), 1) < HEAD
    q = q * jnp.asarray(1.0 / math.sqrt(HEAD), q.dtype)
    outs = []
    for here in (first, jnp.logical_not(first)):
        scores = mm_t(jnp.where(here, q, jnp.zeros_like(q)), k) + bias
        raised = jnp.exp(scores - jnp.max(scores, axis=-1, keepdims=True)).astype(jnp.bfloat16)
        both = mm(raised, jnp.where(here, v, jnp.ones_like(v)))
        outs.append(both / pltpu.roll(both, HEAD, 1))
    return jnp.where(first, outs[0], outs[1])


def opening_kernel(reach, capacity, *refs):
    place, own_in, flags_in, ids_in, gain_in, w_qkv_in, w_out_in, w_xq_in, w_xkv_in = refs[:9]
    outs, (flags, ids, w_qkv, sem) = refs[9:-4], refs[-4:]
    own, gain, w_kv, w_out, w_xq, w_xkv, projected_out = outs[:7]
    bias_out, since_out, ends_out, member_out, live_out, table_out, decode_out = outs[7:]
    pairs = [
        (own_in, own),
        (gain_in, gain),
        (w_qkv_in, w_qkv),
        (flags_in, flags),
        (ids_in, ids),
        (w_out_in, w_out),
        (w_xq_in, w_xq),
        (w_xkv_in, w_xkv),
    ]
    copies = [pltpu.make_async_copy(a, b, sem.at[k]) for k, (a, b) in enumerate(pairs)]
    for copy in copies:
        copy.start()
    rows, width = own.shape
    patch_cap = rows * 5 // 32
    keys = (reach + 1) * rows
    at_query = iota((rows, keys), 0) + reach * rows
    at_key = iota((rows, keys), 1)
    allowed = (at_key <= at_query) & (at_key > at_query - WINDOW)
    allowed = allowed & (at_key >= (reach - place[0]) * rows)
    bias_out[...] = jnp.where(allowed, 0.0, very_negative)
    for copy in copies[:3]:
        copy.wait()
    normed = normed_rows(own[...], gain[...])
    projected_out[...] = mm(normed, w_qkv[...]).astype(jnp.bfloat16)
    w_kv[...] = w_qkv[:, width:]
    copies[3].wait()
    flag = flags[...]
    at_row, at_col = iota((rows, rows), 0), iota((rows, rows), 1)
    upto = at_col <= at_row
    opened = jnp.max(jnp.where(upto & (flag == 1), at_col, 0), axis=1, keepdims=True)
    since_out[...] = iota((rows, 1), 0) - opened
    own_number = jnp.sum(jnp.where(upto, flag, 0), axis=1, keepdims=True) - 1
    decode_out[...] = jnp.where(iota((rows, patch_cap), 1) <= own_number, 0.0, very_negative)
    eight = jnp.broadcast_to(flag, (8, rows)).astype(jnp.float32).astype(jnp.bfloat16)
    number = mm(eight, as_bf16(at_row <= at_col))[:1].astype(jnp.int32) - 1
    at_byte = iota((patch_cap, rows), 1)
    member = number == iota((patch_cap, rows), 0)
    last = jnp.max(jnp.where(member, at_byte, -1), axis=1, keepdims=True)
    live_out[...] = (last >= 0).astype(jnp.float32)
    ends_out[...] = as_bf16(member & (at_byte == last))
    member_out[...] = jnp.where(member, 0.0, very_negative)

    copies[4].wait()
    square = (patch_cap, patch_cap)
    same = iota(square, 0) == iota(square, 1)
    earlier_slot = iota(square, 0) < iota(square, 1)
    id_rows = [ids[k : k + 1, :] for k in range(2)]
    id_cols = [jnp.sum(jnp.where(same, row, 0), axis=1, keepdims=True) for row in id_rows]
    targets = []
    for row in id_rows:
        named = sum((col == row).astype(jnp.int32) for col in id_cols)
        rank = jnp.sum(jnp.where(earlier_slot, named, 0), axis=0, keepdims=True)
        targets.append(row * capacity + rank)
    extra = table_out.shape[0]
    at_extra = iota((extra, patch_cap), 0)
    table = jnp.where(at_extra == 0, targets[0], jnp.where(at_extra == 1, targets[1], 0))
    table_out[...] = jnp.zeros_like(table_out)
    table_out[:, :patch_cap] = table.astype(jnp.float32).astype(jnp.bfloat16)
    for copy in copies[5:]:
        copy.wait()


def opening(byte_states, patch_start, expert_ids, reach, capacity, place, enc_gain, *ws):
    rows, width = byte_states.shape
    w_qkv, w_out, w_xq, w_xkv = ws
    patch_cap = expert_ids.shape[0]
    extra = -(-(patch_cap + 2) // 16) * 16 - patch_cap
    keys = (reach + 1) * rows
    vmem, anywhere = pl.BlockSpec(memory_space=pltpu.VMEM), pl.BlockSpec(memory_space=pltpu.HBM)
    like = jax.ShapeDtypeStruct
    bf16, f32 = jnp.bfloat16, jnp.float32
    return pl.pallas_call(
        functools.partial(opening_kernel, reach, capacity),
        out_shape=(
            like((rows, width), bf16),
            like((1, width), f32),
            like((width, 2 * width), bf16),
            like(w_out.shape, bf16),
            like(w_xq.shape, bf16),
            like(w_xkv.shape, bf16),
            like((rows, 3 * width), bf16),
            like((rows, keys), f32),
            like((rows, 1), jnp.int32),
            like((patch_cap, rows), bf16),
            like((patch_cap, rows), f32),
            like((patch_cap, 1), f32),
            like((extra, width), bf16),
            like((rows, patch_cap), f32),
        ),
        in_specs=[pl.BlockSpec(memory_space=pltpu.SMEM)] + [anywhere] * 8,
        out_specs=(vmem,) * 14,
        scratch_shapes=[
            pltpu.VMEM((1, rows), jnp.int32),
            pltpu.VMEM((2, patch_cap), jnp.int32),
            pltpu.VMEM(w_qkv.shape, bf16),
            pltpu.SemaphoreType.DMA((8,)),
        ],
        cost_estimate=cost(4 * rows * width * 3 * width),
        compiler_params=pltpu.CompilerParams(vmem_limit_bytes=16 * 1024 * 1024),
    )(
        place,
        *[
            pltpu.with_memory_space_constraint(v, pltpu.HBM)
            for v in (
                byte_states,
                patch_start.reshape(1, rows),
                expert_ids.T,
                enc_gain.reshape(1, width),
                *ws,
            )
        ],
    )


def encoder_kernel(reach, *refs):
    instead, earlier, nearest, refs = refs[0], refs[1 : 1 + reach], refs[1 + reach], refs[2 + reach :]
    own, gain, w_kv, w_out, w_xq, w_xkv, projected = refs[:7]
    bias, since, ends, member_bias, live, table = refs[7:13]
    encoded_out, payload_out, pairs_ref, mixed_ref = refs[13:]
    rows, width = own.shape
    patch_cap = ends.shape[0]
    pairs_ref[reach * rows :, :] = projected[:, width:]
    for at, block in enumerate(earlier):
        moved = block[...]
        if at == reach - 1:
            moved = jnp.where(instead[0] == 1, nearest[...], moved)
        moved = normed_rows(moved, gain[...])
        pairs_ref[at * rows : (at + 1) * rows, :] = mm(moved, w_kv[...]).astype(jnp.bfloat16)
    lanes = 2 * HEAD
    for at in range(0, width, lanes):
        mixed = attend_pair(
            projected[:, at : at + lanes],
            pairs_ref[:, at : at + lanes],
            pairs_ref[:, width + at : width + at + lanes],
            bias[...],
        )
        mixed_ref[:, at : at + lanes] = mixed.astype(jnp.bfloat16)
    encoded = (own[...].astype(jnp.float32) + mm(mixed_ref[...], w_out[...])).astype(jnp.bfloat16)
    encoded_out[...] = encoded

    inside = since[...]
    highest = encoded.astype(jnp.float32)
    step = 1
    while step < rows:
        highest = jnp.where(
            inside >= step, jnp.maximum(highest, pltpu.roll(highest, step, 0)), highest
        )
        step *= 2
    pooled = mm(ends[...], highest.astype(jnp.bfloat16))
    patch_queries = mm(pooled.astype(jnp.bfloat16), w_xq[...]).astype(jnp.bfloat16)
    byte_pairs = mm(encoded, w_xkv[...]).astype(jnp.bfloat16)
    alive = live[...] > 0.0
    for at in range(0, width, lanes):
        mixed = attend_pair(
            patch_queries[:, at : at + lanes],
            byte_pairs[:, at : at + lanes],
            byte_pairs[:, width + at : width + at + lanes],
            member_bias[...],
        )
        total = jnp.where(alive, pooled[:, at : at + lanes] + mixed, 0.0)
        payload_out[:patch_cap, at : at + lanes] = total.astype(jnp.bfloat16)
    payload_out[patch_cap:, :] = table[...]


def encode(instead, earlier, nearest, opened):
    rows, width = opened[0].shape
    reach = len(earlier)
    vmem = pl.BlockSpec(memory_space=pltpu.VMEM)
    payload_rows = opened[9].shape[0] + opened[12].shape[0]
    return pl.pallas_call(
        functools.partial(encoder_kernel, reach),
        out_shape=(
            jax.ShapeDtypeStruct((rows, width), jnp.bfloat16),
            jax.ShapeDtypeStruct((payload_rows, width), jnp.bfloat16),
        ),
        in_specs=[pl.BlockSpec(memory_space=pltpu.SMEM)] + [vmem] * (14 + reach),
        out_specs=(vmem, vmem),
        scratch_shapes=[
            pltpu.VMEM(((reach + 1) * rows, 2 * width), jnp.bfloat16),
            pltpu.VMEM((rows, width), jnp.bfloat16),
        ],
        cost_estimate=cost(24 * rows * width * (reach + 1) * rows),
        compiler_params=pltpu.CompilerParams(vmem_limit_bytes=16 * 1024 * 1024),
    )(instead, *earlier, nearest, *opened[:13])


def mm_first(a, b):
    return lax.dot_general(a, b, (((0,), (0,)), ((), ())), preferred_element_type=jnp.float32)


def counted_from(values, step, most):
    return sum((values >= step * k).astype(jnp.int32) for k in range(1, most))


GROUP = 4


def give_back(term, spread, group, halves, order):
    for half, (out, places) in enumerate(zip(halves, order)):
        width = out.shape[-1]
        total = mm_first(spread, term[:, half * width : (half + 1) * width]).astype(jnp.bfloat16)
        block = out.shape[-2]
        for s in range(GROUP):
            out[places[group * GROUP + s]] = total[s * block : (s + 1) * block]


def stream_kernel(patch_cap, capacity, experts, blocks, order, *refs):
    me_ref, own_ref, moved_ref, w_up, gain, router, w_in, w_down = refs[:8]
    outs = refs[8:10]
    hidden_ref, gate_ref, spread_ref, all_hidden, later_spread, routed_ref, parts_ref = refs[10:]
    held, width = own_ref.shape[-2:]
    per = GROUP * capacity
    kept = len(blocks) // 2
    me = me_ref[0]
    slots = iota((per, 1), 0)
    source_of_slot = counted_from(slots, capacity, GROUP)
    place_of_slot = slots - source_of_slot * capacity + me * capacity
    lanes = 128

    def spreader(block):
        at_from, at_to = iota((GROUP * lanes, GROUP * block), 0), iota((GROUP * lanes, GROUP * block), 1)
        source = counted_from(at_from, lanes, GROUP)
        within = at_from - source * lanes
        return as_bf16((at_to == source * block + within) & (within < block))

    spread_held, spread_cap = spreader(held), spreader(patch_cap)

    def matched(table, spread, block):
        targets = mm(table, spread).astype(jnp.int32)
        at = iota((1, GROUP * block), 1)
        source = counted_from(at, block, GROUP)
        first, second = targets[0:1], targets[1:2]
        hit = (first == place_of_slot) | (second == place_of_slot)
        hit = hit & (source == source_of_slot) & (at - source * block < patch_cap)
        named = [counted_from(t, capacity, experts) for t in (first, second)]
        return hit, jnp.where(named[0] == me, named[1], named[0])

    others = []
    for g, begin in enumerate(blocks):
        rows_ref = own_ref if g < kept else moved_ref
        tables = []
        for s in range(begin, begin + GROUP):
            block = rows_ref[s, held - 16 : held, :lanes].astype(jnp.float32)
            tables.append(block[patch_cap - (held - 16) : patch_cap - (held - 16) + 8])
        table = jnp.concatenate(tables, axis=1).astype(jnp.bfloat16)
        hit, other = matched(table, spread_held, held)
        others.append(jnp.sum(jnp.where(hit, other, 0), axis=1, keepdims=True))
        block = rows_ref[begin : begin + GROUP].reshape(GROUP * held, width)
        routed_ref[g * per : (g + 1) * per, :] = mm(as_bf16(hit), block).astype(jnp.bfloat16)
        hit, _ = matched(table, spread_cap, patch_cap)
        if g < kept:
            spread_ref[g] = as_bf16(hit)
        else:
            later_spread[g - kept] = as_bf16(hit)
    other = jnp.concatenate(others, axis=0)

    state = mm(routed_ref[...], w_up[...]).astype(jnp.bfloat16).astype(jnp.float32)
    gained = (state * gain[...]).astype(jnp.bfloat16)
    scale = lax.rsqrt(jnp.mean(state * state, axis=-1, keepdims=True) + epsilon)

    parts_ref[...] = jnp.zeros_like(parts_ref)
    left = router[...]
    for part in range(3):
        here = left.astype(jnp.bfloat16).astype(jnp.float32)
        parts_ref[8 * part : 8 * part + experts, :] = here
        left = left - here
    parts = parts_ref[...].astype(jnp.bfloat16)
    deep = parts.shape[1] // 4
    logits = sum(
        mm_t(gained[:, k * deep : (k + 1) * deep], parts[:, k * deep : (k + 1) * deep])
        for k in range(4)
    )
    logits = logits * scale
    expert_of_lane = iota((1, parts_ref.shape[0]), 1) & 7
    mine = jnp.sum(jnp.where(expert_of_lane == me, logits, 0.0), axis=1, keepdims=True)
    rival = jnp.sum(jnp.where(expert_of_lane == other, logits, 0.0), axis=1, keepdims=True)
    highest = jnp.maximum(mine, rival)
    raised = jnp.exp(mine - highest)
    gate = raised / (raised + jnp.exp(rival - highest))

    hidden_share = all_hidden.shape[1]
    chunk = 256 if hidden_share % 256 == 0 else hidden_share
    for at in range(0, hidden_share, chunk):
        opened = mm(gained, w_in[:, at : at + chunk]) * scale
        upper = mm(gained, w_in[:, hidden_share + at : hidden_share + at + chunk]) * scale
        all_hidden[:, at : at + chunk] = (opened / (1.0 + jnp.exp(-opened)) * upper).astype(
            jnp.bfloat16
        )
    first = kept * per
    hidden_ref[...] = all_hidden[:first, :]
    gate_ref[...] = gate[:first]
    term = (mm(all_hidden[first:, :], w_down[...]) * gate[first:]).astype(jnp.bfloat16)
    for g in range(kept):
        give_back(term[g * per : (g + 1) * per], later_spread[g], g, outs, order)


def share_kernel(order, hidden, gate, spread, w_down, *outs):
    groups, per, _ = spread.shape
    term = (mm(hidden[...], w_down[...]) * gate[...]).astype(jnp.bfloat16)
    for g in range(groups):
        give_back(term[g * per : (g + 1) * per], spread[g], g, outs, order)


def share_shapes(sources, patch_cap, wide):
    half = jax.ShapeDtypeStruct((sources, patch_cap, wide // 2), jnp.bfloat16)
    return (half, half)


def stream(own, moved, blocks, order, patch_cap, capacity, me, w_up, gain, router, w_in, w_down):
    held, width = own.shape[-2:]
    experts, wide = router.shape
    vmem = pl.BlockSpec(memory_space=pltpu.VMEM)
    per = GROUP * capacity
    slots = 2 * len(blocks) * per
    spread = jax.ShapeDtypeStruct((len(blocks), per, GROUP * patch_cap), jnp.bfloat16)
    return pl.pallas_call(
        functools.partial(stream_kernel, patch_cap, capacity, experts, blocks * 2, order),
        out_shape=share_shapes(len(blocks) * GROUP, patch_cap, wide)
        + (
            jax.ShapeDtypeStruct((slots // 2, w_down.shape[0]), jnp.bfloat16),
            jax.ShapeDtypeStruct((slots // 2, 1), jnp.float32),
            spread,
        ),
        in_specs=[pl.BlockSpec(memory_space=pltpu.SMEM)] + [vmem] * 7,
        out_specs=(vmem,) * 5,
        scratch_shapes=[
            pltpu.VMEM((slots, w_down.shape[0]), jnp.bfloat16),
            pltpu.VMEM(spread.shape, jnp.bfloat16),
            pltpu.VMEM((slots, width), jnp.bfloat16),
            pltpu.VMEM((24, wide), jnp.float32),
        ],
        cost_estimate=cost(slots * wide * (width + w_in.shape[1]) // 4),
        compiler_params=pltpu.CompilerParams(vmem_limit_bytes=24 * 1024 * 1024),
    )(me, own, moved, w_up, gain, router, w_in, w_down)


def gated_share(hidden, gate, spread, w_down, order, patch_cap):
    groups = spread.shape[0]
    wide = w_down.shape[1]
    vmem = pl.BlockSpec(memory_space=pltpu.VMEM)
    return pl.pallas_call(
        functools.partial(share_kernel, order),
        out_shape=share_shapes(groups * GROUP, patch_cap, wide),
        in_specs=[vmem] * 4,
        out_specs=(vmem,) * 2,
        cost_estimate=cost(1000),
        compiler_params=pltpu.CompilerParams(vmem_limit_bytes=16 * 1024 * 1024),
    )(hidden, gate, spread, w_down)


def prepare_kernel(encoded, payload, gain, w_dq, w_up, queries, state):
    queries[...] = mm(normed_rows(encoded[...], gain[...]), w_dq[...]).astype(jnp.bfloat16)
    state[...] = mm(payload[: state.shape[0], :], w_up[...]).astype(jnp.bfloat16)


def prepare(encoded, payload, patch_cap, gain, w_dq, w_up):
    vmem = pl.BlockSpec(memory_space=pltpu.VMEM)
    return pl.pallas_call(
        prepare_kernel,
        out_shape=(
            jax.ShapeDtypeStruct(encoded.shape, jnp.bfloat16),
            jax.ShapeDtypeStruct((patch_cap, w_up.shape[1]), jnp.bfloat16),
        ),
        in_specs=[vmem] * 5,
        out_specs=(vmem, vmem),
        cost_estimate=cost(2 * patch_cap * w_up.size),
        compiler_params=pltpu.CompilerParams(vmem_limit_bytes=8 * 1024 * 1024),
    )(encoded, payload, gain.reshape(1, -1), w_dq, w_up)


def decode_kernel(wholes, *refs):
    state, *parts = refs[:-8]
    encoded, queries, bias, w_dkv, w_do, bytes_out, patch_out, mixed_ref = refs[-8:]
    rows, width = encoded.shape
    wide = state.shape[1] // 2
    per = (len(parts) - wholes) // 2
    pairs = 0.0
    for half in range(2):
        here = slice(half * wide, (half + 1) * wide)
        total = state[:, here].astype(jnp.float32)
        for part in parts[wholes + half * per : wholes + (half + 1) * per]:
            total = total + part[0].astype(jnp.float32)
        for part in parts[:wholes]:
            total = total + part[:, here].astype(jnp.float32)
        states = total.astype(jnp.bfloat16)
        patch_out[:, here] = states
        pairs = pairs + mm(states, w_dkv[here, :])
    pairs = pairs.astype(jnp.bfloat16)
    lanes = 2 * HEAD
    for at in range(0, width, lanes):
        mixed = attend_pair(
            queries[:, at : at + lanes],
            pairs[:, at : at + lanes],
            pairs[:, width + at : width + at + lanes],
            bias[...],
        )
        mixed_ref[:, at : at + lanes] = mixed.astype(jnp.bfloat16)
    bytes_out[...] = (encoded[...].astype(jnp.float32) + mm(mixed_ref[...], w_do[...])).astype(
        jnp.bfloat16
    )


def decode(state, wholes, halves, encoded, queries, bias, w_dkv, w_do):
    vmem = pl.BlockSpec(memory_space=pltpu.VMEM)
    parts = [*wholes, *halves[0], *halves[1]]
    return pl.pallas_call(
        functools.partial(decode_kernel, len(wholes)),
        out_shape=(
            jax.ShapeDtypeStruct(encoded.shape, jnp.bfloat16),
            jax.ShapeDtypeStruct(state.shape, jnp.bfloat16),
        ),
        in_specs=[vmem] * (6 + len(parts)),
        out_specs=(vmem, vmem),
        scratch_shapes=[pltpu.VMEM(encoded.shape, jnp.bfloat16)],
        cost_estimate=cost(4 * 256 * w_dkv.size),
        compiler_params=pltpu.CompilerParams(vmem_limit_bytes=12 * 1024 * 1024),
    )(state, *parts, encoded, queries, bias, w_dkv, w_do)


def digits():
    seq, expert = lax.axis_size("seq"), lax.axis_size("expert")
    inner = 2 if seq % 2 == 0 else 1
    core = 2 if expert % 2 == 0 else 1
    return {
        "z": ("seq", inner, seq // inner),
        "x": ("seq", 1, inner),
        "y": ("expert", core, expert // core),
        "c": ("expert", 1, core),
    }


def shift(x, digit, by):
    axis, stride, radix = digit
    pairs = []
    for i in range(lax.axis_size(axis)):
        g = i // stride % radix
        pairs.append((i, i + ((g + by) % radix - g) * stride))
    return lax.ppermute(x, axis, pairs)


def gathered(x, digit, place=0):
    return jnp.stack([x] + [shift(x, digit, d) for d in range(1, digit[2])], axis=place)


def gather_chip(x, beside):
    d = digits()
    half = x.shape[1] // 2
    x = gathered(x, d["z"])
    x, beside = lax.optimization_barrier((x, beside))
    left = gathered(gathered(x[..., :half], d["x"], 1), d["y"], 1)
    right = gathered(gathered(x[..., half:], d["y"], 1), d["x"], 2)
    return jnp.concatenate([left, right], axis=-1), beside


def summed(parts):
    total = parts[0].astype(jnp.float32)
    for part in parts[1:]:
        total = total + part.astype(jnp.float32)
    return total


def earlier_blocks(x, reach, opened):
    both_axes = ("seq", "expert")
    experts = lax.axis_size("expert")
    if reach != 2 or experts % 2:
        earlier = [passed_along(x, both_axes, by) for by in range(reach, 0, -1)]
        return jnp.zeros((1,), jnp.int32), earlier, x
    own = lax.ppermute(x, "expert", [(i, i + 1) for i in range(0, experts, 2)])
    far = lax.optimization_barrier((passed_along(x, both_axes, 2), opened))[0]
    near = lax.ppermute(far, "expert", [(i + 1, i) for i in range(0, experts, 2)])
    odd = lax.axis_index("expert").astype(jnp.int32).reshape(1) & 1
    return odd, [far, near], own


def leg(x, digit, place):
    parts = [lax.index_in_dim(x, d, place, keepdims=False) for d in range(digit[2])]
    return [parts[0]] + [shift(parts[d], digit, -d) for d in range(1, digit[2])]


def narrow(v):
    return v.astype(jnp.bfloat16)


def behind(values, *others):
    return jax.tree.map(lambda v: lax.optimization_barrier((v, others))[0], values)


def ends(legs):
    return [narrow(summed(parts)) for parts in legs]


def mixture(payload, patch_cap, capacity, w_up, moe_gain, w_router, w_in, w_down):
    d = digits()
    wide = w_up.shape[1]
    paired = w_in.reshape(w_in.shape[1], -1)
    own, paired = gather_chip(payload, paired)
    far, ys, xs = own.shape[:3]
    own = own.reshape((-1,) + own.shape[3:])
    moved = [shift(own, d["c"], by) for by in range(1, d["c"][2])]
    assert len(moved) == 1 and ys * xs % GROUP == 0
    moved = moved[0]
    me = lax.axis_index("expert").astype(jnp.int32).reshape(1)
    weights = (w_up, moe_gain.reshape(1, wide), w_router.T, paired, w_down[0])
    w_last = w_down[0]

    if far == 4:
        streams = [[2], [1, 3], [0]]
    else:
        apart = [*range(1, far), 0]
        streams = [apart[at : at + 2] for at in range(0, far, 2)]

    def blocks_of(zs):
        return [z * ys * xs + at for z in zs for at in range(0, ys * xs, GROUP)]

    def order_of(zs):
        near = len(zs)
        left, right = [], []
        for z in range(near):
            for y in range(ys):
                for x in range(xs):
                    left.append((x * ys + y) * near + z)
                    right.append((y * xs + x) * near + z)
        return left, right

    def shaped(halves, zs):
        left, right = halves
        tail = (len(zs),) + left.shape[1:]
        return [left.reshape((xs, ys) + tail), right.reshape((ys, xs) + tail)]

    def begin(zs, moved):
        got = stream(own, moved, blocks_of(zs), order_of(zs), patch_cap, capacity, me, *weights)
        sent = [shift(v, d["c"], -1) for v in shaped(got[:2], zs)]
        return sent, got

    def finish(zs, sent, hidden, gate, spread):
        kept = gated_share(hidden, gate, spread, w_last, order_of(zs), patch_cap)
        return [narrow(summed(pair)) for pair in zip(shaped(kept, zs), sent)]

    def first_leg(sums):
        return [leg(sums[0], d["x"], 0), leg(sums[1], d["y"], 0)]

    def second_leg(sums):
        return [leg(sums[0], d["y"], 0), leg(sums[1], d["x"], 0)]

    wholes = []

    def last_leg(zs, sums):
        made = []
        for at, z in enumerate(zs):
            if z:
                made.append(jnp.concatenate([v[at] for v in sums], axis=-1))
                wholes.append(shift(made[-1], d["z"], -z))
        return made

    first, second, added = None, None, None
    for zs in streams:
        sent, got = begin(zs, moved if added is None else behind(moved, added))
        hidden, gate, spread = got[2:]
        if second:
            made = last_leg(second[0], ends(behind(second[1], gate)))
            gate, second = behind(gate, made), None
        if first:
            sums = ends(behind(first[1], gate))
            gate, first, second = behind(gate, sums), None, (first[0], second_leg(sums))
        added = finish(zs, sent, hidden, gate, spread)
        first = (zs, first_leg(added))
    zs, legs = first
    sums = ends(legs)
    legs = second_leg(sums)
    if second:
        made = last_leg(second[0], ends(behind(second[1], sums)))
        legs = behind(legs, made)
    if zs != [0]:
        sums = ends(legs)
        last_leg(zs, sums)
        at = zs.index(0)
        legs = [[v[at : at + 1]] for v in sums]
    return wholes, legs


def per_device(
    byte_states,
    patch_start,
    expert_ids,
    enc_gain,
    w_qkv,
    w_out,
    w_xq,
    w_xkv,
    w_up,
    moe_gain,
    w_router,
    w_in,
    w_down,
    dec_gain,
    w_dq,
    w_dkv,
    w_do,
):
    byte_dev = byte_states.shape[0]
    patch_cap = expert_ids.shape[0]
    experts = w_router.shape[1]
    capacity = 12 * patch_cap // (5 * experts)
    both_axes = ("seq", "expert")
    reach = -(-WINDOW // byte_dev)
    place = lax.axis_index(both_axes).astype(jnp.int32).reshape(1)
    opened = opening(
        byte_states,
        patch_start,
        expert_ids,
        reach,
        capacity,
        place,
        enc_gain,
        w_qkv,
        w_out,
        w_xq,
        w_xkv,
    )
    instead, earlier, nearest = earlier_blocks(byte_states, reach, opened)
    encoded, payload = encode(instead, earlier, nearest, opened)
    wholes, halves = mixture(payload, patch_cap, capacity, w_up, moe_gain, w_router, w_in, w_down)
    queries, state = prepare(encoded, payload, patch_cap, dec_gain, w_dq, w_up)
    return decode(state, wholes, halves, encoded, queries, opened[13], w_dkv, w_do)


def solution(mesh):
    in_specs = (
        P(("seq", "expert"), None),
        P(("seq", "expert")),
        P(("seq", "expert"), None),
        P(),
        P(),
        P(),
        P(),
        P(),
        P(),
        P(),
        P(),
        P("expert", None, None, "seq"),
        P("expert", "seq", None),
        P(),
        P(),
        P(),
        P(),
    )
    out_specs = (P(("seq", "expert"), None), P(("seq", "expert"), None))
    return jax.shard_map(
        per_device, mesh=mesh, in_specs=in_specs, out_specs=out_specs, check_vma=False
    )
```

time: 122 us -> 103 us (0.84)
  waiting for transfers between devices: 50.4 us -> 28.5 us
  local copies, waits for them, and re-layouts: 13.1 us -> 1.78 us
  starting transfers between devices: 28.7 us -> 39.6 us
  Pallas kernels: 26.9 us -> 30.4 us
    ppermute x17 -> x29, waiting for transfers between devices: 44.9 us -> 24.9 us  [shift(): return lax.ppermute(x, axis, pairs)]
    unnamed x35 -> x21, local copies, waits for them, and re-layouts: 12.7 us -> 1.41 us
    ppermute x17 -> x29, starting transfers between devices: 22.3 us -> 32 us  [shift(): return lax.ppermute(x, axis, pairs)]
    ppermute x2 -> x1, waiting for transfers between devices: 5.5 us -> 1.45 us  [passed_along(): return lax.ppermute(x, axis, pairs)]
    pallas_call x4 -> x9, Pallas kernels: 26.2 us -> 29.7 us  [the longest x3 13.7 us: stream(): pl.pallas_call(functools.partial(stream_kernel, patch_cap, capacity, expe...]
    ppermute x0 -> x2, starting transfers between devices: none -> 2.75 us  [the longest x1 1.47 us: earlier_blocks(): own = lax.ppermute(x, 'expert', [(i, i + 1) for i in range(0, experts, 2)])]
    ppermute x0 -> x2, waiting for transfers between devices: none -> 2.1 us  [the longest x1 2.1 us: earlier_blocks(): lax.ppermute(far, 'expert', [(i + 1, i) for i in range(0, experts, 2)])]
    ppermute x2 -> x1, starting transfers between devices: 6.36 us -> 4.89 us  [passed_along(): return lax.ppermute(x, axis, pairs)]
  transfers between devices with their start and end apart: 19 -> 32, of which waited for: 13 -> 17; matrix products, arithmetic and copies ran while one was open for 5% -> 3% of each run, Pallas kernels for 7% -> 16%
where the time goes in v3:
time: 103 us
  starting transfers between devices  39.6 us (38%)
  Pallas kernels  30.4 us (30%)
  waiting for transfers between devices  28.5 us (28%)
  local copies, waits for them, and re-layouts  1.78 us (2%)
  other arithmetic  1.57 us (2%)
  between operations  1.18 us (1%)
    ppermute x29, starting transfers between devices, shift(): return lax.ppermute(x, axis, pairs)  32 us
    ppermute x29, waiting for transfers between devices, shift(): return lax.ppermute(x, axis, pairs)  24.9 us
    pallas_call x3, Pallas kernels, stream(): pl.pallas_call(functools.partial(stream_kernel, patch_cap, capacity, expe...  13.7 us
    pallas_call x1, Pallas kernels, encode(): pl.pallas_call(functools.partial(encoder_kernel, reach), out_shape=(jax.S...  7.11 us
    ppermute x1, starting transfers between devices, passed_along(): return lax.ppermute(x, axis, pairs)  4.89 us
    pallas_call x1, Pallas kernels, decode(): pl.pallas_call(functools.partial(decode_kernel, len(wholes)), out_shape=(...  3.08 us
    pallas_call x3, Pallas kernels, gated_share(): pl.pallas_call(functools.partial(share_kernel, order), out_shape=share_sh...  3.01 us
    pallas_call x1, Pallas kernels, opening(): pl.pallas_call(functools.partial(opening_kernel, reach, capacity), out_sh...  2.89 us
  transfers between devices with their start and end apart: 32, of which 17 were waited for; matrix products, arithmetic and copies ran while one was open for 3% of the time, Pallas kernels for 16%

profile of v3, /device:TPU:0, one launch (start us, length us, event | category | flops | bytes accessed | tf_op | source)
XLA Modules:
  0.0 103.1 jit_solution(10163550526493476543)
XLA Ops:
  0.6 4.9 %collective-permute-start = (bf16[256,512]{1,0:T(8,128)(2,1)}, bf16[256,512]{1,0:T(8,128)(2,1)S(1)}, u32[]{:S(2)}, u32[]{:S(2)}) collective-permute-start(bf16[256,512]{1,0:T(8,128)(2,1)} %refs_1_.1), channel_id=1, source_target_pairs={{0,2},{1,3},{2,4},{3,5},{4,6},{5,7},{6,8},{7,9},{8,10},{9,11},{10,... | collective-permute-start | bytes 786440 | tf_op jit(solution)/shard_map/ppermute | solution.py:23
  5.5 1.5 %collective-permute-start.2 = (bf16[256,512]{1,0:T(8,128)(2,1)}, bf16[256,512]{1,0:T(8,128)(2,1)S(1)}, u32[]{:S(2)}, u32[]{:S(2)}) collective-permute-start(bf16[256,512]{1,0:T(8,128)(2,1)} %refs_1_.1), channel_id=1, source_target_pairs={{0,1},{2,3},{4,5},{6,7},{8,9},{10,11},{12,13},{14,15},{16,17},{18,... | collective-permute-start | bytes 786440 | tf_op jit(solution)/shard_map/ppermute | solution.py:537
  7.0 2.9 %shard_map.176 = (bf16[256,512]{1,0:T(8,128)(2,1)S(1)}, f32[1,512]{1,0:T(1,128)S(1)}, bf16[512,1024]{1,0:T(8,128)(2,1)S(1)}, bf16[512,512]{1,0:T(8,128)(2,1)S(1)...) custom-call(s32[1]{0:T(128)} %bitcast.1.refs_0_, ...), custom_call_target="tpu_custom_call" | custom-call | flops 805306368 | tf_op jit(solution)/shard_map/pallas_call | solution.py:141
  9.9 1.4 %collective-permute-done.refs_1_ = bf16[256,512]{1,0:T(8,128)(2,1)S(1)} collective-permute-done((bf16[256,512]{1,0:T(8,128)(2,1)}, bf16[256,512]{1,0:T(8,128)(2,1)S(1)}, u32[]{:S(2)}, u32[]{:S(2)}) %collective-permute-start) | collective-permute-done | bytes 262176 | tf_op jit(solution)/shard_map/ppermute | solution.py:23
  11.4 1.3 %collective-permute-start.1 = (bf16[256,512]{1,0:T(8,128)(2,1)S(1)}, bf16[256,512]{1,0:T(8,128)(2,1)S(1)}, u32[]{:S(2)}, u32[]{:S(2)}) collective-permute-start(bf16[256,512]{1,0:T(8,128)(2,1)S(1)} %collective-permute-done.refs_1_), channel_id=1, source_target_pairs={{1,0},{3,2},{5,4},{7,6},{9,8},{11,10},{13,12},{15,14},{17,16},{19,... | collective-permute-start | bytes 786440 | tf_op jit(solution)/shard_map/ppermute | solution.py:539
  12.7 2.1 %collective-permute-done.1.refs_2_ = bf16[256,512]{1,0:T(8,128)(2,1)S(1)} collective-permute-done((bf16[256,512]{1,0:T(8,128)(2,1)S(1)}, bf16[256,512]{1,0:T(8,128)(2,1)S(1)}, u32[]{:S(2)}, u32[]{:S(2)}) %collective-permute-start.1) | collective-permute-done | bytes 262176 | tf_op jit(solution)/shard_map/ppermute | solution.py:539
  14.8 7.1 %shard_map.177 = (bf16[256,512]{1,0:T(8,128)(2,1)S(1)}, bf16[48,512]{1,0:T(8,128)(2,1)S(1)}) custom-call(s32[1]{0:T(128)S(6)} %and.5.refs_0_, bf16[256,512]{1,0:T(8,128)(2,1)S(1)} %collective-permute-done.refs_1_, bf16[256,512]{1,0:T(8,128)(2,1)S(1)} %collective-permute-done.1.refs_2_, bf16[256,512]{1,0:T(8,128)(2,1)S(1)} %collective-permute-done.2.refs_3_, ...), custom_call_target="tpu_custom_call" | custom-call | flops 2415919104 | tf_op jit(solution)/shard_map/pallas_call | solution.py:239
  21.9 4.3 %collective-permute-start.3 = (bf16[48,512]{1,0:T(8,128)(2,1)S(1)}, bf16[48,512]{1,0:T(8,128)(2,1)S(1)}, u32[]{:S(2)}, u32[]{:S(2)}) collective-permute-start(bf16[48,512]{1,0:T(8,128)(2,1)S(1)} %get-tuple-element.85.payload), channel_id=1, source_target_pairs={{0,8},{4,12},{8,16},{12,20},{16,24},{20,28},{24,0},{28,4},{1,9},{5... | collective-permute-start | bytes 147464 | tf_op jit(solution)/shard_map/ppermute | solution.py:507
  26.2 2.6 %collective-permute-start.4 = (bf16[48,512]{1,0:T(8,128)(2,1)S(1)}, bf16[48,512]{1,0:T(8,128)(2,1)S(1)}, u32[]{:S(2)}, u32[]{:S(2)}) collective-permute-start(bf16[48,512]{1,0:T(8,128)(2,1)S(1)} %get-tuple-element.85.payload), channel_id=1, source_target_pairs={{0,16},{4,20},{8,24},{12,28},{16,0},{20,4},{24,8},{28,12},{1,17},{... | collective-permute-start | bytes 147464 | tf_op jit(solution)/shard_map/ppermute | solution.py:507
  28.8 1.4 %collective-permute-start.5 = (bf16[48,512]{1,0:T(8,128)(2,1)S(1)}, bf16[48,512]{1,0:T(8,128)(2,1)S(1)}, u32[]{:S(2)}, u32[]{:S(2)}) collective-permute-start(bf16[48,512]{1,0:T(8,128)(2,1)S(1)} %get-tuple-element.85.payload), channel_id=1, source_target_pairs={{0,24},{4,28},{8,0},{12,4},{16,8},{20,12},{24,16},{28,20},{1,25},{... | collective-permute-start | bytes 147464 | tf_op jit(solution)/shard_map/ppermute | solution.py:507
  30.1 1.4 %copy.25 = bf16[256,8,2,768]{3,1,2,0:T(8,128)(2,1)S(1)} copy(bf16[256,8,2,768]{3,2,1,0:T(2,128)(2,1)S(1)} %bitcast.162) | data formatting | bytes 12582912
  31.5 1.1 %collective-permute-done.4 = bf16[48,512]{1,0:T(8,128)(2,1)S(1)} collective-permute-done((bf16[48,512]{1,0:T(8,128)(2,1)S(1)}, bf16[48,512]{1,0:T(8,128)(2,1)S(1)}, u32[]{:S(2)}, u32[]{:S(2)}) %collective-permute-start.4) | collective-permute-done | bytes 49184 | tf_op jit(solution)/shard_map/ppermute | solution.py:507
  32.7 0.4 collective-permute-done.5
  33.1 0.7 collective-permute-start.6
  33.8 0.6 collective-permute-start.8
  34.4 3.4 %collective-permute-done.6 = bf16[4,48,256]{2,1,0:T(8,128)(2,1)S(1)} collective-permute-done((bf16[4,48,256]{2,1,0:T(8,128)(2,1)S(1)}, bf16[4,48,256]{2,1,0:T(8,128)(2,1)S(1)}, u32[]{:S(2)}, u32[]{:S(2)}) %collective-permute-start.6) | collective-permute-done | bytes 98336 | tf_op jit(solution)/shard_map/ppermute | solution.py:507
  37.9 0.5 collective-permute-done.8
  38.4 2.3 %collective-permute-start.9 = (bf16[4,2,48,256]{3,2,0,1:T(8,128)(2,1)S(1)}, bf16[4,2,48,256]{3,2,0,1:T(8,128)(2,1)S(1)}, u32[]{:S(2)}, u32[]{:S(2)}) collective-permute-start(bf16[4,2,48,256]{3,2,0,1:T(8,128)(2,1)S(1)} %get-tuple-element.155), channel_id=1, source_target_pairs={{0,4},{4,0},{8,12},{12,8},{16,20},{20,16},{24,28},{28,24},{1,5},{5... | collective-permute-start | bytes 589832 | tf_op jit(solution)/shard_map/ppermute | solution.py:507
  40.7 2.9 %collective-permute-done.7 = bf16[4,2,48,256]{3,2,0,1:T(8,128)(2,1)S(1)} collective-permute-done((bf16[4,2,48,256]{3,2,0,1:T(8,128)(2,1)S(1)}, bf16[4,2,48,256]{3,2,0,1:T(8,128)(2,1)S(1)}, u32[]{:S(2)}, u32[]{:S(2)}) %collective-permute-start.7) | collective-permute-done | bytes 196640 | tf_op jit(solution)/shard_map/ppermute | solution.py:507
  43.5 0.8 collective-permute-done.9
  44.3 0.1 maximum_maximum_fusion
  44.5 2.3 %collective-permute-done.10.refs_2_ = bf16[16,48,512]{2,1,0:T(8,128)(2,1)S(1)} collective-permute-done((bf16[16,48,512]{2,1,0:T(8,128)(2,1)S(1)}, bf16[16,48,512]{2,1,0:T(8,128)(2,1)S(1)}, u32[]{:S(2)}, u32[]{:S(2)}) %collective-permute-start.10) | collective-permute-done | bytes 786464 | tf_op jit(solution)/shard_map/ppermute | solution.py:507
  46.8 3.6 %shard_map.179 = (bf16[4,40,1024]{2,1,0:T(8,128)(2,1)S(1)}, bf16[4,40,1024]{2,1,0:T(8,128)(2,1)S(1)}, bf16[96,768]{1,0:T(8,128)(2,1)S(1)}, f32[96,1]{1,0:T(8,128)S(1)}, bf16[1,96,160]{2,1,0:T(8,128)(2,1)S(1)}) custom-call(s32[1]{0:T(128)} %bitcast.refs_0_, bf16[16,48,512]{2,1,0:T(8,128)(2,1)S(1)} %bitcast.137, ...), custom_call_target="tpu_custom_call" | custom-call | flops 201326592 | tf_op jit(solution)/shard_map/pallas_call | solution.py:385
  50.4 0.2 collective-permute-start.11
  50.6 0.4 collective-permute-start.12
  51.0 0.8 shard_map.180
  51.8 0.3 collective-permute-done.11
  52.1 0.1 fusion.5
  52.2 2.1 %collective-permute-start.13 = (bf16[2,1,40,1024]{3,2,1,0:T(8,128)(2,1)S(1)}, bf16[2,1,40,1024]{3,2,1,0:T(8,128)(2,1)S(1)}, u32[]{:S(2)}, u32[]{:S(2)}) collective-permute-start(bf16[2,1,40,1024]{3,2,1,0:T(8,128)(2,1)S(1)} %get-tuple-element.145), channel_id=1, source_target_pairs={{0,4},{4,0},{8,12},{12,8},{16,20},{20,16},{24,28},{28,24},{1,5},{5... | collective-permute-start | bytes 491528 | tf_op jit(solution)/shard_map/ppermute | solution.py:507
  54.3 0.1 fusion.4
  54.6 6.5 %shard_map.181 = (bf16[8,40,1024]{2,1,0:T(8,128)(2,1)S(1)}, bf16[8,40,1024]{2,1,0:T(8,128)(2,1)S(1)}, bf16[192,768]{1,0:T(8,128)(2,1)S(1)}, f32[192,1]{1,0:T(8,128)S(1)}, bf16[2,96,160]{2,1,0:T(8,128)(2,1)S(1)}) custom-call(s32[1]{0:T(128)} %bitcast.refs_0_, bf16[16,48,512]{2,1,0:T(8,128)(2,1)S(1)} %bitcast.138, ...), custom_call_target="tpu_custom_call" | custom-call | flops 402653184 | tf_op jit(solution)/shard_map/pallas_call | solution.py:385
  61.2 0.5 collective-permute-start.15
  61.7 0.1 fusion.8
  61.8 2.1 %collective-permute-start.17 = (bf16[1,40,1024]{2,1,0:T(8,128)(2,1)S(1)}, bf16[1,40,1024]{2,1,0:T(8,128)(2,1)S(1)}, u32[]{:S(2)}, u32[]{:S(2)}) collective-permute-start(bf16[1,40,1024]{2,1,0:T(8,128)(2,1)S(1)} %get-tuple-element.165), channel_id=1, source_target_pairs={{0,2},{1,3},{2,0},{3,1},{4,6},{5,7},{6,4},{7,5},{8,10},{9,11},{10,... | collective-permute-start | bytes 245768 | tf_op jit(solution)/shard_map/ppermute | solution.py:507
  63.9 0.3 collective-permute-start.18
  64.2 1.4 %shard_map.182 = (bf16[8,40,1024]{2,1,0:T(8,128)(2,1)S(1)}, bf16[8,40,1024]{2,1,0:T(8,128)(2,1)S(1)}) custom-call(bf16[192,768]{1,0:T(8,128)(2,1)S(1)} %get-tuple-element.100.hidden, f32[192,1]{1,0:T(8,128)S(1)} %get-tuple-element.103.gate, bf16[2,96,160]{2,1,0:T(8,128)(2,1)S(1)} %get-tuple-element.104.spread, bf16[768,2048]{1,0:T(8,128)(2,1)S(1)} %bitcast.130), custom_call_target="tpu_custom_call" | custom-call | flops 1000 | tf_op jit(solution)/shard_map/pallas_call | solution.py:410
  65.6 0.2 fusion.1
  65.9 0.2 fusion
  66.2 3.6 %shard_map.183 = (bf16[4,40,1024]{2,1,0:T(8,128)(2,1)S(1)}, bf16[4,40,1024]{2,1,0:T(8,128)(2,1)S(1)}, bf16[96,768]{1,0:T(8,128)(2,1)S(1)}, f32[96,1]{1,0:T(8,128)S(1)}, bf16[1,96,160]{2,1,0:T(8,128)(2,1)S(1)}) custom-call(s32[1]{0:T(128)} %bitcast.refs_0_, bf16[16,48,512]{2,1,0:T(8,128)(2,1)S(1)} %bitcast.139, ...), custom_call_target="tpu_custom_call" | custom-call | flops 201326592 | tf_op jit(solution)/shard_map/pallas_call | solution.py:385
  69.8 1.8 %collective-permute-start.20 = (bf16[2,2,40,1024]{3,2,1,0:T(8,128)(2,1)S(1)}, bf16[2,2,40,1024]{3,2,1,0:T(8,128)(2,1)S(1)}, u32[]{:S(2)}, u32[]{:S(2)}) collective-permute-start(bf16[2,2,40,1024]{3,2,1,0:T(8,128)(2,1)S(1)} %get-tuple-element.137), channel_id=1, source_target_pairs={{0,4},{4,0},{8,12},{12,8},{16,20},{20,16},{24,28},{28,24},{1,5},{5... | collective-permute-start | bytes 983048 | tf_op jit(solution)/shard_map/ppermute | solution.py:507
  71.7 1.6 %collective-permute-start.19 = (bf16[40,2048]{1,0:T(8,128)(2,1)S(1)}, bf16[40,2048]{1,0:T(8,128)(2,1)S(1)}, u32[]{:S(2)}, u32[]{:S(2)}) collective-permute-start(bf16[40,2048]{1,0:T(8,128)(2,1)S(1)} %pad_maximum_fusion.3), channel_id=1, source_target_pairs={{0,16},{4,20},{8,24},{12,28},{16,0},{20,4},{24,8},{28,12},{1,17},{... | collective-permute-start | bytes 491528 | tf_op jit(solution)/shard_map/ppermute | solution.py:507
  73.3 0.5 collective-permute-start.22
  73.8 5.2 %collective-permute-done.20 = bf16[2,2,40,1024]{3,2,1,0:T(8,128)(2,1)S(1)} collective-permute-done((bf16[2,2,40,1024]{3,2,1,0:T(8,128)(2,1)S(1)}, bf16[2,2,40,1024]{3,2,1,0:T(8,128)(2,1)S(1)}, u32[]{:S(2)}, u32[]{:S(2)}) %collective-permute-start.20) | collective-permute-done | bytes 327712 | tf_op jit(solution)/shard_map/ppermute | solution.py:507
  79.0 0.1 add_convert_fusion.1
  79.1 1.4 %collective-permute-done.21 = bf16[2,2,40,1024]{3,2,1,0:T(8,128)(2,1)S(1)} collective-permute-done((bf16[2,2,40,1024]{3,2,1,0:T(8,128)(2,1)S(1)}, bf16[2,2,40,1024]{3,2,1,0:T(8,128)(2,1)S(1)}, u32[]{:S(2)}, u32[]{:S(2)}) %collective-permute-start.21) | collective-permute-done | bytes 327712 | tf_op jit(solution)/shard_map/ppermute | solution.py:507
  80.5 0.1 add_convert_fusion
  80.6 0.8 shard_map.184
  81.4 0.1 fusion.2
  81.6 0.4 collective-permute-start.25
  81.9 0.1 fusion.3
  82.1 1.2 %collective-permute-start.23 = (bf16[2,1,40,1024]{3,2,1,0:T(8,128)(2,1)S(1)}, bf16[2,1,40,1024]{3,2,1,0:T(8,128)(2,1)S(1)}, u32[]{:S(2)}, u32[]{:S(2)}) collective-permute-start(bf16[2,1,40,1024]{3,2,1,0:T(8,128)(2,1)S(1)} %slice_bitcast_fusion.9), channel_id=1, source_target_pairs={{0,4},{4,0},{8,12},{12,8},{16,20},{20,16},{24,28},{28,24},{1,5},{5... | collective-permute-start | bytes 491528 | tf_op jit(solution)/shard_map/ppermute | solution.py:507
  83.3 1.0 collective-permute-start.26
  84.3 1.7 %collective-permute-start.27 = (bf16[2,40,1024]{2,1,0:T(8,128)(2,1)S(1)}, bf16[2,40,1024]{2,1,0:T(8,128)(2,1)S(1)}, u32[]{:S(2)}, u32[]{:S(2)}) collective-permute-start(bf16[2,40,1024]{2,1,0:T(8,128)(2,1)S(1)} %get-tuple-element.143), channel_id=1, source_target_pairs={{0,4},{4,0},{8,12},{12,8},{16,20},{20,16},{24,28},{28,24},{1,5},{5... | collective-permute-start | bytes 491528 | tf_op jit(solution)/shard_map/ppermute | solution.py:507
  86.0 1.8 %collective-permute-done.25 = bf16[2,1,40,1024]{3,2,1,0:T(8,128)(2,1)S(1)} collective-permute-done((bf16[2,1,40,1024]{3,2,1,0:T(8,128)(2,1)S(1)}, bf16[2,1,40,1024]{3,2,1,0:T(8,128)(2,1)S(1)}, u32[]{:S(2)}, u32[]{:S(2)}) %collective-permute-start.25) | collective-permute-done | bytes 163872 | tf_op jit(solution)/shard_map/ppermute | solution.py:507
  87.8 0.5 collective-permute-done.23
  88.4 1.1 %collective-permute-done.26 = bf16[2,40,1024]{2,1,0:T(8,128)(2,1)S(1)} collective-permute-done((bf16[2,40,1024]{2,1,0:T(8,128)(2,1)S(1)}, bf16[2,40,1024]{2,1,0:T(8,128)(2,1)S(1)}, u32[]{:S(2)}, u32[]{:S(2)}) %collective-permute-start.26) | collective-permute-done | bytes 163872 | tf_op jit(solution)/shard_map/ppermute | solution.py:507
  89.6 0.4 collective-permute-done.27
  90.1 1.3 %collective-permute-start.31 = (bf16[1,40,1024]{2,1,0:T(8,128)(2,1)S(1)}, bf16[1,40,1024]{2,1,0:T(8,128)(2,1)S(1)}, u32[]{:S(2)}, u32[]{:S(2)}) collective-permute-start(bf16[1,40,1024]{2,1,0:T(8,128)(2,1)S(1)} %get-tuple-element.156), channel_id=1, source_target_pairs={{0,4},{4,0},{8,12},{12,8},{16,20},{20,16},{24,28},{28,24},{1,5},{5... | collective-permute-start | bytes 245768 | tf_op jit(solution)/shard_map/ppermute | solution.py:507
  91.5 0.7 collective-permute-start.29
  92.1 3.3 %collective-permute-start.28 = (bf16[40,2048]{1,0:T(8,128)(2,1)S(1)}, bf16[40,2048]{1,0:T(8,128)(2,1)S(1)}, u32[]{:S(2)}, u32[]{:S(2)}) collective-permute-start(bf16[40,2048]{1,0:T(8,128)(2,1)S(1)} %pad_maximum_fusion.4), channel_id=1, source_target_pairs={{0,24},{4,28},{8,0},{12,4},{16,8},{20,12},{24,16},{28,20},{1,25},{... | collective-permute-start | bytes 491528 | tf_op jit(solution)/shard_map/ppermute | solution.py:507
  95.4 0.9 collective-permute-start.30
  96.4 0.7 shard_map.178
  97.1 2.8 %collective-permute-done.30.refs_5_ = bf16[1,40,1024]{2,1,0:T(8,128)(2,1)S(1)} collective-permute-done((bf16[1,40,1024]{2,1,0:T(8,128)(2,1)S(1)}, bf16[1,40,1024]{2,1,0:T(8,128)(2,1)S(1)}, u32[]{:S(2)}, u32[]{:S(2)}) %collective-permute-start.30) | collective-permute-done | bytes 81952 | tf_op jit(solution)/shard_map/ppermute | solution.py:507
  100.0 3.1 %shard_map.185 = (bf16[256,512]{1,0:T(8,128)(2,1)}, bf16[40,2048]{1,0:T(8,128)(2,1)}) custom-call(bf16[40,2048]{1,0:T(8,128)(2,1)S(1)} %get-tuple-element.86.refs_0_, bf16[40,2048]{1,0:T(8,128)(2,1)S(1)} %collective-permute-done.19.refs_1_, bf16[40,2048]{1,0:T(8,128)(2,1)S(1)} %collective-permute-done.28.refs_2_, ...), custom_call_target="tpu_custom_call" | custom-call | flops 2147483648 | tf_op jit(solution)/shard_map/pallas_call | solution.py:475
  (70 shorter events, 1.1 us)
Async XLA Ops:
  0.6 10.7 %collective-permute-start = (bf16[256,512]{1,0:T(8,128)(2,1)}, bf16[256,512]{1,0:T(8,128)(2,1)S(1)}, u32[]{:S(2)}, u32[]{:S(2)}) collective-permute-start(bf16[256,512]{1,0:T(8,128)(2,1)} %refs_1_.1), channel_id=1, source_target_pairs={{0,2},{1,3},{2,4},{3,5},{4,6},{5,7},{6,8},{7,9},{8,10},{9,11},{10,... | collective-permute-start | bytes 786440 | tf_op jit(solution)/shard_map/ppermute | solution.py:23
  5.5 7.2 %collective-permute-start.2 = (bf16[256,512]{1,0:T(8,128)(2,1)}, bf16[256,512]{1,0:T(8,128)(2,1)S(1)}, u32[]{:S(2)}, u32[]{:S(2)}) collective-permute-start(bf16[256,512]{1,0:T(8,128)(2,1)} %refs_1_.1), channel_id=1, source_target_pairs={{0,1},{2,3},{4,5},{6,7},{8,9},{10,11},{12,13},{14,15},{16,17},{18,... | collective-permute-start | bytes 786440 | tf_op jit(solution)/shard_map/ppermute | solution.py:537
  7.0 23.1 %slice-start = ((s8[6291456]{0:T(1024)(128)(4,1)}), s8[4194304]{0:T(1024)(128)(4,1)S(1)}, s32[]{:S(2)}) async-start(s8[6291456]{0:T(1024)(128)(4,1)} %bitcast.160), calls=%async_computation | async-start | bytes 8388608
  11.4 3.4 %collective-permute-start.1 = (bf16[256,512]{1,0:T(8,128)(2,1)S(1)}, bf16[256,512]{1,0:T(8,128)(2,1)S(1)}, u32[]{:S(2)}, u32[]{:S(2)}) collective-permute-start(bf16[256,512]{1,0:T(8,128)(2,1)S(1)} %collective-permute-done.refs_1_), channel_id=1, source_target_pairs={{1,0},{3,2},{5,4},{7,6},{9,8},{11,10},{13,12},{15,14},{17,16},{19,... | collective-permute-start | bytes 786440 | tf_op jit(solution)/shard_map/ppermute | solution.py:539
  12.7 17.5 %slice-start.1 = ((s8[6291456]{0:T(1024)(128)(4,1)}), s8[2097152]{0:T(1024)(128)(4,1)S(1)}, s32[]{:S(2)}) async-start(s8[6291456]{0:T(1024)(128)(4,1)} %bitcast.160), calls=%async_computation.1 | async-start | bytes 4194304
  21.9 9.6 %collective-permute-start.3 = (bf16[48,512]{1,0:T(8,128)(2,1)S(1)}, bf16[48,512]{1,0:T(8,128)(2,1)S(1)}, u32[]{:S(2)}, u32[]{:S(2)}) collective-permute-start(bf16[48,512]{1,0:T(8,128)(2,1)S(1)} %get-tuple-element.85.payload), channel_id=1, source_target_pairs={{0,8},{4,12},{8,16},{12,20},{16,24},{20,28},{24,0},{28,4},{1,9},{5... | collective-permute-start | bytes 147464 | tf_op jit(solution)/shard_map/ppermute | solution.py:507
  26.2 6.5 %collective-permute-start.4 = (bf16[48,512]{1,0:T(8,128)(2,1)S(1)}, bf16[48,512]{1,0:T(8,128)(2,1)S(1)}, u32[]{:S(2)}, u32[]{:S(2)}) collective-permute-start(bf16[48,512]{1,0:T(8,128)(2,1)S(1)} %get-tuple-element.85.payload), channel_id=1, source_target_pairs={{0,16},{4,20},{8,24},{12,28},{16,0},{20,4},{24,8},{28,12},{1,17},{... | collective-permute-start | bytes 147464 | tf_op jit(solution)/shard_map/ppermute | solution.py:507
  28.8 4.2 %collective-permute-start.5 = (bf16[48,512]{1,0:T(8,128)(2,1)S(1)}, bf16[48,512]{1,0:T(8,128)(2,1)S(1)}, u32[]{:S(2)}, u32[]{:S(2)}) collective-permute-start(bf16[48,512]{1,0:T(8,128)(2,1)S(1)} %get-tuple-element.85.payload), channel_id=1, source_target_pairs={{0,24},{4,28},{8,0},{12,4},{16,8},{20,12},{24,16},{28,20},{1,25},{... | collective-permute-start | bytes 147464 | tf_op jit(solution)/shard_map/ppermute | solution.py:507
  33.0 13.8 %copy-start.1 = (bf16[512,2048]{1,0:T(8,128)(2,1)S(1)}, bf16[512,2048]{1,0:T(8,128)(2,1)}, u32[]{:S(2)}) copy-start(bf16[512,2048]{1,0:T(8,128)(2,1)} %refs_3_.5) | copy-start | bytes 6291460
  33.1 4.7 %collective-permute-start.6 = (bf16[4,48,256]{2,1,0:T(8,128)(2,1)S(1)}, bf16[4,48,256]{2,1,0:T(8,128)(2,1)S(1)}, u32[]{:S(2)}, u32[]{:S(2)}) collective-permute-start(bf16[4,48,256]{2,1,0:T(8,128)(2,1)S(1)} %get-tuple-element.153), channel_id=1, source_target_pairs={{0,4},{4,0},{8,12},{12,8},{16,20},{20,16},{24,28},{28,24},{1,5},{5... | collective-permute-start | bytes 294920 | tf_op jit(solution)/shard_map/ppermute | solution.py:507
  33.8 4.6 %collective-permute-start.8 = (bf16[4,48,256]{2,1,0:T(8,128)(2,1)S(1)}, bf16[4,48,256]{2,1,0:T(8,128)(2,1)S(1)}, u32[]{:S(2)}, u32[]{:S(2)}) collective-permute-start(bf16[4,48,256]{2,1,0:T(8,128)(2,1)S(1)} %get-tuple-element.152), channel_id=1, source_target_pairs={{0,2},{1,3},{2,0},{3,1},{4,6},{5,7},{6,4},{7,5},{8,10},{9,11},{10,... | collective-permute-start | bytes 294920 | tf_op jit(solution)/shard_map/ppermute | solution.py:507
  37.8 5.7 %collective-permute-start.7 = (bf16[4,2,48,256]{3,2,0,1:T(8,128)(2,1)S(1)}, bf16[4,2,48,256]{3,2,0,1:T(8,128)(2,1)S(1)}, u32[]{:S(2)}, u32[]{:S(2)}) collective-permute-start(bf16[4,2,48,256]{3,2,0,1:T(8,128)(2,1)S(1)} %get-tuple-element.149), channel_id=1, source_target_pairs={{0,2},{1,3},{2,0},{3,1},{4,6},{5,7},{6,4},{7,5},{8,10},{9,11},{10,... | collective-permute-start | bytes 589832 | tf_op jit(solution)/shard_map/ppermute | solution.py:507
  38.4 8.4 %copy-start.3 = (f32[2048,4]{0,1:T(4,128)S(1)}, f32[2048,4]{0,1:T(4,128)}, u32[]{:S(2)}) copy-start(f32[2048,4]{0,1:T(4,128)} %param.27) | copy-start | bytes 98308
  38.4 5.9 %collective-permute-start.9 = (bf16[4,2,48,256]{3,2,0,1:T(8,128)(2,1)S(1)}, bf16[4,2,48,256]{3,2,0,1:T(8,128)(2,1)S(1)}, u32[]{:S(2)}, u32[]{:S(2)}) collective-permute-start(bf16[4,2,48,256]{3,2,0,1:T(8,128)(2,1)S(1)} %get-tuple-element.155), channel_id=1, source_target_pairs={{0,4},{4,0},{8,12},{12,8},{16,20},{20,16},{24,28},{28,24},{1,5},{5... | collective-permute-start | bytes 589832 | tf_op jit(solution)/shard_map/ppermute | solution.py:507
  44.3 2.5 %copy-start.4 = (f32[2048]{0:T(1024)S(1)}, f32[2048]{0:T(1024)}, u32[]{:S(2)}) copy-start(f32[2048]{0:T(1024)} %param.26) | copy-start | bytes 24580
  44.3 2.5 %copy-start = (bf16[1,768,2048]{2,1,0:T(8,128)(2,1)S(1)}, bf16[1,768,2048]{2,1,0:T(8,128)(2,1)}, u32[]{:S(2)}) copy-start(bf16[1,768,2048]{2,1,0:T(8,128)(2,1)} %param.29) | copy-start | bytes 9437188
  44.5 2.4 %collective-permute-start.10 = (bf16[16,48,512]{2,1,0:T(8,128)(2,1)S(1)}, bf16[16,48,512]{2,1,0:T(8,128)(2,1)S(1)}, u32[]{:S(2)}, u32[]{:S(2)}) collective-permute-start(bf16[16,48,512]{2,1,0:T(8,128)(2,1)S(1)} %bitcast.136), channel_id=1, source_target_pairs={{0,1},{1,0},{2,3},{3,2},{4,5},{5,4},{6,7},{7,6},{8,9},{9,8},{10,11... | collective-permute-start | bytes 2359304 | tf_op jit(solution)/shard_map/ppermute | solution.py:507
  50.4 1.7 %collective-permute-start.11 = (bf16[2,2,1,40,1024]{4,3,1,2,0:T(8,128)(2,1)S(1)}, bf16[2,2,1,40,1024]{4,3,1,2,0:T(8,128)(2,1)S(1)}, u32[]{:S(2)}, u32[]{:S(2)}) collective-permute-start(bf16[2,2,1,40,1024]{4,3,1,2,0:T(8,128)(2,1)S(1)} %bitcast.159), channel_id=1, source_target_pairs={{0,1},{1,0},{2,3},{3,2},{4,5},{5,4},{6,7},{7,6},{8,9},{9,8},{10,11... | collective-permute-start | bytes 983048 | tf_op jit(solution)/shard_map/ppermute | solution.py:507
  50.6 3.7 %collective-permute-start.12 = (bf16[2,2,1,40,1024]{4,3,1,2,0:T(8,128)(2,1)S(1)}, bf16[2,2,1,40,1024]{4,3,1,2,0:T(8,128)(2,1)S(1)}, u32[]{:S(2)}, u32[]{:S(2)}) collective-permute-start(bf16[2,2,1,40,1024]{4,3,1,2,0:T(8,128)(2,1)S(1)} %bitcast.158), channel_id=1, source_target_pairs={{0,1},{1,0},{2,3},{3,2},{4,5},{5,4},{6,7},{7,6},{8,9},{9,8},{10,11... | collective-permute-start | bytes 983048 | tf_op jit(solution)/shard_map/ppermute | solution.py:507
  52.2 9.4 %collective-permute-start.13 = (bf16[2,1,40,1024]{3,2,1,0:T(8,128)(2,1)S(1)}, bf16[2,1,40,1024]{3,2,1,0:T(8,128)(2,1)S(1)}, u32[]{:S(2)}, u32[]{:S(2)}) collective-permute-start(bf16[2,1,40,1024]{3,2,1,0:T(8,128)(2,1)S(1)} %get-tuple-element.145), channel_id=1, source_target_pairs={{0,4},{4,0},{8,12},{12,8},{16,20},{20,16},{24,28},{28,24},{1,5},{5... | collective-permute-start | bytes 491528 | tf_op jit(solution)/shard_map/ppermute | solution.py:507
  54.5 7.2 %collective-permute-start.14 = (bf16[2,1,40,1024]{3,2,1,0:T(8,128)(2,1)S(1)}, bf16[2,1,40,1024]{3,2,1,0:T(8,128)(2,1)S(1)}, u32[]{:S(2)}, u32[]{:S(2)}) collective-permute-start(bf16[2,1,40,1024]{3,2,1,0:T(8,128)(2,1)S(1)} %get-tuple-element.147), channel_id=1, source_target_pairs={{0,2},{1,3},{2,0},{3,1},{4,6},{5,7},{6,4},{7,5},{8,10},{9,11},{10,... | collective-permute-start | bytes 491528 | tf_op jit(solution)/shard_map/ppermute | solution.py:507
  61.1 4.8 %collective-permute-start.16 = (bf16[2,2,2,40,1024]{4,3,2,1,0:T(8,128)(2,1)S(1)}, bf16[2,2,2,40,1024]{4,3,2,1,0:T(8,128)(2,1)S(1)}, u32[]{:S(2)}, u32[]{:S(2)}) collective-permute-start(bf16[2,2,2,40,1024]{4,3,2,1,0:T(8,128)(2,1)S(1)} %bitcast.154), channel_id=1, source_target_pairs={{0,1},{1,0},{2,3},{3,2},{4,5},{5,4},{6,7},{7,6},{8,9},{9,8},{10,11... | collective-permute-start | bytes 1966088 | tf_op jit(solution)/shard_map/ppermute | solution.py:507
  61.2 4.4 %collective-permute-start.15 = (bf16[2,2,2,40,1024]{4,3,2,1,0:T(8,128)(2,1)S(1)}, bf16[2,2,2,40,1024]{4,3,2,1,0:T(8,128)(2,1)S(1)}, u32[]{:S(2)}, u32[]{:S(2)}) collective-permute-start(bf16[2,2,2,40,1024]{4,3,2,1,0:T(8,128)(2,1)S(1)} %bitcast.155), channel_id=1, source_target_pairs={{0,1},{1,0},{2,3},{3,2},{4,5},{5,4},{6,7},{7,6},{8,9},{9,8},{10,11... | collective-permute-start | bytes 1966088 | tf_op jit(solution)/shard_map/ppermute | solution.py:507
  61.8 8.0 %collective-permute-start.17 = (bf16[1,40,1024]{2,1,0:T(8,128)(2,1)S(1)}, bf16[1,40,1024]{2,1,0:T(8,128)(2,1)S(1)}, u32[]{:S(2)}, u32[]{:S(2)}) collective-permute-start(bf16[1,40,1024]{2,1,0:T(8,128)(2,1)S(1)} %get-tuple-element.165), channel_id=1, source_target_pairs={{0,2},{1,3},{2,0},{3,1},{4,6},{5,7},{6,4},{7,5},{8,10},{9,11},{10,... | collective-permute-start | bytes 245768 | tf_op jit(solution)/shard_map/ppermute | solution.py:507
  63.9 5.9 %collective-permute-start.18 = (bf16[1,40,1024]{2,1,0:T(8,128)(2,1)S(1)}, bf16[1,40,1024]{2,1,0:T(8,128)(2,1)S(1)}, u32[]{:S(2)}, u32[]{:S(2)}) collective-permute-start(bf16[1,40,1024]{2,1,0:T(8,128)(2,1)S(1)} %get-tuple-element.167), channel_id=1, source_target_pairs={{0,4},{4,0},{8,12},{12,8},{16,20},{20,16},{24,28},{28,24},{1,5},{5... | collective-permute-start | bytes 245768 | tf_op jit(solution)/shard_map/ppermute | solution.py:507
  69.8 9.2 %collective-permute-start.20 = (bf16[2,2,40,1024]{3,2,1,0:T(8,128)(2,1)S(1)}, bf16[2,2,40,1024]{3,2,1,0:T(8,128)(2,1)S(1)}, u32[]{:S(2)}, u32[]{:S(2)}) collective-permute-start(bf16[2,2,40,1024]{3,2,1,0:T(8,128)(2,1)S(1)} %get-tuple-element.137), channel_id=1, source_target_pairs={{0,4},{4,0},{8,12},{12,8},{16,20},{20,16},{24,28},{28,24},{1,5},{5... | collective-permute-start | bytes 983048 | tf_op jit(solution)/shard_map/ppermute | solution.py:507
  71.6 8.9 %collective-permute-start.21 = (bf16[2,2,40,1024]{3,2,1,0:T(8,128)(2,1)S(1)}, bf16[2,2,40,1024]{3,2,1,0:T(8,128)(2,1)S(1)}, u32[]{:S(2)}, u32[]{:S(2)}) collective-permute-start(bf16[2,2,40,1024]{3,2,1,0:T(8,128)(2,1)S(1)} %get-tuple-element.139), channel_id=1, source_target_pairs={{0,2},{1,3},{2,0},{3,1},{4,6},{5,7},{6,4},{7,5},{8,10},{9,11},{10,... | collective-permute-start | bytes 983048 | tf_op jit(solution)/shard_map/ppermute | solution.py:507
  71.7 28.2 %collective-permute-start.19 = (bf16[40,2048]{1,0:T(8,128)(2,1)S(1)}, bf16[40,2048]{1,0:T(8,128)(2,1)S(1)}, u32[]{:S(2)}, u32[]{:S(2)}) collective-permute-start(bf16[40,2048]{1,0:T(8,128)(2,1)S(1)} %pad_maximum_fusion.3), channel_id=1, source_target_pairs={{0,16},{4,20},{8,24},{12,28},{16,0},{20,4},{24,8},{28,12},{1,17},{... | collective-permute-start | bytes 491528 | tf_op jit(solution)/shard_map/ppermute | solution.py:507
  73.3 8.1 %collective-permute-start.24 = (bf16[2,2,1,40,1024]{4,3,1,2,0:T(8,128)(2,1)S(1)}, bf16[2,2,1,40,1024]{4,3,1,2,0:T(8,128)(2,1)S(1)}, u32[]{:S(2)}, u32[]{:S(2)}) collective-permute-start(bf16[2,2,1,40,1024]{4,3,1,2,0:T(8,128)(2,1)S(1)} %bitcast.157), channel_id=1, source_target_pairs={{0,1},{1,0},{2,3},{3,2},{4,5},{5,4},{6,7},{7,6},{8,9},{9,8},{10,11... | collective-permute-start | bytes 983048 | tf_op jit(solution)/shard_map/ppermute | solution.py:507
  73.3 8.6 %collective-permute-start.22 = (bf16[2,2,1,40,1024]{4,3,1,2,0:T(8,128)(2,1)S(1)}, bf16[2,2,1,40,1024]{4,3,1,2,0:T(8,128)(2,1)S(1)}, u32[]{:S(2)}, u32[]{:S(2)}) collective-permute-start(bf16[2,2,1,40,1024]{4,3,1,2,0:T(8,128)(2,1)S(1)} %bitcast.156), channel_id=1, source_target_pairs={{0,1},{1,0},{2,3},{3,2},{4,5},{5,4},{6,7},{7,6},{8,9},{9,8},{10,11... | collective-permute-start | bytes 983048 | tf_op jit(solution)/shard_map/ppermute | solution.py:507
  81.6 6.2 %collective-permute-start.25 = (bf16[2,1,40,1024]{3,2,1,0:T(8,128)(2,1)S(1)}, bf16[2,1,40,1024]{3,2,1,0:T(8,128)(2,1)S(1)}, u32[]{:S(2)}, u32[]{:S(2)}) collective-permute-start(bf16[2,1,40,1024]{3,2,1,0:T(8,128)(2,1)S(1)} %slice_bitcast_fusion.7), channel_id=1, source_target_pairs={{0,2},{1,3},{2,0},{3,1},{4,6},{5,7},{6,4},{7,5},{8,10},{9,11},{10,... | collective-permute-start | bytes 491528 | tf_op jit(solution)/shard_map/ppermute | solution.py:507
  82.1 6.2 %collective-permute-start.23 = (bf16[2,1,40,1024]{3,2,1,0:T(8,128)(2,1)S(1)}, bf16[2,1,40,1024]{3,2,1,0:T(8,128)(2,1)S(1)}, u32[]{:S(2)}, u32[]{:S(2)}) collective-permute-start(bf16[2,1,40,1024]{3,2,1,0:T(8,128)(2,1)S(1)} %slice_bitcast_fusion.9), channel_id=1, source_target_pairs={{0,4},{4,0},{8,12},{12,8},{16,20},{20,16},{24,28},{28,24},{1,5},{5... | collective-permute-start | bytes 491528 | tf_op jit(solution)/shard_map/ppermute | solution.py:507
  83.3 6.2 %collective-permute-start.26 = (bf16[2,40,1024]{2,1,0:T(8,128)(2,1)S(1)}, bf16[2,40,1024]{2,1,0:T(8,128)(2,1)S(1)}, u32[]{:S(2)}, u32[]{:S(2)}) collective-permute-start(bf16[2,40,1024]{2,1,0:T(8,128)(2,1)S(1)} %get-tuple-element.141), channel_id=1, source_target_pairs={{0,2},{1,3},{2,0},{3,1},{4,6},{5,7},{6,4},{7,5},{8,10},{9,11},{10,... | collective-permute-start | bytes 491528 | tf_op jit(solution)/shard_map/ppermute | solution.py:507
  84.3 5.8 %collective-permute-start.27 = (bf16[2,40,1024]{2,1,0:T(8,128)(2,1)S(1)}, bf16[2,40,1024]{2,1,0:T(8,128)(2,1)S(1)}, u32[]{:S(2)}, u32[]{:S(2)}) collective-permute-start(bf16[2,40,1024]{2,1,0:T(8,128)(2,1)S(1)} %get-tuple-element.143), channel_id=1, source_target_pairs={{0,4},{4,0},{8,12},{12,8},{16,20},{20,16},{24,28},{28,24},{1,5},{5... | collective-permute-start | bytes 491528 | tf_op jit(solution)/shard_map/ppermute | solution.py:507
  88.4 8.0 %copy-start.2 = (bf16[512,512]{1,0:T(8,128)(2,1)S(1)}, bf16[512,512]{1,0:T(8,128)(2,1)}, u32[]{:S(2)}) copy-start(bf16[512,512]{1,0:T(8,128)(2,1)} %w_dq.1) | copy-start | bytes 1572868
  88.4 8.0 %copy-start.5 = (f32[512]{0:T(512)S(1)}, f32[512]{0:T(512)}, u32[]{:S(2)}) copy-start(f32[512]{0:T(512)} %param.30) | copy-start | bytes 6148
  89.6 10.4 %copy-start.6 = (bf16[2048,1024]{1,0:T(8,128)(2,1)S(1)}, bf16[2048,1024]{1,0:T(8,128)(2,1)}, u32[]{:S(2)}) copy-start(bf16[2048,1024]{1,0:T(8,128)(2,1)} %refs_11_.1) | copy-start | bytes 12582916
  90.1 7.0 %collective-permute-start.31 = (bf16[1,40,1024]{2,1,0:T(8,128)(2,1)S(1)}, bf16[1,40,1024]{2,1,0:T(8,128)(2,1)S(1)}, u32[]{:S(2)}, u32[]{:S(2)}) collective-permute-start(bf16[1,40,1024]{2,1,0:T(8,128)(2,1)S(1)} %get-tuple-element.156), channel_id=1, source_target_pairs={{0,4},{4,0},{8,12},{12,8},{16,20},{20,16},{24,28},{28,24},{1,5},{5... | collective-permute-start | bytes 245768 | tf_op jit(solution)/shard_map/ppermute | solution.py:507
  91.5 8.5 %collective-permute-start.29 = (bf16[40,2048]{1,0:T(8,128)(2,1)S(1)}, bf16[40,2048]{1,0:T(8,128)(2,1)S(1)}, u32[]{:S(2)}, u32[]{:S(2)}) collective-permute-start(bf16[40,2048]{1,0:T(8,128)(2,1)S(1)} %pad_maximum_fusion.5), channel_id=1, source_target_pairs={{0,8},{4,12},{8,16},{12,20},{16,24},{20,28},{24,0},{28,4},{1,9},{5... | collective-permute-start | bytes 491528 | tf_op jit(solution)/shard_map/ppermute | solution.py:507
  92.1 7.8 %copy-start.7 = (bf16[512,512]{1,0:T(8,128)(2,1)S(1)}, bf16[512,512]{1,0:T(8,128)(2,1)}, u32[]{:S(2)}) copy-start(bf16[512,512]{1,0:T(8,128)(2,1)} %refs_12_.1) | copy-start | bytes 1572868
  92.1 7.8 %collective-permute-start.28 = (bf16[40,2048]{1,0:T(8,128)(2,1)S(1)}, bf16[40,2048]{1,0:T(8,128)(2,1)S(1)}, u32[]{:S(2)}, u32[]{:S(2)}) collective-permute-start(bf16[40,2048]{1,0:T(8,128)(2,1)S(1)} %pad_maximum_fusion.4), channel_id=1, source_target_pairs={{0,24},{4,28},{8,0},{12,4},{16,8},{20,12},{24,16},{28,20},{1,25},{... | collective-permute-start | bytes 491528 | tf_op jit(solution)/shard_map/ppermute | solution.py:507
  95.4 4.5 %collective-permute-start.30 = (bf16[1,40,1024]{2,1,0:T(8,128)(2,1)S(1)}, bf16[1,40,1024]{2,1,0:T(8,128)(2,1)S(1)}, u32[]{:S(2)}, u32[]{:S(2)}) collective-permute-start(bf16[1,40,1024]{2,1,0:T(8,128)(2,1)S(1)} %get-tuple-element.158), channel_id=1, source_target_pairs={{0,2},{1,3},{2,0},{3,1},{4,6},{5,7},{6,4},{7,5},{8,10},{9,11},{10,... | collective-permute-start | bytes 245768 | tf_op jit(solution)/shard_map/ppermute | solution.py:507

commit v4 on v3

--- a/solution.py
+++ b/solution.py
@@ -634,11 +634,11 @@
         added = finish(zs, sent, hidden, gate, spread)
         first = (zs, first_leg(added))
     zs, legs = first
+    if second:
+        made = last_leg(second[0], ends(second[1]))
+        legs = behind(legs, made)
     sums = ends(legs)
     legs = second_leg(sums)
-    if second:
-        made = last_leg(second[0], ends(behind(second[1], sums)))
-        legs = behind(legs, made)
     if zs != [0]:
         sums = ends(legs)
         last_leg(zs, sums)

time: 103 us -> 101 us (0.981)
  waiting for transfers between devices: 28.5 us -> 26.3 us
    ppermute x29, waiting for transfers between devices: 24.9 us -> 22.8 us  [shift(): return lax.ppermute(x, axis, pairs)]
  transfers between devices with their start and end apart: 32 -> 32, of which waited for: 17 -> 16; matrix products, arithmetic and copies ran while one was open for 3% -> 3% of each run, Pallas kernels for 16% -> 17%
where the time goes in v4:
time: 101 us
  starting transfers between devices  39.7 us (39%)
  Pallas kernels  30.4 us (30%)
  waiting for transfers between devices  26.3 us (26%)
  local copies, waits for them, and re-layouts  1.78 us (2%)
  other arithmetic  1.58 us (2%)
  between operations  1.18 us (1%)
    ppermute x29, starting transfers between devices, shift(): return lax.ppermute(x, axis, pairs)  32 us
    ppermute x29, waiting for transfers between devices, shift(): return lax.ppermute(x, axis, pairs)  22.8 us
    pallas_call x3, Pallas kernels, stream(): pl.pallas_call(functools.partial(stream_kernel, patch_cap, capacity, expe...  13.7 us
    pallas_call x1, Pallas kernels, encode(): pl.pallas_call(functools.partial(encoder_kernel, reach), out_shape=(jax.S...  7.11 us
    ppermute x1, starting transfers between devices, passed_along(): return lax.ppermute(x, axis, pairs)  4.89 us
    pallas_call x1, Pallas kernels, decode(): pl.pallas_call(functools.partial(decode_kernel, len(wholes)), out_shape=(...  3.08 us
    pallas_call x3, Pallas kernels, gated_share(): pl.pallas_call(functools.partial(share_kernel, order), out_shape=share_sh...  3.01 us
    pallas_call x1, Pallas kernels, opening(): pl.pallas_call(functools.partial(opening_kernel, reach, capacity), out_sh...  2.89 us
  transfers between devices with their start and end apart: 32, of which 16 were waited for; matrix products, arithmetic and copies ran while one was open for 3% of the time, Pallas kernels for 17%

profile of v4, /device:TPU:0, one launch (start us, length us, event | category | flops | bytes accessed | tf_op | source)
XLA Modules:
  0.0 100.9 jit_solution(2062486720259231945)
XLA Ops:
  0.6 4.9 %collective-permute-start = (bf16[256,512]{1,0:T(8,128)(2,1)}, bf16[256,512]{1,0:T(8,128)(2,1)S(1)}, u32[]{:S(2)}, u32[]{:S(2)}) collective-permute-start(bf16[256,512]{1,0:T(8,128)(2,1)} %refs_1_.1), channel_id=1, source_target_pairs={{0,2},{1,3},{2,4},{3,5},{4,6},{5,7},{6,8},{7,9},{8,10},{9,11},{10,... | collective-permute-start | bytes 786440 | tf_op jit(solution)/shard_map/ppermute | solution.py:23
  5.5 1.5 %collective-permute-start.2 = (bf16[256,512]{1,0:T(8,128)(2,1)}, bf16[256,512]{1,0:T(8,128)(2,1)S(1)}, u32[]{:S(2)}, u32[]{:S(2)}) collective-permute-start(bf16[256,512]{1,0:T(8,128)(2,1)} %refs_1_.1), channel_id=1, source_target_pairs={{0,1},{2,3},{4,5},{6,7},{8,9},{10,11},{12,13},{14,15},{16,17},{18,... | collective-permute-start | bytes 786440 | tf_op jit(solution)/shard_map/ppermute | solution.py:537
  7.0 2.9 %shard_map.176 = (bf16[256,512]{1,0:T(8,128)(2,1)S(1)}, f32[1,512]{1,0:T(1,128)S(1)}, bf16[512,1024]{1,0:T(8,128)(2,1)S(1)}, bf16[512,512]{1,0:T(8,128)(2,1)S(1)...) custom-call(s32[1]{0:T(128)} %bitcast.1.refs_0_, ...), custom_call_target="tpu_custom_call" | custom-call | flops 805306368 | tf_op jit(solution)/shard_map/pallas_call | solution.py:141
  9.9 1.4 %collective-permute-done.refs_1_ = bf16[256,512]{1,0:T(8,128)(2,1)S(1)} collective-permute-done((bf16[256,512]{1,0:T(8,128)(2,1)}, bf16[256,512]{1,0:T(8,128)(2,1)S(1)}, u32[]{:S(2)}, u32[]{:S(2)}) %collective-permute-start) | collective-permute-done | bytes 262176 | tf_op jit(solution)/shard_map/ppermute | solution.py:23
  11.4 1.3 %collective-permute-start.1 = (bf16[256,512]{1,0:T(8,128)(2,1)S(1)}, bf16[256,512]{1,0:T(8,128)(2,1)S(1)}, u32[]{:S(2)}, u32[]{:S(2)}) collective-permute-start(bf16[256,512]{1,0:T(8,128)(2,1)S(1)} %collective-permute-done.refs_1_), channel_id=1, source_target_pairs={{1,0},{3,2},{5,4},{7,6},{9,8},{11,10},{13,12},{15,14},{17,16},{19,... | collective-permute-start | bytes 786440 | tf_op jit(solution)/shard_map/ppermute | solution.py:539
  12.7 2.1 %collective-permute-done.1.refs_2_ = bf16[256,512]{1,0:T(8,128)(2,1)S(1)} collective-permute-done((bf16[256,512]{1,0:T(8,128)(2,1)S(1)}, bf16[256,512]{1,0:T(8,128)(2,1)S(1)}, u32[]{:S(2)}, u32[]{:S(2)}) %collective-permute-start.1) | collective-permute-done | bytes 262176 | tf_op jit(solution)/shard_map/ppermute | solution.py:539
  14.8 7.1 %shard_map.177 = (bf16[256,512]{1,0:T(8,128)(2,1)S(1)}, bf16[48,512]{1,0:T(8,128)(2,1)S(1)}) custom-call(s32[1]{0:T(128)S(6)} %and.5.refs_0_, bf16[256,512]{1,0:T(8,128)(2,1)S(1)} %collective-permute-done.refs_1_, bf16[256,512]{1,0:T(8,128)(2,1)S(1)} %collective-permute-done.1.refs_2_, bf16[256,512]{1,0:T(8,128)(2,1)S(1)} %collective-permute-done.2.refs_3_, ...), custom_call_target="tpu_custom_call" | custom-call | flops 2415919104 | tf_op jit(solution)/shard_map/pallas_call | solution.py:239
  21.9 4.3 %collective-permute-start.3 = (bf16[48,512]{1,0:T(8,128)(2,1)S(1)}, bf16[48,512]{1,0:T(8,128)(2,1)S(1)}, u32[]{:S(2)}, u32[]{:S(2)}) collective-permute-start(bf16[48,512]{1,0:T(8,128)(2,1)S(1)} %get-tuple-element.81.payload), channel_id=1, source_target_pairs={{0,8},{4,12},{8,16},{12,20},{16,24},{20,28},{24,0},{28,4},{1,9},{5... | collective-permute-start | bytes 147464 | tf_op jit(solution)/shard_map/ppermute | solution.py:507
  26.2 2.6 %collective-permute-start.4 = (bf16[48,512]{1,0:T(8,128)(2,1)S(1)}, bf16[48,512]{1,0:T(8,128)(2,1)S(1)}, u32[]{:S(2)}, u32[]{:S(2)}) collective-permute-start(bf16[48,512]{1,0:T(8,128)(2,1)S(1)} %get-tuple-element.81.payload), channel_id=1, source_target_pairs={{0,16},{4,20},{8,24},{12,28},{16,0},{20,4},{24,8},{28,12},{1,17},{... | collective-permute-start | bytes 147464 | tf_op jit(solution)/shard_map/ppermute | solution.py:507
  28.8 1.4 %collective-permute-start.5 = (bf16[48,512]{1,0:T(8,128)(2,1)S(1)}, bf16[48,512]{1,0:T(8,128)(2,1)S(1)}, u32[]{:S(2)}, u32[]{:S(2)}) collective-permute-start(bf16[48,512]{1,0:T(8,128)(2,1)S(1)} %get-tuple-element.81.payload), channel_id=1, source_target_pairs={{0,24},{4,28},{8,0},{12,4},{16,8},{20,12},{24,16},{28,20},{1,25},{... | collective-permute-start | bytes 147464 | tf_op jit(solution)/shard_map/ppermute | solution.py:507
  30.1 1.4 %copy.25 = bf16[256,8,2,768]{3,1,2,0:T(8,128)(2,1)S(1)} copy(bf16[256,8,2,768]{3,2,1,0:T(2,128)(2,1)S(1)} %bitcast.162) | data formatting | bytes 12582912
  31.5 1.1 %collective-permute-done.4 = bf16[48,512]{1,0:T(8,128)(2,1)S(1)} collective-permute-done((bf16[48,512]{1,0:T(8,128)(2,1)S(1)}, bf16[48,512]{1,0:T(8,128)(2,1)S(1)}, u32[]{:S(2)}, u32[]{:S(2)}) %collective-permute-start.4) | collective-permute-done | bytes 49184 | tf_op jit(solution)/shard_map/ppermute | solution.py:507
  32.7 0.4 collective-permute-done.5
  33.1 0.7 collective-permute-start.6
  33.8 0.6 collective-permute-start.8
  34.4 3.4 %collective-permute-done.6 = bf16[4,48,256]{2,1,0:T(8,128)(2,1)S(1)} collective-permute-done((bf16[4,48,256]{2,1,0:T(8,128)(2,1)S(1)}, bf16[4,48,256]{2,1,0:T(8,128)(2,1)S(1)}, u32[]{:S(2)}, u32[]{:S(2)}) %collective-permute-start.6) | collective-permute-done | bytes 98336 | tf_op jit(solution)/shard_map/ppermute | solution.py:507
  37.8 0.1 collective-permute-start.7
  37.9 0.5 collective-permute-done.8
  38.4 2.3 %collective-permute-start.9 = (bf16[4,2,48,256]{3,2,0,1:T(8,128)(2,1)S(1)}, bf16[4,2,48,256]{3,2,0,1:T(8,128)(2,1)S(1)}, u32[]{:S(2)}, u32[]{:S(2)}) collective-permute-start(bf16[4,2,48,256]{3,2,0,1:T(8,128)(2,1)S(1)} %get-tuple-element.147), channel_id=1, source_target_pairs={{0,4},{4,0},{8,12},{12,8},{16,20},{20,16},{24,28},{28,24},{1,5},{5... | collective-permute-start | bytes 589832 | tf_op jit(solution)/shard_map/ppermute | solution.py:507
  40.7 2.9 %collective-permute-done.7 = bf16[4,2,48,256]{3,2,0,1:T(8,128)(2,1)S(1)} collective-permute-done((bf16[4,2,48,256]{3,2,0,1:T(8,128)(2,1)S(1)}, bf16[4,2,48,256]{3,2,0,1:T(8,128)(2,1)S(1)}, u32[]{:S(2)}, u32[]{:S(2)}) %collective-permute-start.7) | collective-permute-done | bytes 196640 | tf_op jit(solution)/shard_map/ppermute | solution.py:507
  43.5 0.8 collective-permute-done.9
  44.3 0.1 maximum_maximum_fusion
  44.5 2.3 %collective-permute-done.10.refs_2_ = bf16[16,48,512]{2,1,0:T(8,128)(2,1)S(1)} collective-permute-done((bf16[16,48,512]{2,1,0:T(8,128)(2,1)S(1)}, bf16[16,48,512]{2,1,0:T(8,128)(2,1)S(1)}, u32[]{:S(2)}, u32[]{:S(2)}) %collective-permute-start.10) | collective-permute-done | bytes 786464 | tf_op jit(solution)/shard_map/ppermute | solution.py:507
  46.8 3.6 %shard_map.179 = (bf16[4,40,1024]{2,1,0:T(8,128)(2,1)S(1)}, bf16[4,40,1024]{2,1,0:T(8,128)(2,1)S(1)}, bf16[96,768]{1,0:T(8,128)(2,1)S(1)}, f32[96,1]{1,0:T(8,128)S(1)}, bf16[1,96,160]{2,1,0:T(8,128)(2,1)S(1)}) custom-call(s32[1]{0:T(128)} %bitcast.refs_0_, bf16[16,48,512]{2,1,0:T(8,128)(2,1)S(1)} %bitcast.137, ...), custom_call_target="tpu_custom_call" | custom-call | flops 201326592 | tf_op jit(solution)/shard_map/pallas_call | solution.py:385
  50.4 0.2 collective-permute-start.11
  50.6 0.4 collective-permute-start.12
  51.0 0.8 shard_map.180
  51.8 0.3 collective-permute-done.11
  52.1 0.1 fusion.5
  52.2 2.1 %collective-permute-start.13 = (bf16[2,1,40,1024]{3,2,1,0:T(8,128)(2,1)S(1)}, bf16[2,1,40,1024]{3,2,1,0:T(8,128)(2,1)S(1)}, u32[]{:S(2)}, u32[]{:S(2)}) collective-permute-start(bf16[2,1,40,1024]{3,2,1,0:T(8,128)(2,1)S(1)} %get-tuple-element.137), channel_id=1, source_target_pairs={{0,4},{4,0},{8,12},{12,8},{16,20},{20,16},{24,28},{28,24},{1,5},{5... | collective-permute-start | bytes 491528 | tf_op jit(solution)/shard_map/ppermute | solution.py:507
  54.3 0.1 fusion.4
  54.6 6.5 %shard_map.181 = (bf16[8,40,1024]{2,1,0:T(8,128)(2,1)S(1)}, bf16[8,40,1024]{2,1,0:T(8,128)(2,1)S(1)}, bf16[192,768]{1,0:T(8,128)(2,1)S(1)}, f32[192,1]{1,0:T(8,128)S(1)}, bf16[2,96,160]{2,1,0:T(8,128)(2,1)S(1)}) custom-call(s32[1]{0:T(128)} %bitcast.refs_0_, bf16[16,48,512]{2,1,0:T(8,128)(2,1)S(1)} %bitcast.138, ...), custom_call_target="tpu_custom_call" | custom-call | flops 402653184 | tf_op jit(solution)/shard_map/pallas_call | solution.py:385
  61.2 0.5 collective-permute-start.15
  61.7 0.1 fusion.10
  61.8 2.1 %collective-permute-start.17 = (bf16[1,40,1024]{2,1,0:T(8,128)(2,1)S(1)}, bf16[1,40,1024]{2,1,0:T(8,128)(2,1)S(1)}, u32[]{:S(2)}, u32[]{:S(2)}) collective-permute-start(bf16[1,40,1024]{2,1,0:T(8,128)(2,1)S(1)} %get-tuple-element.157), channel_id=1, source_target_pairs={{0,2},{1,3},{2,0},{3,1},{4,6},{5,7},{6,4},{7,5},{8,10},{9,11},{10,... | collective-permute-start | bytes 245768 | tf_op jit(solution)/shard_map/ppermute | solution.py:507
  63.9 0.3 collective-permute-start.18
  64.2 1.4 %shard_map.182 = (bf16[8,40,1024]{2,1,0:T(8,128)(2,1)S(1)}, bf16[8,40,1024]{2,1,0:T(8,128)(2,1)S(1)}) custom-call(bf16[192,768]{1,0:T(8,128)(2,1)S(1)} %get-tuple-element.96.hidden, f32[192,1]{1,0:T(8,128)S(1)} %get-tuple-element.99.gate, bf16[2,96,160]{2,1,0:T(8,128)(2,1)S(1)} %get-tuple-element.100.spread, bf16[768,2048]{1,0:T(8,128)(2,1)S(1)} %bitcast.130), custom_call_target="tpu_custom_call" | custom-call | flops 1000 | tf_op jit(solution)/shard_map/pallas_call | solution.py:410
  65.6 0.2 fusion.1
  65.9 0.2 fusion
  66.2 3.6 %shard_map.183 = (bf16[4,40,1024]{2,1,0:T(8,128)(2,1)S(1)}, bf16[4,40,1024]{2,1,0:T(8,128)(2,1)S(1)}, bf16[96,768]{1,0:T(8,128)(2,1)S(1)}, f32[96,1]{1,0:T(8,128)S(1)}, bf16[1,96,160]{2,1,0:T(8,128)(2,1)S(1)}) custom-call(s32[1]{0:T(128)} %bitcast.refs_0_, bf16[16,48,512]{2,1,0:T(8,128)(2,1)S(1)} %bitcast.139, ...), custom_call_target="tpu_custom_call" | custom-call | flops 201326592 | tf_op jit(solution)/shard_map/pallas_call | solution.py:385
  69.8 1.8 %collective-permute-start.20 = (bf16[2,2,40,1024]{3,2,1,0:T(8,128)(2,1)S(1)}, bf16[2,2,40,1024]{3,2,1,0:T(8,128)(2,1)S(1)}, u32[]{:S(2)}, u32[]{:S(2)}) collective-permute-start(bf16[2,2,40,1024]{3,2,1,0:T(8,128)(2,1)S(1)} %get-tuple-element.129), channel_id=1, source_target_pairs={{0,4},{4,0},{8,12},{12,8},{16,20},{20,16},{24,28},{28,24},{1,5},{5... | collective-permute-start | bytes 983048 | tf_op jit(solution)/shard_map/ppermute | solution.py:507
  71.7 1.6 %collective-permute-start.19 = (bf16[40,2048]{1,0:T(8,128)(2,1)S(1)}, bf16[40,2048]{1,0:T(8,128)(2,1)S(1)}, u32[]{:S(2)}, u32[]{:S(2)}) collective-permute-start(bf16[40,2048]{1,0:T(8,128)(2,1)S(1)} %pad_maximum_fusion.3), channel_id=1, source_target_pairs={{0,16},{4,20},{8,24},{12,28},{16,0},{20,4},{24,8},{28,12},{1,17},{... | collective-permute-start | bytes 491528 | tf_op jit(solution)/shard_map/ppermute | solution.py:507
  73.3 0.5 collective-permute-start.26
  73.8 5.2 %collective-permute-done.20 = bf16[2,2,40,1024]{3,2,1,0:T(8,128)(2,1)S(1)} collective-permute-done((bf16[2,2,40,1024]{3,2,1,0:T(8,128)(2,1)S(1)}, bf16[2,2,40,1024]{3,2,1,0:T(8,128)(2,1)S(1)}, u32[]{:S(2)}, u32[]{:S(2)}) %collective-permute-start.20) | collective-permute-done | bytes 327712 | tf_op jit(solution)/shard_map/ppermute | solution.py:507
  79.0 1.5 %collective-permute-done.22 = bf16[2,2,40,1024]{3,2,1,0:T(8,128)(2,1)S(1)} collective-permute-done((bf16[2,2,40,1024]{3,2,1,0:T(8,128)(2,1)S(1)}, bf16[2,2,40,1024]{3,2,1,0:T(8,128)(2,1)S(1)}, u32[]{:S(2)}, u32[]{:S(2)}) %collective-permute-start.22) | collective-permute-done | bytes 327712 | tf_op jit(solution)/shard_map/ppermute | solution.py:507
  80.5 0.1 add_convert_fusion.1
  80.6 0.1 add_convert_fusion
  80.7 0.4 collective-permute-start.21
  81.1 1.2 %collective-permute-start.23 = (bf16[2,40,1024]{2,1,0:T(8,128)(2,1)S(1)}, bf16[2,40,1024]{2,1,0:T(8,128)(2,1)S(1)}, u32[]{:S(2)}, u32[]{:S(2)}) collective-permute-start(bf16[2,40,1024]{2,1,0:T(8,128)(2,1)S(1)} %slice_bitcast_fusion.8), channel_id=1, source_target_pairs={{0,4},{4,0},{8,12},{12,8},{16,20},{20,16},{24,28},{28,24},{1,5},{5... | collective-permute-start | bytes 491528 | tf_op jit(solution)/shard_map/ppermute | solution.py:507
  82.3 0.8 shard_map.184
  83.2 0.1 fusion.2
  83.3 1.0 collective-permute-start.30
  84.3 0.1 fusion.3
  84.4 1.7 %collective-permute-start.27 = (bf16[2,1,40,1024]{3,2,1,0:T(8,128)(2,1)S(1)}, bf16[2,1,40,1024]{3,2,1,0:T(8,128)(2,1)S(1)}, u32[]{:S(2)}, u32[]{:S(2)}) collective-permute-start(bf16[2,1,40,1024]{3,2,1,0:T(8,128)(2,1)S(1)} %get-tuple-element.135), channel_id=1, source_target_pairs={{0,4},{4,0},{8,12},{12,8},{16,20},{20,16},{24,28},{28,24},{1,5},{5... | collective-permute-start | bytes 491528 | tf_op jit(solution)/shard_map/ppermute | solution.py:507
  86.2 1.2 %collective-permute-done.21 = bf16[2,40,1024]{2,1,0:T(8,128)(2,1)S(1)} collective-permute-done((bf16[2,40,1024]{2,1,0:T(8,128)(2,1)S(1)}, bf16[2,40,1024]{2,1,0:T(8,128)(2,1)S(1)}, u32[]{:S(2)}, u32[]{:S(2)}) %collective-permute-start.21) | collective-permute-done | bytes 163872 | tf_op jit(solution)/shard_map/ppermute | solution.py:507
  87.4 0.7 collective-permute-done.23
  88.3 0.5 collective-permute-start.25
  88.7 3.5 %collective-permute-start.24 = (bf16[40,2048]{1,0:T(8,128)(2,1)S(1)}, bf16[40,2048]{1,0:T(8,128)(2,1)S(1)}, u32[]{:S(2)}, u32[]{:S(2)}) collective-permute-start(bf16[40,2048]{1,0:T(8,128)(2,1)S(1)} %pad_maximum_fusion.4), channel_id=1, source_target_pairs={{0,24},{4,28},{8,0},{12,4},{16,8},{20,12},{24,16},{28,20},{1,25},{... | collective-permute-start | bytes 491528 | tf_op jit(solution)/shard_map/ppermute | solution.py:507
  92.3 1.0 collective-permute-start.31
  93.3 1.3 %collective-permute-start.28 = (bf16[1,40,1024]{2,1,0:T(8,128)(2,1)S(1)}, bf16[1,40,1024]{2,1,0:T(8,128)(2,1)S(1)}, u32[]{:S(2)}, u32[]{:S(2)}) collective-permute-start(bf16[1,40,1024]{2,1,0:T(8,128)(2,1)S(1)} %get-tuple-element.150), channel_id=1, source_target_pairs={{0,2},{1,3},{2,0},{3,1},{4,6},{5,7},{6,4},{7,5},{8,10},{9,11},{10,... | collective-permute-start | bytes 245768 | tf_op jit(solution)/shard_map/ppermute | solution.py:507
  94.6 0.7 shard_map.178
  95.4 1.4 %collective-permute-done.31.refs_7_ = bf16[1,40,1024]{2,1,0:T(8,128)(2,1)S(1)} collective-permute-done((bf16[1,40,1024]{2,1,0:T(8,128)(2,1)S(1)}, bf16[1,40,1024]{2,1,0:T(8,128)(2,1)S(1)}, u32[]{:S(2)}, u32[]{:S(2)}) %collective-permute-start.31) | collective-permute-done | bytes 81952 | tf_op jit(solution)/shard_map/ppermute | solution.py:507
  96.8 1.1 %collective-permute-done.28.refs_5_ = bf16[1,40,1024]{2,1,0:T(8,128)(2,1)S(1)} collective-permute-done((bf16[1,40,1024]{2,1,0:T(8,128)(2,1)S(1)}, bf16[1,40,1024]{2,1,0:T(8,128)(2,1)S(1)}, u32[]{:S(2)}, u32[]{:S(2)}) %collective-permute-start.28) | collective-permute-done | bytes 81952 | tf_op jit(solution)/shard_map/ppermute | solution.py:507
  97.9 3.1 %shard_map.185 = (bf16[256,512]{1,0:T(8,128)(2,1)}, bf16[40,2048]{1,0:T(8,128)(2,1)}) custom-call(bf16[40,2048]{1,0:T(8,128)(2,1)S(1)} %get-tuple-element.82.refs_0_, bf16[40,2048]{1,0:T(8,128)(2,1)S(1)} %collective-permute-done.19.refs_1_, bf16[40,2048]{1,0:T(8,128)(2,1)S(1)} %collective-permute-done.24.refs_2_, ...), custom_call_target="tpu_custom_call" | custom-call | flops 2147483648 | tf_op jit(solution)/shard_map/pallas_call | solution.py:475
  (70 shorter events, 1.1 us)
Async XLA Ops:
  0.6 10.7 %collective-permute-start = (bf16[256,512]{1,0:T(8,128)(2,1)}, bf16[256,512]{1,0:T(8,128)(2,1)S(1)}, u32[]{:S(2)}, u32[]{:S(2)}) collective-permute-start(bf16[256,512]{1,0:T(8,128)(2,1)} %refs_1_.1), channel_id=1, source_target_pairs={{0,2},{1,3},{2,4},{3,5},{4,6},{5,7},{6,8},{7,9},{8,10},{9,11},{10,... | collective-permute-start | bytes 786440 | tf_op jit(solution)/shard_map/ppermute | solution.py:23
  5.5 7.2 %collective-permute-start.2 = (bf16[256,512]{1,0:T(8,128)(2,1)}, bf16[256,512]{1,0:T(8,128)(2,1)S(1)}, u32[]{:S(2)}, u32[]{:S(2)}) collective-permute-start(bf16[256,512]{1,0:T(8,128)(2,1)} %refs_1_.1), channel_id=1, source_target_pairs={{0,1},{2,3},{4,5},{6,7},{8,9},{10,11},{12,13},{14,15},{16,17},{18,... | collective-permute-start | bytes 786440 | tf_op jit(solution)/shard_map/ppermute | solution.py:537
  7.0 23.1 %slice-start = ((s8[6291456]{0:T(1024)(128)(4,1)}), s8[4194304]{0:T(1024)(128)(4,1)S(1)}, s32[]{:S(2)}) async-start(s8[6291456]{0:T(1024)(128)(4,1)} %bitcast.160), calls=%async_computation | async-start | bytes 8388608
  11.4 3.4 %collective-permute-start.1 = (bf16[256,512]{1,0:T(8,128)(2,1)S(1)}, bf16[256,512]{1,0:T(8,128)(2,1)S(1)}, u32[]{:S(2)}, u32[]{:S(2)}) collective-permute-start(bf16[256,512]{1,0:T(8,128)(2,1)S(1)} %collective-permute-done.refs_1_), channel_id=1, source_target_pairs={{1,0},{3,2},{5,4},{7,6},{9,8},{11,10},{13,12},{15,14},{17,16},{19,... | collective-permute-start | bytes 786440 | tf_op jit(solution)/shard_map/ppermute | solution.py:539
  12.7 17.5 %slice-start.1 = ((s8[6291456]{0:T(1024)(128)(4,1)}), s8[2097152]{0:T(1024)(128)(4,1)S(1)}, s32[]{:S(2)}) async-start(s8[6291456]{0:T(1024)(128)(4,1)} %bitcast.160), calls=%async_computation.1 | async-start | bytes 4194304
  21.9 9.6 %collective-permute-start.3 = (bf16[48,512]{1,0:T(8,128)(2,1)S(1)}, bf16[48,512]{1,0:T(8,128)(2,1)S(1)}, u32[]{:S(2)}, u32[]{:S(2)}) collective-permute-start(bf16[48,512]{1,0:T(8,128)(2,1)S(1)} %get-tuple-element.81.payload), channel_id=1, source_target_pairs={{0,8},{4,12},{8,16},{12,20},{16,24},{20,28},{24,0},{28,4},{1,9},{5... | collective-permute-start | bytes 147464 | tf_op jit(solution)/shard_map/ppermute | solution.py:507
  26.2 6.5 %collective-permute-start.4 = (bf16[48,512]{1,0:T(8,128)(2,1)S(1)}, bf16[48,512]{1,0:T(8,128)(2,1)S(1)}, u32[]{:S(2)}, u32[]{:S(2)}) collective-permute-start(bf16[48,512]{1,0:T(8,128)(2,1)S(1)} %get-tuple-element.81.payload), channel_id=1, source_target_pairs={{0,16},{4,20},{8,24},{12,28},{16,0},{20,4},{24,8},{28,12},{1,17},{... | collective-permute-start | bytes 147464 | tf_op jit(solution)/shard_map/ppermute | solution.py:507
  28.8 4.2 %collective-permute-start.5 = (bf16[48,512]{1,0:T(8,128)(2,1)S(1)}, bf16[48,512]{1,0:T(8,128)(2,1)S(1)}, u32[]{:S(2)}, u32[]{:S(2)}) collective-permute-start(bf16[48,512]{1,0:T(8,128)(2,1)S(1)} %get-tuple-element.81.payload), channel_id=1, source_target_pairs={{0,24},{4,28},{8,0},{12,4},{16,8},{20,12},{24,16},{28,20},{1,25},{... | collective-permute-start | bytes 147464 | tf_op jit(solution)/shard_map/ppermute | solution.py:507
  33.0 13.8 %copy-start.1 = (bf16[512,2048]{1,0:T(8,128)(2,1)S(1)}, bf16[512,2048]{1,0:T(8,128)(2,1)}, u32[]{:S(2)}) copy-start(bf16[512,2048]{1,0:T(8,128)(2,1)} %refs_3_.5) | copy-start | bytes 6291460
  33.1 4.7 %collective-permute-start.6 = (bf16[4,48,256]{2,1,0:T(8,128)(2,1)S(1)}, bf16[4,48,256]{2,1,0:T(8,128)(2,1)S(1)}, u32[]{:S(2)}, u32[]{:S(2)}) collective-permute-start(bf16[4,48,256]{2,1,0:T(8,128)(2,1)S(1)} %get-tuple-element.145), channel_id=1, source_target_pairs={{0,4},{4,0},{8,12},{12,8},{16,20},{20,16},{24,28},{28,24},{1,5},{5... | collective-permute-start | bytes 294920 | tf_op jit(solution)/shard_map/ppermute | solution.py:507
  33.8 4.6 %collective-permute-start.8 = (bf16[4,48,256]{2,1,0:T(8,128)(2,1)S(1)}, bf16[4,48,256]{2,1,0:T(8,128)(2,1)S(1)}, u32[]{:S(2)}, u32[]{:S(2)}) collective-permute-start(bf16[4,48,256]{2,1,0:T(8,128)(2,1)S(1)} %get-tuple-element.144), channel_id=1, source_target_pairs={{0,2},{1,3},{2,0},{3,1},{4,6},{5,7},{6,4},{7,5},{8,10},{9,11},{10,... | collective-permute-start | bytes 294920 | tf_op jit(solution)/shard_map/ppermute | solution.py:507
  37.8 5.7 %collective-permute-start.7 = (bf16[4,2,48,256]{3,2,0,1:T(8,128)(2,1)S(1)}, bf16[4,2,48,256]{3,2,0,1:T(8,128)(2,1)S(1)}, u32[]{:S(2)}, u32[]{:S(2)}) collective-permute-start(bf16[4,2,48,256]{3,2,0,1:T(8,128)(2,1)S(1)} %get-tuple-element.141), channel_id=1, source_target_pairs={{0,2},{1,3},{2,0},{3,1},{4,6},{5,7},{6,4},{7,5},{8,10},{9,11},{10,... | collective-permute-start | bytes 589832 | tf_op jit(solution)/shard_map/ppermute | solution.py:507
  38.4 8.4 %copy-start.3 = (f32[2048,4]{0,1:T(4,128)S(1)}, f32[2048,4]{0,1:T(4,128)}, u32[]{:S(2)}) copy-start(f32[2048,4]{0,1:T(4,128)} %param.27) | copy-start | bytes 98308
  38.4 5.9 %collective-permute-start.9 = (bf16[4,2,48,256]{3,2,0,1:T(8,128)(2,1)S(1)}, bf16[4,2,48,256]{3,2,0,1:T(8,128)(2,1)S(1)}, u32[]{:S(2)}, u32[]{:S(2)}) collective-permute-start(bf16[4,2,48,256]{3,2,0,1:T(8,128)(2,1)S(1)} %get-tuple-element.147), channel_id=1, source_target_pairs={{0,4},{4,0},{8,12},{12,8},{16,20},{20,16},{24,28},{28,24},{1,5},{5... | collective-permute-start | bytes 589832 | tf_op jit(solution)/shard_map/ppermute | solution.py:507
  44.3 2.5 %copy-start.4 = (f32[2048]{0:T(1024)S(1)}, f32[2048]{0:T(1024)}, u32[]{:S(2)}) copy-start(f32[2048]{0:T(1024)} %param.26) | copy-start | bytes 24580
  44.3 2.5 %copy-start = (bf16[1,768,2048]{2,1,0:T(8,128)(2,1)S(1)}, bf16[1,768,2048]{2,1,0:T(8,128)(2,1)}, u32[]{:S(2)}) copy-start(bf16[1,768,2048]{2,1,0:T(8,128)(2,1)} %param.29) | copy-start | bytes 9437188
  44.5 2.4 %collective-permute-start.10 = (bf16[16,48,512]{2,1,0:T(8,128)(2,1)S(1)}, bf16[16,48,512]{2,1,0:T(8,128)(2,1)S(1)}, u32[]{:S(2)}, u32[]{:S(2)}) collective-permute-start(bf16[16,48,512]{2,1,0:T(8,128)(2,1)S(1)} %bitcast.136), channel_id=1, source_target_pairs={{0,1},{1,0},{2,3},{3,2},{4,5},{5,4},{6,7},{7,6},{8,9},{9,8},{10,11... | collective-permute-start | bytes 2359304 | tf_op jit(solution)/shard_map/ppermute | solution.py:507
  50.4 1.7 %collective-permute-start.11 = (bf16[2,2,1,40,1024]{4,3,1,2,0:T(8,128)(2,1)S(1)}, bf16[2,2,1,40,1024]{4,3,1,2,0:T(8,128)(2,1)S(1)}, u32[]{:S(2)}, u32[]{:S(2)}) collective-permute-start(bf16[2,2,1,40,1024]{4,3,1,2,0:T(8,128)(2,1)S(1)} %bitcast.159), channel_id=1, source_target_pairs={{0,1},{1,0},{2,3},{3,2},{4,5},{5,4},{6,7},{7,6},{8,9},{9,8},{10,11... | collective-permute-start | bytes 983048 | tf_op jit(solution)/shard_map/ppermute | solution.py:507
  50.6 3.7 %collective-permute-start.12 = (bf16[2,2,1,40,1024]{4,3,1,2,0:T(8,128)(2,1)S(1)}, bf16[2,2,1,40,1024]{4,3,1,2,0:T(8,128)(2,1)S(1)}, u32[]{:S(2)}, u32[]{:S(2)}) collective-permute-start(bf16[2,2,1,40,1024]{4,3,1,2,0:T(8,128)(2,1)S(1)} %bitcast.158), channel_id=1, source_target_pairs={{0,1},{1,0},{2,3},{3,2},{4,5},{5,4},{6,7},{7,6},{8,9},{9,8},{10,11... | collective-permute-start | bytes 983048 | tf_op jit(solution)/shard_map/ppermute | solution.py:507
  52.2 9.4 %collective-permute-start.13 = (bf16[2,1,40,1024]{3,2,1,0:T(8,128)(2,1)S(1)}, bf16[2,1,40,1024]{3,2,1,0:T(8,128)(2,1)S(1)}, u32[]{:S(2)}, u32[]{:S(2)}) collective-permute-start(bf16[2,1,40,1024]{3,2,1,0:T(8,128)(2,1)S(1)} %get-tuple-element.137), channel_id=1, source_target_pairs={{0,4},{4,0},{8,12},{12,8},{16,20},{20,16},{24,28},{28,24},{1,5},{5... | collective-permute-start | bytes 491528 | tf_op jit(solution)/shard_map/ppermute | solution.py:507
  54.5 7.2 %collective-permute-start.14 = (bf16[2,1,40,1024]{3,2,1,0:T(8,128)(2,1)S(1)}, bf16[2,1,40,1024]{3,2,1,0:T(8,128)(2,1)S(1)}, u32[]{:S(2)}, u32[]{:S(2)}) collective-permute-start(bf16[2,1,40,1024]{3,2,1,0:T(8,128)(2,1)S(1)} %get-tuple-element.139), channel_id=1, source_target_pairs={{0,2},{1,3},{2,0},{3,1},{4,6},{5,7},{6,4},{7,5},{8,10},{9,11},{10,... | collective-permute-start | bytes 491528 | tf_op jit(solution)/shard_map/ppermute | solution.py:507
  61.1 4.8 %collective-permute-start.16 = (bf16[2,2,2,40,1024]{4,3,2,1,0:T(8,128)(2,1)S(1)}, bf16[2,2,2,40,1024]{4,3,2,1,0:T(8,128)(2,1)S(1)}, u32[]{:S(2)}, u32[]{:S(2)}) collective-permute-start(bf16[2,2,2,40,1024]{4,3,2,1,0:T(8,128)(2,1)S(1)} %bitcast.154), channel_id=1, source_target_pairs={{0,1},{1,0},{2,3},{3,2},{4,5},{5,4},{6,7},{7,6},{8,9},{9,8},{10,11... | collective-permute-start | bytes 1966088 | tf_op jit(solution)/shard_map/ppermute | solution.py:507
  61.2 4.4 %collective-permute-start.15 = (bf16[2,2,2,40,1024]{4,3,2,1,0:T(8,128)(2,1)S(1)}, bf16[2,2,2,40,1024]{4,3,2,1,0:T(8,128)(2,1)S(1)}, u32[]{:S(2)}, u32[]{:S(2)}) collective-permute-start(bf16[2,2,2,40,1024]{4,3,2,1,0:T(8,128)(2,1)S(1)} %bitcast.155), channel_id=1, source_target_pairs={{0,1},{1,0},{2,3},{3,2},{4,5},{5,4},{6,7},{7,6},{8,9},{9,8},{10,11... | collective-permute-start | bytes 1966088 | tf_op jit(solution)/shard_map/ppermute | solution.py:507
  61.8 8.0 %collective-permute-start.17 = (bf16[1,40,1024]{2,1,0:T(8,128)(2,1)S(1)}, bf16[1,40,1024]{2,1,0:T(8,128)(2,1)S(1)}, u32[]{:S(2)}, u32[]{:S(2)}) collective-permute-start(bf16[1,40,1024]{2,1,0:T(8,128)(2,1)S(1)} %get-tuple-element.157), channel_id=1, source_target_pairs={{0,2},{1,3},{2,0},{3,1},{4,6},{5,7},{6,4},{7,5},{8,10},{9,11},{10,... | collective-permute-start | bytes 245768 | tf_op jit(solution)/shard_map/ppermute | solution.py:507
  63.9 5.9 %collective-permute-start.18 = (bf16[1,40,1024]{2,1,0:T(8,128)(2,1)S(1)}, bf16[1,40,1024]{2,1,0:T(8,128)(2,1)S(1)}, u32[]{:S(2)}, u32[]{:S(2)}) collective-permute-start(bf16[1,40,1024]{2,1,0:T(8,128)(2,1)S(1)} %get-tuple-element.159), channel_id=1, source_target_pairs={{0,4},{4,0},{8,12},{12,8},{16,20},{20,16},{24,28},{28,24},{1,5},{5... | collective-permute-start | bytes 245768 | tf_op jit(solution)/shard_map/ppermute | solution.py:507
  69.8 9.2 %collective-permute-start.20 = (bf16[2,2,40,1024]{3,2,1,0:T(8,128)(2,1)S(1)}, bf16[2,2,40,1024]{3,2,1,0:T(8,128)(2,1)S(1)}, u32[]{:S(2)}, u32[]{:S(2)}) collective-permute-start(bf16[2,2,40,1024]{3,2,1,0:T(8,128)(2,1)S(1)} %get-tuple-element.129), channel_id=1, source_target_pairs={{0,4},{4,0},{8,12},{12,8},{16,20},{20,16},{24,28},{28,24},{1,5},{5... | collective-permute-start | bytes 983048 | tf_op jit(solution)/shard_map/ppermute | solution.py:507
  71.6 8.9 %collective-permute-start.22 = (bf16[2,2,40,1024]{3,2,1,0:T(8,128)(2,1)S(1)}, bf16[2,2,40,1024]{3,2,1,0:T(8,128)(2,1)S(1)}, u32[]{:S(2)}, u32[]{:S(2)}) collective-permute-start(bf16[2,2,40,1024]{3,2,1,0:T(8,128)(2,1)S(1)} %get-tuple-element.131), channel_id=1, source_target_pairs={{0,2},{1,3},{2,0},{3,1},{4,6},{5,7},{6,4},{7,5},{8,10},{9,11},{10,... | collective-permute-start | bytes 983048 | tf_op jit(solution)/shard_map/ppermute | solution.py:507
  71.7 23.6 %collective-permute-start.19 = (bf16[40,2048]{1,0:T(8,128)(2,1)S(1)}, bf16[40,2048]{1,0:T(8,128)(2,1)S(1)}, u32[]{:S(2)}, u32[]{:S(2)}) collective-permute-start(bf16[40,2048]{1,0:T(8,128)(2,1)S(1)} %pad_maximum_fusion.3), channel_id=1, source_target_pairs={{0,16},{4,20},{8,24},{12,28},{16,0},{20,4},{24,8},{28,12},{1,17},{... | collective-permute-start | bytes 491528 | tf_op jit(solution)/shard_map/ppermute | solution.py:507
  73.3 9.9 %collective-permute-start.29 = (bf16[2,2,1,40,1024]{4,3,1,2,0:T(8,128)(2,1)S(1)}, bf16[2,2,1,40,1024]{4,3,1,2,0:T(8,128)(2,1)S(1)}, u32[]{:S(2)}, u32[]{:S(2)}) collective-permute-start(bf16[2,2,1,40,1024]{4,3,1,2,0:T(8,128)(2,1)S(1)} %bitcast.157), channel_id=1, source_target_pairs={{0,1},{1,0},{2,3},{3,2},{4,5},{5,4},{6,7},{7,6},{8,9},{9,8},{10,11... | collective-permute-start | bytes 983048 | tf_op jit(solution)/shard_map/ppermute | solution.py:507
  73.3 11.0 %collective-permute-start.26 = (bf16[2,2,1,40,1024]{4,3,1,2,0:T(8,128)(2,1)S(1)}, bf16[2,2,1,40,1024]{4,3,1,2,0:T(8,128)(2,1)S(1)}, u32[]{:S(2)}, u32[]{:S(2)}) collective-permute-start(bf16[2,2,1,40,1024]{4,3,1,2,0:T(8,128)(2,1)S(1)} %bitcast.156), channel_id=1, source_target_pairs={{0,1},{1,0},{2,3},{3,2},{4,5},{5,4},{6,7},{7,6},{8,9},{9,8},{10,11... | collective-permute-start | bytes 983048 | tf_op jit(solution)/shard_map/ppermute | solution.py:507
  80.7 6.6 %collective-permute-start.21 = (bf16[2,40,1024]{2,1,0:T(8,128)(2,1)S(1)}, bf16[2,40,1024]{2,1,0:T(8,128)(2,1)S(1)}, u32[]{:S(2)}, u32[]{:S(2)}) collective-permute-start(bf16[2,40,1024]{2,1,0:T(8,128)(2,1)S(1)} %slice_bitcast_fusion.10), channel_id=1, source_target_pairs={{0,2},{1,3},{2,0},{3,1},{4,6},{5,7},{6,4},{7,5},{8,10},{9,11},{10,... | collective-permute-start | bytes 491528 | tf_op jit(solution)/shard_map/ppermute | solution.py:507
  81.1 7.1 %collective-permute-start.23 = (bf16[2,40,1024]{2,1,0:T(8,128)(2,1)S(1)}, bf16[2,40,1024]{2,1,0:T(8,128)(2,1)S(1)}, u32[]{:S(2)}, u32[]{:S(2)}) collective-permute-start(bf16[2,40,1024]{2,1,0:T(8,128)(2,1)S(1)} %slice_bitcast_fusion.8), channel_id=1, source_target_pairs={{0,4},{4,0},{8,12},{12,8},{16,20},{20,16},{24,28},{28,24},{1,5},{5... | collective-permute-start | bytes 491528 | tf_op jit(solution)/shard_map/ppermute | solution.py:507
  83.3 8.9 %collective-permute-start.30 = (bf16[2,1,40,1024]{3,2,1,0:T(8,128)(2,1)S(1)}, bf16[2,1,40,1024]{3,2,1,0:T(8,128)(2,1)S(1)}, u32[]{:S(2)}, u32[]{:S(2)}) collective-permute-start(bf16[2,1,40,1024]{3,2,1,0:T(8,128)(2,1)S(1)} %get-tuple-element.133), channel_id=1, source_target_pairs={{0,2},{1,3},{2,0},{3,1},{4,6},{5,7},{6,4},{7,5},{8,10},{9,11},{10,... | collective-permute-start | bytes 491528 | tf_op jit(solution)/shard_map/ppermute | solution.py:507
  84.4 8.8 %collective-permute-start.27 = (bf16[2,1,40,1024]{3,2,1,0:T(8,128)(2,1)S(1)}, bf16[2,1,40,1024]{3,2,1,0:T(8,128)(2,1)S(1)}, u32[]{:S(2)}, u32[]{:S(2)}) collective-permute-start(bf16[2,1,40,1024]{3,2,1,0:T(8,128)(2,1)S(1)} %get-tuple-element.135), channel_id=1, source_target_pairs={{0,4},{4,0},{8,12},{12,8},{16,20},{20,16},{24,28},{28,24},{1,5},{5... | collective-permute-start | bytes 491528 | tf_op jit(solution)/shard_map/ppermute | solution.py:507
  87.4 7.2 %copy-start.2 = (bf16[512,512]{1,0:T(8,128)(2,1)S(1)}, bf16[512,512]{1,0:T(8,128)(2,1)}, u32[]{:S(2)}) copy-start(bf16[512,512]{1,0:T(8,128)(2,1)} %w_dq.1) | copy-start | bytes 1572868
  87.4 7.2 %copy-start.5 = (f32[512]{0:T(512)S(1)}, f32[512]{0:T(512)}, u32[]{:S(2)}) copy-start(f32[512]{0:T(512)} %param.30) | copy-start | bytes 6148
  88.3 9.6 %collective-permute-start.25 = (bf16[40,2048]{1,0:T(8,128)(2,1)S(1)}, bf16[40,2048]{1,0:T(8,128)(2,1)S(1)}, u32[]{:S(2)}, u32[]{:S(2)}) collective-permute-start(bf16[40,2048]{1,0:T(8,128)(2,1)S(1)} %pad_maximum_fusion.5), channel_id=1, source_target_pairs={{0,8},{4,12},{8,16},{12,20},{16,24},{20,28},{24,0},{28,4},{1,9},{5... | collective-permute-start | bytes 491528 | tf_op jit(solution)/shard_map/ppermute | solution.py:507
  88.7 9.1 %copy-start.6 = (bf16[2048,1024]{1,0:T(8,128)(2,1)S(1)}, bf16[2048,1024]{1,0:T(8,128)(2,1)}, u32[]{:S(2)}) copy-start(bf16[2048,1024]{1,0:T(8,128)(2,1)} %refs_11_.1) | copy-start | bytes 12582916
  88.7 9.1 %collective-permute-start.24 = (bf16[40,2048]{1,0:T(8,128)(2,1)S(1)}, bf16[40,2048]{1,0:T(8,128)(2,1)S(1)}, u32[]{:S(2)}, u32[]{:S(2)}) collective-permute-start(bf16[40,2048]{1,0:T(8,128)(2,1)S(1)} %pad_maximum_fusion.4), channel_id=1, source_target_pairs={{0,24},{4,28},{8,0},{12,4},{16,8},{20,12},{24,16},{28,20},{1,25},{... | collective-permute-start | bytes 491528 | tf_op jit(solution)/shard_map/ppermute | solution.py:507
  92.3 4.5 %collective-permute-start.31 = (bf16[1,40,1024]{2,1,0:T(8,128)(2,1)S(1)}, bf16[1,40,1024]{2,1,0:T(8,128)(2,1)S(1)}, u32[]{:S(2)}, u32[]{:S(2)}) collective-permute-start(bf16[1,40,1024]{2,1,0:T(8,128)(2,1)S(1)} %get-tuple-element.148), channel_id=1, source_target_pairs={{0,4},{4,0},{8,12},{12,8},{16,20},{20,16},{24,28},{28,24},{1,5},{5... | collective-permute-start | bytes 245768 | tf_op jit(solution)/shard_map/ppermute | solution.py:507
  93.3 4.6 %copy-start.7 = (bf16[512,512]{1,0:T(8,128)(2,1)S(1)}, bf16[512,512]{1,0:T(8,128)(2,1)}, u32[]{:S(2)}) copy-start(bf16[512,512]{1,0:T(8,128)(2,1)} %refs_12_.1) | copy-start | bytes 1572868
  93.3 4.5 %collective-permute-start.28 = (bf16[1,40,1024]{2,1,0:T(8,128)(2,1)S(1)}, bf16[1,40,1024]{2,1,0:T(8,128)(2,1)S(1)}, u32[]{:S(2)}, u32[]{:S(2)}) collective-permute-start(bf16[1,40,1024]{2,1,0:T(8,128)(2,1)S(1)} %get-tuple-element.150), channel_id=1, source_target_pairs={{0,2},{1,3},{2,0},{3,1},{4,6},{5,7},{6,4},{7,5},{8,10},{9,11},{10,... | collective-permute-start | bytes 245768 | tf_op jit(solution)/shard_map/ppermute | solution.py:507

commit v5 on v4

--- a/solution.py
+++ b/solution.py
@@ -49,23 +49,49 @@
     return lax.broadcasted_iota(jnp.int32, shape, dim)
 
 
-def attend_pair(q, k, v, bias):
+def attend_part(q, k, v, bias):
     first = iota((1, 2 * HEAD), 1) < HEAD
     q = q * jnp.asarray(1.0 / math.sqrt(HEAD), q.dtype)
-    outs = []
+    parts = []
     for here in (first, jnp.logical_not(first)):
         scores = mm_t(jnp.where(here, q, jnp.zeros_like(q)), k) + bias
-        raised = jnp.exp(scores - jnp.max(scores, axis=-1, keepdims=True)).astype(jnp.bfloat16)
-        both = mm(raised, jnp.where(here, v, jnp.ones_like(v)))
-        outs.append(both / pltpu.roll(both, HEAD, 1))
+        highest = jnp.max(scores, axis=-1, keepdims=True)
+        raised = jnp.exp(scores - highest).astype(jnp.bfloat16)
+        parts.append((highest, mm(raised, jnp.where(here, v, jnp.ones_like(v)))))
+    return parts
+
+
+def divided(sums):
+    first = iota((1, 2 * HEAD), 1) < HEAD
+    outs = [both / pltpu.roll(both, HEAD, 1) for both in sums]
     return jnp.where(first, outs[0], outs[1])
+
+
+def attend_pair(q, k, v, bias):
+    return divided([both for _, both in attend_part(q, k, v, bias)])
+
+
+def attend_stacked(q, k, v, bias):
+    rows, width = q.shape
+    lane = iota((1, width), 1)
+    heads = [(lane >= at) & (lane < at + HEAD) for at in range(0, width, HEAD)]
+    scaled = q.astype(jnp.float32) * (1.0 / math.sqrt(HEAD))
+    stack = jnp.concatenate([jnp.where(here, scaled, 0.0) for here in heads], axis=0)
+    scores = mm_t(stack.astype(jnp.bfloat16), k) + jnp.concatenate([bias] * len(heads), axis=0)
+    raised = jnp.exp(scores - jnp.max(scores, axis=-1, keepdims=True))
+    mixed = mm(raised.astype(jnp.bfloat16), v) / jnp.sum(raised, axis=-1, keepdims=True)
+    out = jnp.zeros((rows, width), jnp.float32)
+    for number, here in enumerate(heads):
+        out = jnp.where(here, mixed[number * rows : (number + 1) * rows], out)
+    return out
 
 
 def opening_kernel(reach, capacity, *refs):
     place, own_in, flags_in, ids_in, gain_in, w_qkv_in, w_out_in, w_xq_in, w_xkv_in = refs[:9]
     outs, (flags, ids, w_qkv, sem) = refs[9:-4], refs[-4:]
-    own, gain, w_kv, w_out, w_xq, w_xkv, projected_out = outs[:7]
-    bias_out, since_out, ends_out, member_out, live_out, table_out, decode_out = outs[7:]
+    own, gain, w_kv, w_out, w_xq, w_xkv, queries_out = outs[:7]
+    bias_out, since_out, ends_out, member_out, live_out, table_out = outs[7:13]
+    highest_out, sums_out, decode_out = outs[13:]
     pairs = [
         (own_in, own),
         (gain_in, gain),
@@ -81,17 +107,30 @@
         copy.start()
     rows, width = own.shape
     patch_cap = rows * 5 // 32
-    keys = (reach + 1) * rows
-    at_query = iota((rows, keys), 0) + reach * rows
+    keys = reach * rows
+    at_query = iota((rows, keys), 0) + keys
     at_key = iota((rows, keys), 1)
-    allowed = (at_key <= at_query) & (at_key > at_query - WINDOW)
-    allowed = allowed & (at_key >= (reach - place[0]) * rows)
+    allowed = (at_key > at_query - WINDOW) & (at_key >= (reach - place[0]) * rows)
     bias_out[...] = jnp.where(allowed, 0.0, very_negative)
     for copy in copies[:3]:
         copy.wait()
     normed = normed_rows(own[...], gain[...])
-    projected_out[...] = mm(normed, w_qkv[...]).astype(jnp.bfloat16)
+    projected = mm(normed, w_qkv[...]).astype(jnp.bfloat16)
+    queries_out[...] = projected[:, :width]
     w_kv[...] = w_qkv[:, width:]
+    back = iota((rows, rows), 0) - iota((rows, rows), 1)
+    own_bias = jnp.where((back >= 0) & (back < WINDOW), 0.0, very_negative)
+    lanes = 2 * HEAD
+    for at in range(0, width, lanes):
+        parts = attend_part(
+            projected[:, at : at + lanes],
+            projected[:, width + at : width + at + lanes],
+            projected[:, 2 * width + at : 2 * width + at + lanes],
+            own_bias,
+        )
+        for head, (highest, both) in enumerate(parts, at // HEAD):
+            highest_out[head] = jnp.broadcast_to(highest, both.shape)
+            sums_out[head] = both
     copies[3].wait()
     flag = flags[...]
     at_row, at_col = iota((rows, rows), 0), iota((rows, rows), 1)
@@ -134,7 +173,8 @@
     w_qkv, w_out, w_xq, w_xkv = ws
     patch_cap = expert_ids.shape[0]
     extra = -(-(patch_cap + 2) // 16) * 16 - patch_cap
-    keys = (reach + 1) * rows
+    keys = reach * rows
+    heads = width // HEAD
     vmem, anywhere = pl.BlockSpec(memory_space=pltpu.VMEM), pl.BlockSpec(memory_space=pltpu.HBM)
     like = jax.ShapeDtypeStruct
     bf16, f32 = jnp.bfloat16, jnp.float32
@@ -147,17 +187,19 @@
             like(w_out.shape, bf16),
             like(w_xq.shape, bf16),
             like(w_xkv.shape, bf16),
-            like((rows, 3 * width), bf16),
+            like((rows, width), bf16),
             like((rows, keys), f32),
             like((rows, 1), jnp.int32),
             like((patch_cap, rows), bf16),
             like((patch_cap, rows), f32),
             like((patch_cap, 1), f32),
             like((extra, width), bf16),
+            like((heads, rows, 2 * HEAD), f32),
+            like((heads, rows, 2 * HEAD), f32),
             like((rows, patch_cap), f32),
         ),
         in_specs=[pl.BlockSpec(memory_space=pltpu.SMEM)] + [anywhere] * 8,
-        out_specs=(vmem,) * 14,
+        out_specs=(vmem,) * 16,
         scratch_shapes=[
             pltpu.VMEM((1, rows), jnp.int32),
             pltpu.VMEM((2, patch_cap), jnp.int32),
@@ -182,28 +224,29 @@
 
 
 def encoder_kernel(reach, *refs):
-    instead, earlier, nearest, refs = refs[0], refs[1 : 1 + reach], refs[1 + reach], refs[2 + reach :]
-    own, gain, w_kv, w_out, w_xq, w_xkv, projected = refs[:7]
-    bias, since, ends, member_bias, live, table = refs[7:13]
-    encoded_out, payload_out, pairs_ref, mixed_ref = refs[13:]
+    earlier, refs = refs[:reach], refs[reach:]
+    own, gain, w_kv, w_out, w_xq, w_xkv, queries = refs[:7]
+    bias, since, ends, member_bias, live, table, own_highest, own_sums = refs[7:15]
+    encoded_out, payload_out, pairs_ref, mixed_ref = refs[15:]
     rows, width = own.shape
     patch_cap = ends.shape[0]
-    pairs_ref[reach * rows :, :] = projected[:, width:]
     for at, block in enumerate(earlier):
-        moved = block[...]
-        if at == reach - 1:
-            moved = jnp.where(instead[0] == 1, nearest[...], moved)
-        moved = normed_rows(moved, gain[...])
+        moved = normed_rows(block[...], gain[...])
         pairs_ref[at * rows : (at + 1) * rows, :] = mm(moved, w_kv[...]).astype(jnp.bfloat16)
     lanes = 2 * HEAD
     for at in range(0, width, lanes):
-        mixed = attend_pair(
-            projected[:, at : at + lanes],
+        parts = attend_part(
+            queries[:, at : at + lanes],
             pairs_ref[:, at : at + lanes],
             pairs_ref[:, width + at : width + at + lanes],
             bias[...],
         )
-        mixed_ref[:, at : at + lanes] = mixed.astype(jnp.bfloat16)
+        sums = []
+        for head, (highest, both) in enumerate(parts, at // HEAD):
+            before = own_highest[head]
+            top = jnp.maximum(highest, before)
+            sums.append(both * jnp.exp(highest - top) + own_sums[head] * jnp.exp(before - top))
+        mixed_ref[:, at : at + lanes] = divided(sums).astype(jnp.bfloat16)
     encoded = (own[...].astype(jnp.float32) + mm(mixed_ref[...], w_out[...])).astype(jnp.bfloat16)
     encoded_out[...] = encoded
 
@@ -218,20 +261,15 @@
     pooled = mm(ends[...], highest.astype(jnp.bfloat16))
     patch_queries = mm(pooled.astype(jnp.bfloat16), w_xq[...]).astype(jnp.bfloat16)
     byte_pairs = mm(encoded, w_xkv[...]).astype(jnp.bfloat16)
-    alive = live[...] > 0.0
-    for at in range(0, width, lanes):
-        mixed = attend_pair(
-            patch_queries[:, at : at + lanes],
-            byte_pairs[:, at : at + lanes],
-            byte_pairs[:, width + at : width + at + lanes],
-            member_bias[...],
-        )
-        total = jnp.where(alive, pooled[:, at : at + lanes] + mixed, 0.0)
-        payload_out[:patch_cap, at : at + lanes] = total.astype(jnp.bfloat16)
+    mixed = attend_stacked(
+        patch_queries, byte_pairs[:, :width], byte_pairs[:, width:], member_bias[...]
+    )
+    total = jnp.where(live[...] > 0.0, pooled + mixed, 0.0)
+    payload_out[:patch_cap, :] = total.astype(jnp.bfloat16)
     payload_out[patch_cap:, :] = table[...]
 
 
-def encode(instead, earlier, nearest, opened):
+def encode(earlier, opened):
     rows, width = opened[0].shape
     reach = len(earlier)
     vmem = pl.BlockSpec(memory_space=pltpu.VMEM)
@@ -242,15 +280,15 @@
             jax.ShapeDtypeStruct((rows, width), jnp.bfloat16),
             jax.ShapeDtypeStruct((payload_rows, width), jnp.bfloat16),
         ),
-        in_specs=[pl.BlockSpec(memory_space=pltpu.SMEM)] + [vmem] * (14 + reach),
+        in_specs=[vmem] * (15 + reach),
         out_specs=(vmem, vmem),
         scratch_shapes=[
-            pltpu.VMEM(((reach + 1) * rows, 2 * width), jnp.bfloat16),
+            pltpu.VMEM((reach * rows, 2 * width), jnp.bfloat16),
             pltpu.VMEM((rows, width), jnp.bfloat16),
         ],
         cost_estimate=cost(24 * rows * width * (reach + 1) * rows),
         compiler_params=pltpu.CompilerParams(vmem_limit_bytes=16 * 1024 * 1024),
-    )(instead, *earlier, nearest, *opened[:13])
+    )(*earlier, *opened[:15])
 
 
 def mm_first(a, b):
@@ -526,19 +564,6 @@
     for part in parts[1:]:
         total = total + part.astype(jnp.float32)
     return total
-
-
-def earlier_blocks(x, reach, opened):
-    both_axes = ("seq", "expert")
-    experts = lax.axis_size("expert")
-    if reach != 2 or experts % 2:
-        earlier = [passed_along(x, both_axes, by) for by in range(reach, 0, -1)]
-        return jnp.zeros((1,), jnp.int32), earlier, x
-    own = lax.ppermute(x, "expert", [(i, i + 1) for i in range(0, experts, 2)])
-    far = lax.optimization_barrier((passed_along(x, both_axes, 2), opened))[0]
-    near = lax.ppermute(far, "expert", [(i + 1, i) for i in range(0, experts, 2)])
-    odd = lax.axis_index("expert").astype(jnp.int32).reshape(1) & 1
-    return odd, [far, near], own
 
 
 def leg(x, digit, place):
@@ -686,11 +711,11 @@
         w_xq,
         w_xkv,
     )
-    instead, earlier, nearest = earlier_blocks(byte_states, reach, opened)
-    encoded, payload = encode(instead, earlier, nearest, opened)
+    earlier = [passed_along(byte_states, both_axes, by) for by in range(reach, 0, -1)]
+    encoded, payload = encode(earlier, opened)
     wholes, halves = mixture(payload, patch_cap, capacity, w_up, moe_gain, w_router, w_in, w_down)
     queries, state = prepare(encoded, payload, patch_cap, dec_gain, w_dq, w_up)
-    return decode(state, wholes, halves, encoded, queries, opened[13], w_dkv, w_do)
+    return decode(state, wholes, halves, encoded, queries, opened[15], w_dkv, w_do)
 
 
 def solution(mesh):

time: 101 us -> 99 us (0.980)
  starting transfers between devices: 39.7 us -> 38.3 us
    ppermute x2 -> x0, starting transfers between devices: 2.75 us -> none  [the longest x1 1.47 us: earlier_blocks(): own = lax.ppermute(x, 'expert', [(i, i + 1) for i in range(0, experts, 2)])]
    ppermute x2 -> x0, waiting for transfers between devices: 2.1 us -> none  [the longest x1 2.1 us: earlier_blocks(): lax.ppermute(far, 'expert', [(i + 1, i) for i in range(0, experts, 2)])]
    ppermute x29, waiting for transfers between devices: 22.8 us -> 24.6 us  [shift(): return lax.ppermute(x, axis, pairs)]
    pallas_call x1, Pallas kernels: 7.11 us -> 5.4 us  [encode(): pl.pallas_call(functools.partial(encoder_kernel, reach), out_shape=(jax.S...]
    ppermute x1 -> x2, starting transfers between devices: 4.89 us -> 6.36 us  [passed_along(): return lax.ppermute(x, axis, pairs)]
  transfers between devices with their start and end apart: 32 -> 31, of which waited for: 16 -> 14; matrix products, arithmetic and copies ran while one was open for 3% -> 3% of each run, Pallas kernels for 17% -> 18%
where the time goes in v5:
time: 99 us; the launch traced here: 98.8 us
  starting transfers between devices  38.3 us (39%)
  Pallas kernels  29.5 us (30%)
  waiting for transfers between devices  26.4 us (27%)
  local copies, waits for them, and re-layouts  1.78 us (2%)
  other arithmetic  1.58 us (2%)
  between operations  1.15 us (1%)
    ppermute x29, starting transfers between devices, shift(): return lax.ppermute(x, axis, pairs)  32 us
    ppermute x29, waiting for transfers between devices, shift(): return lax.ppermute(x, axis, pairs)  24.6 us
    pallas_call x3, Pallas kernels, stream(): pl.pallas_call(functools.partial(stream_kernel, patch_cap, capacity, expe...  13.7 us
    ppermute x2, starting transfers between devices, passed_along(): return lax.ppermute(x, axis, pairs)  6.36 us
    pallas_call x1, Pallas kernels, encode(): pl.pallas_call(functools.partial(encoder_kernel, reach), out_shape=(jax.S...  5.4 us
    pallas_call x1, Pallas kernels, opening(): pl.pallas_call(functools.partial(opening_kernel, reach, capacity), out_sh...  3.65 us
    pallas_call x1, Pallas kernels, decode(): pl.pallas_call(functools.partial(decode_kernel, len(wholes)), out_shape=(...  3.12 us
    pallas_call x3, Pallas kernels, gated_share(): pl.pallas_call(functools.partial(share_kernel, order), out_shape=share_sh...  3.02 us
  transfers between devices with their start and end apart: 31, of which 14 were waited for; matrix products, arithmetic and copies ran while one was open for 3% of the time, Pallas kernels for 18%

profile of v5, /device:TPU:0, one launch (start us, length us, event | category | flops | bytes accessed | tf_op | source)
XLA Modules:
  0.0 98.8 jit_solution(3031747934987035579)
XLA Ops:
  0.6 4.9 %collective-permute-start = (bf16[256,512]{1,0:T(8,128)(2,1)}, bf16[256,512]{1,0:T(8,128)(2,1)S(1)}, u32[]{:S(2)}, u32[]{:S(2)}) collective-permute-start(bf16[256,512]{1,0:T(8,128)(2,1)} %refs_1_.1), channel_id=1, source_target_pairs={{0,2},{1,3},{2,4},{3,5},{4,6},{5,7},{6,8},{7,9},{8,10},{9,11},{10,... | collective-permute-start | bytes 786440 | tf_op jit(solution)/shard_map/ppermute | solution.py:23
  5.5 1.5 %collective-permute-start.1 = (bf16[256,512]{1,0:T(8,128)(2,1)}, bf16[256,512]{1,0:T(8,128)(2,1)S(1)}, u32[]{:S(2)}, u32[]{:S(2)}) collective-permute-start(bf16[256,512]{1,0:T(8,128)(2,1)} %refs_1_.1), channel_id=1, source_target_pairs={{0,1},{1,2},{2,3},{3,4},{4,5},{5,6},{6,7},{7,8},{8,9},{9,10},{10,1... | collective-permute-start | bytes 786440 | tf_op jit(solution)/shard_map/ppermute | solution.py:23
  7.0 3.7 %shard_map.176 = (bf16[256,512]{1,0:T(8,128)(2,1)S(1)}, f32[1,512]{1,0:T(1,128)S(1)}, bf16[512,1024]{1,0:T(8,128)(2,1)S(1)}, bf16[512,512]{1,0:T(8,128)(2,1)S(1)...) custom-call(s32[1]{0:T(128)} %bitcast.refs_0_, ...), custom_call_target="tpu_custom_call" | custom-call | flops 805306368 | tf_op jit(solution)/shard_map/pallas_call | solution.py:181
  10.7 1.8 %collective-permute-done.refs_0_ = bf16[256,512]{1,0:T(8,128)(2,1)S(1)} collective-permute-done((bf16[256,512]{1,0:T(8,128)(2,1)}, bf16[256,512]{1,0:T(8,128)(2,1)S(1)}, u32[]{:S(2)}, u32[]{:S(2)}) %collective-permute-start) | collective-permute-done | bytes 262176 | tf_op jit(solution)/shard_map/ppermute | solution.py:23
  12.5 5.4 %shard_map.177 = (bf16[256,512]{1,0:T(8,128)(2,1)S(1)}, bf16[48,512]{1,0:T(8,128)(2,1)S(1)}) custom-call(bf16[256,512]{1,0:T(8,128)(2,1)S(1)} %collective-permute-done.refs_0_, bf16[256,512]{1,0:T(8,128)(2,1)S(1)} %collective-permute-done.1.refs_1_, bf16[256,512]{1,0:T(8,128)(2,1)S(1)} %get-tuple-element.66.refs_2_, f32[1,512]{1,0:T(1,128)S(1)} %get-tuple-element.67.refs_3_, ...), custom_call_target="tpu_custom_call" | custom-call | flops 2415919104 | tf_op jit(solution)/shard_map/pallas_call | solution.py:277
  17.9 5.9 %collective-permute-start.2 = (bf16[48,512]{1,0:T(8,128)(2,1)S(1)}, bf16[48,512]{1,0:T(8,128)(2,1)S(1)}, u32[]{:S(2)}, u32[]{:S(2)}) collective-permute-start(bf16[48,512]{1,0:T(8,128)(2,1)S(1)} %get-tuple-element.82.payload), channel_id=1, source_target_pairs={{0,8},{4,12},{8,16},{12,20},{16,24},{20,28},{24,0},{28,4},{1,9},{5... | collective-permute-start | bytes 147464 | tf_op jit(solution)/shard_map/ppermute | solution.py:545
  23.9 2.6 %collective-permute-start.3 = (bf16[48,512]{1,0:T(8,128)(2,1)S(1)}, bf16[48,512]{1,0:T(8,128)(2,1)S(1)}, u32[]{:S(2)}, u32[]{:S(2)}) collective-permute-start(bf16[48,512]{1,0:T(8,128)(2,1)S(1)} %get-tuple-element.82.payload), channel_id=1, source_target_pairs={{0,16},{4,20},{8,24},{12,28},{16,0},{20,4},{24,8},{28,12},{1,17},{... | collective-permute-start | bytes 147464 | tf_op jit(solution)/shard_map/ppermute | solution.py:545
  26.5 1.4 %collective-permute-start.4 = (bf16[48,512]{1,0:T(8,128)(2,1)S(1)}, bf16[48,512]{1,0:T(8,128)(2,1)S(1)}, u32[]{:S(2)}, u32[]{:S(2)}) collective-permute-start(bf16[48,512]{1,0:T(8,128)(2,1)S(1)} %get-tuple-element.82.payload), channel_id=1, source_target_pairs={{0,24},{4,28},{8,0},{12,4},{16,8},{20,12},{24,16},{28,20},{1,25},{... | collective-permute-start | bytes 147464 | tf_op jit(solution)/shard_map/ppermute | solution.py:545
  27.8 1.4 %copy.25 = bf16[256,8,2,768]{3,1,2,0:T(8,128)(2,1)S(1)} copy(bf16[256,8,2,768]{3,2,1,0:T(2,128)(2,1)S(1)} %bitcast.162) | data formatting | bytes 12582912
  29.2 1.3 %collective-permute-done.4 = bf16[48,512]{1,0:T(8,128)(2,1)S(1)} collective-permute-done((bf16[48,512]{1,0:T(8,128)(2,1)S(1)}, bf16[48,512]{1,0:T(8,128)(2,1)S(1)}, u32[]{:S(2)}, u32[]{:S(2)}) %collective-permute-start.4) | collective-permute-done | bytes 49184 | tf_op jit(solution)/shard_map/ppermute | solution.py:545
  30.6 0.7 collective-permute-start.5
  31.3 0.6 collective-permute-start.7
  31.9 3.8 %collective-permute-done.5 = bf16[4,48,256]{2,1,0:T(8,128)(2,1)S(1)} collective-permute-done((bf16[4,48,256]{2,1,0:T(8,128)(2,1)S(1)}, bf16[4,48,256]{2,1,0:T(8,128)(2,1)S(1)}, u32[]{:S(2)}, u32[]{:S(2)}) %collective-permute-start.5) | collective-permute-done | bytes 98336 | tf_op jit(solution)/shard_map/ppermute | solution.py:545
  35.7 0.1 collective-permute-start.6
  35.8 0.7 collective-permute-done.7
  36.5 1.1 %collective-permute-start.8 = (bf16[4,2,48,256]{3,2,0,1:T(8,128)(2,1)S(1)}, bf16[4,2,48,256]{3,2,0,1:T(8,128)(2,1)S(1)}, u32[]{:S(2)}, u32[]{:S(2)}) collective-permute-start(bf16[4,2,48,256]{3,2,0,1:T(8,128)(2,1)S(1)} %get-tuple-element.149), channel_id=1, source_target_pairs={{0,4},{4,0},{8,12},{12,8},{16,20},{20,16},{24,28},{28,24},{1,5},{5... | collective-permute-start | bytes 589832 | tf_op jit(solution)/shard_map/ppermute | solution.py:545
  37.6 3.8 %collective-permute-done.6 = bf16[4,2,48,256]{3,2,0,1:T(8,128)(2,1)S(1)} collective-permute-done((bf16[4,2,48,256]{3,2,0,1:T(8,128)(2,1)S(1)}, bf16[4,2,48,256]{3,2,0,1:T(8,128)(2,1)S(1)}, u32[]{:S(2)}, u32[]{:S(2)}) %collective-permute-start.6) | collective-permute-done | bytes 196640 | tf_op jit(solution)/shard_map/ppermute | solution.py:545
  41.5 0.8 collective-permute-done.8
  42.3 0.1 maximum_maximum_fusion
  42.4 0.1 collective-permute-start.9
  42.5 2.3 %collective-permute-done.9.refs_2_ = bf16[16,48,512]{2,1,0:T(8,128)(2,1)S(1)} collective-permute-done((bf16[16,48,512]{2,1,0:T(8,128)(2,1)S(1)}, bf16[16,48,512]{2,1,0:T(8,128)(2,1)S(1)}, u32[]{:S(2)}, u32[]{:S(2)}) %collective-permute-start.9) | collective-permute-done | bytes 786464 | tf_op jit(solution)/shard_map/ppermute | solution.py:545
  44.8 3.6 %shard_map.179 = (bf16[4,40,1024]{2,1,0:T(8,128)(2,1)S(1)}, bf16[4,40,1024]{2,1,0:T(8,128)(2,1)S(1)}, bf16[96,768]{1,0:T(8,128)(2,1)S(1)}, f32[96,1]{1,0:T(8,128)S(1)}, bf16[1,96,160]{2,1,0:T(8,128)(2,1)S(1)}) custom-call(s32[1]{0:T(128)} %bitcast.5.refs_0_, bf16[16,48,512]{2,1,0:T(8,128)(2,1)S(1)} %bitcast.137, ...), custom_call_target="tpu_custom_call" | custom-call | flops 201326592 | tf_op jit(solution)/shard_map/pallas_call | solution.py:423
  48.4 0.2 collective-permute-start.10
  48.6 0.4 collective-permute-start.11
  49.0 0.8 shard_map.180
  49.8 0.3 collective-permute-done.10
  50.1 0.1 fusion.5
  50.2 1.1 %collective-permute-start.12 = (bf16[2,1,40,1024]{3,2,1,0:T(8,128)(2,1)S(1)}, bf16[2,1,40,1024]{3,2,1,0:T(8,128)(2,1)S(1)}, u32[]{:S(2)}, u32[]{:S(2)}) collective-permute-start(bf16[2,1,40,1024]{3,2,1,0:T(8,128)(2,1)S(1)} %get-tuple-element.139), channel_id=1, source_target_pairs={{0,4},{4,0},{8,12},{12,8},{16,20},{20,16},{24,28},{28,24},{1,5},{5... | collective-permute-start | bytes 491528 | tf_op jit(solution)/shard_map/ppermute | solution.py:545
  51.3 0.1 fusion.4
  51.5 1.3 %collective-permute-start.13 = (bf16[2,1,40,1024]{3,2,1,0:T(8,128)(2,1)S(1)}, bf16[2,1,40,1024]{3,2,1,0:T(8,128)(2,1)S(1)}, u32[]{:S(2)}, u32[]{:S(2)}) collective-permute-start(bf16[2,1,40,1024]{3,2,1,0:T(8,128)(2,1)S(1)} %get-tuple-element.141), channel_id=1, source_target_pairs={{0,2},{1,3},{2,0},{3,1},{4,6},{5,7},{6,4},{7,5},{8,10},{9,11},{10,... | collective-permute-start | bytes 491528 | tf_op jit(solution)/shard_map/ppermute | solution.py:545
  52.8 6.5 %shard_map.181 = (bf16[8,40,1024]{2,1,0:T(8,128)(2,1)S(1)}, bf16[8,40,1024]{2,1,0:T(8,128)(2,1)S(1)}, bf16[192,768]{1,0:T(8,128)(2,1)S(1)}, f32[192,1]{1,0:T(8,128)S(1)}, bf16[2,96,160]{2,1,0:T(8,128)(2,1)S(1)}) custom-call(s32[1]{0:T(128)} %bitcast.5.refs_0_, bf16[16,48,512]{2,1,0:T(8,128)(2,1)S(1)} %bitcast.138, ...), custom_call_target="tpu_custom_call" | custom-call | flops 402653184 | tf_op jit(solution)/shard_map/pallas_call | solution.py:423
  59.4 0.5 collective-permute-start.14
  59.9 0.1 fusion.10
  60.0 0.8 collective-permute-start.16
  60.9 1.1 %collective-permute-start.17 = (bf16[1,40,1024]{2,1,0:T(8,128)(2,1)S(1)}, bf16[1,40,1024]{2,1,0:T(8,128)(2,1)S(1)}, u32[]{:S(2)}, u32[]{:S(2)}) collective-permute-start(bf16[1,40,1024]{2,1,0:T(8,128)(2,1)S(1)} %get-tuple-element.161), channel_id=1, source_target_pairs={{0,4},{4,0},{8,12},{12,8},{16,20},{20,16},{24,28},{28,24},{1,5},{5... | collective-permute-start | bytes 245768 | tf_op jit(solution)/shard_map/ppermute | solution.py:545
  61.9 1.4 %shard_map.182 = (bf16[8,40,1024]{2,1,0:T(8,128)(2,1)S(1)}, bf16[8,40,1024]{2,1,0:T(8,128)(2,1)S(1)}) custom-call(bf16[192,768]{1,0:T(8,128)(2,1)S(1)} %get-tuple-element.97.hidden, f32[192,1]{1,0:T(8,128)S(1)} %get-tuple-element.100.gate, bf16[2,96,160]{2,1,0:T(8,128)(2,1)S(1)} %get-tuple-element.101.spread, bf16[768,2048]{1,0:T(8,128)(2,1)S(1)} %bitcast.130), custom_call_target="tpu_custom_call" | custom-call | flops 1000 | tf_op jit(solution)/shard_map/pallas_call | solution.py:448
  63.3 0.2 fusion.1
  63.6 0.2 fusion
  63.9 3.6 %shard_map.183 = (bf16[4,40,1024]{2,1,0:T(8,128)(2,1)S(1)}, bf16[4,40,1024]{2,1,0:T(8,128)(2,1)S(1)}, bf16[96,768]{1,0:T(8,128)(2,1)S(1)}, f32[96,1]{1,0:T(8,128)S(1)}, bf16[1,96,160]{2,1,0:T(8,128)(2,1)S(1)}) custom-call(s32[1]{0:T(128)} %bitcast.5.refs_0_, bf16[16,48,512]{2,1,0:T(8,128)(2,1)S(1)} %bitcast.139, ...), custom_call_target="tpu_custom_call" | custom-call | flops 201326592 | tf_op jit(solution)/shard_map/pallas_call | solution.py:423
  67.5 1.1 %collective-permute-start.19 = (bf16[2,2,40,1024]{3,2,1,0:T(8,128)(2,1)S(1)}, bf16[2,2,40,1024]{3,2,1,0:T(8,128)(2,1)S(1)}, u32[]{:S(2)}, u32[]{:S(2)}) collective-permute-start(bf16[2,2,40,1024]{3,2,1,0:T(8,128)(2,1)S(1)} %get-tuple-element.131), channel_id=1, source_target_pairs={{0,4},{4,0},{8,12},{12,8},{16,20},{20,16},{24,28},{28,24},{1,5},{5... | collective-permute-start | bytes 983048 | tf_op jit(solution)/shard_map/ppermute | solution.py:545
  68.6 1.2 %collective-permute-start.21 = (bf16[2,2,40,1024]{3,2,1,0:T(8,128)(2,1)S(1)}, bf16[2,2,40,1024]{3,2,1,0:T(8,128)(2,1)S(1)}, u32[]{:S(2)}, u32[]{:S(2)}) collective-permute-start(bf16[2,2,40,1024]{3,2,1,0:T(8,128)(2,1)S(1)} %get-tuple-element.133), channel_id=1, source_target_pairs={{0,2},{1,3},{2,0},{3,1},{4,6},{5,7},{6,4},{7,5},{8,10},{9,11},{10,... | collective-permute-start | bytes 983048 | tf_op jit(solution)/shard_map/ppermute | solution.py:545
  69.9 0.7 collective-permute-start.18
  70.6 0.5 collective-permute-start.25
  71.1 5.6 %collective-permute-done.19 = bf16[2,2,40,1024]{3,2,1,0:T(8,128)(2,1)S(1)} collective-permute-done((bf16[2,2,40,1024]{3,2,1,0:T(8,128)(2,1)S(1)}, bf16[2,2,40,1024]{3,2,1,0:T(8,128)(2,1)S(1)}, u32[]{:S(2)}, u32[]{:S(2)}) %collective-permute-start.19) | collective-permute-done | bytes 327712 | tf_op jit(solution)/shard_map/ppermute | solution.py:545
  76.7 0.7 collective-permute-done.21
  77.5 0.1 add_convert_fusion.1
  77.6 0.1 add_convert_fusion
  77.7 1.3 %collective-permute-start.20 = (bf16[2,40,1024]{2,1,0:T(8,128)(2,1)S(1)}, bf16[2,40,1024]{2,1,0:T(8,128)(2,1)S(1)}, u32[]{:S(2)}, u32[]{:S(2)}) collective-permute-start(bf16[2,40,1024]{2,1,0:T(8,128)(2,1)S(1)} %slice_bitcast_fusion.10), channel_id=1, source_target_pairs={{0,2},{1,3},{2,0},{3,1},{4,6},{5,7},{6,4},{7,5},{8,10},{9,11},{10,... | collective-permute-start | bytes 491528 | tf_op jit(solution)/shard_map/ppermute | solution.py:545
  79.0 1.1 %collective-permute-start.22 = (bf16[2,40,1024]{2,1,0:T(8,128)(2,1)S(1)}, bf16[2,40,1024]{2,1,0:T(8,128)(2,1)S(1)}, u32[]{:S(2)}, u32[]{:S(2)}) collective-permute-start(bf16[2,40,1024]{2,1,0:T(8,128)(2,1)S(1)} %slice_bitcast_fusion.8), channel_id=1, source_target_pairs={{0,4},{4,0},{8,12},{12,8},{16,20},{20,16},{24,28},{28,24},{1,5},{5... | collective-permute-start | bytes 491528 | tf_op jit(solution)/shard_map/ppermute | solution.py:545
  80.2 0.8 shard_map.184
  81.0 0.1 fusion.2
  81.1 0.8 collective-permute-start.29
  81.9 0.1 fusion.3
  82.0 1.1 %collective-permute-start.26 = (bf16[2,1,40,1024]{3,2,1,0:T(8,128)(2,1)S(1)}, bf16[2,1,40,1024]{3,2,1,0:T(8,128)(2,1)S(1)}, u32[]{:S(2)}, u32[]{:S(2)}) collective-permute-start(bf16[2,1,40,1024]{3,2,1,0:T(8,128)(2,1)S(1)} %get-tuple-element.137), channel_id=1, source_target_pairs={{0,4},{4,0},{8,12},{12,8},{16,20},{20,16},{24,28},{28,24},{1,5},{5... | collective-permute-start | bytes 491528 | tf_op jit(solution)/shard_map/ppermute | solution.py:545
  83.1 1.4 %collective-permute-done.20 = bf16[2,40,1024]{2,1,0:T(8,128)(2,1)S(1)} collective-permute-done((bf16[2,40,1024]{2,1,0:T(8,128)(2,1)S(1)}, bf16[2,40,1024]{2,1,0:T(8,128)(2,1)S(1)}, u32[]{:S(2)}, u32[]{:S(2)}) %collective-permute-start.20) | collective-permute-done | bytes 163872 | tf_op jit(solution)/shard_map/ppermute | solution.py:545
  84.7 1.0 %collective-permute-done.22 = bf16[2,40,1024]{2,1,0:T(8,128)(2,1)S(1)} collective-permute-done((bf16[2,40,1024]{2,1,0:T(8,128)(2,1)S(1)}, bf16[2,40,1024]{2,1,0:T(8,128)(2,1)S(1)}, u32[]{:S(2)}, u32[]{:S(2)}) %collective-permute-start.22) | collective-permute-done | bytes 163872 | tf_op jit(solution)/shard_map/ppermute | solution.py:545
  85.8 0.6 collective-permute-start.24
  86.4 3.3 %collective-permute-start.23 = (bf16[40,2048]{1,0:T(8,128)(2,1)S(1)}, bf16[40,2048]{1,0:T(8,128)(2,1)S(1)}, u32[]{:S(2)}, u32[]{:S(2)}) collective-permute-start(bf16[40,2048]{1,0:T(8,128)(2,1)S(1)} %pad_maximum_fusion.4), channel_id=1, source_target_pairs={{0,24},{4,28},{8,0},{12,4},{16,8},{20,12},{24,16},{28,20},{1,25},{... | collective-permute-start | bytes 491528 | tf_op jit(solution)/shard_map/ppermute | solution.py:545
  89.8 1.3 %collective-permute-start.30 = (bf16[1,40,1024]{2,1,0:T(8,128)(2,1)S(1)}, bf16[1,40,1024]{2,1,0:T(8,128)(2,1)S(1)}, u32[]{:S(2)}, u32[]{:S(2)}) collective-permute-start(bf16[1,40,1024]{2,1,0:T(8,128)(2,1)S(1)} %get-tuple-element.150), channel_id=1, source_target_pairs={{0,4},{4,0},{8,12},{12,8},{16,20},{20,16},{24,28},{28,24},{1,5},{5... | collective-permute-start | bytes 245768 | tf_op jit(solution)/shard_map/ppermute | solution.py:545
  91.2 1.1 %collective-permute-start.27 = (bf16[1,40,1024]{2,1,0:T(8,128)(2,1)S(1)}, bf16[1,40,1024]{2,1,0:T(8,128)(2,1)S(1)}, u32[]{:S(2)}, u32[]{:S(2)}) collective-permute-start(bf16[1,40,1024]{2,1,0:T(8,128)(2,1)S(1)} %get-tuple-element.152), channel_id=1, source_target_pairs={{0,2},{1,3},{2,0},{3,1},{4,6},{5,7},{6,4},{7,5},{8,10},{9,11},{10,... | collective-permute-start | bytes 245768 | tf_op jit(solution)/shard_map/ppermute | solution.py:545
  92.2 0.7 shard_map.178
  92.9 1.4 %collective-permute-done.30.refs_7_ = bf16[1,40,1024]{2,1,0:T(8,128)(2,1)S(1)} collective-permute-done((bf16[1,40,1024]{2,1,0:T(8,128)(2,1)S(1)}, bf16[1,40,1024]{2,1,0:T(8,128)(2,1)S(1)}, u32[]{:S(2)}, u32[]{:S(2)}) %collective-permute-start.30) | collective-permute-done | bytes 81952 | tf_op jit(solution)/shard_map/ppermute | solution.py:545
  94.3 1.4 %collective-permute-done.27.refs_5_ = bf16[1,40,1024]{2,1,0:T(8,128)(2,1)S(1)} collective-permute-done((bf16[1,40,1024]{2,1,0:T(8,128)(2,1)S(1)}, bf16[1,40,1024]{2,1,0:T(8,128)(2,1)S(1)}, u32[]{:S(2)}, u32[]{:S(2)}) %collective-permute-start.27) | collective-permute-done | bytes 81952 | tf_op jit(solution)/shard_map/ppermute | solution.py:545
  95.7 3.1 %shard_map.185 = (bf16[256,512]{1,0:T(8,128)(2,1)}, bf16[40,2048]{1,0:T(8,128)(2,1)}) custom-call(bf16[40,2048]{1,0:T(8,128)(2,1)S(1)} %get-tuple-element.83.refs_0_, bf16[40,2048]{1,0:T(8,128)(2,1)S(1)} %collective-permute-done.18.refs_1_, bf16[40,2048]{1,0:T(8,128)(2,1)S(1)} %collective-permute-done.23.refs_2_, ...), custom_call_target="tpu_custom_call" | custom-call | flops 2147483648 | tf_op jit(solution)/shard_map/pallas_call | solution.py:513
  (68 shorter events, 0.9 us)
Async XLA Ops:
  0.6 11.9 %collective-permute-start = (bf16[256,512]{1,0:T(8,128)(2,1)}, bf16[256,512]{1,0:T(8,128)(2,1)S(1)}, u32[]{:S(2)}, u32[]{:S(2)}) collective-permute-start(bf16[256,512]{1,0:T(8,128)(2,1)} %refs_1_.1), channel_id=1, source_target_pairs={{0,2},{1,3},{2,4},{3,5},{4,6},{5,7},{6,8},{7,9},{8,10},{9,11},{10,... | collective-permute-start | bytes 786440 | tf_op jit(solution)/shard_map/ppermute | solution.py:23
  5.5 7.0 %collective-permute-start.1 = (bf16[256,512]{1,0:T(8,128)(2,1)}, bf16[256,512]{1,0:T(8,128)(2,1)S(1)}, u32[]{:S(2)}, u32[]{:S(2)}) collective-permute-start(bf16[256,512]{1,0:T(8,128)(2,1)} %refs_1_.1), channel_id=1, source_target_pairs={{0,1},{1,2},{2,3},{3,4},{4,5},{5,6},{6,7},{7,8},{8,9},{9,10},{10,1... | collective-permute-start | bytes 786440 | tf_op jit(solution)/shard_map/ppermute | solution.py:23
  7.0 20.8 %slice-start = ((s8[6291456]{0:T(1024)(128)(4,1)}), s8[4194304]{0:T(1024)(128)(4,1)S(1)}, s32[]{:S(2)}) async-start(s8[6291456]{0:T(1024)(128)(4,1)} %bitcast.160), calls=%async_computation | async-start | bytes 8388608
  12.5 15.3 %slice-start.1 = ((s8[6291456]{0:T(1024)(128)(4,1)}), s8[2097152]{0:T(1024)(128)(4,1)S(1)}, s32[]{:S(2)}) async-start(s8[6291456]{0:T(1024)(128)(4,1)} %bitcast.160), calls=%async_computation.1 | async-start | bytes 4194304
  17.9 11.2 %collective-permute-start.2 = (bf16[48,512]{1,0:T(8,128)(2,1)S(1)}, bf16[48,512]{1,0:T(8,128)(2,1)S(1)}, u32[]{:S(2)}, u32[]{:S(2)}) collective-permute-start(bf16[48,512]{1,0:T(8,128)(2,1)S(1)} %get-tuple-element.82.payload), channel_id=1, source_target_pairs={{0,8},{4,12},{8,16},{12,20},{16,24},{20,28},{24,0},{28,4},{1,9},{5... | collective-permute-start | bytes 147464 | tf_op jit(solution)/shard_map/ppermute | solution.py:545
  23.9 5.3 %collective-permute-start.3 = (bf16[48,512]{1,0:T(8,128)(2,1)S(1)}, bf16[48,512]{1,0:T(8,128)(2,1)S(1)}, u32[]{:S(2)}, u32[]{:S(2)}) collective-permute-start(bf16[48,512]{1,0:T(8,128)(2,1)S(1)} %get-tuple-element.82.payload), channel_id=1, source_target_pairs={{0,16},{4,20},{8,24},{12,28},{16,0},{20,4},{24,8},{28,12},{1,17},{... | collective-permute-start | bytes 147464 | tf_op jit(solution)/shard_map/ppermute | solution.py:545
  26.5 4.1 %collective-permute-start.4 = (bf16[48,512]{1,0:T(8,128)(2,1)S(1)}, bf16[48,512]{1,0:T(8,128)(2,1)S(1)}, u32[]{:S(2)}, u32[]{:S(2)}) collective-permute-start(bf16[48,512]{1,0:T(8,128)(2,1)S(1)} %get-tuple-element.82.payload), channel_id=1, source_target_pairs={{0,24},{4,28},{8,0},{12,4},{16,8},{20,12},{24,16},{28,20},{1,25},{... | collective-permute-start | bytes 147464 | tf_op jit(solution)/shard_map/ppermute | solution.py:545
  30.5 14.3 %copy-start.1 = (bf16[512,2048]{1,0:T(8,128)(2,1)S(1)}, bf16[512,2048]{1,0:T(8,128)(2,1)}, u32[]{:S(2)}) copy-start(bf16[512,2048]{1,0:T(8,128)(2,1)} %refs_3_.5) | copy-start | bytes 6291460
  30.6 5.1 %collective-permute-start.5 = (bf16[4,48,256]{2,1,0:T(8,128)(2,1)S(1)}, bf16[4,48,256]{2,1,0:T(8,128)(2,1)S(1)}, u32[]{:S(2)}, u32[]{:S(2)}) collective-permute-start(bf16[4,48,256]{2,1,0:T(8,128)(2,1)S(1)} %get-tuple-element.147), channel_id=1, source_target_pairs={{0,4},{4,0},{8,12},{12,8},{16,20},{20,16},{24,28},{28,24},{1,5},{5... | collective-permute-start | bytes 294920 | tf_op jit(solution)/shard_map/ppermute | solution.py:545
  31.3 5.2 %collective-permute-start.7 = (bf16[4,48,256]{2,1,0:T(8,128)(2,1)S(1)}, bf16[4,48,256]{2,1,0:T(8,128)(2,1)S(1)}, u32[]{:S(2)}, u32[]{:S(2)}) collective-permute-start(bf16[4,48,256]{2,1,0:T(8,128)(2,1)S(1)} %get-tuple-element.146), channel_id=1, source_target_pairs={{0,2},{1,3},{2,0},{3,1},{4,6},{5,7},{6,4},{7,5},{8,10},{9,11},{10,... | collective-permute-start | bytes 294920 | tf_op jit(solution)/shard_map/ppermute | solution.py:545
  35.7 5.7 %collective-permute-start.6 = (bf16[4,2,48,256]{3,2,0,1:T(8,128)(2,1)S(1)}, bf16[4,2,48,256]{3,2,0,1:T(8,128)(2,1)S(1)}, u32[]{:S(2)}, u32[]{:S(2)}) collective-permute-start(bf16[4,2,48,256]{3,2,0,1:T(8,128)(2,1)S(1)} %get-tuple-element.143), channel_id=1, source_target_pairs={{0,2},{1,3},{2,0},{3,1},{4,6},{5,7},{6,4},{7,5},{8,10},{9,11},{10,... | collective-permute-start | bytes 589832 | tf_op jit(solution)/shard_map/ppermute | solution.py:545
  36.5 8.3 %copy-start.3 = (f32[2048,4]{0,1:T(4,128)S(1)}, f32[2048,4]{0,1:T(4,128)}, u32[]{:S(2)}) copy-start(f32[2048,4]{0,1:T(4,128)} %param.27) | copy-start | bytes 98308
  36.5 5.7 %collective-permute-start.8 = (bf16[4,2,48,256]{3,2,0,1:T(8,128)(2,1)S(1)}, bf16[4,2,48,256]{3,2,0,1:T(8,128)(2,1)S(1)}, u32[]{:S(2)}, u32[]{:S(2)}) collective-permute-start(bf16[4,2,48,256]{3,2,0,1:T(8,128)(2,1)S(1)} %get-tuple-element.149), channel_id=1, source_target_pairs={{0,4},{4,0},{8,12},{12,8},{16,20},{20,16},{24,28},{28,24},{1,5},{5... | collective-permute-start | bytes 589832 | tf_op jit(solution)/shard_map/ppermute | solution.py:545
  42.3 2.5 %copy-start = (bf16[1,768,2048]{2,1,0:T(8,128)(2,1)S(1)}, bf16[1,768,2048]{2,1,0:T(8,128)(2,1)}, u32[]{:S(2)}) copy-start(bf16[1,768,2048]{2,1,0:T(8,128)(2,1)} %param.29) | copy-start | bytes 9437188
  42.3 2.5 %copy-start.4 = (f32[2048]{0:T(1024)S(1)}, f32[2048]{0:T(1024)}, u32[]{:S(2)}) copy-start(f32[2048]{0:T(1024)} %param.26) | copy-start | bytes 24580
  42.4 2.4 %collective-permute-start.9 = (bf16[16,48,512]{2,1,0:T(8,128)(2,1)S(1)}, bf16[16,48,512]{2,1,0:T(8,128)(2,1)S(1)}, u32[]{:S(2)}, u32[]{:S(2)}) collective-permute-start(bf16[16,48,512]{2,1,0:T(8,128)(2,1)S(1)} %bitcast.136), channel_id=1, source_target_pairs={{0,1},{1,0},{2,3},{3,2},{4,5},{5,4},{6,7},{7,6},{8,9},{9,8},{10,11... | collective-permute-start | bytes 2359304 | tf_op jit(solution)/shard_map/ppermute | solution.py:545
  48.4 1.7 %collective-permute-start.10 = (bf16[2,2,1,40,1024]{4,3,1,2,0:T(8,128)(2,1)S(1)}, bf16[2,2,1,40,1024]{4,3,1,2,0:T(8,128)(2,1)S(1)}, u32[]{:S(2)}, u32[]{:S(2)}) collective-permute-start(bf16[2,2,1,40,1024]{4,3,1,2,0:T(8,128)(2,1)S(1)} %bitcast.159), channel_id=1, source_target_pairs={{0,1},{1,0},{2,3},{3,2},{4,5},{5,4},{6,7},{7,6},{8,9},{9,8},{10,11... | collective-permute-start | bytes 983048 | tf_op jit(solution)/shard_map/ppermute | solution.py:545
  48.6 2.7 %collective-permute-start.11 = (bf16[2,2,1,40,1024]{4,3,1,2,0:T(8,128)(2,1)S(1)}, bf16[2,2,1,40,1024]{4,3,1,2,0:T(8,128)(2,1)S(1)}, u32[]{:S(2)}, u32[]{:S(2)}) collective-permute-start(bf16[2,2,1,40,1024]{4,3,1,2,0:T(8,128)(2,1)S(1)} %bitcast.158), channel_id=1, source_target_pairs={{0,1},{1,0},{2,3},{3,2},{4,5},{5,4},{6,7},{7,6},{8,9},{9,8},{10,11... | collective-permute-start | bytes 983048 | tf_op jit(solution)/shard_map/ppermute | solution.py:545
  50.2 9.7 %collective-permute-start.12 = (bf16[2,1,40,1024]{3,2,1,0:T(8,128)(2,1)S(1)}, bf16[2,1,40,1024]{3,2,1,0:T(8,128)(2,1)S(1)}, u32[]{:S(2)}, u32[]{:S(2)}) collective-permute-start(bf16[2,1,40,1024]{3,2,1,0:T(8,128)(2,1)S(1)} %get-tuple-element.139), channel_id=1, source_target_pairs={{0,4},{4,0},{8,12},{12,8},{16,20},{20,16},{24,28},{28,24},{1,5},{5... | collective-permute-start | bytes 491528 | tf_op jit(solution)/shard_map/ppermute | solution.py:545
  51.5 8.4 %collective-permute-start.13 = (bf16[2,1,40,1024]{3,2,1,0:T(8,128)(2,1)S(1)}, bf16[2,1,40,1024]{3,2,1,0:T(8,128)(2,1)S(1)}, u32[]{:S(2)}, u32[]{:S(2)}) collective-permute-start(bf16[2,1,40,1024]{3,2,1,0:T(8,128)(2,1)S(1)} %get-tuple-element.141), channel_id=1, source_target_pairs={{0,2},{1,3},{2,0},{3,1},{4,6},{5,7},{6,4},{7,5},{8,10},{9,11},{10,... | collective-permute-start | bytes 491528 | tf_op jit(solution)/shard_map/ppermute | solution.py:545
  59.3 4.3 %collective-permute-start.15 = (bf16[2,2,2,40,1024]{4,3,2,1,0:T(8,128)(2,1)S(1)}, bf16[2,2,2,40,1024]{4,3,2,1,0:T(8,128)(2,1)S(1)}, u32[]{:S(2)}, u32[]{:S(2)}) collective-permute-start(bf16[2,2,2,40,1024]{4,3,2,1,0:T(8,128)(2,1)S(1)} %bitcast.154), channel_id=1, source_target_pairs={{0,1},{1,0},{2,3},{3,2},{4,5},{5,4},{6,7},{7,6},{8,9},{9,8},{10,11... | collective-permute-start | bytes 1966088 | tf_op jit(solution)/shard_map/ppermute | solution.py:545
  59.4 3.9 %collective-permute-start.14 = (bf16[2,2,2,40,1024]{4,3,2,1,0:T(8,128)(2,1)S(1)}, bf16[2,2,2,40,1024]{4,3,2,1,0:T(8,128)(2,1)S(1)}, u32[]{:S(2)}, u32[]{:S(2)}) collective-permute-start(bf16[2,2,2,40,1024]{4,3,2,1,0:T(8,128)(2,1)S(1)} %bitcast.155), channel_id=1, source_target_pairs={{0,1},{1,0},{2,3},{3,2},{4,5},{5,4},{6,7},{7,6},{8,9},{9,8},{10,11... | collective-permute-start | bytes 1966088 | tf_op jit(solution)/shard_map/ppermute | solution.py:545
  60.0 7.5 %collective-permute-start.16 = (bf16[1,40,1024]{2,1,0:T(8,128)(2,1)S(1)}, bf16[1,40,1024]{2,1,0:T(8,128)(2,1)S(1)}, u32[]{:S(2)}, u32[]{:S(2)}) collective-permute-start(bf16[1,40,1024]{2,1,0:T(8,128)(2,1)S(1)} %get-tuple-element.159), channel_id=1, source_target_pairs={{0,2},{1,3},{2,0},{3,1},{4,6},{5,7},{6,4},{7,5},{8,10},{9,11},{10,... | collective-permute-start | bytes 245768 | tf_op jit(solution)/shard_map/ppermute | solution.py:545
  60.9 6.7 %collective-permute-start.17 = (bf16[1,40,1024]{2,1,0:T(8,128)(2,1)S(1)}, bf16[1,40,1024]{2,1,0:T(8,128)(2,1)S(1)}, u32[]{:S(2)}, u32[]{:S(2)}) collective-permute-start(bf16[1,40,1024]{2,1,0:T(8,128)(2,1)S(1)} %get-tuple-element.161), channel_id=1, source_target_pairs={{0,4},{4,0},{8,12},{12,8},{16,20},{20,16},{24,28},{28,24},{1,5},{5... | collective-permute-start | bytes 245768 | tf_op jit(solution)/shard_map/ppermute | solution.py:545
  67.5 9.2 %collective-permute-start.19 = (bf16[2,2,40,1024]{3,2,1,0:T(8,128)(2,1)S(1)}, bf16[2,2,40,1024]{3,2,1,0:T(8,128)(2,1)S(1)}, u32[]{:S(2)}, u32[]{:S(2)}) collective-permute-start(bf16[2,2,40,1024]{3,2,1,0:T(8,128)(2,1)S(1)} %get-tuple-element.131), channel_id=1, source_target_pairs={{0,4},{4,0},{8,12},{12,8},{16,20},{20,16},{24,28},{28,24},{1,5},{5... | collective-permute-start | bytes 983048 | tf_op jit(solution)/shard_map/ppermute | solution.py:545
  68.6 8.8 %collective-permute-start.21 = (bf16[2,2,40,1024]{3,2,1,0:T(8,128)(2,1)S(1)}, bf16[2,2,40,1024]{3,2,1,0:T(8,128)(2,1)S(1)}, u32[]{:S(2)}, u32[]{:S(2)}) collective-permute-start(bf16[2,2,40,1024]{3,2,1,0:T(8,128)(2,1)S(1)} %get-tuple-element.133), channel_id=1, source_target_pairs={{0,2},{1,3},{2,0},{3,1},{4,6},{5,7},{6,4},{7,5},{8,10},{9,11},{10,... | collective-permute-start | bytes 983048 | tf_op jit(solution)/shard_map/ppermute | solution.py:545
  69.9 23.0 %collective-permute-start.18 = (bf16[40,2048]{1,0:T(8,128)(2,1)S(1)}, bf16[40,2048]{1,0:T(8,128)(2,1)S(1)}, u32[]{:S(2)}, u32[]{:S(2)}) collective-permute-start(bf16[40,2048]{1,0:T(8,128)(2,1)S(1)} %pad_maximum_fusion.3), channel_id=1, source_target_pairs={{0,16},{4,20},{8,24},{12,28},{16,0},{20,4},{24,8},{28,12},{1,17},{... | collective-permute-start | bytes 491528 | tf_op jit(solution)/shard_map/ppermute | solution.py:545
  70.6 10.4 %collective-permute-start.28 = (bf16[2,2,1,40,1024]{4,3,1,2,0:T(8,128)(2,1)S(1)}, bf16[2,2,1,40,1024]{4,3,1,2,0:T(8,128)(2,1)S(1)}, u32[]{:S(2)}, u32[]{:S(2)}) collective-permute-start(bf16[2,2,1,40,1024]{4,3,1,2,0:T(8,128)(2,1)S(1)} %bitcast.157), channel_id=1, source_target_pairs={{0,1},{1,0},{2,3},{3,2},{4,5},{5,4},{6,7},{7,6},{8,9},{9,8},{10,11... | collective-permute-start | bytes 983048 | tf_op jit(solution)/shard_map/ppermute | solution.py:545
  70.6 11.3 %collective-permute-start.25 = (bf16[2,2,1,40,1024]{4,3,1,2,0:T(8,128)(2,1)S(1)}, bf16[2,2,1,40,1024]{4,3,1,2,0:T(8,128)(2,1)S(1)}, u32[]{:S(2)}, u32[]{:S(2)}) collective-permute-start(bf16[2,2,1,40,1024]{4,3,1,2,0:T(8,128)(2,1)S(1)} %bitcast.156), channel_id=1, source_target_pairs={{0,1},{1,0},{2,3},{3,2},{4,5},{5,4},{6,7},{7,6},{8,9},{9,8},{10,11... | collective-permute-start | bytes 983048 | tf_op jit(solution)/shard_map/ppermute | solution.py:545
  77.7 6.9 %collective-permute-start.20 = (bf16[2,40,1024]{2,1,0:T(8,128)(2,1)S(1)}, bf16[2,40,1024]{2,1,0:T(8,128)(2,1)S(1)}, u32[]{:S(2)}, u32[]{:S(2)}) collective-permute-start(bf16[2,40,1024]{2,1,0:T(8,128)(2,1)S(1)} %slice_bitcast_fusion.10), channel_id=1, source_target_pairs={{0,2},{1,3},{2,0},{3,1},{4,6},{5,7},{6,4},{7,5},{8,10},{9,11},{10,... | collective-permute-start | bytes 491528 | tf_op jit(solution)/shard_map/ppermute | solution.py:545
  79.0 6.6 %collective-permute-start.22 = (bf16[2,40,1024]{2,1,0:T(8,128)(2,1)S(1)}, bf16[2,40,1024]{2,1,0:T(8,128)(2,1)S(1)}, u32[]{:S(2)}, u32[]{:S(2)}) collective-permute-start(bf16[2,40,1024]{2,1,0:T(8,128)(2,1)S(1)} %slice_bitcast_fusion.8), channel_id=1, source_target_pairs={{0,4},{4,0},{8,12},{12,8},{16,20},{20,16},{24,28},{28,24},{1,5},{5... | collective-permute-start | bytes 491528 | tf_op jit(solution)/shard_map/ppermute | solution.py:545
  81.1 8.6 %collective-permute-start.29 = (bf16[2,1,40,1024]{3,2,1,0:T(8,128)(2,1)S(1)}, bf16[2,1,40,1024]{3,2,1,0:T(8,128)(2,1)S(1)}, u32[]{:S(2)}, u32[]{:S(2)}) collective-permute-start(bf16[2,1,40,1024]{3,2,1,0:T(8,128)(2,1)S(1)} %get-tuple-element.135), channel_id=1, source_target_pairs={{0,2},{1,3},{2,0},{3,1},{4,6},{5,7},{6,4},{7,5},{8,10},{9,11},{10,... | collective-permute-start | bytes 491528 | tf_op jit(solution)/shard_map/ppermute | solution.py:545
  82.0 9.0 %collective-permute-start.26 = (bf16[2,1,40,1024]{3,2,1,0:T(8,128)(2,1)S(1)}, bf16[2,1,40,1024]{3,2,1,0:T(8,128)(2,1)S(1)}, u32[]{:S(2)}, u32[]{:S(2)}) collective-permute-start(bf16[2,1,40,1024]{3,2,1,0:T(8,128)(2,1)S(1)} %get-tuple-element.137), channel_id=1, source_target_pairs={{0,4},{4,0},{8,12},{12,8},{16,20},{20,16},{24,28},{28,24},{1,5},{5... | collective-permute-start | bytes 491528 | tf_op jit(solution)/shard_map/ppermute | solution.py:545
  84.7 7.6 %copy-start.2 = (bf16[512,512]{1,0:T(8,128)(2,1)S(1)}, bf16[512,512]{1,0:T(8,128)(2,1)}, u32[]{:S(2)}) copy-start(bf16[512,512]{1,0:T(8,128)(2,1)} %w_dq.1) | copy-start | bytes 1572868
  84.7 7.5 %copy-start.5 = (f32[512]{0:T(512)S(1)}, f32[512]{0:T(512)}, u32[]{:S(2)}) copy-start(f32[512]{0:T(512)} %param.30) | copy-start | bytes 6148
  85.8 9.9 %collective-permute-start.24 = (bf16[40,2048]{1,0:T(8,128)(2,1)S(1)}, bf16[40,2048]{1,0:T(8,128)(2,1)S(1)}, u32[]{:S(2)}, u32[]{:S(2)}) collective-permute-start(bf16[40,2048]{1,0:T(8,128)(2,1)S(1)} %pad_maximum_fusion.5), channel_id=1, source_target_pairs={{0,8},{4,12},{8,16},{12,20},{16,24},{20,28},{24,0},{28,4},{1,9},{5... | collective-permute-start | bytes 491528 | tf_op jit(solution)/shard_map/ppermute | solution.py:545
  86.4 9.3 %copy-start.6 = (bf16[2048,1024]{1,0:T(8,128)(2,1)S(1)}, bf16[2048,1024]{1,0:T(8,128)(2,1)}, u32[]{:S(2)}) copy-start(bf16[2048,1024]{1,0:T(8,128)(2,1)} %refs_11_.1) | copy-start | bytes 12582916
  86.4 9.3 %collective-permute-start.23 = (bf16[40,2048]{1,0:T(8,128)(2,1)S(1)}, bf16[40,2048]{1,0:T(8,128)(2,1)S(1)}, u32[]{:S(2)}, u32[]{:S(2)}) collective-permute-start(bf16[40,2048]{1,0:T(8,128)(2,1)S(1)} %pad_maximum_fusion.4), channel_id=1, source_target_pairs={{0,24},{4,28},{8,0},{12,4},{16,8},{20,12},{24,16},{28,20},{1,25},{... | collective-permute-start | bytes 491528 | tf_op jit(solution)/shard_map/ppermute | solution.py:545
  89.8 4.5 %collective-permute-start.30 = (bf16[1,40,1024]{2,1,0:T(8,128)(2,1)S(1)}, bf16[1,40,1024]{2,1,0:T(8,128)(2,1)S(1)}, u32[]{:S(2)}, u32[]{:S(2)}) collective-permute-start(bf16[1,40,1024]{2,1,0:T(8,128)(2,1)S(1)} %get-tuple-element.150), channel_id=1, source_target_pairs={{0,4},{4,0},{8,12},{12,8},{16,20},{20,16},{24,28},{28,24},{1,5},{5... | collective-permute-start | bytes 245768 | tf_op jit(solution)/shard_map/ppermute | solution.py:545
  91.1 4.6 %copy-start.7 = (bf16[512,512]{1,0:T(8,128)(2,1)S(1)}, bf16[512,512]{1,0:T(8,128)(2,1)}, u32[]{:S(2)}) copy-start(bf16[512,512]{1,0:T(8,128)(2,1)} %refs_12_.1) | copy-start | bytes 1572868
  91.2 4.5 %collective-permute-start.27 = (bf16[1,40,1024]{2,1,0:T(8,128)(2,1)S(1)}, bf16[1,40,1024]{2,1,0:T(8,128)(2,1)S(1)}, u32[]{:S(2)}, u32[]{:S(2)}) collective-permute-start(bf16[1,40,1024]{2,1,0:T(8,128)(2,1)S(1)} %get-tuple-element.152), channel_id=1, source_target_pairs={{0,2},{1,3},{2,0},{3,1},{4,6},{5,7},{6,4},{7,5},{8,10},{9,11},{10,... | collective-permute-start | bytes 245768 | tf_op jit(solution)/shard_map/ppermute | solution.py:545

commit v6 on v5

--- a/solution.py
+++ b/solution.py
@@ -67,17 +67,31 @@
     return jnp.where(first, outs[0], outs[1])
 
 
-def attend_pair(q, k, v, bias):
-    return divided([both for _, both in attend_part(q, k, v, bias)])
+def head_lanes(width):
+    lane = iota((1, width), 1)
+    return [(lane >= at) & (lane < at + HEAD) for at in range(0, width, HEAD)]
+
+
+def stacked(x):
+    blocks = [jnp.where(here, x, 0.0) for here in head_lanes(x.shape[1])]
+    return jnp.concatenate(blocks, axis=0).astype(jnp.bfloat16)
+
+
+def attend_columns(q, k, v, bias):
+    keys, width = k.shape
+    scaled = k.astype(jnp.float32) * (1.0 / math.sqrt(HEAD))
+    scores = mm_t(stacked(scaled), q).reshape(width // HEAD, keys, q.shape[0]) + bias[None]
+    raised = jnp.exp(scores - jnp.max(scores, axis=1, keepdims=True))
+    weights = raised / jnp.sum(raised, axis=1, keepdims=True)
+    weights = weights.reshape(-1, q.shape[0]).astype(jnp.bfloat16)
+    return mm_first(weights, stacked(v.astype(jnp.float32)))
 
 
 def attend_stacked(q, k, v, bias):
     rows, width = q.shape
-    lane = iota((1, width), 1)
-    heads = [(lane >= at) & (lane < at + HEAD) for at in range(0, width, HEAD)]
+    heads = head_lanes(width)
     scaled = q.astype(jnp.float32) * (1.0 / math.sqrt(HEAD))
-    stack = jnp.concatenate([jnp.where(here, scaled, 0.0) for here in heads], axis=0)
-    scores = mm_t(stack.astype(jnp.bfloat16), k) + jnp.concatenate([bias] * len(heads), axis=0)
+    scores = mm_t(stacked(scaled), k) + jnp.concatenate([bias] * len(heads), axis=0)
     raised = jnp.exp(scores - jnp.max(scores, axis=-1, keepdims=True))
     mixed = mm(raised.astype(jnp.bfloat16), v) / jnp.sum(raised, axis=-1, keepdims=True)
     out = jnp.zeros((rows, width), jnp.float32)
@@ -137,12 +151,11 @@
     upto = at_col <= at_row
     opened = jnp.max(jnp.where(upto & (flag == 1), at_col, 0), axis=1, keepdims=True)
     since_out[...] = iota((rows, 1), 0) - opened
-    own_number = jnp.sum(jnp.where(upto, flag, 0), axis=1, keepdims=True) - 1
-    decode_out[...] = jnp.where(iota((rows, patch_cap), 1) <= own_number, 0.0, very_negative)
     eight = jnp.broadcast_to(flag, (8, rows)).astype(jnp.float32).astype(jnp.bfloat16)
     number = mm(eight, as_bf16(at_row <= at_col))[:1].astype(jnp.int32) - 1
     at_byte = iota((patch_cap, rows), 1)
     member = number == iota((patch_cap, rows), 0)
+    decode_out[...] = jnp.where(iota((patch_cap, rows), 0) <= number, 0.0, very_negative)
     last = jnp.max(jnp.where(member, at_byte, -1), axis=1, keepdims=True)
     live_out[...] = (last >= 0).astype(jnp.float32)
     ends_out[...] = as_bf16(member & (at_byte == last))
@@ -196,7 +209,7 @@
             like((extra, width), bf16),
             like((heads, rows, 2 * HEAD), f32),
             like((heads, rows, 2 * HEAD), f32),
-            like((rows, patch_cap), f32),
+            like((patch_cap, rows), f32),
         ),
         in_specs=[pl.BlockSpec(memory_space=pltpu.SMEM)] + [anywhere] * 8,
         out_specs=(vmem,) * 16,
@@ -476,9 +489,9 @@
 
 
 def decode_kernel(wholes, *refs):
-    state, *parts = refs[:-8]
-    encoded, queries, bias, w_dkv, w_do, bytes_out, patch_out, mixed_ref = refs[-8:]
-    rows, width = encoded.shape
+    state, *parts = refs[:-7]
+    encoded, queries, bias, w_dkv, w_do, bytes_out, patch_out = refs[-7:]
+    width = encoded.shape[1]
     wide = state.shape[1] // 2
     per = (len(parts) - wholes) // 2
     pairs = 0.0
@@ -493,18 +506,10 @@
         patch_out[:, here] = states
         pairs = pairs + mm(states, w_dkv[here, :])
     pairs = pairs.astype(jnp.bfloat16)
-    lanes = 2 * HEAD
-    for at in range(0, width, lanes):
-        mixed = attend_pair(
-            queries[:, at : at + lanes],
-            pairs[:, at : at + lanes],
-            pairs[:, width + at : width + at + lanes],
-            bias[...],
-        )
-        mixed_ref[:, at : at + lanes] = mixed.astype(jnp.bfloat16)
-    bytes_out[...] = (encoded[...].astype(jnp.float32) + mm(mixed_ref[...], w_do[...])).astype(
-        jnp.bfloat16
-    )
+    mixed = attend_columns(queries[...], pairs[:, :width], pairs[:, width:], bias[...])
+    bytes_out[...] = (
+        encoded[...].astype(jnp.float32) + mm(mixed.astype(jnp.bfloat16), w_do[...])
+    ).astype(jnp.bfloat16)
 
 
 def decode(state, wholes, halves, encoded, queries, bias, w_dkv, w_do):
@@ -518,7 +523,6 @@
         ),
         in_specs=[vmem] * (6 + len(parts)),
         out_specs=(vmem, vmem),
-        scratch_shapes=[pltpu.VMEM(encoded.shape, jnp.bfloat16)],
         cost_estimate=cost(4 * 256 * w_dkv.size),
         compiler_params=pltpu.CompilerParams(vmem_limit_bytes=12 * 1024 * 1024),
     )(state, *parts, encoded, queries, bias, w_dkv, w_do)

time: 99 us -> 98.2 us (level)
  no operation moved by 1% of the time
where the time goes in v6:
time: 98.2 us; the launch traced here: 98 us
  starting transfers between devices  38.3 us (39%)
  Pallas kernels  28.8 us (29%)
  waiting for transfers between devices  26.4 us (27%)
  local copies, waits for them, and re-layouts  1.78 us (2%)
  other arithmetic  1.58 us (2%)
  between operations  1.15 us (1%)
    ppermute x29, starting transfers between devices, shift(): return lax.ppermute(x, axis, pairs)  32 us
    ppermute x29, waiting for transfers between devices, shift(): return lax.ppermute(x, axis, pairs)  24.6 us
    pallas_call x3, Pallas kernels, stream(): pl.pallas_call(functools.partial(stream_kernel, patch_cap, capacity, expe...  13.7 us
    ppermute x2, starting transfers between devices, passed_along(): return lax.ppermute(x, axis, pairs)  6.36 us
    pallas_call x1, Pallas kernels, encode(): pl.pallas_call(functools.partial(encoder_kernel, reach), out_shape=(jax.S...  5.38 us
    pallas_call x1, Pallas kernels, opening(): pl.pallas_call(functools.partial(opening_kernel, reach, capacity), out_sh...  3.66 us
    pallas_call x3, Pallas kernels, gated_share(): pl.pallas_call(functools.partial(share_kernel, order), out_shape=share_sh...  2.99 us
    pallas_call x1, Pallas kernels, decode(): pl.pallas_call(functools.partial(decode_kernel, len(wholes)), out_shape=(...  2.37 us
  transfers between devices with their start and end apart: 31, of which 14 were waited for; matrix products, arithmetic and copies ran while one was open for 3% of the time, Pallas kernels for 18%

profile of v6, /device:TPU:0, one launch (start us, length us, event | category | flops | bytes accessed | tf_op | source)
XLA Modules:
  0.0 98.0 jit_solution(13749059838620910006)
XLA Ops:
  0.6 4.9 %collective-permute-start = (bf16[256,512]{1,0:T(8,128)(2,1)}, bf16[256,512]{1,0:T(8,128)(2,1)S(1)}, u32[]{:S(2)}, u32[]{:S(2)}) collective-permute-start(bf16[256,512]{1,0:T(8,128)(2,1)} %refs_1_.1), channel_id=1, source_target_pairs={{0,2},{1,3},{2,4},{3,5},{4,6},{5,7},{6,8},{7,9},{8,10},{9,11},{10,... | collective-permute-start | bytes 786440 | tf_op jit(solution)/shard_map/ppermute | solution.py:23
  5.5 1.5 %collective-permute-start.1 = (bf16[256,512]{1,0:T(8,128)(2,1)}, bf16[256,512]{1,0:T(8,128)(2,1)S(1)}, u32[]{:S(2)}, u32[]{:S(2)}) collective-permute-start(bf16[256,512]{1,0:T(8,128)(2,1)} %refs_1_.1), channel_id=1, source_target_pairs={{0,1},{1,2},{2,3},{3,4},{4,5},{5,6},{6,7},{7,8},{8,9},{9,10},{10,1... | collective-permute-start | bytes 786440 | tf_op jit(solution)/shard_map/ppermute | solution.py:23
  7.0 3.7 %shard_map.176 = (bf16[256,512]{1,0:T(8,128)(2,1)S(1)}, f32[1,512]{1,0:T(1,128)S(1)}, bf16[512,1024]{1,0:T(8,128)(2,1)S(1)}, bf16[512,512]{1,0:T(8,128)(2,1)S(1)...) custom-call(s32[1]{0:T(128)} %bitcast.refs_0_, ...), custom_call_target="tpu_custom_call" | custom-call | flops 805306368 | tf_op jit(solution)/shard_map/pallas_call | solution.py:194
  10.7 1.8 %collective-permute-done.refs_0_ = bf16[256,512]{1,0:T(8,128)(2,1)S(1)} collective-permute-done((bf16[256,512]{1,0:T(8,128)(2,1)}, bf16[256,512]{1,0:T(8,128)(2,1)S(1)}, u32[]{:S(2)}, u32[]{:S(2)}) %collective-permute-start) | collective-permute-done | bytes 262176 | tf_op jit(solution)/shard_map/ppermute | solution.py:23
  12.5 5.4 %shard_map.177 = (bf16[256,512]{1,0:T(8,128)(2,1)S(1)}, bf16[48,512]{1,0:T(8,128)(2,1)S(1)}) custom-call(bf16[256,512]{1,0:T(8,128)(2,1)S(1)} %collective-permute-done.refs_0_, bf16[256,512]{1,0:T(8,128)(2,1)S(1)} %collective-permute-done.1.refs_1_, bf16[256,512]{1,0:T(8,128)(2,1)S(1)} %get-tuple-element.66.refs_2_, f32[1,512]{1,0:T(1,128)S(1)} %get-tuple-element.67.refs_3_, ...), custom_call_target="tpu_custom_call" | custom-call | flops 2415919104 | tf_op jit(solution)/shard_map/pallas_call | solution.py:290
  17.9 5.9 %collective-permute-start.2 = (bf16[48,512]{1,0:T(8,128)(2,1)S(1)}, bf16[48,512]{1,0:T(8,128)(2,1)S(1)}, u32[]{:S(2)}, u32[]{:S(2)}) collective-permute-start(bf16[48,512]{1,0:T(8,128)(2,1)S(1)} %get-tuple-element.82.payload), channel_id=1, source_target_pairs={{0,8},{4,12},{8,16},{12,20},{16,24},{20,28},{24,0},{28,4},{1,9},{5... | collective-permute-start | bytes 147464 | tf_op jit(solution)/shard_map/ppermute | solution.py:549
  23.9 2.6 %collective-permute-start.3 = (bf16[48,512]{1,0:T(8,128)(2,1)S(1)}, bf16[48,512]{1,0:T(8,128)(2,1)S(1)}, u32[]{:S(2)}, u32[]{:S(2)}) collective-permute-start(bf16[48,512]{1,0:T(8,128)(2,1)S(1)} %get-tuple-element.82.payload), channel_id=1, source_target_pairs={{0,16},{4,20},{8,24},{12,28},{16,0},{20,4},{24,8},{28,12},{1,17},{... | collective-permute-start | bytes 147464 | tf_op jit(solution)/shard_map/ppermute | solution.py:549
  26.4 1.4 %collective-permute-start.4 = (bf16[48,512]{1,0:T(8,128)(2,1)S(1)}, bf16[48,512]{1,0:T(8,128)(2,1)S(1)}, u32[]{:S(2)}, u32[]{:S(2)}) collective-permute-start(bf16[48,512]{1,0:T(8,128)(2,1)S(1)} %get-tuple-element.82.payload), channel_id=1, source_target_pairs={{0,24},{4,28},{8,0},{12,4},{16,8},{20,12},{24,16},{28,20},{1,25},{... | collective-permute-start | bytes 147464 | tf_op jit(solution)/shard_map/ppermute | solution.py:549
  27.8 1.4 %copy.25 = bf16[256,8,2,768]{3,1,2,0:T(8,128)(2,1)S(1)} copy(bf16[256,8,2,768]{3,2,1,0:T(2,128)(2,1)S(1)} %bitcast.162) | data formatting | bytes 12582912
  29.2 1.3 %collective-permute-done.4 = bf16[48,512]{1,0:T(8,128)(2,1)S(1)} collective-permute-done((bf16[48,512]{1,0:T(8,128)(2,1)S(1)}, bf16[48,512]{1,0:T(8,128)(2,1)S(1)}, u32[]{:S(2)}, u32[]{:S(2)}) %collective-permute-start.4) | collective-permute-done | bytes 49184 | tf_op jit(solution)/shard_map/ppermute | solution.py:549
  30.6 0.7 collective-permute-start.5
  31.3 0.6 collective-permute-start.7
  31.9 3.8 %collective-permute-done.5 = bf16[4,48,256]{2,1,0:T(8,128)(2,1)S(1)} collective-permute-done((bf16[4,48,256]{2,1,0:T(8,128)(2,1)S(1)}, bf16[4,48,256]{2,1,0:T(8,128)(2,1)S(1)}, u32[]{:S(2)}, u32[]{:S(2)}) %collective-permute-start.5) | collective-permute-done | bytes 98336 | tf_op jit(solution)/shard_map/ppermute | solution.py:549
  35.8 0.7 collective-permute-done.7
  36.5 1.1 %collective-permute-start.8 = (bf16[4,2,48,256]{3,2,0,1:T(8,128)(2,1)S(1)}, bf16[4,2,48,256]{3,2,0,1:T(8,128)(2,1)S(1)}, u32[]{:S(2)}, u32[]{:S(2)}) collective-permute-start(bf16[4,2,48,256]{3,2,0,1:T(8,128)(2,1)S(1)} %get-tuple-element.149), channel_id=1, source_target_pairs={{0,4},{4,0},{8,12},{12,8},{16,20},{20,16},{24,28},{28,24},{1,5},{5... | collective-permute-start | bytes 589832 | tf_op jit(solution)/shard_map/ppermute | solution.py:549
  37.6 3.8 %collective-permute-done.6 = bf16[4,2,48,256]{3,2,0,1:T(8,128)(2,1)S(1)} collective-permute-done((bf16[4,2,48,256]{3,2,0,1:T(8,128)(2,1)S(1)}, bf16[4,2,48,256]{3,2,0,1:T(8,128)(2,1)S(1)}, u32[]{:S(2)}, u32[]{:S(2)}) %collective-permute-start.6) | collective-permute-done | bytes 196640 | tf_op jit(solution)/shard_map/ppermute | solution.py:549
  41.5 0.8 collective-permute-done.8
  42.3 0.1 maximum_maximum_fusion
  42.4 0.1 collective-permute-start.9
  42.5 2.3 %collective-permute-done.9.refs_2_ = bf16[16,48,512]{2,1,0:T(8,128)(2,1)S(1)} collective-permute-done((bf16[16,48,512]{2,1,0:T(8,128)(2,1)S(1)}, bf16[16,48,512]{2,1,0:T(8,128)(2,1)S(1)}, u32[]{:S(2)}, u32[]{:S(2)}) %collective-permute-start.9) | collective-permute-done | bytes 786464 | tf_op jit(solution)/shard_map/ppermute | solution.py:549
  44.8 3.6 %shard_map.179 = (bf16[4,40,1024]{2,1,0:T(8,128)(2,1)S(1)}, bf16[4,40,1024]{2,1,0:T(8,128)(2,1)S(1)}, bf16[96,768]{1,0:T(8,128)(2,1)S(1)}, f32[96,1]{1,0:T(8,128)S(1)}, bf16[1,96,160]{2,1,0:T(8,128)(2,1)S(1)}) custom-call(s32[1]{0:T(128)} %bitcast.5.refs_0_, bf16[16,48,512]{2,1,0:T(8,128)(2,1)S(1)} %bitcast.137, ...), custom_call_target="tpu_custom_call" | custom-call | flops 201326592 | tf_op jit(solution)/shard_map/pallas_call | solution.py:436
  48.4 0.2 collective-permute-start.10
  48.6 0.4 collective-permute-start.11
  49.0 0.8 shard_map.180
  49.8 0.3 collective-permute-done.10
  50.1 0.1 fusion.5
  50.2 1.1 %collective-permute-start.12 = (bf16[2,1,40,1024]{3,2,1,0:T(8,128)(2,1)S(1)}, bf16[2,1,40,1024]{3,2,1,0:T(8,128)(2,1)S(1)}, u32[]{:S(2)}, u32[]{:S(2)}) collective-permute-start(bf16[2,1,40,1024]{3,2,1,0:T(8,128)(2,1)S(1)} %get-tuple-element.139), channel_id=1, source_target_pairs={{0,4},{4,0},{8,12},{12,8},{16,20},{20,16},{24,28},{28,24},{1,5},{5... | collective-permute-start | bytes 491528 | tf_op jit(solution)/shard_map/ppermute | solution.py:549
  51.3 0.1 fusion.4
  51.4 1.3 %collective-permute-start.13 = (bf16[2,1,40,1024]{3,2,1,0:T(8,128)(2,1)S(1)}, bf16[2,1,40,1024]{3,2,1,0:T(8,128)(2,1)S(1)}, u32[]{:S(2)}, u32[]{:S(2)}) collective-permute-start(bf16[2,1,40,1024]{3,2,1,0:T(8,128)(2,1)S(1)} %get-tuple-element.141), channel_id=1, source_target_pairs={{0,2},{1,3},{2,0},{3,1},{4,6},{5,7},{6,4},{7,5},{8,10},{9,11},{10,... | collective-permute-start | bytes 491528 | tf_op jit(solution)/shard_map/ppermute | solution.py:549
  52.8 6.5 %shard_map.181 = (bf16[8,40,1024]{2,1,0:T(8,128)(2,1)S(1)}, bf16[8,40,1024]{2,1,0:T(8,128)(2,1)S(1)}, bf16[192,768]{1,0:T(8,128)(2,1)S(1)}, f32[192,1]{1,0:T(8,128)S(1)}, bf16[2,96,160]{2,1,0:T(8,128)(2,1)S(1)}) custom-call(s32[1]{0:T(128)} %bitcast.5.refs_0_, bf16[16,48,512]{2,1,0:T(8,128)(2,1)S(1)} %bitcast.138, ...), custom_call_target="tpu_custom_call" | custom-call | flops 402653184 | tf_op jit(solution)/shard_map/pallas_call | solution.py:436
  59.3 0.1 collective-permute-start.15
  59.4 0.5 collective-permute-start.14
  59.9 0.1 fusion.10
  60.0 0.8 collective-permute-start.16
  60.8 1.1 %collective-permute-start.17 = (bf16[1,40,1024]{2,1,0:T(8,128)(2,1)S(1)}, bf16[1,40,1024]{2,1,0:T(8,128)(2,1)S(1)}, u32[]{:S(2)}, u32[]{:S(2)}) collective-permute-start(bf16[1,40,1024]{2,1,0:T(8,128)(2,1)S(1)} %get-tuple-element.161), channel_id=1, source_target_pairs={{0,4},{4,0},{8,12},{12,8},{16,20},{20,16},{24,28},{28,24},{1,5},{5... | collective-permute-start | bytes 245768 | tf_op jit(solution)/shard_map/ppermute | solution.py:549
  61.9 1.4 %shard_map.182 = (bf16[8,40,1024]{2,1,0:T(8,128)(2,1)S(1)}, bf16[8,40,1024]{2,1,0:T(8,128)(2,1)S(1)}) custom-call(bf16[192,768]{1,0:T(8,128)(2,1)S(1)} %get-tuple-element.97.hidden, f32[192,1]{1,0:T(8,128)S(1)} %get-tuple-element.100.gate, bf16[2,96,160]{2,1,0:T(8,128)(2,1)S(1)} %get-tuple-element.101.spread, bf16[768,2048]{1,0:T(8,128)(2,1)S(1)} %bitcast.130), custom_call_target="tpu_custom_call" | custom-call | flops 1000 | tf_op jit(solution)/shard_map/pallas_call | solution.py:461
  63.3 0.2 fusion.1
  63.6 0.2 fusion
  63.9 3.6 %shard_map.183 = (bf16[4,40,1024]{2,1,0:T(8,128)(2,1)S(1)}, bf16[4,40,1024]{2,1,0:T(8,128)(2,1)S(1)}, bf16[96,768]{1,0:T(8,128)(2,1)S(1)}, f32[96,1]{1,0:T(8,128)S(1)}, bf16[1,96,160]{2,1,0:T(8,128)(2,1)S(1)}) custom-call(s32[1]{0:T(128)} %bitcast.5.refs_0_, bf16[16,48,512]{2,1,0:T(8,128)(2,1)S(1)} %bitcast.139, ...), custom_call_target="tpu_custom_call" | custom-call | flops 201326592 | tf_op jit(solution)/shard_map/pallas_call | solution.py:436
  67.5 1.1 %collective-permute-start.19 = (bf16[2,2,40,1024]{3,2,1,0:T(8,128)(2,1)S(1)}, bf16[2,2,40,1024]{3,2,1,0:T(8,128)(2,1)S(1)}, u32[]{:S(2)}, u32[]{:S(2)}) collective-permute-start(bf16[2,2,40,1024]{3,2,1,0:T(8,128)(2,1)S(1)} %get-tuple-element.131), channel_id=1, source_target_pairs={{0,4},{4,0},{8,12},{12,8},{16,20},{20,16},{24,28},{28,24},{1,5},{5... | collective-permute-start | bytes 983048 | tf_op jit(solution)/shard_map/ppermute | solution.py:549
  68.6 1.3 %collective-permute-start.21 = (bf16[2,2,40,1024]{3,2,1,0:T(8,128)(2,1)S(1)}, bf16[2,2,40,1024]{3,2,1,0:T(8,128)(2,1)S(1)}, u32[]{:S(2)}, u32[]{:S(2)}) collective-permute-start(bf16[2,2,40,1024]{3,2,1,0:T(8,128)(2,1)S(1)} %get-tuple-element.133), channel_id=1, source_target_pairs={{0,2},{1,3},{2,0},{3,1},{4,6},{5,7},{6,4},{7,5},{8,10},{9,11},{10,... | collective-permute-start | bytes 983048 | tf_op jit(solution)/shard_map/ppermute | solution.py:549
  69.9 0.7 collective-permute-start.18
  70.6 0.5 collective-permute-start.25
  71.1 5.6 %collective-permute-done.19 = bf16[2,2,40,1024]{3,2,1,0:T(8,128)(2,1)S(1)} collective-permute-done((bf16[2,2,40,1024]{3,2,1,0:T(8,128)(2,1)S(1)}, bf16[2,2,40,1024]{3,2,1,0:T(8,128)(2,1)S(1)}, u32[]{:S(2)}, u32[]{:S(2)}) %collective-permute-start.19) | collective-permute-done | bytes 327712 | tf_op jit(solution)/shard_map/ppermute | solution.py:549
  76.7 0.7 collective-permute-done.21
  77.5 0.1 add_convert_fusion.1
  77.6 0.1 add_convert_fusion
  77.7 1.3 %collective-permute-start.20 = (bf16[2,40,1024]{2,1,0:T(8,128)(2,1)S(1)}, bf16[2,40,1024]{2,1,0:T(8,128)(2,1)S(1)}, u32[]{:S(2)}, u32[]{:S(2)}) collective-permute-start(bf16[2,40,1024]{2,1,0:T(8,128)(2,1)S(1)} %slice_bitcast_fusion.10), channel_id=1, source_target_pairs={{0,2},{1,3},{2,0},{3,1},{4,6},{5,7},{6,4},{7,5},{8,10},{9,11},{10,... | collective-permute-start | bytes 491528 | tf_op jit(solution)/shard_map/ppermute | solution.py:549
  79.0 1.1 %collective-permute-start.22 = (bf16[2,40,1024]{2,1,0:T(8,128)(2,1)S(1)}, bf16[2,40,1024]{2,1,0:T(8,128)(2,1)S(1)}, u32[]{:S(2)}, u32[]{:S(2)}) collective-permute-start(bf16[2,40,1024]{2,1,0:T(8,128)(2,1)S(1)} %slice_bitcast_fusion.8), channel_id=1, source_target_pairs={{0,4},{4,0},{8,12},{12,8},{16,20},{20,16},{24,28},{28,24},{1,5},{5... | collective-permute-start | bytes 491528 | tf_op jit(solution)/shard_map/ppermute | solution.py:549
  80.2 0.8 shard_map.184
  81.0 0.1 fusion.2
  81.1 0.8 collective-permute-start.29
  81.9 0.1 fusion.3
  82.0 1.1 %collective-permute-start.26 = (bf16[2,1,40,1024]{3,2,1,0:T(8,128)(2,1)S(1)}, bf16[2,1,40,1024]{3,2,1,0:T(8,128)(2,1)S(1)}, u32[]{:S(2)}, u32[]{:S(2)}) collective-permute-start(bf16[2,1,40,1024]{3,2,1,0:T(8,128)(2,1)S(1)} %get-tuple-element.137), channel_id=1, source_target_pairs={{0,4},{4,0},{8,12},{12,8},{16,20},{20,16},{24,28},{28,24},{1,5},{5... | collective-permute-start | bytes 491528 | tf_op jit(solution)/shard_map/ppermute | solution.py:549
  83.1 1.5 %collective-permute-done.20 = bf16[2,40,1024]{2,1,0:T(8,128)(2,1)S(1)} collective-permute-done((bf16[2,40,1024]{2,1,0:T(8,128)(2,1)S(1)}, bf16[2,40,1024]{2,1,0:T(8,128)(2,1)S(1)}, u32[]{:S(2)}, u32[]{:S(2)}) %collective-permute-start.20) | collective-permute-done | bytes 163872 | tf_op jit(solution)/shard_map/ppermute | solution.py:549
  84.7 1.0 %collective-permute-done.22 = bf16[2,40,1024]{2,1,0:T(8,128)(2,1)S(1)} collective-permute-done((bf16[2,40,1024]{2,1,0:T(8,128)(2,1)S(1)}, bf16[2,40,1024]{2,1,0:T(8,128)(2,1)S(1)}, u32[]{:S(2)}, u32[]{:S(2)}) %collective-permute-start.22) | collective-permute-done | bytes 163872 | tf_op jit(solution)/shard_map/ppermute | solution.py:549
  85.8 0.6 collective-permute-start.24
  86.4 3.4 %collective-permute-start.23 = (bf16[40,2048]{1,0:T(8,128)(2,1)S(1)}, bf16[40,2048]{1,0:T(8,128)(2,1)S(1)}, u32[]{:S(2)}, u32[]{:S(2)}) collective-permute-start(bf16[40,2048]{1,0:T(8,128)(2,1)S(1)} %pad_maximum_fusion.4), channel_id=1, source_target_pairs={{0,24},{4,28},{8,0},{12,4},{16,8},{20,12},{24,16},{28,20},{1,25},{... | collective-permute-start | bytes 491528 | tf_op jit(solution)/shard_map/ppermute | solution.py:549
  89.8 1.2 %collective-permute-start.30 = (bf16[1,40,1024]{2,1,0:T(8,128)(2,1)S(1)}, bf16[1,40,1024]{2,1,0:T(8,128)(2,1)S(1)}, u32[]{:S(2)}, u32[]{:S(2)}) collective-permute-start(bf16[1,40,1024]{2,1,0:T(8,128)(2,1)S(1)} %get-tuple-element.150), channel_id=1, source_target_pairs={{0,4},{4,0},{8,12},{12,8},{16,20},{20,16},{24,28},{28,24},{1,5},{5... | collective-permute-start | bytes 245768 | tf_op jit(solution)/shard_map/ppermute | solution.py:549
  91.1 1.1 %collective-permute-start.27 = (bf16[1,40,1024]{2,1,0:T(8,128)(2,1)S(1)}, bf16[1,40,1024]{2,1,0:T(8,128)(2,1)S(1)}, u32[]{:S(2)}, u32[]{:S(2)}) collective-permute-start(bf16[1,40,1024]{2,1,0:T(8,128)(2,1)S(1)} %get-tuple-element.152), channel_id=1, source_target_pairs={{0,2},{1,3},{2,0},{3,1},{4,6},{5,7},{6,4},{7,5},{8,10},{9,11},{10,... | collective-permute-start | bytes 245768 | tf_op jit(solution)/shard_map/ppermute | solution.py:549
  92.2 0.7 shard_map.178
  92.9 1.4 %collective-permute-done.30.refs_7_ = bf16[1,40,1024]{2,1,0:T(8,128)(2,1)S(1)} collective-permute-done((bf16[1,40,1024]{2,1,0:T(8,128)(2,1)S(1)}, bf16[1,40,1024]{2,1,0:T(8,128)(2,1)S(1)}, u32[]{:S(2)}, u32[]{:S(2)}) %collective-permute-start.30) | collective-permute-done | bytes 81952 | tf_op jit(solution)/shard_map/ppermute | solution.py:549
  94.3 1.3 %collective-permute-done.27.refs_5_ = bf16[1,40,1024]{2,1,0:T(8,128)(2,1)S(1)} collective-permute-done((bf16[1,40,1024]{2,1,0:T(8,128)(2,1)S(1)}, bf16[1,40,1024]{2,1,0:T(8,128)(2,1)S(1)}, u32[]{:S(2)}, u32[]{:S(2)}) %collective-permute-start.27) | collective-permute-done | bytes 81952 | tf_op jit(solution)/shard_map/ppermute | solution.py:549
  95.7 2.4 %shard_map.185 = (bf16[256,512]{1,0:T(8,128)(2,1)}, bf16[40,2048]{1,0:T(8,128)(2,1)}) custom-call(bf16[40,2048]{1,0:T(8,128)(2,1)S(1)} %get-tuple-element.83.refs_0_, bf16[40,2048]{1,0:T(8,128)(2,1)S(1)} %collective-permute-done.18.refs_1_, bf16[40,2048]{1,0:T(8,128)(2,1)S(1)} %collective-permute-done.23.refs_2_, ...), custom_call_target="tpu_custom_call" | custom-call | flops 2147483648 | tf_op jit(solution)/shard_map/pallas_call | solution.py:518
  (68 shorter events, 0.9 us)
Async XLA Ops:
  0.6 11.9 %collective-permute-start = (bf16[256,512]{1,0:T(8,128)(2,1)}, bf16[256,512]{1,0:T(8,128)(2,1)S(1)}, u32[]{:S(2)}, u32[]{:S(2)}) collective-permute-start(bf16[256,512]{1,0:T(8,128)(2,1)} %refs_1_.1), channel_id=1, source_target_pairs={{0,2},{1,3},{2,4},{3,5},{4,6},{5,7},{6,8},{7,9},{8,10},{9,11},{10,... | collective-permute-start | bytes 786440 | tf_op jit(solution)/shard_map/ppermute | solution.py:23
  5.5 7.0 %collective-permute-start.1 = (bf16[256,512]{1,0:T(8,128)(2,1)}, bf16[256,512]{1,0:T(8,128)(2,1)S(1)}, u32[]{:S(2)}, u32[]{:S(2)}) collective-permute-start(bf16[256,512]{1,0:T(8,128)(2,1)} %refs_1_.1), channel_id=1, source_target_pairs={{0,1},{1,2},{2,3},{3,4},{4,5},{5,6},{6,7},{7,8},{8,9},{9,10},{10,1... | collective-permute-start | bytes 786440 | tf_op jit(solution)/shard_map/ppermute | solution.py:23
  7.0 20.8 %slice-start = ((s8[6291456]{0:T(1024)(128)(4,1)}), s8[4194304]{0:T(1024)(128)(4,1)S(1)}, s32[]{:S(2)}) async-start(s8[6291456]{0:T(1024)(128)(4,1)} %bitcast.160), calls=%async_computation | async-start | bytes 8388608
  12.5 15.3 %slice-start.1 = ((s8[6291456]{0:T(1024)(128)(4,1)}), s8[2097152]{0:T(1024)(128)(4,1)S(1)}, s32[]{:S(2)}) async-start(s8[6291456]{0:T(1024)(128)(4,1)} %bitcast.160), calls=%async_computation.1 | async-start | bytes 4194304
  17.9 11.3 %collective-permute-start.2 = (bf16[48,512]{1,0:T(8,128)(2,1)S(1)}, bf16[48,512]{1,0:T(8,128)(2,1)S(1)}, u32[]{:S(2)}, u32[]{:S(2)}) collective-permute-start(bf16[48,512]{1,0:T(8,128)(2,1)S(1)} %get-tuple-element.82.payload), channel_id=1, source_target_pairs={{0,8},{4,12},{8,16},{12,20},{16,24},{20,28},{24,0},{28,4},{1,9},{5... | collective-permute-start | bytes 147464 | tf_op jit(solution)/shard_map/ppermute | solution.py:549
  23.9 5.3 %collective-permute-start.3 = (bf16[48,512]{1,0:T(8,128)(2,1)S(1)}, bf16[48,512]{1,0:T(8,128)(2,1)S(1)}, u32[]{:S(2)}, u32[]{:S(2)}) collective-permute-start(bf16[48,512]{1,0:T(8,128)(2,1)S(1)} %get-tuple-element.82.payload), channel_id=1, source_target_pairs={{0,16},{4,20},{8,24},{12,28},{16,0},{20,4},{24,8},{28,12},{1,17},{... | collective-permute-start | bytes 147464 | tf_op jit(solution)/shard_map/ppermute | solution.py:549
  26.4 4.1 %collective-permute-start.4 = (bf16[48,512]{1,0:T(8,128)(2,1)S(1)}, bf16[48,512]{1,0:T(8,128)(2,1)S(1)}, u32[]{:S(2)}, u32[]{:S(2)}) collective-permute-start(bf16[48,512]{1,0:T(8,128)(2,1)S(1)} %get-tuple-element.82.payload), channel_id=1, source_target_pairs={{0,24},{4,28},{8,0},{12,4},{16,8},{20,12},{24,16},{28,20},{1,25},{... | collective-permute-start | bytes 147464 | tf_op jit(solution)/shard_map/ppermute | solution.py:549
  30.5 14.3 %copy-start.1 = (bf16[512,2048]{1,0:T(8,128)(2,1)S(1)}, bf16[512,2048]{1,0:T(8,128)(2,1)}, u32[]{:S(2)}) copy-start(bf16[512,2048]{1,0:T(8,128)(2,1)} %refs_3_.5) | copy-start | bytes 6291460
  30.6 5.1 %collective-permute-start.5 = (bf16[4,48,256]{2,1,0:T(8,128)(2,1)S(1)}, bf16[4,48,256]{2,1,0:T(8,128)(2,1)S(1)}, u32[]{:S(2)}, u32[]{:S(2)}) collective-permute-start(bf16[4,48,256]{2,1,0:T(8,128)(2,1)S(1)} %get-tuple-element.147), channel_id=1, source_target_pairs={{0,4},{4,0},{8,12},{12,8},{16,20},{20,16},{24,28},{28,24},{1,5},{5... | collective-permute-start | bytes 294920 | tf_op jit(solution)/shard_map/ppermute | solution.py:549
  31.3 5.2 %collective-permute-start.7 = (bf16[4,48,256]{2,1,0:T(8,128)(2,1)S(1)}, bf16[4,48,256]{2,1,0:T(8,128)(2,1)S(1)}, u32[]{:S(2)}, u32[]{:S(2)}) collective-permute-start(bf16[4,48,256]{2,1,0:T(8,128)(2,1)S(1)} %get-tuple-element.146), channel_id=1, source_target_pairs={{0,2},{1,3},{2,0},{3,1},{4,6},{5,7},{6,4},{7,5},{8,10},{9,11},{10,... | collective-permute-start | bytes 294920 | tf_op jit(solution)/shard_map/ppermute | solution.py:549
  35.7 5.7 %collective-permute-start.6 = (bf16[4,2,48,256]{3,2,0,1:T(8,128)(2,1)S(1)}, bf16[4,2,48,256]{3,2,0,1:T(8,128)(2,1)S(1)}, u32[]{:S(2)}, u32[]{:S(2)}) collective-permute-start(bf16[4,2,48,256]{3,2,0,1:T(8,128)(2,1)S(1)} %get-tuple-element.143), channel_id=1, source_target_pairs={{0,2},{1,3},{2,0},{3,1},{4,6},{5,7},{6,4},{7,5},{8,10},{9,11},{10,... | collective-permute-start | bytes 589832 | tf_op jit(solution)/shard_map/ppermute | solution.py:549
  36.5 8.3 %copy-start.3 = (f32[2048,4]{0,1:T(4,128)S(1)}, f32[2048,4]{0,1:T(4,128)}, u32[]{:S(2)}) copy-start(f32[2048,4]{0,1:T(4,128)} %param.27) | copy-start | bytes 98308
  36.5 5.7 %collective-permute-start.8 = (bf16[4,2,48,256]{3,2,0,1:T(8,128)(2,1)S(1)}, bf16[4,2,48,256]{3,2,0,1:T(8,128)(2,1)S(1)}, u32[]{:S(2)}, u32[]{:S(2)}) collective-permute-start(bf16[4,2,48,256]{3,2,0,1:T(8,128)(2,1)S(1)} %get-tuple-element.149), channel_id=1, source_target_pairs={{0,4},{4,0},{8,12},{12,8},{16,20},{20,16},{24,28},{28,24},{1,5},{5... | collective-permute-start | bytes 589832 | tf_op jit(solution)/shard_map/ppermute | solution.py:549
  42.3 2.5 %copy-start = (bf16[1,768,2048]{2,1,0:T(8,128)(2,1)S(1)}, bf16[1,768,2048]{2,1,0:T(8,128)(2,1)}, u32[]{:S(2)}) copy-start(bf16[1,768,2048]{2,1,0:T(8,128)(2,1)} %param.29) | copy-start | bytes 9437188
  42.3 2.5 %copy-start.4 = (f32[2048]{0:T(1024)S(1)}, f32[2048]{0:T(1024)}, u32[]{:S(2)}) copy-start(f32[2048]{0:T(1024)} %param.26) | copy-start | bytes 24580
  42.4 2.4 %collective-permute-start.9 = (bf16[16,48,512]{2,1,0:T(8,128)(2,1)S(1)}, bf16[16,48,512]{2,1,0:T(8,128)(2,1)S(1)}, u32[]{:S(2)}, u32[]{:S(2)}) collective-permute-start(bf16[16,48,512]{2,1,0:T(8,128)(2,1)S(1)} %bitcast.136), channel_id=1, source_target_pairs={{0,1},{1,0},{2,3},{3,2},{4,5},{5,4},{6,7},{7,6},{8,9},{9,8},{10,11... | collective-permute-start | bytes 2359304 | tf_op jit(solution)/shard_map/ppermute | solution.py:549
  48.4 1.7 %collective-permute-start.10 = (bf16[2,2,1,40,1024]{4,3,1,2,0:T(8,128)(2,1)S(1)}, bf16[2,2,1,40,1024]{4,3,1,2,0:T(8,128)(2,1)S(1)}, u32[]{:S(2)}, u32[]{:S(2)}) collective-permute-start(bf16[2,2,1,40,1024]{4,3,1,2,0:T(8,128)(2,1)S(1)} %bitcast.159), channel_id=1, source_target_pairs={{0,1},{1,0},{2,3},{3,2},{4,5},{5,4},{6,7},{7,6},{8,9},{9,8},{10,11... | collective-permute-start | bytes 983048 | tf_op jit(solution)/shard_map/ppermute | solution.py:549
  48.6 2.7 %collective-permute-start.11 = (bf16[2,2,1,40,1024]{4,3,1,2,0:T(8,128)(2,1)S(1)}, bf16[2,2,1,40,1024]{4,3,1,2,0:T(8,128)(2,1)S(1)}, u32[]{:S(2)}, u32[]{:S(2)}) collective-permute-start(bf16[2,2,1,40,1024]{4,3,1,2,0:T(8,128)(2,1)S(1)} %bitcast.158), channel_id=1, source_target_pairs={{0,1},{1,0},{2,3},{3,2},{4,5},{5,4},{6,7},{7,6},{8,9},{9,8},{10,11... | collective-permute-start | bytes 983048 | tf_op jit(solution)/shard_map/ppermute | solution.py:549
  50.2 9.7 %collective-permute-start.12 = (bf16[2,1,40,1024]{3,2,1,0:T(8,128)(2,1)S(1)}, bf16[2,1,40,1024]{3,2,1,0:T(8,128)(2,1)S(1)}, u32[]{:S(2)}, u32[]{:S(2)}) collective-permute-start(bf16[2,1,40,1024]{3,2,1,0:T(8,128)(2,1)S(1)} %get-tuple-element.139), channel_id=1, source_target_pairs={{0,4},{4,0},{8,12},{12,8},{16,20},{20,16},{24,28},{28,24},{1,5},{5... | collective-permute-start | bytes 491528 | tf_op jit(solution)/shard_map/ppermute | solution.py:549
  51.4 8.4 %collective-permute-start.13 = (bf16[2,1,40,1024]{3,2,1,0:T(8,128)(2,1)S(1)}, bf16[2,1,40,1024]{3,2,1,0:T(8,128)(2,1)S(1)}, u32[]{:S(2)}, u32[]{:S(2)}) collective-permute-start(bf16[2,1,40,1024]{3,2,1,0:T(8,128)(2,1)S(1)} %get-tuple-element.141), channel_id=1, source_target_pairs={{0,2},{1,3},{2,0},{3,1},{4,6},{5,7},{6,4},{7,5},{8,10},{9,11},{10,... | collective-permute-start | bytes 491528 | tf_op jit(solution)/shard_map/ppermute | solution.py:549
  59.3 4.3 %collective-permute-start.15 = (bf16[2,2,2,40,1024]{4,3,2,1,0:T(8,128)(2,1)S(1)}, bf16[2,2,2,40,1024]{4,3,2,1,0:T(8,128)(2,1)S(1)}, u32[]{:S(2)}, u32[]{:S(2)}) collective-permute-start(bf16[2,2,2,40,1024]{4,3,2,1,0:T(8,128)(2,1)S(1)} %bitcast.154), channel_id=1, source_target_pairs={{0,1},{1,0},{2,3},{3,2},{4,5},{5,4},{6,7},{7,6},{8,9},{9,8},{10,11... | collective-permute-start | bytes 1966088 | tf_op jit(solution)/shard_map/ppermute | solution.py:549
  59.4 3.9 %collective-permute-start.14 = (bf16[2,2,2,40,1024]{4,3,2,1,0:T(8,128)(2,1)S(1)}, bf16[2,2,2,40,1024]{4,3,2,1,0:T(8,128)(2,1)S(1)}, u32[]{:S(2)}, u32[]{:S(2)}) collective-permute-start(bf16[2,2,2,40,1024]{4,3,2,1,0:T(8,128)(2,1)S(1)} %bitcast.155), channel_id=1, source_target_pairs={{0,1},{1,0},{2,3},{3,2},{4,5},{5,4},{6,7},{7,6},{8,9},{9,8},{10,11... | collective-permute-start | bytes 1966088 | tf_op jit(solution)/shard_map/ppermute | solution.py:549
  60.0 7.5 %collective-permute-start.16 = (bf16[1,40,1024]{2,1,0:T(8,128)(2,1)S(1)}, bf16[1,40,1024]{2,1,0:T(8,128)(2,1)S(1)}, u32[]{:S(2)}, u32[]{:S(2)}) collective-permute-start(bf16[1,40,1024]{2,1,0:T(8,128)(2,1)S(1)} %get-tuple-element.159), channel_id=1, source_target_pairs={{0,2},{1,3},{2,0},{3,1},{4,6},{5,7},{6,4},{7,5},{8,10},{9,11},{10,... | collective-permute-start | bytes 245768 | tf_op jit(solution)/shard_map/ppermute | solution.py:549
  60.8 6.6 %collective-permute-start.17 = (bf16[1,40,1024]{2,1,0:T(8,128)(2,1)S(1)}, bf16[1,40,1024]{2,1,0:T(8,128)(2,1)S(1)}, u32[]{:S(2)}, u32[]{:S(2)}) collective-permute-start(bf16[1,40,1024]{2,1,0:T(8,128)(2,1)S(1)} %get-tuple-element.161), channel_id=1, source_target_pairs={{0,4},{4,0},{8,12},{12,8},{16,20},{20,16},{24,28},{28,24},{1,5},{5... | collective-permute-start | bytes 245768 | tf_op jit(solution)/shard_map/ppermute | solution.py:549
  67.5 9.2 %collective-permute-start.19 = (bf16[2,2,40,1024]{3,2,1,0:T(8,128)(2,1)S(1)}, bf16[2,2,40,1024]{3,2,1,0:T(8,128)(2,1)S(1)}, u32[]{:S(2)}, u32[]{:S(2)}) collective-permute-start(bf16[2,2,40,1024]{3,2,1,0:T(8,128)(2,1)S(1)} %get-tuple-element.131), channel_id=1, source_target_pairs={{0,4},{4,0},{8,12},{12,8},{16,20},{20,16},{24,28},{28,24},{1,5},{5... | collective-permute-start | bytes 983048 | tf_op jit(solution)/shard_map/ppermute | solution.py:549
  68.6 8.9 %collective-permute-start.21 = (bf16[2,2,40,1024]{3,2,1,0:T(8,128)(2,1)S(1)}, bf16[2,2,40,1024]{3,2,1,0:T(8,128)(2,1)S(1)}, u32[]{:S(2)}, u32[]{:S(2)}) collective-permute-start(bf16[2,2,40,1024]{3,2,1,0:T(8,128)(2,1)S(1)} %get-tuple-element.133), channel_id=1, source_target_pairs={{0,2},{1,3},{2,0},{3,1},{4,6},{5,7},{6,4},{7,5},{8,10},{9,11},{10,... | collective-permute-start | bytes 983048 | tf_op jit(solution)/shard_map/ppermute | solution.py:549
  69.9 23.0 %collective-permute-start.18 = (bf16[40,2048]{1,0:T(8,128)(2,1)S(1)}, bf16[40,2048]{1,0:T(8,128)(2,1)S(1)}, u32[]{:S(2)}, u32[]{:S(2)}) collective-permute-start(bf16[40,2048]{1,0:T(8,128)(2,1)S(1)} %pad_maximum_fusion.3), channel_id=1, source_target_pairs={{0,16},{4,20},{8,24},{12,28},{16,0},{20,4},{24,8},{28,12},{1,17},{... | collective-permute-start | bytes 491528 | tf_op jit(solution)/shard_map/ppermute | solution.py:549
  70.6 10.4 %collective-permute-start.28 = (bf16[2,2,1,40,1024]{4,3,1,2,0:T(8,128)(2,1)S(1)}, bf16[2,2,1,40,1024]{4,3,1,2,0:T(8,128)(2,1)S(1)}, u32[]{:S(2)}, u32[]{:S(2)}) collective-permute-start(bf16[2,2,1,40,1024]{4,3,1,2,0:T(8,128)(2,1)S(1)} %bitcast.157), channel_id=1, source_target_pairs={{0,1},{1,0},{2,3},{3,2},{4,5},{5,4},{6,7},{7,6},{8,9},{9,8},{10,11... | collective-permute-start | bytes 983048 | tf_op jit(solution)/shard_map/ppermute | solution.py:549
  70.6 11.3 %collective-permute-start.25 = (bf16[2,2,1,40,1024]{4,3,1,2,0:T(8,128)(2,1)S(1)}, bf16[2,2,1,40,1024]{4,3,1,2,0:T(8,128)(2,1)S(1)}, u32[]{:S(2)}, u32[]{:S(2)}) collective-permute-start(bf16[2,2,1,40,1024]{4,3,1,2,0:T(8,128)(2,1)S(1)} %bitcast.156), channel_id=1, source_target_pairs={{0,1},{1,0},{2,3},{3,2},{4,5},{5,4},{6,7},{7,6},{8,9},{9,8},{10,11... | collective-permute-start | bytes 983048 | tf_op jit(solution)/shard_map/ppermute | solution.py:549
  77.7 6.9 %collective-permute-start.20 = (bf16[2,40,1024]{2,1,0:T(8,128)(2,1)S(1)}, bf16[2,40,1024]{2,1,0:T(8,128)(2,1)S(1)}, u32[]{:S(2)}, u32[]{:S(2)}) collective-permute-start(bf16[2,40,1024]{2,1,0:T(8,128)(2,1)S(1)} %slice_bitcast_fusion.10), channel_id=1, source_target_pairs={{0,2},{1,3},{2,0},{3,1},{4,6},{5,7},{6,4},{7,5},{8,10},{9,11},{10,... | collective-permute-start | bytes 491528 | tf_op jit(solution)/shard_map/ppermute | solution.py:549
  79.0 6.7 %collective-permute-start.22 = (bf16[2,40,1024]{2,1,0:T(8,128)(2,1)S(1)}, bf16[2,40,1024]{2,1,0:T(8,128)(2,1)S(1)}, u32[]{:S(2)}, u32[]{:S(2)}) collective-permute-start(bf16[2,40,1024]{2,1,0:T(8,128)(2,1)S(1)} %slice_bitcast_fusion.8), channel_id=1, source_target_pairs={{0,4},{4,0},{8,12},{12,8},{16,20},{20,16},{24,28},{28,24},{1,5},{5... | collective-permute-start | bytes 491528 | tf_op jit(solution)/shard_map/ppermute | solution.py:549
  81.1 8.6 %collective-permute-start.29 = (bf16[2,1,40,1024]{3,2,1,0:T(8,128)(2,1)S(1)}, bf16[2,1,40,1024]{3,2,1,0:T(8,128)(2,1)S(1)}, u32[]{:S(2)}, u32[]{:S(2)}) collective-permute-start(bf16[2,1,40,1024]{3,2,1,0:T(8,128)(2,1)S(1)} %get-tuple-element.135), channel_id=1, source_target_pairs={{0,2},{1,3},{2,0},{3,1},{4,6},{5,7},{6,4},{7,5},{8,10},{9,11},{10,... | collective-permute-start | bytes 491528 | tf_op jit(solution)/shard_map/ppermute | solution.py:549
  82.0 9.0 %collective-permute-start.26 = (bf16[2,1,40,1024]{3,2,1,0:T(8,128)(2,1)S(1)}, bf16[2,1,40,1024]{3,2,1,0:T(8,128)(2,1)S(1)}, u32[]{:S(2)}, u32[]{:S(2)}) collective-permute-start(bf16[2,1,40,1024]{3,2,1,0:T(8,128)(2,1)S(1)} %get-tuple-element.137), channel_id=1, source_target_pairs={{0,4},{4,0},{8,12},{12,8},{16,20},{20,16},{24,28},{28,24},{1,5},{5... | collective-permute-start | bytes 491528 | tf_op jit(solution)/shard_map/ppermute | solution.py:549
  84.7 7.6 %copy-start.2 = (bf16[512,512]{1,0:T(8,128)(2,1)S(1)}, bf16[512,512]{1,0:T(8,128)(2,1)}, u32[]{:S(2)}) copy-start(bf16[512,512]{1,0:T(8,128)(2,1)} %w_dq.1) | copy-start | bytes 1572868
  84.7 7.5 %copy-start.5 = (f32[512]{0:T(512)S(1)}, f32[512]{0:T(512)}, u32[]{:S(2)}) copy-start(f32[512]{0:T(512)} %param.30) | copy-start | bytes 6148
  85.8 9.9 %collective-permute-start.24 = (bf16[40,2048]{1,0:T(8,128)(2,1)S(1)}, bf16[40,2048]{1,0:T(8,128)(2,1)S(1)}, u32[]{:S(2)}, u32[]{:S(2)}) collective-permute-start(bf16[40,2048]{1,0:T(8,128)(2,1)S(1)} %pad_maximum_fusion.5), channel_id=1, source_target_pairs={{0,8},{4,12},{8,16},{12,20},{16,24},{20,28},{24,0},{28,4},{1,9},{5... | collective-permute-start | bytes 491528 | tf_op jit(solution)/shard_map/ppermute | solution.py:549
  86.4 9.3 %copy-start.6 = (bf16[2048,1024]{1,0:T(8,128)(2,1)S(1)}, bf16[2048,1024]{1,0:T(8,128)(2,1)}, u32[]{:S(2)}) copy-start(bf16[2048,1024]{1,0:T(8,128)(2,1)} %refs_11_.1) | copy-start | bytes 12582916
  86.4 9.3 %collective-permute-start.23 = (bf16[40,2048]{1,0:T(8,128)(2,1)S(1)}, bf16[40,2048]{1,0:T(8,128)(2,1)S(1)}, u32[]{:S(2)}, u32[]{:S(2)}) collective-permute-start(bf16[40,2048]{1,0:T(8,128)(2,1)S(1)} %pad_maximum_fusion.4), channel_id=1, source_target_pairs={{0,24},{4,28},{8,0},{12,4},{16,8},{20,12},{24,16},{28,20},{1,25},{... | collective-permute-start | bytes 491528 | tf_op jit(solution)/shard_map/ppermute | solution.py:549
  89.8 4.5 %collective-permute-start.30 = (bf16[1,40,1024]{2,1,0:T(8,128)(2,1)S(1)}, bf16[1,40,1024]{2,1,0:T(8,128)(2,1)S(1)}, u32[]{:S(2)}, u32[]{:S(2)}) collective-permute-start(bf16[1,40,1024]{2,1,0:T(8,128)(2,1)S(1)} %get-tuple-element.150), channel_id=1, source_target_pairs={{0,4},{4,0},{8,12},{12,8},{16,20},{20,16},{24,28},{28,24},{1,5},{5... | collective-permute-start | bytes 245768 | tf_op jit(solution)/shard_map/ppermute | solution.py:549
  91.1 4.6 %copy-start.7 = (bf16[512,512]{1,0:T(8,128)(2,1)S(1)}, bf16[512,512]{1,0:T(8,128)(2,1)}, u32[]{:S(2)}) copy-start(bf16[512,512]{1,0:T(8,128)(2,1)} %refs_12_.1) | copy-start | bytes 1572868
  91.1 4.5 %collective-permute-start.27 = (bf16[1,40,1024]{2,1,0:T(8,128)(2,1)S(1)}, bf16[1,40,1024]{2,1,0:T(8,128)(2,1)S(1)}, u32[]{:S(2)}, u32[]{:S(2)}) collective-permute-start(bf16[1,40,1024]{2,1,0:T(8,128)(2,1)S(1)} %get-tuple-element.152), channel_id=1, source_target_pairs={{0,2},{1,3},{2,0},{3,1},{4,6},{5,7},{6,4},{7,5},{8,10},{9,11},{10,... | collective-permute-start | bytes 245768 | tf_op jit(solution)/shard_map/ppermute | solution.py:549

commit v7 on v6

--- a/solution.py
+++ b/solution.py
@@ -325,10 +325,10 @@
 
 
 def stream_kernel(patch_cap, capacity, experts, blocks, order, *refs):
-    me_ref, own_ref, moved_ref, w_up, gain, router, w_in, w_down = refs[:8]
-    outs = refs[8:10]
-    hidden_ref, gate_ref, spread_ref, all_hidden, later_spread, routed_ref, parts_ref = refs[10:]
-    held, width = own_ref.shape[-2:]
+    me_ref, *rows_refs, w_up, gain, router, w_in, w_down = refs[:10]
+    outs = refs[10:12]
+    hidden_ref, gate_ref, spread_ref, all_hidden, later_spread, routed_ref, parts_ref = refs[12:]
+    held = rows_refs[0].shape[1]
     per = GROUP * capacity
     kept = len(blocks) // 2
     me = me_ref[0]
@@ -357,16 +357,20 @@
 
     others = []
     for g, begin in enumerate(blocks):
-        rows_ref = own_ref if g < kept else moved_ref
+        left_ref, right_ref = rows_refs[:2] if g < kept else rows_refs[2:]
         tables = []
         for s in range(begin, begin + GROUP):
-            block = rows_ref[s, held - 16 : held, :lanes].astype(jnp.float32)
+            block = left_ref[s, held - 16 : held, :lanes].astype(jnp.float32)
             tables.append(block[patch_cap - (held - 16) : patch_cap - (held - 16) + 8])
         table = jnp.concatenate(tables, axis=1).astype(jnp.bfloat16)
         hit, other = matched(table, spread_held, held)
         others.append(jnp.sum(jnp.where(hit, other, 0), axis=1, keepdims=True))
-        block = rows_ref[begin : begin + GROUP].reshape(GROUP * held, width)
-        routed_ref[g * per : (g + 1) * per, :] = mm(as_bf16(hit), block).astype(jnp.bfloat16)
+        half = left_ref.shape[2]
+        for at, ref in ((0, left_ref), (half, right_ref)):
+            block = ref[begin : begin + GROUP].reshape(GROUP * held, half)
+            routed_ref[g * per : (g + 1) * per, at : at + half] = mm(as_bf16(hit), block).astype(
+                jnp.bfloat16
+            )
         hit, _ = matched(table, spread_cap, patch_cap)
         if g < kept:
             spread_ref[g] = as_bf16(hit)
@@ -427,7 +431,7 @@
 
 
 def stream(own, moved, blocks, order, patch_cap, capacity, me, w_up, gain, router, w_in, w_down):
-    held, width = own.shape[-2:]
+    width = w_up.shape[0]
     experts, wide = router.shape
     vmem = pl.BlockSpec(memory_space=pltpu.VMEM)
     per = GROUP * capacity
@@ -441,7 +445,7 @@
             jax.ShapeDtypeStruct((slots // 2, 1), jnp.float32),
             spread,
         ),
-        in_specs=[pl.BlockSpec(memory_space=pltpu.SMEM)] + [vmem] * 7,
+        in_specs=[pl.BlockSpec(memory_space=pltpu.SMEM)] + [vmem] * 9,
         out_specs=(vmem,) * 5,
         scratch_shapes=[
             pltpu.VMEM((slots, w_down.shape[0]), jnp.bfloat16),
@@ -451,7 +455,7 @@
         ],
         cost_estimate=cost(slots * wide * (width + w_in.shape[1]) // 4),
         compiler_params=pltpu.CompilerParams(vmem_limit_bytes=24 * 1024 * 1024),
-    )(me, own, moved, w_up, gain, router, w_in, w_down)
+    )(me, *own, *moved, w_up, gain, router, w_in, w_down)
 
 
 def gated_share(hidden, gate, spread, w_down, order, patch_cap):
@@ -560,7 +564,7 @@
     x, beside = lax.optimization_barrier((x, beside))
     left = gathered(gathered(x[..., :half], d["x"], 1), d["y"], 1)
     right = gathered(gathered(x[..., half:], d["y"], 1), d["x"], 2)
-    return jnp.concatenate([left, right], axis=-1), beside
+    return left, right, beside
 
 
 def summed(parts):
@@ -591,12 +595,11 @@
     d = digits()
     wide = w_up.shape[1]
     paired = w_in.reshape(w_in.shape[1], -1)
-    own, paired = gather_chip(payload, paired)
-    far, ys, xs = own.shape[:3]
-    own = own.reshape((-1,) + own.shape[3:])
-    moved = [shift(own, d["c"], by) for by in range(1, d["c"][2])]
-    assert len(moved) == 1 and ys * xs % GROUP == 0
-    moved = moved[0]
+    *own, paired = gather_chip(payload, paired)
+    far, ys, xs = own[0].shape[:3]
+    own = [v.reshape((-1,) + v.shape[3:]) for v in own]
+    assert d["c"][2] == 2 and ys * xs % GROUP == 0
+    moved = [shift(v, d["c"], 1) for v in own]
     me = lax.axis_index("expert").astype(jnp.int32).reshape(1)
     weights = (w_up, moe_gain.reshape(1, wide), w_router.T, paired, w_down[0])
     w_last = w_down[0]

time: 98.2 us -> 97.8 us (level)
  waiting for transfers between devices: 26.4 us -> 24.6 us
  starting transfers between devices: 38.3 us -> 39.9 us
    ppermute x29 -> x30, waiting for transfers between devices: 24.6 us -> 22.8 us  [shift(): return lax.ppermute(x, axis, pairs)]
    ppermute x29 -> x30, starting transfers between devices: 32 us -> 33.6 us  [shift(): return lax.ppermute(x, axis, pairs)]
  transfers between devices with their start and end apart: 31 -> 32, of which waited for: 14 -> 14; matrix products, arithmetic and copies ran while one was open for 3% -> 3% of each run, Pallas kernels for 18% -> 18%
where the time goes in v7:
time: 97.8 us; the launch traced here: 97.6 us
  starting transfers between devices  39.9 us (41%)
  Pallas kernels  28.5 us (29%)
  waiting for transfers between devices  24.6 us (25%)
  local copies, waits for them, and re-layouts  1.78 us (2%)
  other arithmetic  1.57 us (2%)
  between operations  1.16 us (1%)
    ppermute x30, starting transfers between devices, shift(): return lax.ppermute(x, axis, pairs)  33.6 us
    ppermute x30, waiting for transfers between devices, shift(): return lax.ppermute(x, axis, pairs)  22.8 us
    pallas_call x3, Pallas kernels, stream(): pl.pallas_call(functools.partial(stream_kernel, patch_cap, capacity, expe...  13.6 us
    ppermute x2, starting transfers between devices, passed_along(): return lax.ppermute(x, axis, pairs)  6.36 us
    pallas_call x1, Pallas kernels, encode(): pl.pallas_call(functools.partial(encoder_kernel, reach), out_shape=(jax.S...  5.38 us
    pallas_call x1, Pallas kernels, opening(): pl.pallas_call(functools.partial(opening_kernel, reach, capacity), out_sh...  3.66 us
    pallas_call x3, Pallas kernels, gated_share(): pl.pallas_call(functools.partial(share_kernel, order), out_shape=share_sh...  2.77 us
    pallas_call x1, Pallas kernels, decode(): pl.pallas_call(functools.partial(decode_kernel, len(wholes)), out_shape=(...  2.37 us
  transfers between devices with their start and end apart: 32, of which 14 were waited for; matrix products, arithmetic and copies ran while one was open for 3% of the time, Pallas kernels for 18%

profile of v7, /device:TPU:0, one launch (start us, length us, event | category | flops | bytes accessed | tf_op | source)
XLA Modules:
  0.0 97.6 jit_solution(11009462327246781963)
XLA Ops:
  0.6 4.9 %collective-permute-start = (bf16[256,512]{1,0:T(8,128)(2,1)}, bf16[256,512]{1,0:T(8,128)(2,1)S(1)}, u32[]{:S(2)}, u32[]{:S(2)}) collective-permute-start(bf16[256,512]{1,0:T(8,128)(2,1)} %refs_1_.1), channel_id=1, source_target_pairs={{0,2},{1,3},{2,4},{3,5},{4,6},{5,7},{6,8},{7,9},{8,10},{9,11},{10,... | collective-permute-start | bytes 786440 | tf_op jit(solution)/shard_map/ppermute | solution.py:23
  5.5 1.5 %collective-permute-start.1 = (bf16[256,512]{1,0:T(8,128)(2,1)}, bf16[256,512]{1,0:T(8,128)(2,1)S(1)}, u32[]{:S(2)}, u32[]{:S(2)}) collective-permute-start(bf16[256,512]{1,0:T(8,128)(2,1)} %refs_1_.1), channel_id=1, source_target_pairs={{0,1},{1,2},{2,3},{3,4},{4,5},{5,6},{6,7},{7,8},{8,9},{9,10},{10,1... | collective-permute-start | bytes 786440 | tf_op jit(solution)/shard_map/ppermute | solution.py:23
  7.0 3.7 %shard_map.176 = (bf16[256,512]{1,0:T(8,128)(2,1)S(1)}, f32[1,512]{1,0:T(1,128)S(1)}, bf16[512,1024]{1,0:T(8,128)(2,1)S(1)}, bf16[512,512]{1,0:T(8,128)(2,1)S(1)...) custom-call(s32[1]{0:T(128)} %bitcast.refs_0_, ...), custom_call_target="tpu_custom_call" | custom-call | flops 805306368 | tf_op jit(solution)/shard_map/pallas_call | solution.py:194
  10.7 1.8 %collective-permute-done.refs_0_ = bf16[256,512]{1,0:T(8,128)(2,1)S(1)} collective-permute-done((bf16[256,512]{1,0:T(8,128)(2,1)}, bf16[256,512]{1,0:T(8,128)(2,1)S(1)}, u32[]{:S(2)}, u32[]{:S(2)}) %collective-permute-start) | collective-permute-done | bytes 262176 | tf_op jit(solution)/shard_map/ppermute | solution.py:23
  12.5 5.4 %shard_map.177 = (bf16[256,512]{1,0:T(8,128)(2,1)S(1)}, bf16[48,512]{1,0:T(8,128)(2,1)S(1)}) custom-call(bf16[256,512]{1,0:T(8,128)(2,1)S(1)} %collective-permute-done.refs_0_, bf16[256,512]{1,0:T(8,128)(2,1)S(1)} %collective-permute-done.1.refs_1_, bf16[256,512]{1,0:T(8,128)(2,1)S(1)} %get-tuple-element.68.refs_2_, f32[1,512]{1,0:T(1,128)S(1)} %get-tuple-element.69.refs_3_, ...), custom_call_target="tpu_custom_call" | custom-call | flops 2415919104 | tf_op jit(solution)/shard_map/pallas_call | solution.py:290
  17.9 5.9 %collective-permute-start.2 = (bf16[48,512]{1,0:T(8,128)(2,1)S(1)}, bf16[48,512]{1,0:T(8,128)(2,1)S(1)}, u32[]{:S(2)}, u32[]{:S(2)}) collective-permute-start(bf16[48,512]{1,0:T(8,128)(2,1)S(1)} %get-tuple-element.84.payload), channel_id=1, source_target_pairs={{0,8},{4,12},{8,16},{12,20},{16,24},{20,28},{24,0},{28,4},{1,9},{5... | collective-permute-start | bytes 147464 | tf_op jit(solution)/shard_map/ppermute | solution.py:553
  23.9 2.6 %collective-permute-start.3 = (bf16[48,512]{1,0:T(8,128)(2,1)S(1)}, bf16[48,512]{1,0:T(8,128)(2,1)S(1)}, u32[]{:S(2)}, u32[]{:S(2)}) collective-permute-start(bf16[48,512]{1,0:T(8,128)(2,1)S(1)} %get-tuple-element.84.payload), channel_id=1, source_target_pairs={{0,16},{4,20},{8,24},{12,28},{16,0},{20,4},{24,8},{28,12},{1,17},{... | collective-permute-start | bytes 147464 | tf_op jit(solution)/shard_map/ppermute | solution.py:553
  26.4 1.4 %collective-permute-start.4 = (bf16[48,512]{1,0:T(8,128)(2,1)S(1)}, bf16[48,512]{1,0:T(8,128)(2,1)S(1)}, u32[]{:S(2)}, u32[]{:S(2)}) collective-permute-start(bf16[48,512]{1,0:T(8,128)(2,1)S(1)} %get-tuple-element.84.payload), channel_id=1, source_target_pairs={{0,24},{4,28},{8,0},{12,4},{16,8},{20,12},{24,16},{28,20},{1,25},{... | collective-permute-start | bytes 147464 | tf_op jit(solution)/shard_map/ppermute | solution.py:553
  27.8 1.4 %copy.25 = bf16[256,8,2,768]{3,1,2,0:T(8,128)(2,1)S(1)} copy(bf16[256,8,2,768]{3,2,1,0:T(2,128)(2,1)S(1)} %bitcast.165) | data formatting | bytes 12582912
  29.2 1.3 %collective-permute-done.4 = bf16[48,512]{1,0:T(8,128)(2,1)S(1)} collective-permute-done((bf16[48,512]{1,0:T(8,128)(2,1)S(1)}, bf16[48,512]{1,0:T(8,128)(2,1)S(1)}, u32[]{:S(2)}, u32[]{:S(2)}) %collective-permute-start.4) | collective-permute-done | bytes 49184 | tf_op jit(solution)/shard_map/ppermute | solution.py:553
  30.6 0.1 collective-permute-start.7
  30.7 1.2 %collective-permute-start.5 = (bf16[4,48,256]{2,1,0:T(8,128)(2,1)S(1)}, bf16[4,48,256]{2,1,0:T(8,128)(2,1)S(1)}, u32[]{:S(2)}, u32[]{:S(2)}) collective-permute-start(bf16[4,48,256]{2,1,0:T(8,128)(2,1)S(1)} %get-tuple-element.151), channel_id=1, source_target_pairs={{0,4},{4,0},{8,12},{12,8},{16,20},{20,16},{24,28},{28,24},{1,5},{5... | collective-permute-start | bytes 294920 | tf_op jit(solution)/shard_map/ppermute | solution.py:553
  31.9 3.9 %collective-permute-done.7 = bf16[4,48,256]{2,1,0:T(8,128)(2,1)S(1)} collective-permute-done((bf16[4,48,256]{2,1,0:T(8,128)(2,1)S(1)}, bf16[4,48,256]{2,1,0:T(8,128)(2,1)S(1)}, u32[]{:S(2)}, u32[]{:S(2)}) %collective-permute-start.7) | collective-permute-done | bytes 98336 | tf_op jit(solution)/shard_map/ppermute | solution.py:553
  35.8 0.9 collective-permute-start.8
  36.8 1.6 %collective-permute-start.6 = (bf16[4,2,48,256]{3,2,0,1:T(8,128)(2,1)S(1)}, bf16[4,2,48,256]{3,2,0,1:T(8,128)(2,1)S(1)}, u32[]{:S(2)}, u32[]{:S(2)}) collective-permute-start(bf16[4,2,48,256]{3,2,0,1:T(8,128)(2,1)S(1)} %get-tuple-element.153), channel_id=1, source_target_pairs={{0,2},{1,3},{2,0},{3,1},{4,6},{5,7},{6,4},{7,5},{8,10},{9,11},{10,... | collective-permute-start | bytes 589832 | tf_op jit(solution)/shard_map/ppermute | solution.py:553
  38.3 3.2 %collective-permute-done.8 = bf16[4,2,48,256]{3,2,0,1:T(8,128)(2,1)S(1)} collective-permute-done((bf16[4,2,48,256]{3,2,0,1:T(8,128)(2,1)S(1)}, bf16[4,2,48,256]{3,2,0,1:T(8,128)(2,1)S(1)}, u32[]{:S(2)}, u32[]{:S(2)}) %collective-permute-start.8) | collective-permute-done | bytes 196640 | tf_op jit(solution)/shard_map/ppermute | solution.py:553
  41.7 0.1 collective-permute-start.10
  41.7 0.8 collective-permute-done.6
  42.6 0.1 collective-permute-start.9
  42.7 0.8 collective-permute-done.10.refs_4_
  43.5 0.9 collective-permute-done.9.refs_3_
  44.4 3.6 %shard_map.179 = (bf16[4,40,1024]{2,1,0:T(8,128)(2,1)S(1)}, bf16[4,40,1024]{2,1,0:T(8,128)(2,1)S(1)}, bf16[96,768]{1,0:T(8,128)(2,1)S(1)}, f32[96,1]{1,0:T(8,128)S(1)}, bf16[1,96,160]{2,1,0:T(8,128)(2,1)S(1)}) custom-call(s32[1]{0:T(128)} %bitcast.5.refs_0_, bf16[16,48,256]{2,1,0:T(8,128)(2,1)S(1)} %bitcast.140, bf16[16,48,256]{2,1,0:T(8,128)(2,1)S(1)} %bitcast.136, ...), custom_call_target="tpu_custom_call" | custom-call | flops 201326592 | tf_op jit(solution)/shard_map/pallas_call | solution.py:440
  48.0 0.2 collective-permute-start.11
  48.2 0.4 collective-permute-start.12
  48.6 0.8 shard_map.180
  49.4 0.3 collective-permute-done.11
  49.7 0.1 fusion.5
  49.8 1.3 %collective-permute-start.13 = (bf16[2,1,40,1024]{3,2,1,0:T(8,128)(2,1)S(1)}, bf16[2,1,40,1024]{3,2,1,0:T(8,128)(2,1)S(1)}, u32[]{:S(2)}, u32[]{:S(2)}) collective-permute-start(bf16[2,1,40,1024]{3,2,1,0:T(8,128)(2,1)S(1)} %get-tuple-element.143), channel_id=1, source_target_pairs={{0,4},{4,0},{8,12},{12,8},{16,20},{20,16},{24,28},{28,24},{1,5},{5... | collective-permute-start | bytes 491528 | tf_op jit(solution)/shard_map/ppermute | solution.py:553
  51.1 0.1 fusion.4
  51.2 0.6 collective-permute-start.14
  51.9 6.5 %shard_map.181 = (bf16[8,40,1024]{2,1,0:T(8,128)(2,1)S(1)}, bf16[8,40,1024]{2,1,0:T(8,128)(2,1)S(1)}, bf16[192,768]{1,0:T(8,128)(2,1)S(1)}, f32[192,1]{1,0:T(8,128)S(1)}, bf16[2,96,160]{2,1,0:T(8,128)(2,1)S(1)}) custom-call(s32[1]{0:T(128)} %bitcast.5.refs_0_, bf16[16,48,256]{2,1,0:T(8,128)(2,1)S(1)} %bitcast.141, bf16[16,48,256]{2,1,0:T(8,128)(2,1)S(1)} %bitcast.137, ...), custom_call_target="tpu_custom_call" | custom-call | flops 402653184 | tf_op jit(solution)/shard_map/pallas_call | solution.py:440
  58.5 0.5 collective-permute-start.15
  59.0 0.1 fusion.10
  59.1 1.5 %collective-permute-start.17 = (bf16[1,40,1024]{2,1,0:T(8,128)(2,1)S(1)}, bf16[1,40,1024]{2,1,0:T(8,128)(2,1)S(1)}, u32[]{:S(2)}, u32[]{:S(2)}) collective-permute-start(bf16[1,40,1024]{2,1,0:T(8,128)(2,1)S(1)} %get-tuple-element.163), channel_id=1, source_target_pairs={{0,2},{1,3},{2,0},{3,1},{4,6},{5,7},{6,4},{7,5},{8,10},{9,11},{10,... | collective-permute-start | bytes 245768 | tf_op jit(solution)/shard_map/ppermute | solution.py:553
  60.6 1.1 %collective-permute-start.18 = (bf16[1,40,1024]{2,1,0:T(8,128)(2,1)S(1)}, bf16[1,40,1024]{2,1,0:T(8,128)(2,1)S(1)}, u32[]{:S(2)}, u32[]{:S(2)}) collective-permute-start(bf16[1,40,1024]{2,1,0:T(8,128)(2,1)S(1)} %get-tuple-element.165), channel_id=1, source_target_pairs={{0,4},{4,0},{8,12},{12,8},{16,20},{20,16},{24,28},{28,24},{1,5},{5... | collective-permute-start | bytes 245768 | tf_op jit(solution)/shard_map/ppermute | solution.py:553
  61.7 1.1 %shard_map.182 = (bf16[8,40,1024]{2,1,0:T(8,128)(2,1)S(1)}, bf16[8,40,1024]{2,1,0:T(8,128)(2,1)S(1)}) custom-call(bf16[192,768]{1,0:T(8,128)(2,1)S(1)} %get-tuple-element.100.hidden, f32[192,1]{1,0:T(8,128)S(1)} %get-tuple-element.103.gate, bf16[2,96,160]{2,1,0:T(8,128)(2,1)S(1)} %get-tuple-element.104.spread, bf16[768,2048]{1,0:T(8,128)(2,1)S(1)} %bitcast.129), custom_call_target="tpu_custom_call" | custom-call | flops 1000 | tf_op jit(solution)/shard_map/pallas_call | solution.py:465
  62.9 0.2 fusion.1
  63.2 0.2 fusion
  63.5 3.6 %shard_map.183 = (bf16[4,40,1024]{2,1,0:T(8,128)(2,1)S(1)}, bf16[4,40,1024]{2,1,0:T(8,128)(2,1)S(1)}, bf16[96,768]{1,0:T(8,128)(2,1)S(1)}, f32[96,1]{1,0:T(8,128)S(1)}, bf16[1,96,160]{2,1,0:T(8,128)(2,1)S(1)}) custom-call(s32[1]{0:T(128)} %bitcast.5.refs_0_, bf16[16,48,256]{2,1,0:T(8,128)(2,1)S(1)} %bitcast.142, bf16[16,48,256]{2,1,0:T(8,128)(2,1)S(1)} %bitcast.138, ...), custom_call_target="tpu_custom_call" | custom-call | flops 201326592 | tf_op jit(solution)/shard_map/pallas_call | solution.py:440
  67.1 1.3 %collective-permute-start.20 = (bf16[2,2,40,1024]{3,2,1,0:T(8,128)(2,1)S(1)}, bf16[2,2,40,1024]{3,2,1,0:T(8,128)(2,1)S(1)}, u32[]{:S(2)}, u32[]{:S(2)}) collective-permute-start(bf16[2,2,40,1024]{3,2,1,0:T(8,128)(2,1)S(1)} %get-tuple-element.135), channel_id=1, source_target_pairs={{0,4},{4,0},{8,12},{12,8},{16,20},{20,16},{24,28},{28,24},{1,5},{5... | collective-permute-start | bytes 983048 | tf_op jit(solution)/shard_map/ppermute | solution.py:553
  68.4 0.6 collective-permute-start.22
  69.0 1.4 %collective-permute-start.19 = (bf16[40,2048]{1,0:T(8,128)(2,1)S(1)}, bf16[40,2048]{1,0:T(8,128)(2,1)S(1)}, u32[]{:S(2)}, u32[]{:S(2)}) collective-permute-start(bf16[40,2048]{1,0:T(8,128)(2,1)S(1)} %pad_maximum_fusion.5), channel_id=1, source_target_pairs={{0,16},{4,20},{8,24},{12,28},{16,0},{20,4},{24,8},{28,12},{1,17},{... | collective-permute-start | bytes 491528 | tf_op jit(solution)/shard_map/ppermute | solution.py:553
  70.4 0.5 collective-permute-start.26
  70.9 5.4 %collective-permute-done.20 = bf16[2,2,40,1024]{3,2,1,0:T(8,128)(2,1)S(1)} collective-permute-done((bf16[2,2,40,1024]{3,2,1,0:T(8,128)(2,1)S(1)}, bf16[2,2,40,1024]{3,2,1,0:T(8,128)(2,1)S(1)}, u32[]{:S(2)}, u32[]{:S(2)}) %collective-permute-start.20) | collective-permute-done | bytes 327712 | tf_op jit(solution)/shard_map/ppermute | solution.py:553
  76.3 0.9 collective-permute-done.22
  77.2 0.1 add_convert_fusion.1
  77.3 0.1 add_convert_fusion
  77.4 0.7 collective-permute-start.21
  78.2 1.7 %collective-permute-start.23 = (bf16[2,40,1024]{2,1,0:T(8,128)(2,1)S(1)}, bf16[2,40,1024]{2,1,0:T(8,128)(2,1)S(1)}, u32[]{:S(2)}, u32[]{:S(2)}) collective-permute-start(bf16[2,40,1024]{2,1,0:T(8,128)(2,1)S(1)} %slice_bitcast_fusion.8), channel_id=1, source_target_pairs={{0,4},{4,0},{8,12},{12,8},{16,20},{20,16},{24,28},{28,24},{1,5},{5... | collective-permute-start | bytes 491528 | tf_op jit(solution)/shard_map/ppermute | solution.py:553
  79.9 0.8 shard_map.184
  80.7 0.1 fusion.2
  80.9 0.6 collective-permute-start.30
  81.5 0.1 fusion.3
  81.6 1.3 %collective-permute-start.27 = (bf16[2,1,40,1024]{3,2,1,0:T(8,128)(2,1)S(1)}, bf16[2,1,40,1024]{3,2,1,0:T(8,128)(2,1)S(1)}, u32[]{:S(2)}, u32[]{:S(2)}) collective-permute-start(bf16[2,1,40,1024]{3,2,1,0:T(8,128)(2,1)S(1)} %get-tuple-element.141), channel_id=1, source_target_pairs={{0,4},{4,0},{8,12},{12,8},{16,20},{20,16},{24,28},{28,24},{1,5},{5... | collective-permute-start | bytes 491528 | tf_op jit(solution)/shard_map/ppermute | solution.py:553
  82.9 1.5 %collective-permute-done.21 = bf16[2,40,1024]{2,1,0:T(8,128)(2,1)S(1)} collective-permute-done((bf16[2,40,1024]{2,1,0:T(8,128)(2,1)S(1)}, bf16[2,40,1024]{2,1,0:T(8,128)(2,1)S(1)}, u32[]{:S(2)}, u32[]{:S(2)}) %collective-permute-start.21) | collective-permute-done | bytes 163872 | tf_op jit(solution)/shard_map/ppermute | solution.py:553
  84.4 0.8 collective-permute-done.23
  85.4 0.6 collective-permute-start.25
  86.0 3.3 %collective-permute-start.24 = (bf16[40,2048]{1,0:T(8,128)(2,1)S(1)}, bf16[40,2048]{1,0:T(8,128)(2,1)S(1)}, u32[]{:S(2)}, u32[]{:S(2)}) collective-permute-start(bf16[40,2048]{1,0:T(8,128)(2,1)S(1)} %pad_maximum_fusion.6), channel_id=1, source_target_pairs={{0,24},{4,28},{8,0},{12,4},{16,8},{20,12},{24,16},{28,20},{1,25},{... | collective-permute-start | bytes 491528 | tf_op jit(solution)/shard_map/ppermute | solution.py:553
  89.4 1.3 %collective-permute-start.31 = (bf16[1,40,1024]{2,1,0:T(8,128)(2,1)S(1)}, bf16[1,40,1024]{2,1,0:T(8,128)(2,1)S(1)}, u32[]{:S(2)}, u32[]{:S(2)}) collective-permute-start(bf16[1,40,1024]{2,1,0:T(8,128)(2,1)S(1)} %get-tuple-element.154), channel_id=1, source_target_pairs={{0,4},{4,0},{8,12},{12,8},{16,20},{20,16},{24,28},{28,24},{1,5},{5... | collective-permute-start | bytes 245768 | tf_op jit(solution)/shard_map/ppermute | solution.py:553
  90.7 0.9 collective-permute-start.28
  91.7 0.7 shard_map.178
  92.4 1.5 %collective-permute-done.31.refs_7_ = bf16[1,40,1024]{2,1,0:T(8,128)(2,1)S(1)} collective-permute-done((bf16[1,40,1024]{2,1,0:T(8,128)(2,1)S(1)}, bf16[1,40,1024]{2,1,0:T(8,128)(2,1)S(1)}, u32[]{:S(2)}, u32[]{:S(2)}) %collective-permute-start.31) | collective-permute-done | bytes 81952 | tf_op jit(solution)/shard_map/ppermute | solution.py:553
  93.9 1.3 %collective-permute-done.28.refs_5_ = bf16[1,40,1024]{2,1,0:T(8,128)(2,1)S(1)} collective-permute-done((bf16[1,40,1024]{2,1,0:T(8,128)(2,1)S(1)}, bf16[1,40,1024]{2,1,0:T(8,128)(2,1)S(1)}, u32[]{:S(2)}, u32[]{:S(2)}) %collective-permute-start.28) | collective-permute-done | bytes 81952 | tf_op jit(solution)/shard_map/ppermute | solution.py:553
  95.2 2.4 %shard_map.185 = (bf16[256,512]{1,0:T(8,128)(2,1)}, bf16[40,2048]{1,0:T(8,128)(2,1)}) custom-call(bf16[40,2048]{1,0:T(8,128)(2,1)S(1)} %get-tuple-element.85.refs_0_, bf16[40,2048]{1,0:T(8,128)(2,1)S(1)} %collective-permute-done.19.refs_1_, bf16[40,2048]{1,0:T(8,128)(2,1)S(1)} %collective-permute-done.24.refs_2_, ...), custom_call_target="tpu_custom_call" | custom-call | flops 2147483648 | tf_op jit(solution)/shard_map/pallas_call | solution.py:522
  (72 shorter events, 1.0 us)
Async XLA Ops:
  0.6 11.9 %collective-permute-start = (bf16[256,512]{1,0:T(8,128)(2,1)}, bf16[256,512]{1,0:T(8,128)(2,1)S(1)}, u32[]{:S(2)}, u32[]{:S(2)}) collective-permute-start(bf16[256,512]{1,0:T(8,128)(2,1)} %refs_1_.1), channel_id=1, source_target_pairs={{0,2},{1,3},{2,4},{3,5},{4,6},{5,7},{6,8},{7,9},{8,10},{9,11},{10,... | collective-permute-start | bytes 786440 | tf_op jit(solution)/shard_map/ppermute | solution.py:23
  5.5 7.0 %collective-permute-start.1 = (bf16[256,512]{1,0:T(8,128)(2,1)}, bf16[256,512]{1,0:T(8,128)(2,1)S(1)}, u32[]{:S(2)}, u32[]{:S(2)}) collective-permute-start(bf16[256,512]{1,0:T(8,128)(2,1)} %refs_1_.1), channel_id=1, source_target_pairs={{0,1},{1,2},{2,3},{3,4},{4,5},{5,6},{6,7},{7,8},{8,9},{9,10},{10,1... | collective-permute-start | bytes 786440 | tf_op jit(solution)/shard_map/ppermute | solution.py:23
  7.0 20.8 %slice-start = ((s8[6291456]{0:T(1024)(128)(4,1)}), s8[4194304]{0:T(1024)(128)(4,1)S(1)}, s32[]{:S(2)}) async-start(s8[6291456]{0:T(1024)(128)(4,1)} %bitcast.163), calls=%async_computation | async-start | bytes 8388608
  12.5 15.3 %slice-start.1 = ((s8[6291456]{0:T(1024)(128)(4,1)}), s8[2097152]{0:T(1024)(128)(4,1)S(1)}, s32[]{:S(2)}) async-start(s8[6291456]{0:T(1024)(128)(4,1)} %bitcast.163), calls=%async_computation.1 | async-start | bytes 4194304
  17.9 11.3 %collective-permute-start.2 = (bf16[48,512]{1,0:T(8,128)(2,1)S(1)}, bf16[48,512]{1,0:T(8,128)(2,1)S(1)}, u32[]{:S(2)}, u32[]{:S(2)}) collective-permute-start(bf16[48,512]{1,0:T(8,128)(2,1)S(1)} %get-tuple-element.84.payload), channel_id=1, source_target_pairs={{0,8},{4,12},{8,16},{12,20},{16,24},{20,28},{24,0},{28,4},{1,9},{5... | collective-permute-start | bytes 147464 | tf_op jit(solution)/shard_map/ppermute | solution.py:553
  23.9 5.3 %collective-permute-start.3 = (bf16[48,512]{1,0:T(8,128)(2,1)S(1)}, bf16[48,512]{1,0:T(8,128)(2,1)S(1)}, u32[]{:S(2)}, u32[]{:S(2)}) collective-permute-start(bf16[48,512]{1,0:T(8,128)(2,1)S(1)} %get-tuple-element.84.payload), channel_id=1, source_target_pairs={{0,16},{4,20},{8,24},{12,28},{16,0},{20,4},{24,8},{28,12},{1,17},{... | collective-permute-start | bytes 147464 | tf_op jit(solution)/shard_map/ppermute | solution.py:553
  26.4 4.1 %collective-permute-start.4 = (bf16[48,512]{1,0:T(8,128)(2,1)S(1)}, bf16[48,512]{1,0:T(8,128)(2,1)S(1)}, u32[]{:S(2)}, u32[]{:S(2)}) collective-permute-start(bf16[48,512]{1,0:T(8,128)(2,1)S(1)} %get-tuple-element.84.payload), channel_id=1, source_target_pairs={{0,24},{4,28},{8,0},{12,4},{16,8},{20,12},{24,16},{28,20},{1,25},{... | collective-permute-start | bytes 147464 | tf_op jit(solution)/shard_map/ppermute | solution.py:553
  30.5 13.9 %copy-start.1 = (bf16[512,2048]{1,0:T(8,128)(2,1)S(1)}, bf16[512,2048]{1,0:T(8,128)(2,1)}, u32[]{:S(2)}) copy-start(bf16[512,2048]{1,0:T(8,128)(2,1)} %refs_5_.7) | copy-start | bytes 6291460
  30.6 5.2 %collective-permute-start.7 = (bf16[4,48,256]{2,1,0:T(8,128)(2,1)S(1)}, bf16[4,48,256]{2,1,0:T(8,128)(2,1)S(1)}, u32[]{:S(2)}, u32[]{:S(2)}) collective-permute-start(bf16[4,48,256]{2,1,0:T(8,128)(2,1)S(1)} %get-tuple-element.150), channel_id=1, source_target_pairs={{0,2},{1,3},{2,0},{3,1},{4,6},{5,7},{6,4},{7,5},{8,10},{9,11},{10,... | collective-permute-start | bytes 294920 | tf_op jit(solution)/shard_map/ppermute | solution.py:553
  30.7 6.1 %collective-permute-start.5 = (bf16[4,48,256]{2,1,0:T(8,128)(2,1)S(1)}, bf16[4,48,256]{2,1,0:T(8,128)(2,1)S(1)}, u32[]{:S(2)}, u32[]{:S(2)}) collective-permute-start(bf16[4,48,256]{2,1,0:T(8,128)(2,1)S(1)} %get-tuple-element.151), channel_id=1, source_target_pairs={{0,4},{4,0},{8,12},{12,8},{16,20},{20,16},{24,28},{28,24},{1,5},{5... | collective-permute-start | bytes 294920 | tf_op jit(solution)/shard_map/ppermute | solution.py:553
  35.8 5.7 %collective-permute-start.8 = (bf16[4,2,48,256]{3,2,0,1:T(8,128)(2,1)S(1)}, bf16[4,2,48,256]{3,2,0,1:T(8,128)(2,1)S(1)}, u32[]{:S(2)}, u32[]{:S(2)}) collective-permute-start(bf16[4,2,48,256]{3,2,0,1:T(8,128)(2,1)S(1)} %get-tuple-element.147), channel_id=1, source_target_pairs={{0,4},{4,0},{8,12},{12,8},{16,20},{20,16},{24,28},{28,24},{1,5},{5... | collective-permute-start | bytes 589832 | tf_op jit(solution)/shard_map/ppermute | solution.py:553
  36.8 7.6 %copy-start.3 = (f32[2048,4]{0,1:T(4,128)S(1)}, f32[2048,4]{0,1:T(4,128)}, u32[]{:S(2)}) copy-start(f32[2048,4]{0,1:T(4,128)} %param.27) | copy-start | bytes 98308
  36.8 5.7 %collective-permute-start.6 = (bf16[4,2,48,256]{3,2,0,1:T(8,128)(2,1)S(1)}, bf16[4,2,48,256]{3,2,0,1:T(8,128)(2,1)S(1)}, u32[]{:S(2)}, u32[]{:S(2)}) collective-permute-start(bf16[4,2,48,256]{3,2,0,1:T(8,128)(2,1)S(1)} %get-tuple-element.153), channel_id=1, source_target_pairs={{0,2},{1,3},{2,0},{3,1},{4,6},{5,7},{6,4},{7,5},{8,10},{9,11},{10,... | collective-permute-start | bytes 589832 | tf_op jit(solution)/shard_map/ppermute | solution.py:553
  41.6 2.8 %copy-start = (bf16[1,768,2048]{2,1,0:T(8,128)(2,1)S(1)}, bf16[1,768,2048]{2,1,0:T(8,128)(2,1)}, u32[]{:S(2)}) copy-start(bf16[1,768,2048]{2,1,0:T(8,128)(2,1)} %param.29) | copy-start | bytes 9437188
  41.6 2.8 %copy-start.4 = (f32[2048]{0:T(1024)S(1)}, f32[2048]{0:T(1024)}, u32[]{:S(2)}) copy-start(f32[2048]{0:T(1024)} %param.26) | copy-start | bytes 24580
  41.7 1.8 %collective-permute-start.10 = (bf16[16,48,256]{2,1,0:T(8,128)(2,1)S(1)}, bf16[16,48,256]{2,1,0:T(8,128)(2,1)S(1)}, u32[]{:S(2)}, u32[]{:S(2)}) collective-permute-start(bf16[16,48,256]{2,1,0:T(8,128)(2,1)S(1)} %bitcast.135), channel_id=1, source_target_pairs={{0,1},{1,0},{2,3},{3,2},{4,5},{5,4},{6,7},{7,6},{8,9},{9,8},{10,11... | collective-permute-start | bytes 1179656 | tf_op jit(solution)/shard_map/ppermute | solution.py:553
  42.6 1.8 %collective-permute-start.9 = (bf16[16,48,256]{2,1,0:T(8,128)(2,1)S(1)}, bf16[16,48,256]{2,1,0:T(8,128)(2,1)S(1)}, u32[]{:S(2)}, u32[]{:S(2)}) collective-permute-start(bf16[16,48,256]{2,1,0:T(8,128)(2,1)S(1)} %bitcast.139), channel_id=1, source_target_pairs={{0,1},{1,0},{2,3},{3,2},{4,5},{5,4},{6,7},{7,6},{8,9},{9,8},{10,11... | collective-permute-start | bytes 1179656 | tf_op jit(solution)/shard_map/ppermute | solution.py:553
  48.0 1.7 %collective-permute-start.11 = (bf16[2,2,1,40,1024]{4,3,1,2,0:T(8,128)(2,1)S(1)}, bf16[2,2,1,40,1024]{4,3,1,2,0:T(8,128)(2,1)S(1)}, u32[]{:S(2)}, u32[]{:S(2)}) collective-permute-start(bf16[2,2,1,40,1024]{4,3,1,2,0:T(8,128)(2,1)S(1)} %bitcast.162), channel_id=1, source_target_pairs={{0,1},{1,0},{2,3},{3,2},{4,5},{5,4},{6,7},{7,6},{8,9},{9,8},{10,11... | collective-permute-start | bytes 983048 | tf_op jit(solution)/shard_map/ppermute | solution.py:553
  48.2 2.9 %collective-permute-start.12 = (bf16[2,2,1,40,1024]{4,3,1,2,0:T(8,128)(2,1)S(1)}, bf16[2,2,1,40,1024]{4,3,1,2,0:T(8,128)(2,1)S(1)}, u32[]{:S(2)}, u32[]{:S(2)}) collective-permute-start(bf16[2,2,1,40,1024]{4,3,1,2,0:T(8,128)(2,1)S(1)} %bitcast.161), channel_id=1, source_target_pairs={{0,1},{1,0},{2,3},{3,2},{4,5},{5,4},{6,7},{7,6},{8,9},{9,8},{10,11... | collective-permute-start | bytes 983048 | tf_op jit(solution)/shard_map/ppermute | solution.py:553
  49.8 9.1 %collective-permute-start.13 = (bf16[2,1,40,1024]{3,2,1,0:T(8,128)(2,1)S(1)}, bf16[2,1,40,1024]{3,2,1,0:T(8,128)(2,1)S(1)}, u32[]{:S(2)}, u32[]{:S(2)}) collective-permute-start(bf16[2,1,40,1024]{3,2,1,0:T(8,128)(2,1)S(1)} %get-tuple-element.143), channel_id=1, source_target_pairs={{0,4},{4,0},{8,12},{12,8},{16,20},{20,16},{24,28},{28,24},{1,5},{5... | collective-permute-start | bytes 491528 | tf_op jit(solution)/shard_map/ppermute | solution.py:553
  51.2 7.8 %collective-permute-start.14 = (bf16[2,1,40,1024]{3,2,1,0:T(8,128)(2,1)S(1)}, bf16[2,1,40,1024]{3,2,1,0:T(8,128)(2,1)S(1)}, u32[]{:S(2)}, u32[]{:S(2)}) collective-permute-start(bf16[2,1,40,1024]{3,2,1,0:T(8,128)(2,1)S(1)} %get-tuple-element.145), channel_id=1, source_target_pairs={{0,2},{1,3},{2,0},{3,1},{4,6},{5,7},{6,4},{7,5},{8,10},{9,11},{10,... | collective-permute-start | bytes 491528 | tf_op jit(solution)/shard_map/ppermute | solution.py:553
  58.4 4.8 %collective-permute-start.16 = (bf16[2,2,2,40,1024]{4,3,2,1,0:T(8,128)(2,1)S(1)}, bf16[2,2,2,40,1024]{4,3,2,1,0:T(8,128)(2,1)S(1)}, u32[]{:S(2)}, u32[]{:S(2)}) collective-permute-start(bf16[2,2,2,40,1024]{4,3,2,1,0:T(8,128)(2,1)S(1)} %bitcast.157), channel_id=1, source_target_pairs={{0,1},{1,0},{2,3},{3,2},{4,5},{5,4},{6,7},{7,6},{8,9},{9,8},{10,11... | collective-permute-start | bytes 1966088 | tf_op jit(solution)/shard_map/ppermute | solution.py:553
  58.5 4.4 %collective-permute-start.15 = (bf16[2,2,2,40,1024]{4,3,2,1,0:T(8,128)(2,1)S(1)}, bf16[2,2,2,40,1024]{4,3,2,1,0:T(8,128)(2,1)S(1)}, u32[]{:S(2)}, u32[]{:S(2)}) collective-permute-start(bf16[2,2,2,40,1024]{4,3,2,1,0:T(8,128)(2,1)S(1)} %bitcast.158), channel_id=1, source_target_pairs={{0,1},{1,0},{2,3},{3,2},{4,5},{5,4},{6,7},{7,6},{8,9},{9,8},{10,11... | collective-permute-start | bytes 1966088 | tf_op jit(solution)/shard_map/ppermute | solution.py:553
  59.1 8.0 %collective-permute-start.17 = (bf16[1,40,1024]{2,1,0:T(8,128)(2,1)S(1)}, bf16[1,40,1024]{2,1,0:T(8,128)(2,1)S(1)}, u32[]{:S(2)}, u32[]{:S(2)}) collective-permute-start(bf16[1,40,1024]{2,1,0:T(8,128)(2,1)S(1)} %get-tuple-element.163), channel_id=1, source_target_pairs={{0,2},{1,3},{2,0},{3,1},{4,6},{5,7},{6,4},{7,5},{8,10},{9,11},{10,... | collective-permute-start | bytes 245768 | tf_op jit(solution)/shard_map/ppermute | solution.py:553
  60.6 6.5 %collective-permute-start.18 = (bf16[1,40,1024]{2,1,0:T(8,128)(2,1)S(1)}, bf16[1,40,1024]{2,1,0:T(8,128)(2,1)S(1)}, u32[]{:S(2)}, u32[]{:S(2)}) collective-permute-start(bf16[1,40,1024]{2,1,0:T(8,128)(2,1)S(1)} %get-tuple-element.165), channel_id=1, source_target_pairs={{0,4},{4,0},{8,12},{12,8},{16,20},{20,16},{24,28},{28,24},{1,5},{5... | collective-permute-start | bytes 245768 | tf_op jit(solution)/shard_map/ppermute | solution.py:553
  67.1 9.2 %collective-permute-start.20 = (bf16[2,2,40,1024]{3,2,1,0:T(8,128)(2,1)S(1)}, bf16[2,2,40,1024]{3,2,1,0:T(8,128)(2,1)S(1)}, u32[]{:S(2)}, u32[]{:S(2)}) collective-permute-start(bf16[2,2,40,1024]{3,2,1,0:T(8,128)(2,1)S(1)} %get-tuple-element.135), channel_id=1, source_target_pairs={{0,4},{4,0},{8,12},{12,8},{16,20},{20,16},{24,28},{28,24},{1,5},{5... | collective-permute-start | bytes 983048 | tf_op jit(solution)/shard_map/ppermute | solution.py:553
  68.4 8.9 %collective-permute-start.22 = (bf16[2,2,40,1024]{3,2,1,0:T(8,128)(2,1)S(1)}, bf16[2,2,40,1024]{3,2,1,0:T(8,128)(2,1)S(1)}, u32[]{:S(2)}, u32[]{:S(2)}) collective-permute-start(bf16[2,2,40,1024]{3,2,1,0:T(8,128)(2,1)S(1)} %get-tuple-element.137), channel_id=1, source_target_pairs={{0,2},{1,3},{2,0},{3,1},{4,6},{5,7},{6,4},{7,5},{8,10},{9,11},{10,... | collective-permute-start | bytes 983048 | tf_op jit(solution)/shard_map/ppermute | solution.py:553
  69.0 23.3 %collective-permute-start.19 = (bf16[40,2048]{1,0:T(8,128)(2,1)S(1)}, bf16[40,2048]{1,0:T(8,128)(2,1)S(1)}, u32[]{:S(2)}, u32[]{:S(2)}) collective-permute-start(bf16[40,2048]{1,0:T(8,128)(2,1)S(1)} %pad_maximum_fusion.5), channel_id=1, source_target_pairs={{0,16},{4,20},{8,24},{12,28},{16,0},{20,4},{24,8},{28,12},{1,17},{... | collective-permute-start | bytes 491528 | tf_op jit(solution)/shard_map/ppermute | solution.py:553
  70.4 10.3 %collective-permute-start.29 = (bf16[2,2,1,40,1024]{4,3,1,2,0:T(8,128)(2,1)S(1)}, bf16[2,2,1,40,1024]{4,3,1,2,0:T(8,128)(2,1)S(1)}, u32[]{:S(2)}, u32[]{:S(2)}) collective-permute-start(bf16[2,2,1,40,1024]{4,3,1,2,0:T(8,128)(2,1)S(1)} %bitcast.160), channel_id=1, source_target_pairs={{0,1},{1,0},{2,3},{3,2},{4,5},{5,4},{6,7},{7,6},{8,9},{9,8},{10,11... | collective-permute-start | bytes 983048 | tf_op jit(solution)/shard_map/ppermute | solution.py:553
  70.4 11.1 %collective-permute-start.26 = (bf16[2,2,1,40,1024]{4,3,1,2,0:T(8,128)(2,1)S(1)}, bf16[2,2,1,40,1024]{4,3,1,2,0:T(8,128)(2,1)S(1)}, u32[]{:S(2)}, u32[]{:S(2)}) collective-permute-start(bf16[2,2,1,40,1024]{4,3,1,2,0:T(8,128)(2,1)S(1)} %bitcast.159), channel_id=1, source_target_pairs={{0,1},{1,0},{2,3},{3,2},{4,5},{5,4},{6,7},{7,6},{8,9},{9,8},{10,11... | collective-permute-start | bytes 983048 | tf_op jit(solution)/shard_map/ppermute | solution.py:553
  77.4 6.9 %collective-permute-start.21 = (bf16[2,40,1024]{2,1,0:T(8,128)(2,1)S(1)}, bf16[2,40,1024]{2,1,0:T(8,128)(2,1)S(1)}, u32[]{:S(2)}, u32[]{:S(2)}) collective-permute-start(bf16[2,40,1024]{2,1,0:T(8,128)(2,1)S(1)} %slice_bitcast_fusion.10), channel_id=1, source_target_pairs={{0,2},{1,3},{2,0},{3,1},{4,6},{5,7},{6,4},{7,5},{8,10},{9,11},{10,... | collective-permute-start | bytes 491528 | tf_op jit(solution)/shard_map/ppermute | solution.py:553
  78.2 7.1 %collective-permute-start.23 = (bf16[2,40,1024]{2,1,0:T(8,128)(2,1)S(1)}, bf16[2,40,1024]{2,1,0:T(8,128)(2,1)S(1)}, u32[]{:S(2)}, u32[]{:S(2)}) collective-permute-start(bf16[2,40,1024]{2,1,0:T(8,128)(2,1)S(1)} %slice_bitcast_fusion.8), channel_id=1, source_target_pairs={{0,4},{4,0},{8,12},{12,8},{16,20},{20,16},{24,28},{28,24},{1,5},{5... | collective-permute-start | bytes 491528 | tf_op jit(solution)/shard_map/ppermute | solution.py:553
  80.9 8.4 %collective-permute-start.30 = (bf16[2,1,40,1024]{3,2,1,0:T(8,128)(2,1)S(1)}, bf16[2,1,40,1024]{3,2,1,0:T(8,128)(2,1)S(1)}, u32[]{:S(2)}, u32[]{:S(2)}) collective-permute-start(bf16[2,1,40,1024]{3,2,1,0:T(8,128)(2,1)S(1)} %get-tuple-element.139), channel_id=1, source_target_pairs={{0,2},{1,3},{2,0},{3,1},{4,6},{5,7},{6,4},{7,5},{8,10},{9,11},{10,... | collective-permute-start | bytes 491528 | tf_op jit(solution)/shard_map/ppermute | solution.py:553
  81.6 9.0 %collective-permute-start.27 = (bf16[2,1,40,1024]{3,2,1,0:T(8,128)(2,1)S(1)}, bf16[2,1,40,1024]{3,2,1,0:T(8,128)(2,1)S(1)}, u32[]{:S(2)}, u32[]{:S(2)}) collective-permute-start(bf16[2,1,40,1024]{3,2,1,0:T(8,128)(2,1)S(1)} %get-tuple-element.141), channel_id=1, source_target_pairs={{0,4},{4,0},{8,12},{12,8},{16,20},{20,16},{24,28},{28,24},{1,5},{5... | collective-permute-start | bytes 491528 | tf_op jit(solution)/shard_map/ppermute | solution.py:553
  84.4 7.2 %copy-start.2 = (bf16[512,512]{1,0:T(8,128)(2,1)S(1)}, bf16[512,512]{1,0:T(8,128)(2,1)}, u32[]{:S(2)}) copy-start(bf16[512,512]{1,0:T(8,128)(2,1)} %w_dq.1) | copy-start | bytes 1572868
  84.4 7.2 %copy-start.5 = (f32[512]{0:T(512)S(1)}, f32[512]{0:T(512)}, u32[]{:S(2)}) copy-start(f32[512]{0:T(512)} %param.30) | copy-start | bytes 6148
  85.4 9.9 %collective-permute-start.25 = (bf16[40,2048]{1,0:T(8,128)(2,1)S(1)}, bf16[40,2048]{1,0:T(8,128)(2,1)S(1)}, u32[]{:S(2)}, u32[]{:S(2)}) collective-permute-start(bf16[40,2048]{1,0:T(8,128)(2,1)S(1)} %pad_maximum_fusion.7), channel_id=1, source_target_pairs={{0,8},{4,12},{8,16},{12,20},{16,24},{20,28},{24,0},{28,4},{1,9},{5... | collective-permute-start | bytes 491528 | tf_op jit(solution)/shard_map/ppermute | solution.py:553
  85.9 9.3 %copy-start.6 = (bf16[2048,1024]{1,0:T(8,128)(2,1)S(1)}, bf16[2048,1024]{1,0:T(8,128)(2,1)}, u32[]{:S(2)}) copy-start(bf16[2048,1024]{1,0:T(8,128)(2,1)} %refs_11_.1) | copy-start | bytes 12582916
  86.0 9.3 %collective-permute-start.24 = (bf16[40,2048]{1,0:T(8,128)(2,1)S(1)}, bf16[40,2048]{1,0:T(8,128)(2,1)S(1)}, u32[]{:S(2)}, u32[]{:S(2)}) collective-permute-start(bf16[40,2048]{1,0:T(8,128)(2,1)S(1)} %pad_maximum_fusion.6), channel_id=1, source_target_pairs={{0,24},{4,28},{8,0},{12,4},{16,8},{20,12},{24,16},{28,20},{1,25},{... | collective-permute-start | bytes 491528 | tf_op jit(solution)/shard_map/ppermute | solution.py:553
  89.4 4.5 %collective-permute-start.31 = (bf16[1,40,1024]{2,1,0:T(8,128)(2,1)S(1)}, bf16[1,40,1024]{2,1,0:T(8,128)(2,1)S(1)}, u32[]{:S(2)}, u32[]{:S(2)}) collective-permute-start(bf16[1,40,1024]{2,1,0:T(8,128)(2,1)S(1)} %get-tuple-element.154), channel_id=1, source_target_pairs={{0,4},{4,0},{8,12},{12,8},{16,20},{20,16},{24,28},{28,24},{1,5},{5... | collective-permute-start | bytes 245768 | tf_op jit(solution)/shard_map/ppermute | solution.py:553
  90.7 4.6 %copy-start.7 = (bf16[512,512]{1,0:T(8,128)(2,1)S(1)}, bf16[512,512]{1,0:T(8,128)(2,1)}, u32[]{:S(2)}) copy-start(bf16[512,512]{1,0:T(8,128)(2,1)} %refs_12_.1) | copy-start | bytes 1572868
  90.7 4.5 %collective-permute-start.28 = (bf16[1,40,1024]{2,1,0:T(8,128)(2,1)S(1)}, bf16[1,40,1024]{2,1,0:T(8,128)(2,1)S(1)}, u32[]{:S(2)}, u32[]{:S(2)}) collective-permute-start(bf16[1,40,1024]{2,1,0:T(8,128)(2,1)S(1)} %get-tuple-element.156), channel_id=1, source_target_pairs={{0,2},{1,3},{2,0},{3,1},{4,6},{5,7},{6,4},{7,5},{8,10},{9,11},{10,... | collective-permute-start | bytes 245768 | tf_op jit(solution)/shard_map/ppermute | solution.py:553
